TPU v7x, 32 devices: a whole 2x2x4 slice. The times are simulated.
32 devices in a mesh: grp: 4 (over y, core), gy: 2 (over x), gx: 4 (over z).
Axes of the slice: x: 2, y: 2, z: 4, core: 2. Of those that a mesh axis runs over, the one named last changes fastest.
Arguments:
- design: float32 [8, 16, 512], P('grp', 'gy', 'gx'), may hold values from 0 to 1
- populations: float32 [19, 8, 16, 512], P(None, 'grp', 'gy', 'gx'), may hold values from 0.02 to 0.1
- cotangent: float32 [19, 8, 16, 512], P(None, 'grp', 'gy', 'gx'), may hold values from -150 to 150
- wall_mask: int32 [8, 16, 512], P('grp', 'gy', 'gx'), may hold values 0 or 1
- inlet_mask: int32 [8, 16, 512], P('grp', 'gy', 'gx'), may hold values 0 or 1
- beta_step: int32 [], replicated, may hold values from 0 to 64
Outputs:
- final_populations: float32 [19, 8, 16, 512], P(None, 'grp', 'gy', 'gx')
- design_grad: float32 [8, 16, 512], P('grp', 'gy', 'gx')
All inputs are finite; a program needn't handle non-finite values. No bound on the sum of `wall_mask` or of `inlet_mask` on one device may be relied on, other than what follows from the above.
Results may differ from a plain program's by a relative error of at most 0.0003.
Values sent between devices are 32-bit elements; how exact they have to be, the bound alone decides.
No kernel may reach another device: no remote copies, remote signals or barrier semaphores. Data moves between devices by JAX's collectives and lax.ppermute only.
A program may use at most 64 MiB of HBM per device.

v0:
```python
import jax
import jax.numpy as jnp
import numpy as np
from jax import lax
from jax.sharding import PartitionSpec as P

STEPS = 4
BISECT = 30


velocities = np.array(
    [
        [0, 0, 0],
        [1, 0, 0],
        [-1, 0, 0],
        [0, 1, 0],
        [0, -1, 0],
        [0, 0, 1],
        [0, 0, -1],
        [1, 1, 0],
        [-1, -1, 0],
        [1, -1, 0],
        [-1, 1, 0],
        [1, 0, 1],
        [-1, 0, -1],
        [1, 0, -1],
        [-1, 0, 1],
        [0, 1, 1],
        [0, -1, -1],
        [0, 1, -1],
        [0, -1, 1],
    ]
)
opposite = [0, 2, 1, 4, 3, 6, 5, 8, 7, 10, 9, 12, 11, 14, 13, 16, 15, 18, 17]
lattice_weights = [1.0 / 3.0] + [1.0 / 18.0] * 6 + [1.0 / 36.0] * 12
relax_rate = 0.8
inlet_speed = 0.05
alpha_most = 8.0
penalty_shape = 0.1
fluid_share = 0.4


def extended(value, sides, width):
    for axis, dim in sides:
        size, length = (lax.axis_size(axis), value.shape[dim])
        up = [(i, (i + 1) % size) for i in range(size - 1)]
        down = [(j, i) for i, j in up]
        last = lax.slice_in_dim(value, length - width, length, axis=dim)
        leading = lax.slice_in_dim(value, 0, width, axis=dim)
        before = lax.ppermute(last, axis, up)
        after = lax.ppermute(leading, axis, down)
        value = jnp.concatenate([before, value, after], axis=dim)
    return value


def equilibrium(density, speed_z, speed_y, speed_x):
    square = speed_z * speed_z + speed_y * speed_y + speed_x * speed_x
    comps = []
    for i in range(19):
        along = (
            float(velocities[i][0]) * speed_z
            + float(velocities[i][1]) * speed_y
            + float(velocities[i][2]) * speed_x
        )
        comps.append(
            lattice_weights[i] * density * (1.0 + 3.0 * along + 4.5 * along * along - 1.5 * square)
        )
    return jnp.stack(comps)


def moment(popul, axis):
    total = jnp.zeros(popul.shape[1:], popul.dtype)
    for i in range(1, 19):
        if velocities[i][axis] != 0:
            total = total + float(velocities[i][axis]) * popul[i]
    return total


def collide(popul, alpha, wall_mask, inlet_mask):
    density = jnp.sum(popul, axis=0)
    scale = density * (1.0 + alpha)
    feq = equilibrium(
        density, moment(popul, 0) / scale, moment(popul, 1) / scale, moment(popul, 2) / scale
    )
    post = popul + relax_rate * (feq - popul)
    bounce = jnp.stack([popul[opposite[i]] for i in range(19)])
    inlet_values = []
    for i in range(19):
        along = float(velocities[i][0]) * inlet_speed
        inlet_values.append(
            lattice_weights[i]
            * (1.0 + 3.0 * along + 4.5 * along * along - 1.5 * inlet_speed * inlet_speed)
        )
    inlet_feq = jnp.stack([jnp.full(popul.shape[1:], value, popul.dtype) for value in inlet_values])
    return jnp.where(wall_mask[None] > 0, bounce, jnp.where(inlet_mask[None] > 0, inlet_feq, post))


def pick(padded, sign):
    depth, rows, cols = (padded.shape[1] - 2, padded.shape[2] - 2, padded.shape[3] - 2)
    outputs = []
    for i in range(19):
        start_z = 1 - sign * int(velocities[i][0])
        start_y = 1 - sign * int(velocities[i][1])
        start_x = 1 - sign * int(velocities[i][2])
        outputs.append(
            padded[i, start_z : start_z + depth, start_y : start_y + rows, start_x : start_x + cols]
        )
    return jnp.stack(outputs)


def shift_all(popul, sign):
    padded = extended(popul, (("grp", 1), ("gy", 2), ("gx", 3)), 1)
    return pick(padded, sign)


def smooth_field(field):
    padded = extended(field, (("grp", 0), ("gy", 1), ("gx", 2)), 1)
    along_z = 0.25 * padded[:-2] + 0.5 * padded[1:-1] + 0.25 * padded[2:]
    along_y = 0.25 * along_z[:, :-2] + 0.5 * along_z[:, 1:-1] + 0.25 * along_z[:, 2:]
    return 0.25 * along_y[:, :, :-2] + 0.5 * along_y[:, :, 1:-1] + 0.25 * along_y[:, :, 2:]


def project(filtered, thresh, beta):
    denom = jnp.tanh(beta * thresh) + jnp.tanh(beta * (1.0 - thresh))
    return (jnp.tanh(beta * thresh) + jnp.tanh(beta * (filtered - thresh))) / denom


def body(design, populations, cotangent, wall_mask, inlet_mask, beta_step):
    beta = jnp.exp2(beta_step.astype(jnp.float32) / 16.0)
    filtered = smooth_field(design)
    cells = design.size * lax.axis_size("grp") * lax.axis_size("gy") * lax.axis_size("gx")
    flat = filtered.reshape(1, -1)
    offsets = (jnp.arange(1, 1025, dtype=jnp.float32) / 1024.0).reshape(8, 128)
    usable = (jnp.arange(1024) < 1023).astype(jnp.float32)
    low = jnp.zeros((), jnp.float32)
    width = 1.0
    for turn in range(BISECT // 10):
        trials = low + width * offsets

        def block_sums(row):
            return jnp.sum(project(flat, row[:, None], beta), axis=1)

        local = lax.map(block_sums, trials)
        totals = lax.psum(local, ("grp", "gy", "gx"))
        above = (totals.reshape(-1) > fluid_share * cells).astype(jnp.float32)
        count = jnp.sum(above * usable)
        low = low + width * count / 1024.0
        width = width / 1024.0
    eta = low + 0.5 * width
    density_hat = project(filtered, eta, beta)
    alpha = alpha_most * penalty_shape * (1.0 - density_hat) / (penalty_shape + density_hat)
    states = []
    popul = populations
    for step in range(STEPS):
        states.append(popul)
        popul = shift_all(collide(popul, alpha, wall_mask, inlet_mask), 1)
    adjoint = cotangent
    alpha_grad = jnp.zeros_like(alpha)
    for step in reversed(range(STEPS)):
        back = shift_all(adjoint, -1)
        unused, pullback = jax.vjp(
            lambda p, a: collide(p, a, wall_mask, inlet_mask), states[step], alpha
        )
        adjoint, term = pullback(back)
        alpha_grad = alpha_grad + term
    denom = jnp.tanh(beta * eta) + jnp.tanh(beta * (1.0 - eta))
    slope = beta * (1.0 - jnp.tanh(beta * (filtered - eta)) ** 2) / denom
    factor = (
        -alpha_most * penalty_shape * (1.0 + penalty_shape) / (penalty_shape + density_hat) ** 2
    )
    design_grad = smooth_field(alpha_grad * factor * slope)
    return (popul, design_grad)


def solution(mesh):
    placed = (
        P("grp", "gy", "gx"),
        P(None, "grp", "gy", "gx"),
        P(None, "grp", "gy", "gx"),
        P("grp", "gy", "gx"),
        P("grp", "gy", "gx"),
        P(),
    )
    return jax.shard_map(
        body,
        mesh=mesh,
        in_specs=placed,
        out_specs=(P(None, "grp", "gy", "gx"), P("grp", "gy", "gx")),
        check_vma=False,
    )
```

profile of v0, /device:TPU:0, one launch (start us, length us, event | category | flops | bytes accessed | tf_op | source)
XLA Modules:
  0.0 384.6 jit_solution(15240285057462743839)
XLA Ops:
  1.3 2.3 collective-permute-start
  3.7 1.4 collective-permute-start.1
  6.1 5.2 %collective-permute-start.31 = (f32[19,1,8,128]{3,2,1,0:T(8,128)S(1)}, f32[19,1,8,128]{3,2,1,0:T(8,128)S(1)}, u32[]{:S(2)}, u32[]{:S(2)}) collective-permute-start(f32[19,1,8,128]{3,2,1,0:T(8,128)S(1)} %get-tuple-element.490), channel_id=1, source_target_pairs={{0,8},{8,16},{16,24},{1,9},{9,17},{17,25},{2,10},{10,18},{18,26},{... | collective-permute-start | bytes 233480 | tf_op jit(solution)/shard_map/ppermute | solution.py:50
  11.3 1.3 collective-permute-start.30
  14.2 3.4 collective-permute-start.2
  17.6 1.3 collective-permute-start.3
  19.6 3.5 collective-permute-done.3
  23.2 3.5 collective-permute-start.4
  26.7 1.3 collective-permute-start.5
  28.4 4.1 %collective-permute-done.5 = f32[4,10,1]{2,1,0:T(8,128)S(1)} collective-permute-done((f32[4,10,1]{2,1,0:T(8,128)S(1)}, f32[4,10,1]{2,1,0:T(8,128)S(1)}, u32[]{:S(2)}, u32[]{:S(2)}) %collective-permute-start.5) | collective-permute-done | bytes 192 | tf_op jit(solution)/shard_map/ppermute | solution.py:51
  32.7 3.5 while.30
  36.2 41.5 %psum.21 = f32[8,128]{1,0:T(8,128)S(1)} all-reduce(f32[8,128]{1,0:T(8,128)S(1)} %get-tuple-element.83), channel_id=1, replica_groups=mesh['grp'=4,'gy'=2,'gx'=4] {'grp','gy','gx'}, use_global_device_ids=true, to_apply=%region_4.5 | all-reduce | flops 1024 | bytes 8192 | tf_op jit(solution)/shard_map/psum | solution.py:144
  79.0 3.5 while.31
  82.5 40.2 %psum.22 = f32[8,128]{1,0:T(8,128)S(1)} all-reduce(f32[8,128]{1,0:T(8,128)S(1)} %get-tuple-element.84), channel_id=1, replica_groups=mesh['grp'=4,'gy'=2,'gx'=4] {'grp','gy','gx'}, use_global_device_ids=true, to_apply=%region_9.10 | all-reduce | flops 1024 | bytes 8192 | tf_op jit(solution)/shard_map/psum | solution.py:144
  124.0 3.5 while.32
  127.5 40.0 %psum.23 = f32[8,128]{1,0:T(8,128)S(1)} all-reduce(f32[8,128]{1,0:T(8,128)S(1)} %get-tuple-element.85), channel_id=1, replica_groups=mesh['grp'=4,'gy'=2,'gx'=4] {'grp','gy','gx'}, use_global_device_ids=true, to_apply=%region_14.15 | all-reduce | flops 1024 | bytes 8192 | tf_op jit(solution)/shard_map/psum | solution.py:144
  170.2 1.3 collective-permute-start.6
  171.5 3.0 collective-permute-start.7
  174.7 1.3 collective-permute-start.32
  176.0 4.5 %collective-permute-start.33 = (f32[19,4,1,128]{3,2,1,0:T(1,128)S(1)}, f32[19,4,1,128]{3,2,1,0:T(1,128)S(1)}, u32[]{:S(2)}, u32[]{:S(2)}) collective-permute-start(f32[19,4,1,128]{3,2,1,0:T(1,128)S(1)} %get-tuple-element.328), channel_id=1, source_target_pairs={{0,4},{1,5},{2,6},{3,7},{8,12},{9,13},{10,14},{11,15},{16,20},{17,... | collective-permute-start | bytes 116744 | tf_op jit(solution)/shard_map/ppermute | solution.py:50
  180.6 1.3 collective-permute-start.8
  181.9 4.5 %collective-permute-start.9 = (f32[19,4,1,128]{3,2,1,0:T(1,128)S(1)}, f32[19,4,1,128]{3,2,1,0:T(1,128)S(1)}, u32[]{:S(2)}, u32[]{:S(2)}) collective-permute-start(f32[19,4,1,128]{3,2,1,0:T(1,128)S(1)} %get-tuple-element.332), channel_id=1, source_target_pairs={{0,4},{1,5},{2,6},{3,7},{8,12},{9,13},{10,14},{11,15},{16,20},{17,... | collective-permute-start | bytes 116744 | tf_op jit(solution)/shard_map/ppermute | solution.py:50
  189.0 4.5 %collective-permute-start.35 = (f32[19,4,10,1]{0,1,3,2:T(4,128)S(1)}, f32[19,4,10,1]{0,1,3,2:T(4,128)S(1)}, u32[]{:S(2)}, u32[]{:S(2)}) collective-permute-start(f32[19,4,10,1]{0,1,3,2:T(4,128)S(1)} %copy.147), channel_id=1, source_target_pairs={{0,1},{1,2},{2,3},{4,5},{5,6},{6,7},{8,9},{9,10},{10,11},{12,13},{... | collective-permute-start | bytes 9128 | tf_op jit(solution)/shard_map/ppermute | solution.py:50
  199.0 4.8 %collective-permute-start.11 = (f32[19,4,10,1]{0,1,3,2:T(4,128)S(1)}, f32[19,4,10,1]{0,1,3,2:T(4,128)S(1)}, u32[]{:S(2)}, u32[]{:S(2)}) collective-permute-start(f32[19,4,10,1]{0,1,3,2:T(4,128)S(1)} %copy.131), channel_id=1, source_target_pairs={{0,1},{1,2},{2,3},{4,5},{5,6},{6,7},{8,9},{9,10},{10,11},{12,13},{... | collective-permute-start | bytes 9128 | tf_op jit(solution)/shard_map/ppermute | solution.py:50
  207.0 1.3 collective-permute-start.12
  208.3 3.0 collective-permute-start.13
  212.3 1.3 collective-permute-start.14
  213.6 4.5 %collective-permute-start.15 = (f32[19,4,1,128]{3,2,1,0:T(1,128)S(1)}, f32[19,4,1,128]{3,2,1,0:T(1,128)S(1)}, u32[]{:S(2)}, u32[]{:S(2)}) collective-permute-start(f32[19,4,1,128]{3,2,1,0:T(1,128)S(1)} %get-tuple-element.330), channel_id=1, source_target_pairs={{0,4},{1,5},{2,6},{3,7},{8,12},{9,13},{10,14},{11,15},{16,20},{17,... | collective-permute-start | bytes 116744 | tf_op jit(solution)/shard_map/ppermute | solution.py:50
  218.1 1.6 collective-permute-done.15
  222.2 5.0 %collective-permute-start.17 = (f32[19,4,10,1]{0,1,3,2:T(4,128)S(1)}, f32[19,4,10,1]{0,1,3,2:T(4,128)S(1)}, u32[]{:S(2)}, u32[]{:S(2)}) collective-permute-start(f32[19,4,10,1]{0,1,3,2:T(4,128)S(1)} %copy.135), channel_id=1, source_target_pairs={{0,1},{1,2},{2,3},{4,5},{5,6},{6,7},{8,9},{9,10},{10,11},{12,13},{... | collective-permute-start | bytes 9128 | tf_op jit(solution)/shard_map/ppermute | solution.py:50
  230.2 1.3 collective-permute-start.18
  231.5 3.1 collective-permute-start.19
  235.5 1.3 collective-permute-start.20
  236.8 4.5 %collective-permute-start.21 = (f32[19,4,1,128]{3,2,1,0:T(1,128)S(1)}, f32[19,4,1,128]{3,2,1,0:T(1,128)S(1)}, u32[]{:S(2)}, u32[]{:S(2)}) collective-permute-start(f32[19,4,1,128]{3,2,1,0:T(1,128)S(1)} %get-tuple-element.326), channel_id=1, source_target_pairs={{0,4},{1,5},{2,6},{3,7},{8,12},{9,13},{10,14},{11,15},{16,20},{17,... | collective-permute-start | bytes 116744 | tf_op jit(solution)/shard_map/ppermute | solution.py:50
  241.4 1.6 collective-permute-done.21
  245.5 4.8 %collective-permute-start.23 = (f32[19,4,10,1]{0,1,3,2:T(4,128)S(1)}, f32[19,4,10,1]{0,1,3,2:T(4,128)S(1)}, u32[]{:S(2)}, u32[]{:S(2)}) collective-permute-start(f32[19,4,10,1]{0,1,3,2:T(4,128)S(1)} %copy.139), channel_id=1, source_target_pairs={{0,1},{1,2},{2,3},{4,5},{5,6},{6,7},{8,9},{9,10},{10,11},{12,13},{... | collective-permute-start | bytes 9128 | tf_op jit(solution)/shard_map/ppermute | solution.py:50
  254.3 1.3 collective-permute-start.36
  255.6 5.4 %collective-permute-start.37 = (f32[19,1,8,128]{3,2,1,0:T(8,128)S(1)}, f32[19,1,8,128]{3,2,1,0:T(8,128)S(1)}, u32[]{:S(2)}, u32[]{:S(2)}) collective-permute-start(f32[19,1,8,128]{3,2,1,0:T(8,128)S(1)} %get-tuple-element.466), channel_id=1, source_target_pairs={{0,8},{8,16},{16,24},{1,9},{9,17},{17,25},{2,10},{10,18},{18,26},{... | collective-permute-start | bytes 233480 | tf_op jit(solution)/shard_map/ppermute | solution.py:50
  261.9 1.3 collective-permute-start.38
  263.2 4.5 %collective-permute-start.39 = (f32[19,4,1,128]{3,2,1,0:T(1,128)S(1)}, f32[19,4,1,128]{3,2,1,0:T(1,128)S(1)}, u32[]{:S(2)}, u32[]{:S(2)}) collective-permute-start(f32[19,4,1,128]{3,2,1,0:T(1,128)S(1)} %get-tuple-element.322), channel_id=1, source_target_pairs={{0,4},{1,5},{2,6},{3,7},{8,12},{9,13},{10,14},{11,15},{16,20},{17,... | collective-permute-start | bytes 116744 | tf_op jit(solution)/shard_map/ppermute | solution.py:50
  267.8 1.6 collective-permute-done.39
  271.9 4.5 %collective-permute-start.41 = (f32[19,4,10,1]{0,1,3,2:T(4,128)S(1)}, f32[19,4,10,1]{0,1,3,2:T(4,128)S(1)}, u32[]{:S(2)}, u32[]{:S(2)}) collective-permute-start(f32[19,4,10,1]{0,1,3,2:T(4,128)S(1)} %copy.151), channel_id=1, source_target_pairs={{0,1},{1,2},{2,3},{4,5},{5,6},{6,7},{8,9},{9,10},{10,11},{12,13},{... | collective-permute-start | bytes 9128 | tf_op jit(solution)/shard_map/ppermute | solution.py:50
  280.1 1.3 collective-permute-start.42
  281.4 5.7 %collective-permute-start.43 = (f32[19,1,8,128]{3,2,1,0:T(8,128)S(1)}, f32[19,1,8,128]{3,2,1,0:T(8,128)S(1)}, u32[]{:S(2)}, u32[]{:S(2)}) collective-permute-start(f32[19,1,8,128]{3,2,1,0:T(8,128)S(1)} %get-tuple-element.446), channel_id=1, source_target_pairs={{0,8},{8,16},{16,24},{1,9},{9,17},{17,25},{2,10},{10,18},{18,26},{... | collective-permute-start | bytes 233480 | tf_op jit(solution)/shard_map/ppermute | solution.py:50
  287.1 6.3 %collective-permute-start.24 = (f32[19,1,8,128]{3,2,1,0:T(8,128)S(1)}, f32[19,1,8,128]{3,2,1,0:T(8,128)S(1)}, u32[]{:S(2)}, u32[]{:S(2)}) collective-permute-start(f32[19,1,8,128]{3,2,1,0:T(8,128)S(1)} %get-tuple-element.487), channel_id=1, source_target_pairs={{0,8},{8,16},{16,24},{1,9},{9,17},{17,25},{2,10},{10,18},{18,26},{... | collective-permute-start | bytes 233480 | tf_op jit(solution)/shard_map/ppermute | solution.py:50
  293.4 1.3 collective-permute-start.25
  294.8 1.3 collective-permute-start.44
  296.1 4.5 %collective-permute-start.45 = (f32[19,4,1,128]{3,2,1,0:T(1,128)S(1)}, f32[19,4,1,128]{3,2,1,0:T(1,128)S(1)}, u32[]{:S(2)}, u32[]{:S(2)}) collective-permute-start(f32[19,4,1,128]{3,2,1,0:T(1,128)S(1)} %get-tuple-element.320), channel_id=1, source_target_pairs={{0,4},{1,5},{2,6},{3,7},{8,12},{9,13},{10,14},{11,15},{16,20},{17,... | collective-permute-start | bytes 116744 | tf_op jit(solution)/shard_map/ppermute | solution.py:50
  300.7 1.3 collective-permute-start.26
  302.0 1.3 collective-permute-start.27
  305.9 4.8 %collective-permute-start.47 = (f32[19,4,10,1]{0,1,3,2:T(4,128)S(1)}, f32[19,4,10,1]{0,1,3,2:T(4,128)S(1)}, u32[]{:S(2)}, u32[]{:S(2)}) collective-permute-start(f32[19,4,10,1]{0,1,3,2:T(4,128)S(1)} %copy.155), channel_id=1, source_target_pairs={{0,1},{1,2},{2,3},{4,5},{5,6},{6,7},{8,9},{9,10},{10,11},{12,13},{... | collective-permute-start | bytes 9128 | tf_op jit(solution)/shard_map/ppermute | solution.py:50
  311.5 3.9 %collective-permute-start.28 = (f32[19,4,10,1]{0,1,3,2:T(4,128)S(1)}, f32[19,4,10,1]{0,1,3,2:T(4,128)S(1)}, u32[]{:S(2)}, u32[]{:S(2)}) collective-permute-start(f32[19,4,10,1]{0,1,3,2:T(4,128)S(1)} %copy.141), channel_id=1, source_target_pairs={{0,1},{1,2},{2,3},{4,5},{5,6},{6,7},{8,9},{9,10},{10,11},{12,13},{... | collective-permute-start | bytes 9128 | tf_op jit(solution)/shard_map/ppermute | solution.py:50
  322.0 3.8 collective-permute-start.49
  330.0 4.5 %collective-permute-start.51 = (f32[19,4,1,128]{3,2,1,0:T(1,128)S(1)}, f32[19,4,1,128]{3,2,1,0:T(1,128)S(1)}, u32[]{:S(2)}, u32[]{:S(2)}) collective-permute-start(f32[19,4,1,128]{3,2,1,0:T(1,128)S(1)} %get-tuple-element.318), channel_id=1, source_target_pairs={{0,4},{1,5},{2,6},{3,7},{8,12},{9,13},{10,14},{11,15},{16,20},{17,... | collective-permute-start | bytes 116744 | tf_op jit(solution)/shard_map/ppermute | solution.py:50
  338.7 4.9 %collective-permute-start.53 = (f32[19,4,10,1]{0,1,3,2:T(4,128)S(1)}, f32[19,4,10,1]{0,1,3,2:T(4,128)S(1)}, u32[]{:S(2)}, u32[]{:S(2)}) collective-permute-start(f32[19,4,10,1]{0,1,3,2:T(4,128)S(1)} %copy.159), channel_id=1, source_target_pairs={{0,1},{1,2},{2,3},{4,5},{5,6},{6,7},{8,9},{9,10},{10,11},{12,13},{... | collective-permute-start | bytes 9128 | tf_op jit(solution)/shard_map/ppermute | solution.py:50
  356.6 3.0 collective-permute-start.54
  359.6 1.3 collective-permute-start.55
  361.5 2.4 collective-permute-done.55
  363.9 4.2 %collective-permute-start.56 = (f32[4,1,128]{2,1,0:T(1,128)S(1)}, f32[4,1,128]{2,1,0:T(1,128)S(1)}, u32[]{:S(2)}, u32[]{:S(2)}) collective-permute-start(f32[4,1,128]{2,1,0:T(1,128)S(1)} %get-tuple-element.500), channel_id=1, source_target_pairs={{0,4},{1,5},{2,6},{3,7},{8,12},{9,13},{10,14},{11,15},{16,20},{17,... | collective-permute-start | bytes 6152 | tf_op jit(solution)/shard_map/ppermute | solution.py:50
  368.2 1.3 collective-permute-start.57
  370.1 3.5 collective-permute-done.57
  373.7 3.9 %collective-permute-start.58 = (f32[4,10,1]{2,1,0:T(8,128)S(1)}, f32[4,10,1]{2,1,0:T(8,128)S(1)}, u32[]{:S(2)}, u32[]{:S(2)}) collective-permute-start(f32[4,10,1]{2,1,0:T(8,128)S(1)} %get-tuple-element.496), channel_id=1, source_target_pairs={{0,1},{1,2},{2,3},{4,5},{5,6},{6,7},{8,9},{9,10},{10,11},{12,13},{... | collective-permute-start | bytes 488 | tf_op jit(solution)/shard_map/ppermute | solution.py:50
  377.6 1.3 collective-permute-start.59
  379.6 4.1 %collective-permute-done.59 = f32[4,10,1]{2,1,0:T(8,128)S(1)} collective-permute-done((f32[4,10,1]{2,1,0:T(8,128)S(1)}, f32[4,10,1]{2,1,0:T(8,128)S(1)}, u32[]{:S(2)}, u32[]{:S(2)}) %collective-permute-start.59) | collective-permute-done | bytes 192 | tf_op jit(solution)/shard_map/ppermute | solution.py:51
  (573 shorter events, 81.4 us)
Async XLA Ops:
  1.3 12.2 %collective-permute-start = (f32[1,8,128]{2,1,0:T(8,128)S(1)}, f32[1,8,128]{2,1,0:T(8,128)S(1)}, u32[]{:S(2)}, u32[]{:S(2)}) collective-permute-start(f32[1,8,128]{2,1,0:T(8,128)S(1)} %get-tuple-element.591), channel_id=1, source_target_pairs={{0,8},{8,16},{16,24},{1,9},{9,17},{17,25},{2,10},{10,18},{18,26},{... | collective-permute-start | bytes 12296 | tf_op jit(solution)/shard_map/ppermute | solution.py:50
  3.7 8.9 %copy-start = (f32[19,2,8,128]{3,2,1,0:T(8,128)S(1)}, f32[19,2,8,128]{3,2,1,0:T(8,128)}, u32[]{:S(2)}) copy-start(f32[19,2,8,128]{3,2,1,0:T(8,128)} %param.14) | copy-start | bytes 466948
  3.7 8.9 %copy-start.2 = (f32[19,2,8,128]{3,2,1,0:T(8,128)S(1)}, f32[19,2,8,128]{3,2,1,0:T(8,128)}, u32[]{:S(2)}) copy-start(f32[19,2,8,128]{3,2,1,0:T(8,128)} %param.13) | copy-start | bytes 466948
  3.7 10.5 %collective-permute-start.1 = (f32[1,8,128]{2,1,0:T(8,128)S(1)}, f32[1,8,128]{2,1,0:T(8,128)S(1)}, u32[]{:S(2)}, u32[]{:S(2)}) collective-permute-start(f32[1,8,128]{2,1,0:T(8,128)S(1)} %get-tuple-element.590), channel_id=1, source_target_pairs={{8,0},{16,8},{24,16},{9,1},{17,9},{25,17},{10,2},{18,10},{26,18},{... | collective-permute-start | bytes 12296 | tf_op jit(solution)/shard_map/ppermute | solution.py:51
  6.1 168.5 %collective-permute-start.31 = (f32[19,1,8,128]{3,2,1,0:T(8,128)S(1)}, f32[19,1,8,128]{3,2,1,0:T(8,128)S(1)}, u32[]{:S(2)}, u32[]{:S(2)}) collective-permute-start(f32[19,1,8,128]{3,2,1,0:T(8,128)S(1)} %get-tuple-element.490), channel_id=1, source_target_pairs={{0,8},{8,16},{16,24},{1,9},{9,17},{17,25},{2,10},{10,18},{18,26},{... | collective-permute-start | bytes 233480 | tf_op jit(solution)/shard_map/ppermute | solution.py:50
  11.3 163.3 %collective-permute-start.30 = (f32[19,1,8,128]{3,2,1,0:T(8,128)S(1)}, f32[19,1,8,128]{3,2,1,0:T(8,128)S(1)}, u32[]{:S(2)}, u32[]{:S(2)}) collective-permute-start(f32[19,1,8,128]{3,2,1,0:T(8,128)S(1)} %get-tuple-element.491), channel_id=1, source_target_pairs={{8,0},{16,8},{24,16},{9,1},{17,9},{25,17},{10,2},{18,10},{26,18},{... | collective-permute-start | bytes 233480 | tf_op jit(solution)/shard_map/ppermute | solution.py:51
  12.8 0.7 copy-start.5
  14.2 5.4 %collective-permute-start.2 = (f32[4,1,128]{2,1,0:T(1,128)S(1)}, f32[4,1,128]{2,1,0:T(1,128)S(1)}, u32[]{:S(2)}, u32[]{:S(2)}) collective-permute-start(f32[4,1,128]{2,1,0:T(1,128)S(1)} %get-tuple-element.520), channel_id=1, source_target_pairs={{0,4},{1,5},{2,6},{3,7},{8,12},{9,13},{10,14},{11,15},{16,20},{17,... | collective-permute-start | bytes 6152 | tf_op jit(solution)/shard_map/ppermute | solution.py:50
  17.6 5.5 %collective-permute-start.3 = (f32[4,1,128]{2,1,0:T(1,128)S(1)}, f32[4,1,128]{2,1,0:T(1,128)S(1)}, u32[]{:S(2)}, u32[]{:S(2)}) collective-permute-start(f32[4,1,128]{2,1,0:T(1,128)S(1)} %get-tuple-element.521), channel_id=1, source_target_pairs={{4,0},{5,1},{6,2},{7,3},{12,8},{13,9},{14,10},{15,11},{20,16},{21,... | collective-permute-start | bytes 6152 | tf_op jit(solution)/shard_map/ppermute | solution.py:51
  23.2 5.2 %collective-permute-start.4 = (f32[4,10,1]{2,1,0:T(8,128)S(1)}, f32[4,10,1]{2,1,0:T(8,128)S(1)}, u32[]{:S(2)}, u32[]{:S(2)}) collective-permute-start(f32[4,10,1]{2,1,0:T(8,128)S(1)} %get-tuple-element.498), channel_id=1, source_target_pairs={{0,1},{1,2},{2,3},{4,5},{5,6},{6,7},{8,9},{9,10},{10,11},{12,13},{... | collective-permute-start | bytes 488 | tf_op jit(solution)/shard_map/ppermute | solution.py:50
  26.7 5.8 %collective-permute-start.5 = (f32[4,10,1]{2,1,0:T(8,128)S(1)}, f32[4,10,1]{2,1,0:T(8,128)S(1)}, u32[]{:S(2)}, u32[]{:S(2)}) collective-permute-start(f32[4,10,1]{2,1,0:T(8,128)S(1)} %get-tuple-element.499), channel_id=1, source_target_pairs={{1,0},{2,1},{3,2},{5,4},{6,5},{7,6},{9,8},{10,9},{11,10},{13,12},{... | collective-permute-start | bytes 488 | tf_op jit(solution)/shard_map/ppermute | solution.py:51
  169.2 0.9 copy-start.1
  170.2 10.4 %collective-permute-start.6 = (f32[19,1,8,128]{3,2,1,0:T(8,128)S(1)}, f32[19,1,8,128]{3,2,1,0:T(8,128)S(1)}, u32[]{:S(2)}, u32[]{:S(2)}) collective-permute-start(f32[19,1,8,128]{3,2,1,0:T(8,128)S(1)} %get-tuple-element.495), channel_id=1, source_target_pairs={{8,0},{16,8},{24,16},{9,1},{17,9},{25,17},{10,2},{18,10},{26,18},{... | collective-permute-start | bytes 233480 | tf_op jit(solution)/shard_map/ppermute | solution.py:51
  171.5 9.1 %collective-permute-start.7 = (f32[19,1,8,128]{3,2,1,0:T(8,128)S(1)}, f32[19,1,8,128]{3,2,1,0:T(8,128)S(1)}, u32[]{:S(2)}, u32[]{:S(2)}) collective-permute-start(f32[19,1,8,128]{3,2,1,0:T(8,128)S(1)} %get-tuple-element.494), channel_id=1, source_target_pairs={{0,8},{8,16},{16,24},{1,9},{9,17},{17,25},{2,10},{10,18},{18,26},{... | collective-permute-start | bytes 233480 | tf_op jit(solution)/shard_map/ppermute | solution.py:50
  174.7 11.8 %collective-permute-start.32 = (f32[19,4,1,128]{3,2,1,0:T(1,128)S(1)}, f32[19,4,1,128]{3,2,1,0:T(1,128)S(1)}, u32[]{:S(2)}, u32[]{:S(2)}) collective-permute-start(f32[19,4,1,128]{3,2,1,0:T(1,128)S(1)} %get-tuple-element.329), channel_id=1, source_target_pairs={{4,0},{5,1},{6,2},{7,3},{12,8},{13,9},{14,10},{15,11},{20,16},{21,... | collective-permute-start | bytes 116744 | tf_op jit(solution)/shard_map/ppermute | solution.py:51
  176.0 10.5 %collective-permute-start.33 = (f32[19,4,1,128]{3,2,1,0:T(1,128)S(1)}, f32[19,4,1,128]{3,2,1,0:T(1,128)S(1)}, u32[]{:S(2)}, u32[]{:S(2)}) collective-permute-start(f32[19,4,1,128]{3,2,1,0:T(1,128)S(1)} %get-tuple-element.328), channel_id=1, source_target_pairs={{0,4},{1,5},{2,6},{3,7},{8,12},{9,13},{10,14},{11,15},{16,20},{17,... | collective-permute-start | bytes 116744 | tf_op jit(solution)/shard_map/ppermute | solution.py:50
  180.6 15.9 %collective-permute-start.8 = (f32[19,4,1,128]{3,2,1,0:T(1,128)S(1)}, f32[19,4,1,128]{3,2,1,0:T(1,128)S(1)}, u32[]{:S(2)}, u32[]{:S(2)}) collective-permute-start(f32[19,4,1,128]{3,2,1,0:T(1,128)S(1)} %get-tuple-element.333), channel_id=1, source_target_pairs={{4,0},{5,1},{6,2},{7,3},{12,8},{13,9},{14,10},{15,11},{20,16},{21,... | collective-permute-start | bytes 116744 | tf_op jit(solution)/shard_map/ppermute | solution.py:51
  181.9 14.6 %collective-permute-start.9 = (f32[19,4,1,128]{3,2,1,0:T(1,128)S(1)}, f32[19,4,1,128]{3,2,1,0:T(1,128)S(1)}, u32[]{:S(2)}, u32[]{:S(2)}) collective-permute-start(f32[19,4,1,128]{3,2,1,0:T(1,128)S(1)} %get-tuple-element.332), channel_id=1, source_target_pairs={{0,4},{1,5},{2,6},{3,7},{8,12},{9,13},{10,14},{11,15},{16,20},{17,... | collective-permute-start | bytes 116744 | tf_op jit(solution)/shard_map/ppermute | solution.py:50
  187.3 6.3 %collective-permute-start.34 = (f32[19,4,10,1]{0,1,3,2:T(4,128)S(1)}, f32[19,4,10,1]{0,1,3,2:T(4,128)S(1)}, u32[]{:S(2)}, u32[]{:S(2)}) collective-permute-start(f32[19,4,10,1]{0,1,3,2:T(4,128)S(1)} %copy.145), channel_id=1, source_target_pairs={{1,0},{2,1},{3,2},{5,4},{6,5},{7,6},{9,8},{10,9},{11,10},{13,12},{... | collective-permute-start | bytes 9128 | tf_op jit(solution)/shard_map/ppermute | solution.py:51
  189.0 6.0 %collective-permute-start.35 = (f32[19,4,10,1]{0,1,3,2:T(4,128)S(1)}, f32[19,4,10,1]{0,1,3,2:T(4,128)S(1)}, u32[]{:S(2)}, u32[]{:S(2)}) collective-permute-start(f32[19,4,10,1]{0,1,3,2:T(4,128)S(1)} %copy.147), channel_id=1, source_target_pairs={{0,1},{1,2},{2,3},{4,5},{5,6},{6,7},{8,9},{9,10},{10,11},{12,13},{... | collective-permute-start | bytes 9128 | tf_op jit(solution)/shard_map/ppermute | solution.py:50
  197.3 6.6 %collective-permute-start.10 = (f32[19,4,10,1]{0,1,3,2:T(4,128)S(1)}, f32[19,4,10,1]{0,1,3,2:T(4,128)S(1)}, u32[]{:S(2)}, u32[]{:S(2)}) collective-permute-start(f32[19,4,10,1]{0,1,3,2:T(4,128)S(1)} %copy.129), channel_id=1, source_target_pairs={{1,0},{2,1},{3,2},{5,4},{6,5},{7,6},{9,8},{10,9},{11,10},{13,12},{... | collective-permute-start | bytes 9128 | tf_op jit(solution)/shard_map/ppermute | solution.py:51
  199.0 6.3 %collective-permute-start.11 = (f32[19,4,10,1]{0,1,3,2:T(4,128)S(1)}, f32[19,4,10,1]{0,1,3,2:T(4,128)S(1)}, u32[]{:S(2)}, u32[]{:S(2)}) collective-permute-start(f32[19,4,10,1]{0,1,3,2:T(4,128)S(1)} %copy.131), channel_id=1, source_target_pairs={{0,1},{1,2},{2,3},{4,5},{5,6},{6,7},{8,9},{9,10},{10,11},{12,13},{... | collective-permute-start | bytes 9128 | tf_op jit(solution)/shard_map/ppermute | solution.py:50
  207.0 4.3 %collective-permute-start.12 = (f32[19,1,8,128]{3,2,1,0:T(8,128)S(1)}, f32[19,1,8,128]{3,2,1,0:T(8,128)S(1)}, u32[]{:S(2)}, u32[]{:S(2)}) collective-permute-start(f32[19,1,8,128]{3,2,1,0:T(8,128)S(1)} %get-tuple-element.493), channel_id=1, source_target_pairs={{8,0},{16,8},{24,16},{9,1},{17,9},{25,17},{10,2},{18,10},{26,18},{... | collective-permute-start | bytes 233480 | tf_op jit(solution)/shard_map/ppermute | solution.py:51
  208.3 3.9 %collective-permute-start.13 = (f32[19,1,8,128]{3,2,1,0:T(8,128)S(1)}, f32[19,1,8,128]{3,2,1,0:T(8,128)S(1)}, u32[]{:S(2)}, u32[]{:S(2)}) collective-permute-start(f32[19,1,8,128]{3,2,1,0:T(8,128)S(1)} %get-tuple-element.492), channel_id=1, source_target_pairs={{0,8},{8,16},{16,24},{1,9},{9,17},{17,25},{2,10},{10,18},{18,26},{... | collective-permute-start | bytes 233480 | tf_op jit(solution)/shard_map/ppermute | solution.py:50
  212.3 5.9 %collective-permute-start.14 = (f32[19,4,1,128]{3,2,1,0:T(1,128)S(1)}, f32[19,4,1,128]{3,2,1,0:T(1,128)S(1)}, u32[]{:S(2)}, u32[]{:S(2)}) collective-permute-start(f32[19,4,1,128]{3,2,1,0:T(1,128)S(1)} %get-tuple-element.331), channel_id=1, source_target_pairs={{4,0},{5,1},{6,2},{7,3},{12,8},{13,9},{14,10},{15,11},{20,16},{21,... | collective-permute-start | bytes 116744 | tf_op jit(solution)/shard_map/ppermute | solution.py:51
  213.6 6.2 %collective-permute-start.15 = (f32[19,4,1,128]{3,2,1,0:T(1,128)S(1)}, f32[19,4,1,128]{3,2,1,0:T(1,128)S(1)}, u32[]{:S(2)}, u32[]{:S(2)}) collective-permute-start(f32[19,4,1,128]{3,2,1,0:T(1,128)S(1)} %get-tuple-element.330), channel_id=1, source_target_pairs={{0,4},{1,5},{2,6},{3,7},{8,12},{9,13},{10,14},{11,15},{16,20},{17,... | collective-permute-start | bytes 116744 | tf_op jit(solution)/shard_map/ppermute | solution.py:50
  220.5 6.8 %collective-permute-start.16 = (f32[19,4,10,1]{0,1,3,2:T(4,128)S(1)}, f32[19,4,10,1]{0,1,3,2:T(4,128)S(1)}, u32[]{:S(2)}, u32[]{:S(2)}) collective-permute-start(f32[19,4,10,1]{0,1,3,2:T(4,128)S(1)} %copy.133), channel_id=1, source_target_pairs={{1,0},{2,1},{3,2},{5,4},{6,5},{7,6},{9,8},{10,9},{11,10},{13,12},{... | collective-permute-start | bytes 9128 | tf_op jit(solution)/shard_map/ppermute | solution.py:51
  222.2 6.3 %collective-permute-start.17 = (f32[19,4,10,1]{0,1,3,2:T(4,128)S(1)}, f32[19,4,10,1]{0,1,3,2:T(4,128)S(1)}, u32[]{:S(2)}, u32[]{:S(2)}) collective-permute-start(f32[19,4,10,1]{0,1,3,2:T(4,128)S(1)} %copy.135), channel_id=1, source_target_pairs={{0,1},{1,2},{2,3},{4,5},{5,6},{6,7},{8,9},{9,10},{10,11},{12,13},{... | collective-permute-start | bytes 9128 | tf_op jit(solution)/shard_map/ppermute | solution.py:50
  230.2 4.4 %collective-permute-start.18 = (f32[19,1,8,128]{3,2,1,0:T(8,128)S(1)}, f32[19,1,8,128]{3,2,1,0:T(8,128)S(1)}, u32[]{:S(2)}, u32[]{:S(2)}) collective-permute-start(f32[19,1,8,128]{3,2,1,0:T(8,128)S(1)} %get-tuple-element.489), channel_id=1, source_target_pairs={{8,0},{16,8},{24,16},{9,1},{17,9},{25,17},{10,2},{18,10},{26,18},{... | collective-permute-start | bytes 233480 | tf_op jit(solution)/shard_map/ppermute | solution.py:51
  231.5 4.0 %collective-permute-start.19 = (f32[19,1,8,128]{3,2,1,0:T(8,128)S(1)}, f32[19,1,8,128]{3,2,1,0:T(8,128)S(1)}, u32[]{:S(2)}, u32[]{:S(2)}) collective-permute-start(f32[19,1,8,128]{3,2,1,0:T(8,128)S(1)} %get-tuple-element.488), channel_id=1, source_target_pairs={{0,8},{8,16},{16,24},{1,9},{9,17},{17,25},{2,10},{10,18},{18,26},{... | collective-permute-start | bytes 233480 | tf_op jit(solution)/shard_map/ppermute | solution.py:50
  235.5 5.9 %collective-permute-start.20 = (f32[19,4,1,128]{3,2,1,0:T(1,128)S(1)}, f32[19,4,1,128]{3,2,1,0:T(1,128)S(1)}, u32[]{:S(2)}, u32[]{:S(2)}) collective-permute-start(f32[19,4,1,128]{3,2,1,0:T(1,128)S(1)} %get-tuple-element.327), channel_id=1, source_target_pairs={{4,0},{5,1},{6,2},{7,3},{12,8},{13,9},{14,10},{15,11},{20,16},{21,... | collective-permute-start | bytes 116744 | tf_op jit(solution)/shard_map/ppermute | solution.py:51
  236.8 6.2 %collective-permute-start.21 = (f32[19,4,1,128]{3,2,1,0:T(1,128)S(1)}, f32[19,4,1,128]{3,2,1,0:T(1,128)S(1)}, u32[]{:S(2)}, u32[]{:S(2)}) collective-permute-start(f32[19,4,1,128]{3,2,1,0:T(1,128)S(1)} %get-tuple-element.326), channel_id=1, source_target_pairs={{0,4},{1,5},{2,6},{3,7},{8,12},{9,13},{10,14},{11,15},{16,20},{17,... | collective-permute-start | bytes 116744 | tf_op jit(solution)/shard_map/ppermute | solution.py:50
  243.8 6.5 %collective-permute-start.22 = (f32[19,4,10,1]{0,1,3,2:T(4,128)S(1)}, f32[19,4,10,1]{0,1,3,2:T(4,128)S(1)}, u32[]{:S(2)}, u32[]{:S(2)}) collective-permute-start(f32[19,4,10,1]{0,1,3,2:T(4,128)S(1)} %copy.137), channel_id=1, source_target_pairs={{1,0},{2,1},{3,2},{5,4},{6,5},{7,6},{9,8},{10,9},{11,10},{13,12},{... | collective-permute-start | bytes 9128 | tf_op jit(solution)/shard_map/ppermute | solution.py:51
  245.5 6.3 %collective-permute-start.23 = (f32[19,4,10,1]{0,1,3,2:T(4,128)S(1)}, f32[19,4,10,1]{0,1,3,2:T(4,128)S(1)}, u32[]{:S(2)}, u32[]{:S(2)}) collective-permute-start(f32[19,4,10,1]{0,1,3,2:T(4,128)S(1)} %copy.139), channel_id=1, source_target_pairs={{0,1},{1,2},{2,3},{4,5},{5,6},{6,7},{8,9},{9,10},{10,11},{12,13},{... | collective-permute-start | bytes 9128 | tf_op jit(solution)/shard_map/ppermute | solution.py:50
  254.3 6.7 %collective-permute-start.36 = (f32[19,1,8,128]{3,2,1,0:T(8,128)S(1)}, f32[19,1,8,128]{3,2,1,0:T(8,128)S(1)}, u32[]{:S(2)}, u32[]{:S(2)}) collective-permute-start(f32[19,1,8,128]{3,2,1,0:T(8,128)S(1)} %get-tuple-element.467), channel_id=1, source_target_pairs={{8,0},{16,8},{24,16},{9,1},{17,9},{25,17},{10,2},{18,10},{26,18},{... | collective-permute-start | bytes 233480 | tf_op jit(solution)/shard_map/ppermute | solution.py:51
  255.6 6.3 %collective-permute-start.37 = (f32[19,1,8,128]{3,2,1,0:T(8,128)S(1)}, f32[19,1,8,128]{3,2,1,0:T(8,128)S(1)}, u32[]{:S(2)}, u32[]{:S(2)}) collective-permute-start(f32[19,1,8,128]{3,2,1,0:T(8,128)S(1)} %get-tuple-element.466), channel_id=1, source_target_pairs={{0,8},{8,16},{16,24},{1,9},{9,17},{17,25},{2,10},{10,18},{18,26},{... | collective-permute-start | bytes 233480 | tf_op jit(solution)/shard_map/ppermute | solution.py:50
  261.9 5.9 %collective-permute-start.38 = (f32[19,4,1,128]{3,2,1,0:T(1,128)S(1)}, f32[19,4,1,128]{3,2,1,0:T(1,128)S(1)}, u32[]{:S(2)}, u32[]{:S(2)}) collective-permute-start(f32[19,4,1,128]{3,2,1,0:T(1,128)S(1)} %get-tuple-element.323), channel_id=1, source_target_pairs={{4,0},{5,1},{6,2},{7,3},{12,8},{13,9},{14,10},{15,11},{20,16},{21,... | collective-permute-start | bytes 116744 | tf_op jit(solution)/shard_map/ppermute | solution.py:51
  263.2 6.2 %collective-permute-start.39 = (f32[19,4,1,128]{3,2,1,0:T(1,128)S(1)}, f32[19,4,1,128]{3,2,1,0:T(1,128)S(1)}, u32[]{:S(2)}, u32[]{:S(2)}) collective-permute-start(f32[19,4,1,128]{3,2,1,0:T(1,128)S(1)} %get-tuple-element.322), channel_id=1, source_target_pairs={{0,4},{1,5},{2,6},{3,7},{8,12},{9,13},{10,14},{11,15},{16,20},{17,... | collective-permute-start | bytes 116744 | tf_op jit(solution)/shard_map/ppermute | solution.py:50
  270.2 6.3 %collective-permute-start.40 = (f32[19,4,10,1]{0,1,3,2:T(4,128)S(1)}, f32[19,4,10,1]{0,1,3,2:T(4,128)S(1)}, u32[]{:S(2)}, u32[]{:S(2)}) collective-permute-start(f32[19,4,10,1]{0,1,3,2:T(4,128)S(1)} %copy.149), channel_id=1, source_target_pairs={{1,0},{2,1},{3,2},{5,4},{6,5},{7,6},{9,8},{10,9},{11,10},{13,12},{... | collective-permute-start | bytes 9128 | tf_op jit(solution)/shard_map/ppermute | solution.py:51
  271.9 6.0 %collective-permute-start.41 = (f32[19,4,10,1]{0,1,3,2:T(4,128)S(1)}, f32[19,4,10,1]{0,1,3,2:T(4,128)S(1)}, u32[]{:S(2)}, u32[]{:S(2)}) collective-permute-start(f32[19,4,10,1]{0,1,3,2:T(4,128)S(1)} %copy.151), channel_id=1, source_target_pairs={{0,1},{1,2},{2,3},{4,5},{5,6},{6,7},{8,9},{9,10},{10,11},{12,13},{... | collective-permute-start | bytes 9128 | tf_op jit(solution)/shard_map/ppermute | solution.py:50
  280.1 14.6 %collective-permute-start.42 = (f32[19,1,8,128]{3,2,1,0:T(8,128)S(1)}, f32[19,1,8,128]{3,2,1,0:T(8,128)S(1)}, u32[]{:S(2)}, u32[]{:S(2)}) collective-permute-start(f32[19,1,8,128]{3,2,1,0:T(8,128)S(1)} %get-tuple-element.447), channel_id=1, source_target_pairs={{8,0},{16,8},{24,16},{9,1},{17,9},{25,17},{10,2},{18,10},{26,18},{... | collective-permute-start | bytes 233480 | tf_op jit(solution)/shard_map/ppermute | solution.py:51
  281.4 13.4 %collective-permute-start.43 = (f32[19,1,8,128]{3,2,1,0:T(8,128)S(1)}, f32[19,1,8,128]{3,2,1,0:T(8,128)S(1)}, u32[]{:S(2)}, u32[]{:S(2)}) collective-permute-start(f32[19,1,8,128]{3,2,1,0:T(8,128)S(1)} %get-tuple-element.446), channel_id=1, source_target_pairs={{0,8},{8,16},{16,24},{1,9},{9,17},{17,25},{2,10},{10,18},{18,26},{... | collective-permute-start | bytes 233480 | tf_op jit(solution)/shard_map/ppermute | solution.py:50
  287.1 13.5 %collective-permute-start.24 = (f32[19,1,8,128]{3,2,1,0:T(8,128)S(1)}, f32[19,1,8,128]{3,2,1,0:T(8,128)S(1)}, u32[]{:S(2)}, u32[]{:S(2)}) collective-permute-start(f32[19,1,8,128]{3,2,1,0:T(8,128)S(1)} %get-tuple-element.487), channel_id=1, source_target_pairs={{0,8},{8,16},{16,24},{1,9},{9,17},{17,25},{2,10},{10,18},{18,26},{... | collective-permute-start | bytes 233480 | tf_op jit(solution)/shard_map/ppermute | solution.py:50
  293.4 7.2 %collective-permute-start.25 = (f32[19,1,8,128]{3,2,1,0:T(8,128)S(1)}, f32[19,1,8,128]{3,2,1,0:T(8,128)S(1)}, u32[]{:S(2)}, u32[]{:S(2)}) collective-permute-start(f32[19,1,8,128]{3,2,1,0:T(8,128)S(1)} %get-tuple-element.486), channel_id=1, source_target_pairs={{8,0},{16,8},{24,16},{9,1},{17,9},{25,17},{10,2},{18,10},{26,18},{... | collective-permute-start | bytes 233480 | tf_op jit(solution)/shard_map/ppermute | solution.py:51
  294.8 8.6 %collective-permute-start.44 = (f32[19,4,1,128]{3,2,1,0:T(1,128)S(1)}, f32[19,4,1,128]{3,2,1,0:T(1,128)S(1)}, u32[]{:S(2)}, u32[]{:S(2)}) collective-permute-start(f32[19,4,1,128]{3,2,1,0:T(1,128)S(1)} %get-tuple-element.321), channel_id=1, source_target_pairs={{4,0},{5,1},{6,2},{7,3},{12,8},{13,9},{14,10},{15,11},{20,16},{21,... | collective-permute-start | bytes 116744 | tf_op jit(solution)/shard_map/ppermute | solution.py:51
  296.1 7.3 %collective-permute-start.45 = (f32[19,4,1,128]{3,2,1,0:T(1,128)S(1)}, f32[19,4,1,128]{3,2,1,0:T(1,128)S(1)}, u32[]{:S(2)}, u32[]{:S(2)}) collective-permute-start(f32[19,4,1,128]{3,2,1,0:T(1,128)S(1)} %get-tuple-element.320), channel_id=1, source_target_pairs={{0,4},{1,5},{2,6},{3,7},{8,12},{9,13},{10,14},{11,15},{16,20},{17,... | collective-permute-start | bytes 116744 | tf_op jit(solution)/shard_map/ppermute | solution.py:50
  300.7 10.0 %collective-permute-start.26 = (f32[19,4,1,128]{3,2,1,0:T(1,128)S(1)}, f32[19,4,1,128]{3,2,1,0:T(1,128)S(1)}, u32[]{:S(2)}, u32[]{:S(2)}) collective-permute-start(f32[19,4,1,128]{3,2,1,0:T(1,128)S(1)} %get-tuple-element.325), channel_id=1, source_target_pairs={{0,4},{1,5},{2,6},{3,7},{8,12},{9,13},{10,14},{11,15},{16,20},{17,... | collective-permute-start | bytes 116744 | tf_op jit(solution)/shard_map/ppermute | solution.py:50
  302.0 8.7 %collective-permute-start.27 = (f32[19,4,1,128]{3,2,1,0:T(1,128)S(1)}, f32[19,4,1,128]{3,2,1,0:T(1,128)S(1)}, u32[]{:S(2)}, u32[]{:S(2)}) collective-permute-start(f32[19,4,1,128]{3,2,1,0:T(1,128)S(1)} %get-tuple-element.324), channel_id=1, source_target_pairs={{4,0},{5,1},{6,2},{7,3},{12,8},{13,9},{14,10},{15,11},{20,16},{21,... | collective-permute-start | bytes 116744 | tf_op jit(solution)/shard_map/ppermute | solution.py:51
  304.2 13.1 %collective-permute-start.46 = (f32[19,4,10,1]{0,1,3,2:T(4,128)S(1)}, f32[19,4,10,1]{0,1,3,2:T(4,128)S(1)}, u32[]{:S(2)}, u32[]{:S(2)}) collective-permute-start(f32[19,4,10,1]{0,1,3,2:T(4,128)S(1)} %copy.153), channel_id=1, source_target_pairs={{1,0},{2,1},{3,2},{5,4},{6,5},{7,6},{9,8},{10,9},{11,10},{13,12},{... | collective-permute-start | bytes 9128 | tf_op jit(solution)/shard_map/ppermute | solution.py:51
  305.9 12.1 %collective-permute-start.47 = (f32[19,4,10,1]{0,1,3,2:T(4,128)S(1)}, f32[19,4,10,1]{0,1,3,2:T(4,128)S(1)}, u32[]{:S(2)}, u32[]{:S(2)}) collective-permute-start(f32[19,4,10,1]{0,1,3,2:T(4,128)S(1)} %copy.155), channel_id=1, source_target_pairs={{0,1},{1,2},{2,3},{4,5},{5,6},{6,7},{8,9},{9,10},{10,11},{12,13},{... | collective-permute-start | bytes 9128 | tf_op jit(solution)/shard_map/ppermute | solution.py:50
  311.5 14.3 %collective-permute-start.28 = (f32[19,4,10,1]{0,1,3,2:T(4,128)S(1)}, f32[19,4,10,1]{0,1,3,2:T(4,128)S(1)}, u32[]{:S(2)}, u32[]{:S(2)}) collective-permute-start(f32[19,4,10,1]{0,1,3,2:T(4,128)S(1)} %copy.141), channel_id=1, source_target_pairs={{0,1},{1,2},{2,3},{4,5},{5,6},{6,7},{8,9},{9,10},{10,11},{12,13},{... | collective-permute-start | bytes 9128 | tf_op jit(solution)/shard_map/ppermute | solution.py:50
  315.9 10.8 %collective-permute-start.29 = (f32[19,4,10,1]{0,1,3,2:T(4,128)S(1)}, f32[19,4,10,1]{0,1,3,2:T(4,128)S(1)}, u32[]{:S(2)}, u32[]{:S(2)}) collective-permute-start(f32[19,4,10,1]{0,1,3,2:T(4,128)S(1)} %copy.143), channel_id=1, source_target_pairs={{1,0},{2,1},{3,2},{5,4},{6,5},{7,6},{9,8},{10,9},{11,10},{13,12},{... | collective-permute-start | bytes 9128 | tf_op jit(solution)/shard_map/ppermute | solution.py:51
  320.7 7.3 %collective-permute-start.48 = (f32[19,1,8,128]{3,2,1,0:T(8,128)S(1)}, f32[19,1,8,128]{3,2,1,0:T(8,128)S(1)}, u32[]{:S(2)}, u32[]{:S(2)}) collective-permute-start(f32[19,1,8,128]{3,2,1,0:T(8,128)S(1)} %get-tuple-element.427), channel_id=1, source_target_pairs={{8,0},{16,8},{24,16},{9,1},{17,9},{25,17},{10,2},{18,10},{26,18},{... | collective-permute-start | bytes 233480 | tf_op jit(solution)/shard_map/ppermute | solution.py:51
  322.0 6.0 %collective-permute-start.49 = (f32[19,1,8,128]{3,2,1,0:T(8,128)S(1)}, f32[19,1,8,128]{3,2,1,0:T(8,128)S(1)}, u32[]{:S(2)}, u32[]{:S(2)}) collective-permute-start(f32[19,1,8,128]{3,2,1,0:T(8,128)S(1)} %get-tuple-element.426), channel_id=1, source_target_pairs={{0,8},{8,16},{16,24},{1,9},{9,17},{17,25},{2,10},{10,18},{18,26},{... | collective-permute-start | bytes 233480 | tf_op jit(solution)/shard_map/ppermute | solution.py:50
  328.7 7.0 %collective-permute-start.50 = (f32[19,4,1,128]{3,2,1,0:T(1,128)S(1)}, f32[19,4,1,128]{3,2,1,0:T(1,128)S(1)}, u32[]{:S(2)}, u32[]{:S(2)}) collective-permute-start(f32[19,4,1,128]{3,2,1,0:T(1,128)S(1)} %get-tuple-element.319), channel_id=1, source_target_pairs={{4,0},{5,1},{6,2},{7,3},{12,8},{13,9},{14,10},{15,11},{20,16},{21,... | collective-permute-start | bytes 116744 | tf_op jit(solution)/shard_map/ppermute | solution.py:51
  330.0 6.2 %collective-permute-start.51 = (f32[19,4,1,128]{3,2,1,0:T(1,128)S(1)}, f32[19,4,1,128]{3,2,1,0:T(1,128)S(1)}, u32[]{:S(2)}, u32[]{:S(2)}) collective-permute-start(f32[19,4,1,128]{3,2,1,0:T(1,128)S(1)} %get-tuple-element.318), channel_id=1, source_target_pairs={{0,4},{1,5},{2,6},{3,7},{8,12},{9,13},{10,14},{11,15},{16,20},{17,... | collective-permute-start | bytes 116744 | tf_op jit(solution)/shard_map/ppermute | solution.py:50
  337.0 7.8 %collective-permute-start.52 = (f32[19,4,10,1]{0,1,3,2:T(4,128)S(1)}, f32[19,4,10,1]{0,1,3,2:T(4,128)S(1)}, u32[]{:S(2)}, u32[]{:S(2)}) collective-permute-start(f32[19,4,10,1]{0,1,3,2:T(4,128)S(1)} %copy.157), channel_id=1, source_target_pairs={{1,0},{2,1},{3,2},{5,4},{6,5},{7,6},{9,8},{10,9},{11,10},{13,12},{... | collective-permute-start | bytes 9128 | tf_op jit(solution)/shard_map/ppermute | solution.py:51
  338.7 6.9 %collective-permute-start.53 = (f32[19,4,10,1]{0,1,3,2:T(4,128)S(1)}, f32[19,4,10,1]{0,1,3,2:T(4,128)S(1)}, u32[]{:S(2)}, u32[]{:S(2)}) collective-permute-start(f32[19,4,10,1]{0,1,3,2:T(4,128)S(1)} %copy.159), channel_id=1, source_target_pairs={{0,1},{1,2},{2,3},{4,5},{5,6},{6,7},{8,9},{9,10},{10,11},{12,13},{... | collective-permute-start | bytes 9128 | tf_op jit(solution)/shard_map/ppermute | solution.py:50
  356.6 5.0 %collective-permute-start.54 = (f32[1,8,128]{2,1,0:T(8,128)S(1)}, f32[1,8,128]{2,1,0:T(8,128)S(1)}, u32[]{:S(2)}, u32[]{:S(2)}) collective-permute-start(f32[1,8,128]{2,1,0:T(8,128)S(1)} %get-tuple-element.522), channel_id=1, source_target_pairs={{0,8},{8,16},{16,24},{1,9},{9,17},{17,25},{2,10},{10,18},{18,26},{... | collective-permute-start | bytes 12296 | tf_op jit(solution)/shard_map/ppermute | solution.py:50
  359.6 4.4 %collective-permute-start.55 = (f32[1,8,128]{2,1,0:T(8,128)S(1)}, f32[1,8,128]{2,1,0:T(8,128)S(1)}, u32[]{:S(2)}, u32[]{:S(2)}) collective-permute-start(f32[1,8,128]{2,1,0:T(8,128)S(1)} %get-tuple-element.523), channel_id=1, source_target_pairs={{8,0},{16,8},{24,16},{9,1},{17,9},{25,17},{10,2},{18,10},{26,18},{... | collective-permute-start | bytes 12296 | tf_op jit(solution)/shard_map/ppermute | solution.py:51
  363.9 6.2 %collective-permute-start.56 = (f32[4,1,128]{2,1,0:T(1,128)S(1)}, f32[4,1,128]{2,1,0:T(1,128)S(1)}, u32[]{:S(2)}, u32[]{:S(2)}) collective-permute-start(f32[4,1,128]{2,1,0:T(1,128)S(1)} %get-tuple-element.500), channel_id=1, source_target_pairs={{0,4},{1,5},{2,6},{3,7},{8,12},{9,13},{10,14},{11,15},{16,20},{17,... | collective-permute-start | bytes 6152 | tf_op jit(solution)/shard_map/ppermute | solution.py:50
  368.2 5.5 %collective-permute-start.57 = (f32[4,1,128]{2,1,0:T(1,128)S(1)}, f32[4,1,128]{2,1,0:T(1,128)S(1)}, u32[]{:S(2)}, u32[]{:S(2)}) collective-permute-start(f32[4,1,128]{2,1,0:T(1,128)S(1)} %get-tuple-element.501), channel_id=1, source_target_pairs={{4,0},{5,1},{6,2},{7,3},{12,8},{13,9},{14,10},{15,11},{20,16},{21,... | collective-permute-start | bytes 6152 | tf_op jit(solution)/shard_map/ppermute | solution.py:51
  373.7 5.9 %collective-permute-start.58 = (f32[4,10,1]{2,1,0:T(8,128)S(1)}, f32[4,10,1]{2,1,0:T(8,128)S(1)}, u32[]{:S(2)}, u32[]{:S(2)}) collective-permute-start(f32[4,10,1]{2,1,0:T(8,128)S(1)} %get-tuple-element.496), channel_id=1, source_target_pairs={{0,1},{1,2},{2,3},{4,5},{5,6},{6,7},{8,9},{9,10},{10,11},{12,13},{... | collective-permute-start | bytes 488 | tf_op jit(solution)/shard_map/ppermute | solution.py:50
  377.6 6.1 %collective-permute-start.59 = (f32[4,10,1]{2,1,0:T(8,128)S(1)}, f32[4,10,1]{2,1,0:T(8,128)S(1)}, u32[]{:S(2)}, u32[]{:S(2)}) collective-permute-start(f32[4,10,1]{2,1,0:T(8,128)S(1)} %get-tuple-element.497), channel_id=1, source_target_pairs={{1,0},{2,1},{3,2},{5,4},{6,5},{7,6},{9,8},{10,9},{11,10},{13,12},{... | collective-permute-start | bytes 488 | tf_op jit(solution)/shard_map/ppermute | solution.py:51
  (4 other events, 2.7 us)
where the time goes:
time: 387 us; the launch traced here: 385 us
  starting transfers between devices  165 us (43%)
  blocking collectives  122 us (32%)
  other arithmetic  33.8 us (9%)
  waiting for transfers between devices  29.1 us (8%)
  local copies, waits for them, and re-layouts  28.1 us (7%)
  between operations  6.13 us (2%)
    ppermute x30, starting transfers between devices, extended(): before = lax.ppermute(last, axis, up)  126 us
    psum x3, blocking collectives, body(): totals = lax.psum(local, ('grp', 'gy', 'gx'))  122 us
    ppermute x30, starting transfers between devices, extended(): after = lax.ppermute(leading, axis, down)  38.8 us
    ppermute x30, waiting for transfers between devices, extended(): after = lax.ppermute(leading, axis, down)  17.6 us
    unnamed x157, other arithmetic  16.3 us
    ppermute x30, waiting for transfers between devices, extended(): before = lax.ppermute(last, axis, up)  11.4 us
    reduce_sum x24, other arithmetic, block_sums(): return jnp.sum(project(flat, row[:, None], beta), axis=1)  8.58 us
  transfers between devices with their start and end apart: 60, of which 18 were waited for; matrix products, arithmetic and copies ran while one was open for 9% of the time, Pallas kernels for 0%

commit v1 on v0

--- a/solution.py
+++ b/solution.py
@@ -1,7 +1,11 @@
+import functools
+
 import jax
 import jax.numpy as jnp
 import numpy as np
 from jax import lax
+from jax.experimental import pallas as pl
+from jax.experimental.pallas import tpu as pltpu
 from jax.sharding import PartitionSpec as P
 
 STEPS = 4
@@ -125,28 +129,57 @@
     return (jnp.tanh(beta * thresh) + jnp.tanh(beta * (filtered - thresh))) / denom
 
 
+def threshold_kernel(cells, beta_ref, filtered_ref, eta_ref, raised_ref):
+    beta = jnp.full((8, 128), beta_ref[0], jnp.float32)
+    raised_ref[...] = jnp.exp(2.0 * beta_ref[0] * filtered_ref[...])
+    top = jnp.exp(2.0 * beta)
+    rows = filtered_ref.shape[0]
+    span = min(rows, 512)
+
+    def halve(step, ends):
+        low, high = ends
+        middle = 0.5 * (low + high)
+        level = jnp.exp(2.0 * beta * middle)
+
+        def part(index, total):
+            for row in range(0, span, 8):
+                raised = raised_ref[pl.ds(pl.multiple_of(index * span + row, 8), 8), :]
+                total = total + (raised - 1.0) / (raised + level)
+            return total
+
+        total = lax.fori_loop(0, rows // span, part, jnp.zeros((8, 128), jnp.float32))
+        volume = jnp.sum(jnp.sum(total, axis=0, keepdims=True), axis=1, keepdims=True)
+        above = volume * ((top + level) / (top - 1.0)) > fluid_share * cells
+        return jnp.where(above, middle, low), jnp.where(above, high, middle)
+
+    low, high = lax.fori_loop(
+        0, BISECT, halve, (jnp.zeros((8, 128), jnp.float32), jnp.ones((8, 128), jnp.float32))
+    )
+    eta_ref[...] = 0.5 * (low + high)
+
+
+def threshold(filtered, beta, cells):
+    eta = pl.pallas_call(
+        functools.partial(threshold_kernel, cells),
+        out_shape=jax.ShapeDtypeStruct((8, 128), jnp.float32),
+        in_specs=[
+            pl.BlockSpec(memory_space=pltpu.SMEM),
+            pl.BlockSpec(memory_space=pltpu.VMEM),
+        ],
+        out_specs=pl.BlockSpec(memory_space=pltpu.VMEM),
+        scratch_shapes=[pltpu.VMEM(filtered.shape, jnp.float32)],
+        compiler_params=pltpu.CompilerParams(vmem_limit_bytes=40 * 2**20),
+        name="threshold",
+    )(beta.reshape(1), filtered)
+    return eta[0, 0]
+
+
 def body(design, populations, cotangent, wall_mask, inlet_mask, beta_step):
     beta = jnp.exp2(beta_step.astype(jnp.float32) / 16.0)
     filtered = smooth_field(design)
     cells = design.size * lax.axis_size("grp") * lax.axis_size("gy") * lax.axis_size("gx")
-    flat = filtered.reshape(1, -1)
-    offsets = (jnp.arange(1, 1025, dtype=jnp.float32) / 1024.0).reshape(8, 128)
-    usable = (jnp.arange(1024) < 1023).astype(jnp.float32)
-    low = jnp.zeros((), jnp.float32)
-    width = 1.0
-    for turn in range(BISECT // 10):
-        trials = low + width * offsets
-
-        def block_sums(row):
-            return jnp.sum(project(flat, row[:, None], beta), axis=1)
-
-        local = lax.map(block_sums, trials)
-        totals = lax.psum(local, ("grp", "gy", "gx"))
-        above = (totals.reshape(-1) > fluid_share * cells).astype(jnp.float32)
-        count = jnp.sum(above * usable)
-        low = low + width * count / 1024.0
-        width = width / 1024.0
-    eta = low + 0.5 * width
+    everywhere = lax.all_gather(filtered, ("grp", "gy", "gx"))
+    eta = threshold(everywhere.reshape(-1, filtered.shape[-1]), beta, cells)
     density_hat = project(filtered, eta, beta)
     alpha = alpha_most * penalty_shape * (1.0 - density_hat) / (penalty_shape + density_hat)
     states = []

time: 387 us -> 334 us (0.86)
  blocking collectives: 122 us -> 67 us
  other arithmetic: 33.8 us -> 28 us
  Pallas kernels: 0 us -> 5.09 us
    psum x3 -> x0, blocking collectives: 122 us -> none  [body(): totals = lax.psum(local, ('grp', 'gy', 'gx'))]
    all_gather x0 -> x1, blocking collectives: none -> 67 us  [body(): everywhere = lax.all_gather(filtered, ('grp', 'gy', 'gx'))]
    reduce_sum x27 -> x0, other arithmetic: 10.4 us -> none  [the longest x24 8.58 us: block_sums(): return jnp.sum(project(flat, row[:, None], beta), axis=1)]
    pallas_call x0 -> x1, Pallas kernels: none -> 5.09 us  [threshold(): pl.pallas_call(functools.partial(threshold_kernel, cells), out_shape=jax....]
  transfers between devices with their start and end apart: 60 -> 60, of which waited for: 18 -> 18; matrix products, arithmetic and copies ran while one was open for 9% -> 8% of each run, Pallas kernels for 0% -> 2%
where the time goes in v1:
time: 334 us; the launch traced here: 333 us
  starting transfers between devices  166 us (50%)
  blocking collectives  67 us (20%)
  waiting for transfers between devices  32.3 us (10%)
  local copies, waits for them, and re-layouts  29.2 us (9%)
  other arithmetic  28 us (8%)
  between operations  5.28 us (2%)
  Pallas kernels  5.09 us (2%)
    ppermute x30, starting transfers between devices, extended(): before = lax.ppermute(last, axis, up)  127 us
    all_gather x1, blocking collectives, body(): everywhere = lax.all_gather(filtered, ('grp', 'gy', 'gx'))  67 us
    ppermute x30, starting transfers between devices, extended(): after = lax.ppermute(leading, axis, down)  38.8 us
    ppermute x30, waiting for transfers between devices, extended(): after = lax.ppermute(leading, axis, down)  21.4 us
    unnamed x157, other arithmetic  18.6 us
    ppermute x30, waiting for transfers between devices, extended(): before = lax.ppermute(last, axis, up)  10.8 us
  transfers between devices with their start and end apart: 60, of which 18 were waited for; matrix products, arithmetic and copies ran while one was open for 8% of the time, Pallas kernels for 2%

profile of v1, /device:TPU:0, one launch (start us, length us, event | category | flops | bytes accessed | tf_op | source)
XLA Modules:
  0.0 332.5 jit_solution(1581917749845440097)
XLA Ops:
  1.3 2.3 collective-permute-start
  3.7 1.4 collective-permute-start.1
  6.1 5.2 %collective-permute-start.31 = (f32[19,1,8,128]{3,2,1,0:T(8,128)S(1)}, f32[19,1,8,128]{3,2,1,0:T(8,128)S(1)}, u32[]{:S(2)}, u32[]{:S(2)}) collective-permute-start(f32[19,1,8,128]{3,2,1,0:T(8,128)S(1)} %get-tuple-element.368), channel_id=1, source_target_pairs={{0,8},{8,16},{16,24},{1,9},{9,17},{17,25},{2,10},{10,18},{18,26},{... | collective-permute-start | bytes 233480 | tf_op jit(solution)/shard_map/ppermute | solution.py:54
  11.3 1.3 collective-permute-start.30
  14.2 3.4 %collective-permute-start.2 = (f32[4,1,128]{2,1,0:T(1,128)S(1)}, f32[4,1,128]{2,1,0:T(1,128)S(1)}, u32[]{:S(2)}, u32[]{:S(2)}) collective-permute-start(f32[4,1,128]{2,1,0:T(1,128)S(1)} %get-tuple-element.398), channel_id=1, source_target_pairs={{0,4},{1,5},{2,6},{3,7},{8,12},{9,13},{10,14},{11,15},{16,20},{17,... | collective-permute-start | bytes 6152 | tf_op jit(solution)/shard_map/ppermute | solution.py:54
  17.6 1.3 collective-permute-start.3
  19.6 3.5 %collective-permute-done.3 = f32[4,1,128]{2,1,0:T(1,128)S(1)} collective-permute-done((f32[4,1,128]{2,1,0:T(1,128)S(1)}, f32[4,1,128]{2,1,0:T(1,128)S(1)}, u32[]{:S(2)}, u32[]{:S(2)}) %collective-permute-start.3) | collective-permute-done | bytes 2080 | tf_op jit(solution)/shard_map/ppermute | solution.py:55
  23.2 3.5 %collective-permute-start.4 = (f32[4,10,1]{2,1,0:T(8,128)S(1)}, f32[4,10,1]{2,1,0:T(8,128)S(1)}, u32[]{:S(2)}, u32[]{:S(2)}) collective-permute-start(f32[4,10,1]{2,1,0:T(8,128)S(1)} %get-tuple-element.376), channel_id=1, source_target_pairs={{0,1},{1,2},{2,3},{4,5},{5,6},{6,7},{8,9},{9,10},{10,11},{12,13},{... | collective-permute-start | bytes 488 | tf_op jit(solution)/shard_map/ppermute | solution.py:54
  26.7 1.3 collective-permute-start.5
  28.4 4.1 %collective-permute-done.5 = f32[4,10,1]{2,1,0:T(8,128)S(1)} collective-permute-done((f32[4,10,1]{2,1,0:T(8,128)S(1)}, f32[4,10,1]{2,1,0:T(8,128)S(1)}, u32[]{:S(2)}, u32[]{:S(2)}) %collective-permute-start.5) | collective-permute-done | bytes 192 | tf_op jit(solution)/shard_map/ppermute | solution.py:55
  32.7 67.0 %all-gather = f32[64,8,128]{2,1,0:T(8,128)S(1)} all-gather(f32[2,8,128]{2,1,0:T(8,128)S(1)} %fusion.393), channel_id=2, replica_groups=mesh['grp'=4,'gy'=2,'gx'=4] {'grp','gy','gx'}, dimensions={0}, use_global_device_ids=true | all-gather | bytes 270336 | tf_op jit(solution)/shard_map/all_gather | solution.py:181
  99.7 5.1 %threshold.1 = f32[8,128]{1,0:T(8,128)S(1)} custom-call(f32[1]{0:T(128)} %bitcast.1.beta_ref, f32[512,128]{1,0:T(8,128)S(1)} %bitcast.1613), custom_call_target="tpu_custom_call" | custom-call | tf_op jit(solution)/shard_map/threshold/pallas_call | solution.py:162
  109.0 1.3 collective-permute-start.6
  110.3 3.0 collective-permute-start.7
  113.5 1.3 collective-permute-start.32
  114.8 4.5 %collective-permute-start.33 = (f32[19,4,1,128]{3,2,1,0:T(1,128)S(1)}, f32[19,4,1,128]{3,2,1,0:T(1,128)S(1)}, u32[]{:S(2)}, u32[]{:S(2)}) collective-permute-start(f32[19,4,1,128]{3,2,1,0:T(1,128)S(1)} %get-tuple-element.206), channel_id=1, source_target_pairs={{0,4},{1,5},{2,6},{3,7},{8,12},{9,13},{10,14},{11,15},{16,20},{17,... | collective-permute-start | bytes 116744 | tf_op jit(solution)/shard_map/ppermute | solution.py:54
  119.5 1.3 collective-permute-start.8
  120.8 4.5 %collective-permute-start.9 = (f32[19,4,1,128]{3,2,1,0:T(1,128)S(1)}, f32[19,4,1,128]{3,2,1,0:T(1,128)S(1)}, u32[]{:S(2)}, u32[]{:S(2)}) collective-permute-start(f32[19,4,1,128]{3,2,1,0:T(1,128)S(1)} %get-tuple-element.210), channel_id=1, source_target_pairs={{0,4},{1,5},{2,6},{3,7},{8,12},{9,13},{10,14},{11,15},{16,20},{17,... | collective-permute-start | bytes 116744 | tf_op jit(solution)/shard_map/ppermute | solution.py:54
  126.1 1.3 collective-permute-start.34
  127.9 4.5 %collective-permute-start.35 = (f32[19,4,10,1]{0,1,3,2:T(4,128)S(1)}, f32[19,4,10,1]{0,1,3,2:T(4,128)S(1)}, u32[]{:S(2)}, u32[]{:S(2)}) collective-permute-start(f32[19,4,10,1]{0,1,3,2:T(4,128)S(1)} %copy.26), channel_id=1, source_target_pairs={{0,1},{1,2},{2,3},{4,5},{5,6},{6,7},{8,9},{9,10},{10,11},{12,13},{... | collective-permute-start | bytes 9128 | tf_op jit(solution)/shard_map/ppermute | solution.py:54
  136.2 4.2 %collective-permute-start.11 = (f32[19,4,10,1]{0,1,3,2:T(4,128)S(1)}, f32[19,4,10,1]{0,1,3,2:T(4,128)S(1)}, u32[]{:S(2)}, u32[]{:S(2)}) collective-permute-start(f32[19,4,10,1]{0,1,3,2:T(4,128)S(1)} %copy.10), channel_id=1, source_target_pairs={{0,1},{1,2},{2,3},{4,5},{5,6},{6,7},{8,9},{9,10},{10,11},{12,13},{... | collective-permute-start | bytes 9128 | tf_op jit(solution)/shard_map/ppermute | solution.py:54
  140.8 1.3 collective-permute-start.10
  143.0 3.6 %collective-permute-done.10 = f32[19,4,10,1]{0,1,3,2:T(4,128)S(1)} collective-permute-done((f32[19,4,10,1]{0,1,3,2:T(4,128)S(1)}, f32[19,4,10,1]{0,1,3,2:T(4,128)S(1)}, u32[]{:S(2)}, u32[]{:S(2)}) %collective-permute-start.10) | collective-permute-done | bytes 3072 | tf_op jit(solution)/shard_map/ppermute | solution.py:55
  148.8 1.3 collective-permute-start.12
  150.1 3.0 collective-permute-start.13
  154.1 1.3 collective-permute-start.14
  155.4 4.5 %collective-permute-start.15 = (f32[19,4,1,128]{3,2,1,0:T(1,128)S(1)}, f32[19,4,1,128]{3,2,1,0:T(1,128)S(1)}, u32[]{:S(2)}, u32[]{:S(2)}) collective-permute-start(f32[19,4,1,128]{3,2,1,0:T(1,128)S(1)} %get-tuple-element.208), channel_id=1, source_target_pairs={{0,4},{1,5},{2,6},{3,7},{8,12},{9,13},{10,14},{11,15},{16,20},{17,... | collective-permute-start | bytes 116744 | tf_op jit(solution)/shard_map/ppermute | solution.py:54
  159.9 1.6 collective-permute-done.15
  164.0 4.5 %collective-permute-start.17 = (f32[19,4,10,1]{0,1,3,2:T(4,128)S(1)}, f32[19,4,10,1]{0,1,3,2:T(4,128)S(1)}, u32[]{:S(2)}, u32[]{:S(2)}) collective-permute-start(f32[19,4,10,1]{0,1,3,2:T(4,128)S(1)} %copy.14), channel_id=1, source_target_pairs={{0,1},{1,2},{2,3},{4,5},{5,6},{6,7},{8,9},{9,10},{10,11},{12,13},{... | collective-permute-start | bytes 9128 | tf_op jit(solution)/shard_map/ppermute | solution.py:54
  172.2 1.3 collective-permute-start.18
  173.5 4.4 %collective-permute-start.19 = (f32[19,1,8,128]{3,2,1,0:T(8,128)S(1)}, f32[19,1,8,128]{3,2,1,0:T(8,128)S(1)}, u32[]{:S(2)}, u32[]{:S(2)}) collective-permute-start(f32[19,1,8,128]{3,2,1,0:T(8,128)S(1)} %get-tuple-element.366), channel_id=1, source_target_pairs={{0,8},{8,16},{16,24},{1,9},{9,17},{17,25},{2,10},{10,18},{18,26},{... | collective-permute-start | bytes 233480 | tf_op jit(solution)/shard_map/ppermute | solution.py:54
  178.9 1.3 collective-permute-start.20
  180.2 4.5 %collective-permute-start.21 = (f32[19,4,1,128]{3,2,1,0:T(1,128)S(1)}, f32[19,4,1,128]{3,2,1,0:T(1,128)S(1)}, u32[]{:S(2)}, u32[]{:S(2)}) collective-permute-start(f32[19,4,1,128]{3,2,1,0:T(1,128)S(1)} %get-tuple-element.204), channel_id=1, source_target_pairs={{0,4},{1,5},{2,6},{3,7},{8,12},{9,13},{10,14},{11,15},{16,20},{17,... | collective-permute-start | bytes 116744 | tf_op jit(solution)/shard_map/ppermute | solution.py:54
  184.7 1.6 collective-permute-done.21
  188.8 4.7 %collective-permute-start.23 = (f32[19,4,10,1]{0,1,3,2:T(4,128)S(1)}, f32[19,4,10,1]{0,1,3,2:T(4,128)S(1)}, u32[]{:S(2)}, u32[]{:S(2)}) collective-permute-start(f32[19,4,10,1]{0,1,3,2:T(4,128)S(1)} %copy.18), channel_id=1, source_target_pairs={{0,1},{1,2},{2,3},{4,5},{5,6},{6,7},{8,9},{9,10},{10,11},{12,13},{... | collective-permute-start | bytes 9128 | tf_op jit(solution)/shard_map/ppermute | solution.py:54
  198.5 1.3 collective-permute-start.36
  199.8 6.1 %collective-permute-start.37 = (f32[19,1,8,128]{3,2,1,0:T(8,128)S(1)}, f32[19,1,8,128]{3,2,1,0:T(8,128)S(1)}, u32[]{:S(2)}, u32[]{:S(2)}) collective-permute-start(f32[19,1,8,128]{3,2,1,0:T(8,128)S(1)} %get-tuple-element.344), channel_id=1, source_target_pairs={{0,8},{8,16},{16,24},{1,9},{9,17},{17,25},{2,10},{10,18},{18,26},{... | collective-permute-start | bytes 233480 | tf_op jit(solution)/shard_map/ppermute | solution.py:54
  206.9 1.3 collective-permute-start.38
  208.2 4.5 %collective-permute-start.39 = (f32[19,4,1,128]{3,2,1,0:T(1,128)S(1)}, f32[19,4,1,128]{3,2,1,0:T(1,128)S(1)}, u32[]{:S(2)}, u32[]{:S(2)}) collective-permute-start(f32[19,4,1,128]{3,2,1,0:T(1,128)S(1)} %get-tuple-element.200), channel_id=1, source_target_pairs={{0,4},{1,5},{2,6},{3,7},{8,12},{9,13},{10,14},{11,15},{16,20},{17,... | collective-permute-start | bytes 116744 | tf_op jit(solution)/shard_map/ppermute | solution.py:54
  212.8 1.6 collective-permute-done.39
  215.2 1.3 collective-permute-start.40
  216.9 4.5 %collective-permute-start.41 = (f32[19,4,10,1]{0,1,3,2:T(4,128)S(1)}, f32[19,4,10,1]{0,1,3,2:T(4,128)S(1)}, u32[]{:S(2)}, u32[]{:S(2)}) collective-permute-start(f32[19,4,10,1]{0,1,3,2:T(4,128)S(1)} %copy.30), channel_id=1, source_target_pairs={{0,1},{1,2},{2,3},{4,5},{5,6},{6,7},{8,9},{9,10},{10,11},{12,13},{... | collective-permute-start | bytes 9128 | tf_op jit(solution)/shard_map/ppermute | solution.py:54
  225.6 1.3 collective-permute-start.42
  226.9 5.6 %collective-permute-start.43 = (f32[19,1,8,128]{3,2,1,0:T(8,128)S(1)}, f32[19,1,8,128]{3,2,1,0:T(8,128)S(1)}, u32[]{:S(2)}, u32[]{:S(2)}) collective-permute-start(f32[19,1,8,128]{3,2,1,0:T(8,128)S(1)} %get-tuple-element.324), channel_id=1, source_target_pairs={{0,8},{8,16},{16,24},{1,9},{9,17},{17,25},{2,10},{10,18},{18,26},{... | collective-permute-start | bytes 233480 | tf_op jit(solution)/shard_map/ppermute | solution.py:54
  232.5 6.3 %collective-permute-start.24 = (f32[19,1,8,128]{3,2,1,0:T(8,128)S(1)}, f32[19,1,8,128]{3,2,1,0:T(8,128)S(1)}, u32[]{:S(2)}, u32[]{:S(2)}) collective-permute-start(f32[19,1,8,128]{3,2,1,0:T(8,128)S(1)} %get-tuple-element.365), channel_id=1, source_target_pairs={{0,8},{8,16},{16,24},{1,9},{9,17},{17,25},{2,10},{10,18},{18,26},{... | collective-permute-start | bytes 233480 | tf_op jit(solution)/shard_map/ppermute | solution.py:54
  238.8 1.3 collective-permute-start.25
  240.2 1.3 collective-permute-start.44
  241.5 4.5 %collective-permute-start.45 = (f32[19,4,1,128]{3,2,1,0:T(1,128)S(1)}, f32[19,4,1,128]{3,2,1,0:T(1,128)S(1)}, u32[]{:S(2)}, u32[]{:S(2)}) collective-permute-start(f32[19,4,1,128]{3,2,1,0:T(1,128)S(1)} %get-tuple-element.198), channel_id=1, source_target_pairs={{0,4},{1,5},{2,6},{3,7},{8,12},{9,13},{10,14},{11,15},{16,20},{17,... | collective-permute-start | bytes 116744 | tf_op jit(solution)/shard_map/ppermute | solution.py:54
  246.1 1.3 collective-permute-start.26
  247.4 1.3 collective-permute-start.27
  251.3 4.8 %collective-permute-start.47 = (f32[19,4,10,1]{0,1,3,2:T(4,128)S(1)}, f32[19,4,10,1]{0,1,3,2:T(4,128)S(1)}, u32[]{:S(2)}, u32[]{:S(2)}) collective-permute-start(f32[19,4,10,1]{0,1,3,2:T(4,128)S(1)} %copy.34), channel_id=1, source_target_pairs={{0,1},{1,2},{2,3},{4,5},{5,6},{6,7},{8,9},{9,10},{10,11},{12,13},{... | collective-permute-start | bytes 9128 | tf_op jit(solution)/shard_map/ppermute | solution.py:54
  257.0 3.9 %collective-permute-start.28 = (f32[19,4,10,1]{0,1,3,2:T(4,128)S(1)}, f32[19,4,10,1]{0,1,3,2:T(4,128)S(1)}, u32[]{:S(2)}, u32[]{:S(2)}) collective-permute-start(f32[19,4,10,1]{0,1,3,2:T(4,128)S(1)} %copy.20), channel_id=1, source_target_pairs={{0,1},{1,2},{2,3},{4,5},{5,6},{6,7},{8,9},{9,10},{10,11},{12,13},{... | collective-permute-start | bytes 9128 | tf_op jit(solution)/shard_map/ppermute | solution.py:54
  268.7 3.6 %collective-permute-start.49 = (f32[19,1,8,128]{3,2,1,0:T(8,128)S(1)}, f32[19,1,8,128]{3,2,1,0:T(8,128)S(1)}, u32[]{:S(2)}, u32[]{:S(2)}) collective-permute-start(f32[19,1,8,128]{3,2,1,0:T(8,128)S(1)} %get-tuple-element.304), channel_id=1, source_target_pairs={{0,8},{8,16},{16,24},{1,9},{9,17},{17,25},{2,10},{10,18},{18,26},{... | collective-permute-start | bytes 233480 | tf_op jit(solution)/shard_map/ppermute | solution.py:54
  276.4 4.5 %collective-permute-start.51 = (f32[19,4,1,128]{3,2,1,0:T(1,128)S(1)}, f32[19,4,1,128]{3,2,1,0:T(1,128)S(1)}, u32[]{:S(2)}, u32[]{:S(2)}) collective-permute-start(f32[19,4,1,128]{3,2,1,0:T(1,128)S(1)} %get-tuple-element.196), channel_id=1, source_target_pairs={{0,4},{1,5},{2,6},{3,7},{8,12},{9,13},{10,14},{11,15},{16,20},{17,... | collective-permute-start | bytes 116744 | tf_op jit(solution)/shard_map/ppermute | solution.py:54
  285.1 4.9 %collective-permute-start.53 = (f32[19,4,10,1]{0,1,3,2:T(4,128)S(1)}, f32[19,4,10,1]{0,1,3,2:T(4,128)S(1)}, u32[]{:S(2)}, u32[]{:S(2)}) collective-permute-start(f32[19,4,10,1]{0,1,3,2:T(4,128)S(1)} %copy.38), channel_id=1, source_target_pairs={{0,1},{1,2},{2,3},{4,5},{5,6},{6,7},{8,9},{9,10},{10,11},{12,13},{... | collective-permute-start | bytes 9128 | tf_op jit(solution)/shard_map/ppermute | solution.py:54
  304.3 3.0 collective-permute-start.54
  307.3 1.3 collective-permute-start.55
  309.3 2.6 collective-permute-done.55
  311.9 4.2 %collective-permute-start.56 = (f32[4,1,128]{2,1,0:T(1,128)S(1)}, f32[4,1,128]{2,1,0:T(1,128)S(1)}, u32[]{:S(2)}, u32[]{:S(2)}) collective-permute-start(f32[4,1,128]{2,1,0:T(1,128)S(1)} %get-tuple-element.378), channel_id=1, source_target_pairs={{0,4},{1,5},{2,6},{3,7},{8,12},{9,13},{10,14},{11,15},{16,20},{17,... | collective-permute-start | bytes 6152 | tf_op jit(solution)/shard_map/ppermute | solution.py:54
  316.1 1.3 collective-permute-start.57
  318.1 3.5 %collective-permute-done.57 = f32[4,1,128]{2,1,0:T(1,128)S(1)} collective-permute-done((f32[4,1,128]{2,1,0:T(1,128)S(1)}, f32[4,1,128]{2,1,0:T(1,128)S(1)}, u32[]{:S(2)}, u32[]{:S(2)}) %collective-permute-start.57) | collective-permute-done | bytes 2080 | tf_op jit(solution)/shard_map/ppermute | solution.py:55
  321.7 3.9 %collective-permute-start.58 = (f32[4,10,1]{2,1,0:T(8,128)S(1)}, f32[4,10,1]{2,1,0:T(8,128)S(1)}, u32[]{:S(2)}, u32[]{:S(2)}) collective-permute-start(f32[4,10,1]{2,1,0:T(8,128)S(1)} %get-tuple-element.374), channel_id=1, source_target_pairs={{0,1},{1,2},{2,3},{4,5},{5,6},{6,7},{8,9},{9,10},{10,11},{12,13},{... | collective-permute-start | bytes 488 | tf_op jit(solution)/shard_map/ppermute | solution.py:54
  325.6 1.3 collective-permute-start.59
  327.6 4.1 %collective-permute-done.59 = f32[4,10,1]{2,1,0:T(8,128)S(1)} collective-permute-done((f32[4,10,1]{2,1,0:T(8,128)S(1)}, f32[4,10,1]{2,1,0:T(8,128)S(1)}, u32[]{:S(2)}, u32[]{:S(2)}) %collective-permute-start.59) | collective-permute-done | bytes 192 | tf_op jit(solution)/shard_map/ppermute | solution.py:55
  (471 shorter events, 72.3 us)
Async XLA Ops:
  1.3 12.2 %collective-permute-start = (f32[1,8,128]{2,1,0:T(8,128)S(1)}, f32[1,8,128]{2,1,0:T(8,128)S(1)}, u32[]{:S(2)}, u32[]{:S(2)}) collective-permute-start(f32[1,8,128]{2,1,0:T(8,128)S(1)} %get-tuple-element.469), channel_id=1, source_target_pairs={{0,8},{8,16},{16,24},{1,9},{9,17},{17,25},{2,10},{10,18},{18,26},{... | collective-permute-start | bytes 12296 | tf_op jit(solution)/shard_map/ppermute | solution.py:54
  3.7 8.9 %copy-start = (f32[19,2,8,128]{3,2,1,0:T(8,128)S(1)}, f32[19,2,8,128]{3,2,1,0:T(8,128)}, u32[]{:S(2)}) copy-start(f32[19,2,8,128]{3,2,1,0:T(8,128)} %param.8) | copy-start | bytes 466948
  3.7 8.9 %copy-start.2 = (f32[19,2,8,128]{3,2,1,0:T(8,128)S(1)}, f32[19,2,8,128]{3,2,1,0:T(8,128)}, u32[]{:S(2)}) copy-start(f32[19,2,8,128]{3,2,1,0:T(8,128)} %param.7) | copy-start | bytes 466948
  3.7 10.5 %collective-permute-start.1 = (f32[1,8,128]{2,1,0:T(8,128)S(1)}, f32[1,8,128]{2,1,0:T(8,128)S(1)}, u32[]{:S(2)}, u32[]{:S(2)}) collective-permute-start(f32[1,8,128]{2,1,0:T(8,128)S(1)} %get-tuple-element.468), channel_id=1, source_target_pairs={{8,0},{16,8},{24,16},{9,1},{17,9},{25,17},{10,2},{18,10},{26,18},{... | collective-permute-start | bytes 12296 | tf_op jit(solution)/shard_map/ppermute | solution.py:55
  6.1 107.3 %collective-permute-start.31 = (f32[19,1,8,128]{3,2,1,0:T(8,128)S(1)}, f32[19,1,8,128]{3,2,1,0:T(8,128)S(1)}, u32[]{:S(2)}, u32[]{:S(2)}) collective-permute-start(f32[19,1,8,128]{3,2,1,0:T(8,128)S(1)} %get-tuple-element.368), channel_id=1, source_target_pairs={{0,8},{8,16},{16,24},{1,9},{9,17},{17,25},{2,10},{10,18},{18,26},{... | collective-permute-start | bytes 233480 | tf_op jit(solution)/shard_map/ppermute | solution.py:54
  11.3 102.2 %collective-permute-start.30 = (f32[19,1,8,128]{3,2,1,0:T(8,128)S(1)}, f32[19,1,8,128]{3,2,1,0:T(8,128)S(1)}, u32[]{:S(2)}, u32[]{:S(2)}) collective-permute-start(f32[19,1,8,128]{3,2,1,0:T(8,128)S(1)} %get-tuple-element.369), channel_id=1, source_target_pairs={{8,0},{16,8},{24,16},{9,1},{17,9},{25,17},{10,2},{18,10},{26,18},{... | collective-permute-start | bytes 233480 | tf_op jit(solution)/shard_map/ppermute | solution.py:55
  14.2 5.4 %collective-permute-start.2 = (f32[4,1,128]{2,1,0:T(1,128)S(1)}, f32[4,1,128]{2,1,0:T(1,128)S(1)}, u32[]{:S(2)}, u32[]{:S(2)}) collective-permute-start(f32[4,1,128]{2,1,0:T(1,128)S(1)} %get-tuple-element.398), channel_id=1, source_target_pairs={{0,4},{1,5},{2,6},{3,7},{8,12},{9,13},{10,14},{11,15},{16,20},{17,... | collective-permute-start | bytes 6152 | tf_op jit(solution)/shard_map/ppermute | solution.py:54
  17.6 5.5 %collective-permute-start.3 = (f32[4,1,128]{2,1,0:T(1,128)S(1)}, f32[4,1,128]{2,1,0:T(1,128)S(1)}, u32[]{:S(2)}, u32[]{:S(2)}) collective-permute-start(f32[4,1,128]{2,1,0:T(1,128)S(1)} %get-tuple-element.399), channel_id=1, source_target_pairs={{4,0},{5,1},{6,2},{7,3},{12,8},{13,9},{14,10},{15,11},{20,16},{21,... | collective-permute-start | bytes 6152 | tf_op jit(solution)/shard_map/ppermute | solution.py:55
  23.2 5.2 %collective-permute-start.4 = (f32[4,10,1]{2,1,0:T(8,128)S(1)}, f32[4,10,1]{2,1,0:T(8,128)S(1)}, u32[]{:S(2)}, u32[]{:S(2)}) collective-permute-start(f32[4,10,1]{2,1,0:T(8,128)S(1)} %get-tuple-element.376), channel_id=1, source_target_pairs={{0,1},{1,2},{2,3},{4,5},{5,6},{6,7},{8,9},{9,10},{10,11},{12,13},{... | collective-permute-start | bytes 488 | tf_op jit(solution)/shard_map/ppermute | solution.py:54
  26.7 5.8 %collective-permute-start.5 = (f32[4,10,1]{2,1,0:T(8,128)S(1)}, f32[4,10,1]{2,1,0:T(8,128)S(1)}, u32[]{:S(2)}, u32[]{:S(2)}) collective-permute-start(f32[4,10,1]{2,1,0:T(8,128)S(1)} %get-tuple-element.377), channel_id=1, source_target_pairs={{1,0},{2,1},{3,2},{5,4},{6,5},{7,6},{9,8},{10,9},{11,10},{13,12},{... | collective-permute-start | bytes 488 | tf_op jit(solution)/shard_map/ppermute | solution.py:55
  108.0 0.9 copy-start.1
  109.0 10.4 %collective-permute-start.6 = (f32[19,1,8,128]{3,2,1,0:T(8,128)S(1)}, f32[19,1,8,128]{3,2,1,0:T(8,128)S(1)}, u32[]{:S(2)}, u32[]{:S(2)}) collective-permute-start(f32[19,1,8,128]{3,2,1,0:T(8,128)S(1)} %get-tuple-element.373), channel_id=1, source_target_pairs={{8,0},{16,8},{24,16},{9,1},{17,9},{25,17},{10,2},{18,10},{26,18},{... | collective-permute-start | bytes 233480 | tf_op jit(solution)/shard_map/ppermute | solution.py:55
  110.3 9.1 %collective-permute-start.7 = (f32[19,1,8,128]{3,2,1,0:T(8,128)S(1)}, f32[19,1,8,128]{3,2,1,0:T(8,128)S(1)}, u32[]{:S(2)}, u32[]{:S(2)}) collective-permute-start(f32[19,1,8,128]{3,2,1,0:T(8,128)S(1)} %get-tuple-element.372), channel_id=1, source_target_pairs={{0,8},{8,16},{16,24},{1,9},{9,17},{17,25},{2,10},{10,18},{18,26},{... | collective-permute-start | bytes 233480 | tf_op jit(solution)/shard_map/ppermute | solution.py:54
  113.5 11.8 %collective-permute-start.32 = (f32[19,4,1,128]{3,2,1,0:T(1,128)S(1)}, f32[19,4,1,128]{3,2,1,0:T(1,128)S(1)}, u32[]{:S(2)}, u32[]{:S(2)}) collective-permute-start(f32[19,4,1,128]{3,2,1,0:T(1,128)S(1)} %get-tuple-element.207), channel_id=1, source_target_pairs={{4,0},{5,1},{6,2},{7,3},{12,8},{13,9},{14,10},{15,11},{20,16},{21,... | collective-permute-start | bytes 116744 | tf_op jit(solution)/shard_map/ppermute | solution.py:55
  114.8 10.5 %collective-permute-start.33 = (f32[19,4,1,128]{3,2,1,0:T(1,128)S(1)}, f32[19,4,1,128]{3,2,1,0:T(1,128)S(1)}, u32[]{:S(2)}, u32[]{:S(2)}) collective-permute-start(f32[19,4,1,128]{3,2,1,0:T(1,128)S(1)} %get-tuple-element.206), channel_id=1, source_target_pairs={{0,4},{1,5},{2,6},{3,7},{8,12},{9,13},{10,14},{11,15},{16,20},{17,... | collective-permute-start | bytes 116744 | tf_op jit(solution)/shard_map/ppermute | solution.py:54
  119.5 15.9 %collective-permute-start.8 = (f32[19,4,1,128]{3,2,1,0:T(1,128)S(1)}, f32[19,4,1,128]{3,2,1,0:T(1,128)S(1)}, u32[]{:S(2)}, u32[]{:S(2)}) collective-permute-start(f32[19,4,1,128]{3,2,1,0:T(1,128)S(1)} %get-tuple-element.211), channel_id=1, source_target_pairs={{4,0},{5,1},{6,2},{7,3},{12,8},{13,9},{14,10},{15,11},{20,16},{21,... | collective-permute-start | bytes 116744 | tf_op jit(solution)/shard_map/ppermute | solution.py:55
  120.8 14.6 %collective-permute-start.9 = (f32[19,4,1,128]{3,2,1,0:T(1,128)S(1)}, f32[19,4,1,128]{3,2,1,0:T(1,128)S(1)}, u32[]{:S(2)}, u32[]{:S(2)}) collective-permute-start(f32[19,4,1,128]{3,2,1,0:T(1,128)S(1)} %get-tuple-element.210), channel_id=1, source_target_pairs={{0,4},{1,5},{2,6},{3,7},{8,12},{9,13},{10,14},{11,15},{16,20},{17,... | collective-permute-start | bytes 116744 | tf_op jit(solution)/shard_map/ppermute | solution.py:54
  126.1 6.3 %collective-permute-start.34 = (f32[19,4,10,1]{0,1,3,2:T(4,128)S(1)}, f32[19,4,10,1]{0,1,3,2:T(4,128)S(1)}, u32[]{:S(2)}, u32[]{:S(2)}) collective-permute-start(f32[19,4,10,1]{0,1,3,2:T(4,128)S(1)} %copy.24), channel_id=1, source_target_pairs={{1,0},{2,1},{3,2},{5,4},{6,5},{7,6},{9,8},{10,9},{11,10},{13,12},{... | collective-permute-start | bytes 9128 | tf_op jit(solution)/shard_map/ppermute | solution.py:55
  127.9 6.0 %collective-permute-start.35 = (f32[19,4,10,1]{0,1,3,2:T(4,128)S(1)}, f32[19,4,10,1]{0,1,3,2:T(4,128)S(1)}, u32[]{:S(2)}, u32[]{:S(2)}) collective-permute-start(f32[19,4,10,1]{0,1,3,2:T(4,128)S(1)} %copy.26), channel_id=1, source_target_pairs={{0,1},{1,2},{2,3},{4,5},{5,6},{6,7},{8,9},{9,10},{10,11},{12,13},{... | collective-permute-start | bytes 9128 | tf_op jit(solution)/shard_map/ppermute | solution.py:54
  136.2 6.0 %collective-permute-start.11 = (f32[19,4,10,1]{0,1,3,2:T(4,128)S(1)}, f32[19,4,10,1]{0,1,3,2:T(4,128)S(1)}, u32[]{:S(2)}, u32[]{:S(2)}) collective-permute-start(f32[19,4,10,1]{0,1,3,2:T(4,128)S(1)} %copy.10), channel_id=1, source_target_pairs={{0,1},{1,2},{2,3},{4,5},{5,6},{6,7},{8,9},{9,10},{10,11},{12,13},{... | collective-permute-start | bytes 9128 | tf_op jit(solution)/shard_map/ppermute | solution.py:54
  140.8 5.7 %collective-permute-start.10 = (f32[19,4,10,1]{0,1,3,2:T(4,128)S(1)}, f32[19,4,10,1]{0,1,3,2:T(4,128)S(1)}, u32[]{:S(2)}, u32[]{:S(2)}) collective-permute-start(f32[19,4,10,1]{0,1,3,2:T(4,128)S(1)} %copy.8), channel_id=1, source_target_pairs={{1,0},{2,1},{3,2},{5,4},{6,5},{7,6},{9,8},{10,9},{11,10},{13,12},{... | collective-permute-start | bytes 9128 | tf_op jit(solution)/shard_map/ppermute | solution.py:55
  148.8 4.3 %collective-permute-start.12 = (f32[19,1,8,128]{3,2,1,0:T(8,128)S(1)}, f32[19,1,8,128]{3,2,1,0:T(8,128)S(1)}, u32[]{:S(2)}, u32[]{:S(2)}) collective-permute-start(f32[19,1,8,128]{3,2,1,0:T(8,128)S(1)} %get-tuple-element.371), channel_id=1, source_target_pairs={{8,0},{16,8},{24,16},{9,1},{17,9},{25,17},{10,2},{18,10},{26,18},{... | collective-permute-start | bytes 233480 | tf_op jit(solution)/shard_map/ppermute | solution.py:55
  150.1 3.9 %collective-permute-start.13 = (f32[19,1,8,128]{3,2,1,0:T(8,128)S(1)}, f32[19,1,8,128]{3,2,1,0:T(8,128)S(1)}, u32[]{:S(2)}, u32[]{:S(2)}) collective-permute-start(f32[19,1,8,128]{3,2,1,0:T(8,128)S(1)} %get-tuple-element.370), channel_id=1, source_target_pairs={{0,8},{8,16},{16,24},{1,9},{9,17},{17,25},{2,10},{10,18},{18,26},{... | collective-permute-start | bytes 233480 | tf_op jit(solution)/shard_map/ppermute | solution.py:54
  154.1 5.9 %collective-permute-start.14 = (f32[19,4,1,128]{3,2,1,0:T(1,128)S(1)}, f32[19,4,1,128]{3,2,1,0:T(1,128)S(1)}, u32[]{:S(2)}, u32[]{:S(2)}) collective-permute-start(f32[19,4,1,128]{3,2,1,0:T(1,128)S(1)} %get-tuple-element.209), channel_id=1, source_target_pairs={{4,0},{5,1},{6,2},{7,3},{12,8},{13,9},{14,10},{15,11},{20,16},{21,... | collective-permute-start | bytes 116744 | tf_op jit(solution)/shard_map/ppermute | solution.py:55
  155.4 6.2 %collective-permute-start.15 = (f32[19,4,1,128]{3,2,1,0:T(1,128)S(1)}, f32[19,4,1,128]{3,2,1,0:T(1,128)S(1)}, u32[]{:S(2)}, u32[]{:S(2)}) collective-permute-start(f32[19,4,1,128]{3,2,1,0:T(1,128)S(1)} %get-tuple-element.208), channel_id=1, source_target_pairs={{0,4},{1,5},{2,6},{3,7},{8,12},{9,13},{10,14},{11,15},{16,20},{17,... | collective-permute-start | bytes 116744 | tf_op jit(solution)/shard_map/ppermute | solution.py:54
  162.3 6.3 %collective-permute-start.16 = (f32[19,4,10,1]{0,1,3,2:T(4,128)S(1)}, f32[19,4,10,1]{0,1,3,2:T(4,128)S(1)}, u32[]{:S(2)}, u32[]{:S(2)}) collective-permute-start(f32[19,4,10,1]{0,1,3,2:T(4,128)S(1)} %copy.12), channel_id=1, source_target_pairs={{1,0},{2,1},{3,2},{5,4},{6,5},{7,6},{9,8},{10,9},{11,10},{13,12},{... | collective-permute-start | bytes 9128 | tf_op jit(solution)/shard_map/ppermute | solution.py:55
  164.0 6.0 %collective-permute-start.17 = (f32[19,4,10,1]{0,1,3,2:T(4,128)S(1)}, f32[19,4,10,1]{0,1,3,2:T(4,128)S(1)}, u32[]{:S(2)}, u32[]{:S(2)}) collective-permute-start(f32[19,4,10,1]{0,1,3,2:T(4,128)S(1)} %copy.14), channel_id=1, source_target_pairs={{0,1},{1,2},{2,3},{4,5},{5,6},{6,7},{8,9},{9,10},{10,11},{12,13},{... | collective-permute-start | bytes 9128 | tf_op jit(solution)/shard_map/ppermute | solution.py:54
  172.2 5.7 %collective-permute-start.18 = (f32[19,1,8,128]{3,2,1,0:T(8,128)S(1)}, f32[19,1,8,128]{3,2,1,0:T(8,128)S(1)}, u32[]{:S(2)}, u32[]{:S(2)}) collective-permute-start(f32[19,1,8,128]{3,2,1,0:T(8,128)S(1)} %get-tuple-element.367), channel_id=1, source_target_pairs={{8,0},{16,8},{24,16},{9,1},{17,9},{25,17},{10,2},{18,10},{26,18},{... | collective-permute-start | bytes 233480 | tf_op jit(solution)/shard_map/ppermute | solution.py:55
  173.5 5.3 %collective-permute-start.19 = (f32[19,1,8,128]{3,2,1,0:T(8,128)S(1)}, f32[19,1,8,128]{3,2,1,0:T(8,128)S(1)}, u32[]{:S(2)}, u32[]{:S(2)}) collective-permute-start(f32[19,1,8,128]{3,2,1,0:T(8,128)S(1)} %get-tuple-element.366), channel_id=1, source_target_pairs={{0,8},{8,16},{16,24},{1,9},{9,17},{17,25},{2,10},{10,18},{18,26},{... | collective-permute-start | bytes 233480 | tf_op jit(solution)/shard_map/ppermute | solution.py:54
  178.9 5.9 %collective-permute-start.20 = (f32[19,4,1,128]{3,2,1,0:T(1,128)S(1)}, f32[19,4,1,128]{3,2,1,0:T(1,128)S(1)}, u32[]{:S(2)}, u32[]{:S(2)}) collective-permute-start(f32[19,4,1,128]{3,2,1,0:T(1,128)S(1)} %get-tuple-element.205), channel_id=1, source_target_pairs={{4,0},{5,1},{6,2},{7,3},{12,8},{13,9},{14,10},{15,11},{20,16},{21,... | collective-permute-start | bytes 116744 | tf_op jit(solution)/shard_map/ppermute | solution.py:55
  180.2 6.2 %collective-permute-start.21 = (f32[19,4,1,128]{3,2,1,0:T(1,128)S(1)}, f32[19,4,1,128]{3,2,1,0:T(1,128)S(1)}, u32[]{:S(2)}, u32[]{:S(2)}) collective-permute-start(f32[19,4,1,128]{3,2,1,0:T(1,128)S(1)} %get-tuple-element.204), channel_id=1, source_target_pairs={{0,4},{1,5},{2,6},{3,7},{8,12},{9,13},{10,14},{11,15},{16,20},{17,... | collective-permute-start | bytes 116744 | tf_op jit(solution)/shard_map/ppermute | solution.py:54
  187.1 6.5 %collective-permute-start.22 = (f32[19,4,10,1]{0,1,3,2:T(4,128)S(1)}, f32[19,4,10,1]{0,1,3,2:T(4,128)S(1)}, u32[]{:S(2)}, u32[]{:S(2)}) collective-permute-start(f32[19,4,10,1]{0,1,3,2:T(4,128)S(1)} %copy.16), channel_id=1, source_target_pairs={{1,0},{2,1},{3,2},{5,4},{6,5},{7,6},{9,8},{10,9},{11,10},{13,12},{... | collective-permute-start | bytes 9128 | tf_op jit(solution)/shard_map/ppermute | solution.py:55
  188.8 6.0 %collective-permute-start.23 = (f32[19,4,10,1]{0,1,3,2:T(4,128)S(1)}, f32[19,4,10,1]{0,1,3,2:T(4,128)S(1)}, u32[]{:S(2)}, u32[]{:S(2)}) collective-permute-start(f32[19,4,10,1]{0,1,3,2:T(4,128)S(1)} %copy.18), channel_id=1, source_target_pairs={{0,1},{1,2},{2,3},{4,5},{5,6},{6,7},{8,9},{9,10},{10,11},{12,13},{... | collective-permute-start | bytes 9128 | tf_op jit(solution)/shard_map/ppermute | solution.py:54
  198.5 7.5 %collective-permute-start.36 = (f32[19,1,8,128]{3,2,1,0:T(8,128)S(1)}, f32[19,1,8,128]{3,2,1,0:T(8,128)S(1)}, u32[]{:S(2)}, u32[]{:S(2)}) collective-permute-start(f32[19,1,8,128]{3,2,1,0:T(8,128)S(1)} %get-tuple-element.345), channel_id=1, source_target_pairs={{8,0},{16,8},{24,16},{9,1},{17,9},{25,17},{10,2},{18,10},{26,18},{... | collective-permute-start | bytes 233480 | tf_op jit(solution)/shard_map/ppermute | solution.py:55
  199.8 7.0 %collective-permute-start.37 = (f32[19,1,8,128]{3,2,1,0:T(8,128)S(1)}, f32[19,1,8,128]{3,2,1,0:T(8,128)S(1)}, u32[]{:S(2)}, u32[]{:S(2)}) collective-permute-start(f32[19,1,8,128]{3,2,1,0:T(8,128)S(1)} %get-tuple-element.344), channel_id=1, source_target_pairs={{0,8},{8,16},{16,24},{1,9},{9,17},{17,25},{2,10},{10,18},{18,26},{... | collective-permute-start | bytes 233480 | tf_op jit(solution)/shard_map/ppermute | solution.py:54
  206.9 5.9 %collective-permute-start.38 = (f32[19,4,1,128]{3,2,1,0:T(1,128)S(1)}, f32[19,4,1,128]{3,2,1,0:T(1,128)S(1)}, u32[]{:S(2)}, u32[]{:S(2)}) collective-permute-start(f32[19,4,1,128]{3,2,1,0:T(1,128)S(1)} %get-tuple-element.201), channel_id=1, source_target_pairs={{4,0},{5,1},{6,2},{7,3},{12,8},{13,9},{14,10},{15,11},{20,16},{21,... | collective-permute-start | bytes 116744 | tf_op jit(solution)/shard_map/ppermute | solution.py:55
  208.2 6.2 %collective-permute-start.39 = (f32[19,4,1,128]{3,2,1,0:T(1,128)S(1)}, f32[19,4,1,128]{3,2,1,0:T(1,128)S(1)}, u32[]{:S(2)}, u32[]{:S(2)}) collective-permute-start(f32[19,4,1,128]{3,2,1,0:T(1,128)S(1)} %get-tuple-element.200), channel_id=1, source_target_pairs={{0,4},{1,5},{2,6},{3,7},{8,12},{9,13},{10,14},{11,15},{16,20},{17,... | collective-permute-start | bytes 116744 | tf_op jit(solution)/shard_map/ppermute | solution.py:54
  215.2 6.3 %collective-permute-start.40 = (f32[19,4,10,1]{0,1,3,2:T(4,128)S(1)}, f32[19,4,10,1]{0,1,3,2:T(4,128)S(1)}, u32[]{:S(2)}, u32[]{:S(2)}) collective-permute-start(f32[19,4,10,1]{0,1,3,2:T(4,128)S(1)} %copy.28), channel_id=1, source_target_pairs={{1,0},{2,1},{3,2},{5,4},{6,5},{7,6},{9,8},{10,9},{11,10},{13,12},{... | collective-permute-start | bytes 9128 | tf_op jit(solution)/shard_map/ppermute | solution.py:55
  216.9 6.0 %collective-permute-start.41 = (f32[19,4,10,1]{0,1,3,2:T(4,128)S(1)}, f32[19,4,10,1]{0,1,3,2:T(4,128)S(1)}, u32[]{:S(2)}, u32[]{:S(2)}) collective-permute-start(f32[19,4,10,1]{0,1,3,2:T(4,128)S(1)} %copy.30), channel_id=1, source_target_pairs={{0,1},{1,2},{2,3},{4,5},{5,6},{6,7},{8,9},{9,10},{10,11},{12,13},{... | collective-permute-start | bytes 9128 | tf_op jit(solution)/shard_map/ppermute | solution.py:54
  225.6 14.5 %collective-permute-start.42 = (f32[19,1,8,128]{3,2,1,0:T(8,128)S(1)}, f32[19,1,8,128]{3,2,1,0:T(8,128)S(1)}, u32[]{:S(2)}, u32[]{:S(2)}) collective-permute-start(f32[19,1,8,128]{3,2,1,0:T(8,128)S(1)} %get-tuple-element.325), channel_id=1, source_target_pairs={{8,0},{16,8},{24,16},{9,1},{17,9},{25,17},{10,2},{18,10},{26,18},{... | collective-permute-start | bytes 233480 | tf_op jit(solution)/shard_map/ppermute | solution.py:55
  226.9 13.3 %collective-permute-start.43 = (f32[19,1,8,128]{3,2,1,0:T(8,128)S(1)}, f32[19,1,8,128]{3,2,1,0:T(8,128)S(1)}, u32[]{:S(2)}, u32[]{:S(2)}) collective-permute-start(f32[19,1,8,128]{3,2,1,0:T(8,128)S(1)} %get-tuple-element.324), channel_id=1, source_target_pairs={{0,8},{8,16},{16,24},{1,9},{9,17},{17,25},{2,10},{10,18},{18,26},{... | collective-permute-start | bytes 233480 | tf_op jit(solution)/shard_map/ppermute | solution.py:54
  232.5 13.5 %collective-permute-start.24 = (f32[19,1,8,128]{3,2,1,0:T(8,128)S(1)}, f32[19,1,8,128]{3,2,1,0:T(8,128)S(1)}, u32[]{:S(2)}, u32[]{:S(2)}) collective-permute-start(f32[19,1,8,128]{3,2,1,0:T(8,128)S(1)} %get-tuple-element.365), channel_id=1, source_target_pairs={{0,8},{8,16},{16,24},{1,9},{9,17},{17,25},{2,10},{10,18},{18,26},{... | collective-permute-start | bytes 233480 | tf_op jit(solution)/shard_map/ppermute | solution.py:54
  238.8 7.2 %collective-permute-start.25 = (f32[19,1,8,128]{3,2,1,0:T(8,128)S(1)}, f32[19,1,8,128]{3,2,1,0:T(8,128)S(1)}, u32[]{:S(2)}, u32[]{:S(2)}) collective-permute-start(f32[19,1,8,128]{3,2,1,0:T(8,128)S(1)} %get-tuple-element.364), channel_id=1, source_target_pairs={{8,0},{16,8},{24,16},{9,1},{17,9},{25,17},{10,2},{18,10},{26,18},{... | collective-permute-start | bytes 233480 | tf_op jit(solution)/shard_map/ppermute | solution.py:55
  240.2 8.6 %collective-permute-start.44 = (f32[19,4,1,128]{3,2,1,0:T(1,128)S(1)}, f32[19,4,1,128]{3,2,1,0:T(1,128)S(1)}, u32[]{:S(2)}, u32[]{:S(2)}) collective-permute-start(f32[19,4,1,128]{3,2,1,0:T(1,128)S(1)} %get-tuple-element.199), channel_id=1, source_target_pairs={{4,0},{5,1},{6,2},{7,3},{12,8},{13,9},{14,10},{15,11},{20,16},{21,... | collective-permute-start | bytes 116744 | tf_op jit(solution)/shard_map/ppermute | solution.py:55
  241.5 7.3 %collective-permute-start.45 = (f32[19,4,1,128]{3,2,1,0:T(1,128)S(1)}, f32[19,4,1,128]{3,2,1,0:T(1,128)S(1)}, u32[]{:S(2)}, u32[]{:S(2)}) collective-permute-start(f32[19,4,1,128]{3,2,1,0:T(1,128)S(1)} %get-tuple-element.198), channel_id=1, source_target_pairs={{0,4},{1,5},{2,6},{3,7},{8,12},{9,13},{10,14},{11,15},{16,20},{17,... | collective-permute-start | bytes 116744 | tf_op jit(solution)/shard_map/ppermute | solution.py:54
  246.1 10.0 %collective-permute-start.26 = (f32[19,4,1,128]{3,2,1,0:T(1,128)S(1)}, f32[19,4,1,128]{3,2,1,0:T(1,128)S(1)}, u32[]{:S(2)}, u32[]{:S(2)}) collective-permute-start(f32[19,4,1,128]{3,2,1,0:T(1,128)S(1)} %get-tuple-element.203), channel_id=1, source_target_pairs={{0,4},{1,5},{2,6},{3,7},{8,12},{9,13},{10,14},{11,15},{16,20},{17,... | collective-permute-start | bytes 116744 | tf_op jit(solution)/shard_map/ppermute | solution.py:54
  247.4 8.7 %collective-permute-start.27 = (f32[19,4,1,128]{3,2,1,0:T(1,128)S(1)}, f32[19,4,1,128]{3,2,1,0:T(1,128)S(1)}, u32[]{:S(2)}, u32[]{:S(2)}) collective-permute-start(f32[19,4,1,128]{3,2,1,0:T(1,128)S(1)} %get-tuple-element.202), channel_id=1, source_target_pairs={{4,0},{5,1},{6,2},{7,3},{12,8},{13,9},{14,10},{15,11},{20,16},{21,... | collective-permute-start | bytes 116744 | tf_op jit(solution)/shard_map/ppermute | solution.py:55
  249.6 13.1 %collective-permute-start.46 = (f32[19,4,10,1]{0,1,3,2:T(4,128)S(1)}, f32[19,4,10,1]{0,1,3,2:T(4,128)S(1)}, u32[]{:S(2)}, u32[]{:S(2)}) collective-permute-start(f32[19,4,10,1]{0,1,3,2:T(4,128)S(1)} %copy.32), channel_id=1, source_target_pairs={{1,0},{2,1},{3,2},{5,4},{6,5},{7,6},{9,8},{10,9},{11,10},{13,12},{... | collective-permute-start | bytes 9128 | tf_op jit(solution)/shard_map/ppermute | solution.py:55
  251.3 12.2 %collective-permute-start.47 = (f32[19,4,10,1]{0,1,3,2:T(4,128)S(1)}, f32[19,4,10,1]{0,1,3,2:T(4,128)S(1)}, u32[]{:S(2)}, u32[]{:S(2)}) collective-permute-start(f32[19,4,10,1]{0,1,3,2:T(4,128)S(1)} %copy.34), channel_id=1, source_target_pairs={{0,1},{1,2},{2,3},{4,5},{5,6},{6,7},{8,9},{9,10},{10,11},{12,13},{... | collective-permute-start | bytes 9128 | tf_op jit(solution)/shard_map/ppermute | solution.py:54
  257.0 15.3 %collective-permute-start.28 = (f32[19,4,10,1]{0,1,3,2:T(4,128)S(1)}, f32[19,4,10,1]{0,1,3,2:T(4,128)S(1)}, u32[]{:S(2)}, u32[]{:S(2)}) collective-permute-start(f32[19,4,10,1]{0,1,3,2:T(4,128)S(1)} %copy.20), channel_id=1, source_target_pairs={{0,1},{1,2},{2,3},{4,5},{5,6},{6,7},{8,9},{9,10},{10,11},{12,13},{... | collective-permute-start | bytes 9128 | tf_op jit(solution)/shard_map/ppermute | solution.py:54
  261.3 11.7 %collective-permute-start.29 = (f32[19,4,10,1]{0,1,3,2:T(4,128)S(1)}, f32[19,4,10,1]{0,1,3,2:T(4,128)S(1)}, u32[]{:S(2)}, u32[]{:S(2)}) collective-permute-start(f32[19,4,10,1]{0,1,3,2:T(4,128)S(1)} %copy.22), channel_id=1, source_target_pairs={{1,0},{2,1},{3,2},{5,4},{6,5},{7,6},{9,8},{10,9},{11,10},{13,12},{... | collective-permute-start | bytes 9128 | tf_op jit(solution)/shard_map/ppermute | solution.py:55
  267.4 7.1 %collective-permute-start.48 = (f32[19,1,8,128]{3,2,1,0:T(8,128)S(1)}, f32[19,1,8,128]{3,2,1,0:T(8,128)S(1)}, u32[]{:S(2)}, u32[]{:S(2)}) collective-permute-start(f32[19,1,8,128]{3,2,1,0:T(8,128)S(1)} %get-tuple-element.305), channel_id=1, source_target_pairs={{8,0},{16,8},{24,16},{9,1},{17,9},{25,17},{10,2},{18,10},{26,18},{... | collective-permute-start | bytes 233480 | tf_op jit(solution)/shard_map/ppermute | solution.py:55
  268.7 5.8 %collective-permute-start.49 = (f32[19,1,8,128]{3,2,1,0:T(8,128)S(1)}, f32[19,1,8,128]{3,2,1,0:T(8,128)S(1)}, u32[]{:S(2)}, u32[]{:S(2)}) collective-permute-start(f32[19,1,8,128]{3,2,1,0:T(8,128)S(1)} %get-tuple-element.304), channel_id=1, source_target_pairs={{0,8},{8,16},{16,24},{1,9},{9,17},{17,25},{2,10},{10,18},{18,26},{... | collective-permute-start | bytes 233480 | tf_op jit(solution)/shard_map/ppermute | solution.py:54
  275.1 7.0 %collective-permute-start.50 = (f32[19,4,1,128]{3,2,1,0:T(1,128)S(1)}, f32[19,4,1,128]{3,2,1,0:T(1,128)S(1)}, u32[]{:S(2)}, u32[]{:S(2)}) collective-permute-start(f32[19,4,1,128]{3,2,1,0:T(1,128)S(1)} %get-tuple-element.197), channel_id=1, source_target_pairs={{4,0},{5,1},{6,2},{7,3},{12,8},{13,9},{14,10},{15,11},{20,16},{21,... | collective-permute-start | bytes 116744 | tf_op jit(solution)/shard_map/ppermute | solution.py:55
  276.4 6.2 %collective-permute-start.51 = (f32[19,4,1,128]{3,2,1,0:T(1,128)S(1)}, f32[19,4,1,128]{3,2,1,0:T(1,128)S(1)}, u32[]{:S(2)}, u32[]{:S(2)}) collective-permute-start(f32[19,4,1,128]{3,2,1,0:T(1,128)S(1)} %get-tuple-element.196), channel_id=1, source_target_pairs={{0,4},{1,5},{2,6},{3,7},{8,12},{9,13},{10,14},{11,15},{16,20},{17,... | collective-permute-start | bytes 116744 | tf_op jit(solution)/shard_map/ppermute | solution.py:54
  283.4 7.8 %collective-permute-start.52 = (f32[19,4,10,1]{0,1,3,2:T(4,128)S(1)}, f32[19,4,10,1]{0,1,3,2:T(4,128)S(1)}, u32[]{:S(2)}, u32[]{:S(2)}) collective-permute-start(f32[19,4,10,1]{0,1,3,2:T(4,128)S(1)} %copy.36), channel_id=1, source_target_pairs={{1,0},{2,1},{3,2},{5,4},{6,5},{7,6},{9,8},{10,9},{11,10},{13,12},{... | collective-permute-start | bytes 9128 | tf_op jit(solution)/shard_map/ppermute | solution.py:55
  285.1 6.9 %collective-permute-start.53 = (f32[19,4,10,1]{0,1,3,2:T(4,128)S(1)}, f32[19,4,10,1]{0,1,3,2:T(4,128)S(1)}, u32[]{:S(2)}, u32[]{:S(2)}) collective-permute-start(f32[19,4,10,1]{0,1,3,2:T(4,128)S(1)} %copy.38), channel_id=1, source_target_pairs={{0,1},{1,2},{2,3},{4,5},{5,6},{6,7},{8,9},{9,10},{10,11},{12,13},{... | collective-permute-start | bytes 9128 | tf_op jit(solution)/shard_map/ppermute | solution.py:54
  301.9 1.0 copy-start.4
  304.3 5.0 %collective-permute-start.54 = (f32[1,8,128]{2,1,0:T(8,128)S(1)}, f32[1,8,128]{2,1,0:T(8,128)S(1)}, u32[]{:S(2)}, u32[]{:S(2)}) collective-permute-start(f32[1,8,128]{2,1,0:T(8,128)S(1)} %get-tuple-element.400), channel_id=1, source_target_pairs={{0,8},{8,16},{16,24},{1,9},{9,17},{17,25},{2,10},{10,18},{18,26},{... | collective-permute-start | bytes 12296 | tf_op jit(solution)/shard_map/ppermute | solution.py:54
  307.3 4.6 %collective-permute-start.55 = (f32[1,8,128]{2,1,0:T(8,128)S(1)}, f32[1,8,128]{2,1,0:T(8,128)S(1)}, u32[]{:S(2)}, u32[]{:S(2)}) collective-permute-start(f32[1,8,128]{2,1,0:T(8,128)S(1)} %get-tuple-element.401), channel_id=1, source_target_pairs={{8,0},{16,8},{24,16},{9,1},{17,9},{25,17},{10,2},{18,10},{26,18},{... | collective-permute-start | bytes 12296 | tf_op jit(solution)/shard_map/ppermute | solution.py:55
  311.9 6.2 %collective-permute-start.56 = (f32[4,1,128]{2,1,0:T(1,128)S(1)}, f32[4,1,128]{2,1,0:T(1,128)S(1)}, u32[]{:S(2)}, u32[]{:S(2)}) collective-permute-start(f32[4,1,128]{2,1,0:T(1,128)S(1)} %get-tuple-element.378), channel_id=1, source_target_pairs={{0,4},{1,5},{2,6},{3,7},{8,12},{9,13},{10,14},{11,15},{16,20},{17,... | collective-permute-start | bytes 6152 | tf_op jit(solution)/shard_map/ppermute | solution.py:54
  316.1 5.5 %collective-permute-start.57 = (f32[4,1,128]{2,1,0:T(1,128)S(1)}, f32[4,1,128]{2,1,0:T(1,128)S(1)}, u32[]{:S(2)}, u32[]{:S(2)}) collective-permute-start(f32[4,1,128]{2,1,0:T(1,128)S(1)} %get-tuple-element.379), channel_id=1, source_target_pairs={{4,0},{5,1},{6,2},{7,3},{12,8},{13,9},{14,10},{15,11},{20,16},{21,... | collective-permute-start | bytes 6152 | tf_op jit(solution)/shard_map/ppermute | solution.py:55
  321.7 5.9 %collective-permute-start.58 = (f32[4,10,1]{2,1,0:T(8,128)S(1)}, f32[4,10,1]{2,1,0:T(8,128)S(1)}, u32[]{:S(2)}, u32[]{:S(2)}) collective-permute-start(f32[4,10,1]{2,1,0:T(8,128)S(1)} %get-tuple-element.374), channel_id=1, source_target_pairs={{0,1},{1,2},{2,3},{4,5},{5,6},{6,7},{8,9},{9,10},{10,11},{12,13},{... | collective-permute-start | bytes 488 | tf_op jit(solution)/shard_map/ppermute | solution.py:54
  325.6 6.1 %collective-permute-start.59 = (f32[4,10,1]{2,1,0:T(8,128)S(1)}, f32[4,10,1]{2,1,0:T(8,128)S(1)}, u32[]{:S(2)}, u32[]{:S(2)}) collective-permute-start(f32[4,10,1]{2,1,0:T(8,128)S(1)} %get-tuple-element.375), channel_id=1, source_target_pairs={{1,0},{2,1},{3,2},{5,4},{6,5},{7,6},{9,8},{10,9},{11,10},{13,12},{... | collective-permute-start | bytes 488 | tf_op jit(solution)/shard_map/ppermute | solution.py:55
  (7 other events, 4.8 us)

commit v2 on v1

--- a/solution.py
+++ b/solution.py
@@ -178,7 +178,9 @@
     beta = jnp.exp2(beta_step.astype(jnp.float32) / 16.0)
     filtered = smooth_field(design)
     cells = design.size * lax.axis_size("grp") * lax.axis_size("gy") * lax.axis_size("gx")
-    everywhere = lax.all_gather(filtered, ("grp", "gy", "gx"))
+    devices = lax.axis_size("grp") * lax.axis_size("gy") * lax.axis_size("gx")
+    copies = jnp.broadcast_to(filtered, (devices, *filtered.shape))
+    everywhere = lax.all_to_all(copies, ("grp", "gy", "gx"), 0, 0)
     eta = threshold(everywhere.reshape(-1, filtered.shape[-1]), beta, cells)
     density_hat = project(filtered, eta, beta)
     alpha = alpha_most * penalty_shape * (1.0 - density_hat) / (penalty_shape + density_hat)

time: 334 us -> 272 us (0.81)
  blocking collectives: 67 us -> 0 us
  other arithmetic: 28 us -> 18.6 us
  starting transfers between devices: 166 us -> 173 us
  waiting for transfers between devices: 32.3 us -> 37.7 us
    all_gather x1 -> x0, blocking collectives: 67 us -> none  [body(): everywhere = lax.all_gather(filtered, ('grp', 'gy', 'gx'))]
    unnamed x157, other arithmetic: 18.6 us -> 8.86 us
    all_to_all x0 -> x1, starting transfers between devices: none -> 6.34 us  [body(): everywhere = lax.all_to_all(copies, ('grp', 'gy', 'gx'), 0, 0)]
    ppermute x30, waiting for transfers between devices: 10.8 us -> 15.8 us  [extended(): before = lax.ppermute(last, axis, up)]
  transfers between devices with their start and end apart: 60 -> 61, of which waited for: 18 -> 23; matrix products, arithmetic and copies ran while one was open for 8% -> 8% of each run, Pallas kernels for 2% -> 0%
where the time goes in v2:
time: 272 us; the launch traced here: 270 us
  starting transfers between devices  173 us (64%)
  waiting for transfers between devices  37.7 us (14%)
  local copies, waits for them, and re-layouts  30.4 us (11%)
  other arithmetic  18.6 us (7%)
  between operations  5.51 us (2%)
  Pallas kernels  5.11 us (2%)
    ppermute x30, starting transfers between devices, extended(): before = lax.ppermute(last, axis, up)  128 us
    ppermute x30, starting transfers between devices, extended(): after = lax.ppermute(leading, axis, down)  38.8 us
    ppermute x30, waiting for transfers between devices, extended(): after = lax.ppermute(leading, axis, down)  21.9 us
    ppermute x30, waiting for transfers between devices, extended(): before = lax.ppermute(last, axis, up)  15.8 us
    unnamed x157, other arithmetic  8.86 us
    ppermute x8, local copies, waits for them, and re-layouts, extended(): before = lax.ppermute(last, axis, up)  6.82 us
    slice x27, local copies, waits for them, and re-layouts, extended(): last = lax.slice_in_dim(value, length - width, length, axis=dim)  6.4 us
    all_to_all x1, starting transfers between devices, body(): everywhere = lax.all_to_all(copies, ('grp', 'gy', 'gx'), 0, 0)  6.34 us
  transfers between devices with their start and end apart: 61, of which 23 were waited for; matrix products, arithmetic and copies ran while one was open for 8% of the time, Pallas kernels for 0%

profile of v2, /device:TPU:0, one launch (start us, length us, event | category | flops | bytes accessed | tf_op | source)
XLA Modules:
  0.0 270.4 jit_solution(1919233314794191599)
XLA Ops:
  1.3 2.3 collective-permute-start
  3.7 1.4 collective-permute-start.1
  6.1 5.2 %collective-permute-start.31 = (f32[19,1,8,128]{3,2,1,0:T(8,128)S(1)}, f32[19,1,8,128]{3,2,1,0:T(8,128)S(1)}, u32[]{:S(2)}, u32[]{:S(2)}) collective-permute-start(f32[19,1,8,128]{3,2,1,0:T(8,128)S(1)} %get-tuple-element.370), channel_id=1, source_target_pairs={{0,8},{8,16},{16,24},{1,9},{9,17},{17,25},{2,10},{10,18},{18,26},{... | collective-permute-start | bytes 233480 | tf_op jit(solution)/shard_map/ppermute | solution.py:54
  11.3 1.3 collective-permute-start.30
  14.2 3.4 %collective-permute-start.2 = (f32[4,1,128]{2,1,0:T(1,128)S(1)}, f32[4,1,128]{2,1,0:T(1,128)S(1)}, u32[]{:S(2)}, u32[]{:S(2)}) collective-permute-start(f32[4,1,128]{2,1,0:T(1,128)S(1)} %get-tuple-element.400), channel_id=1, source_target_pairs={{0,4},{1,5},{2,6},{3,7},{8,12},{9,13},{10,14},{11,15},{16,20},{17,... | collective-permute-start | bytes 6152 | tf_op jit(solution)/shard_map/ppermute | solution.py:54
  17.6 1.3 collective-permute-start.3
  19.6 3.5 %collective-permute-done.3 = f32[4,1,128]{2,1,0:T(1,128)S(1)} collective-permute-done((f32[4,1,128]{2,1,0:T(1,128)S(1)}, f32[4,1,128]{2,1,0:T(1,128)S(1)}, u32[]{:S(2)}, u32[]{:S(2)}) %collective-permute-start.3) | collective-permute-done | bytes 2080 | tf_op jit(solution)/shard_map/ppermute | solution.py:55
  23.2 3.5 %collective-permute-start.4 = (f32[4,10,1]{2,1,0:T(8,128)S(1)}, f32[4,10,1]{2,1,0:T(8,128)S(1)}, u32[]{:S(2)}, u32[]{:S(2)}) collective-permute-start(f32[4,10,1]{2,1,0:T(8,128)S(1)} %get-tuple-element.378), channel_id=1, source_target_pairs={{0,1},{1,2},{2,3},{4,5},{5,6},{6,7},{8,9},{9,10},{10,11},{12,13},{... | collective-permute-start | bytes 488 | tf_op jit(solution)/shard_map/ppermute | solution.py:54
  26.7 1.3 collective-permute-start.5
  28.4 4.1 %collective-permute-done.5 = f32[4,10,1]{2,1,0:T(8,128)S(1)} collective-permute-done((f32[4,10,1]{2,1,0:T(8,128)S(1)}, f32[4,10,1]{2,1,0:T(8,128)S(1)}, u32[]{:S(2)}, u32[]{:S(2)}) %collective-permute-start.5) | collective-permute-done | bytes 192 | tf_op jit(solution)/shard_map/ppermute | solution.py:55
  33.5 6.3 %all-to-all-start = ((f32[32,2,8,128]{3,2,1,0:T(8,128)}), f32[32,2,8,128]{3,2,1,0:T(8,128)S(1)}, u32[]{:S(2)}, u32[]{:S(2)}) async-start(f32[32,2,8,128]{3,2,1,0:T(8,128)} %broadcast_in_dim.119), calls=%async_computation | async-start | bytes 524288 | tf_op jit(solution)/shard_map/all_to_all | solution.py:183
  39.9 1.3 collective-permute-start.32
  41.2 4.5 %collective-permute-start.33 = (f32[19,4,1,128]{3,2,1,0:T(1,128)S(1)}, f32[19,4,1,128]{3,2,1,0:T(1,128)S(1)}, u32[]{:S(2)}, u32[]{:S(2)}) collective-permute-start(f32[19,4,1,128]{3,2,1,0:T(1,128)S(1)} %get-tuple-element.208), channel_id=1, source_target_pairs={{0,4},{1,5},{2,6},{3,7},{8,12},{9,13},{10,14},{11,15},{16,20},{17,... | collective-permute-start | bytes 116744 | tf_op jit(solution)/shard_map/ppermute | solution.py:54
  46.0 1.4 collective-permute-done.33
  50.0 4.5 %collective-permute-start.35 = (f32[19,4,10,1]{0,1,3,2:T(4,128)S(1)}, f32[19,4,10,1]{0,1,3,2:T(4,128)S(1)}, u32[]{:S(2)}, u32[]{:S(2)}) collective-permute-start(f32[19,4,10,1]{0,1,3,2:T(4,128)S(1)} %copy.116), channel_id=1, source_target_pairs={{0,1},{1,2},{2,3},{4,5},{5,6},{6,7},{8,9},{9,10},{10,11},{12,13},{... | collective-permute-start | bytes 9128 | tf_op jit(solution)/shard_map/ppermute | solution.py:54
  57.4 5.1 %threshold.1 = f32[8,128]{1,0:T(8,128)S(1)} custom-call(f32[1]{0:T(128)} %bitcast.1.beta_ref, f32[512,128]{1,0:T(8,128)S(1)} %bitcast.1613), custom_call_target="tpu_custom_call" | custom-call | tf_op jit(solution)/shard_map/threshold/pallas_call | solution.py:162
  64.6 1.4 constant_dynamic-update-slice_fusion.40
  67.2 1.3 collective-permute-start.6
  68.5 3.0 %collective-permute-start.7 = (f32[19,1,8,128]{3,2,1,0:T(8,128)S(1)}, f32[19,1,8,128]{3,2,1,0:T(8,128)S(1)}, u32[]{:S(2)}, u32[]{:S(2)}) collective-permute-start(f32[19,1,8,128]{3,2,1,0:T(8,128)S(1)} %get-tuple-element.374), channel_id=1, source_target_pairs={{0,8},{8,16},{16,24},{1,9},{9,17},{17,25},{2,10},{10,18},{18,26},{... | collective-permute-start | bytes 233480 | tf_op jit(solution)/shard_map/ppermute | solution.py:54
  72.5 1.3 collective-permute-start.8
  73.8 4.5 %collective-permute-start.9 = (f32[19,4,1,128]{3,2,1,0:T(1,128)S(1)}, f32[19,4,1,128]{3,2,1,0:T(1,128)S(1)}, u32[]{:S(2)}, u32[]{:S(2)}) collective-permute-start(f32[19,4,1,128]{3,2,1,0:T(1,128)S(1)} %get-tuple-element.212), channel_id=1, source_target_pairs={{0,4},{1,5},{2,6},{3,7},{8,12},{9,13},{10,14},{11,15},{16,20},{17,... | collective-permute-start | bytes 116744 | tf_op jit(solution)/shard_map/ppermute | solution.py:54
  78.4 1.6 collective-permute-done.9
  80.8 4.2 %collective-permute-start.11 = (f32[19,4,10,1]{0,1,3,2:T(4,128)S(1)}, f32[19,4,10,1]{0,1,3,2:T(4,128)S(1)}, u32[]{:S(2)}, u32[]{:S(2)}) collective-permute-start(f32[19,4,10,1]{0,1,3,2:T(4,128)S(1)} %copy.100), channel_id=1, source_target_pairs={{0,1},{1,2},{2,3},{4,5},{5,6},{6,7},{8,9},{9,10},{10,11},{12,13},{... | collective-permute-start | bytes 9128 | tf_op jit(solution)/shard_map/ppermute | solution.py:54
  87.5 3.6 %collective-permute-done.10 = f32[19,4,10,1]{0,1,3,2:T(4,128)S(1)} collective-permute-done((f32[19,4,10,1]{0,1,3,2:T(4,128)S(1)}, f32[19,4,10,1]{0,1,3,2:T(4,128)S(1)}, u32[]{:S(2)}, u32[]{:S(2)}) %collective-permute-start.10) | collective-permute-done | bytes 3072 | tf_op jit(solution)/shard_map/ppermute | solution.py:55
  93.4 1.3 collective-permute-start.12
  94.7 3.0 %collective-permute-start.13 = (f32[19,1,8,128]{3,2,1,0:T(8,128)S(1)}, f32[19,1,8,128]{3,2,1,0:T(8,128)S(1)}, u32[]{:S(2)}, u32[]{:S(2)}) collective-permute-start(f32[19,1,8,128]{3,2,1,0:T(8,128)S(1)} %get-tuple-element.372), channel_id=1, source_target_pairs={{0,8},{8,16},{16,24},{1,9},{9,17},{17,25},{2,10},{10,18},{18,26},{... | collective-permute-start | bytes 233480 | tf_op jit(solution)/shard_map/ppermute | solution.py:54
  98.7 1.3 collective-permute-start.14
  100.0 4.5 %collective-permute-start.15 = (f32[19,4,1,128]{3,2,1,0:T(1,128)S(1)}, f32[19,4,1,128]{3,2,1,0:T(1,128)S(1)}, u32[]{:S(2)}, u32[]{:S(2)}) collective-permute-start(f32[19,4,1,128]{3,2,1,0:T(1,128)S(1)} %get-tuple-element.210), channel_id=1, source_target_pairs={{0,4},{1,5},{2,6},{3,7},{8,12},{9,13},{10,14},{11,15},{16,20},{17,... | collective-permute-start | bytes 116744 | tf_op jit(solution)/shard_map/ppermute | solution.py:54
  104.6 1.6 collective-permute-done.15
  108.7 4.5 %collective-permute-start.17 = (f32[19,4,10,1]{0,1,3,2:T(4,128)S(1)}, f32[19,4,10,1]{0,1,3,2:T(4,128)S(1)}, u32[]{:S(2)}, u32[]{:S(2)}) collective-permute-start(f32[19,4,10,1]{0,1,3,2:T(4,128)S(1)} %copy.104), channel_id=1, source_target_pairs={{0,1},{1,2},{2,3},{4,5},{5,6},{6,7},{8,9},{9,10},{10,11},{12,13},{... | collective-permute-start | bytes 9128 | tf_op jit(solution)/shard_map/ppermute | solution.py:54
  117.0 1.3 collective-permute-start.18
  118.3 4.6 %collective-permute-start.19 = (f32[19,1,8,128]{3,2,1,0:T(8,128)S(1)}, f32[19,1,8,128]{3,2,1,0:T(8,128)S(1)}, u32[]{:S(2)}, u32[]{:S(2)}) collective-permute-start(f32[19,1,8,128]{3,2,1,0:T(8,128)S(1)} %get-tuple-element.368), channel_id=1, source_target_pairs={{0,8},{8,16},{16,24},{1,9},{9,17},{17,25},{2,10},{10,18},{18,26},{... | collective-permute-start | bytes 233480 | tf_op jit(solution)/shard_map/ppermute | solution.py:54
  123.9 1.3 collective-permute-start.20
  125.2 4.5 %collective-permute-start.21 = (f32[19,4,1,128]{3,2,1,0:T(1,128)S(1)}, f32[19,4,1,128]{3,2,1,0:T(1,128)S(1)}, u32[]{:S(2)}, u32[]{:S(2)}) collective-permute-start(f32[19,4,1,128]{3,2,1,0:T(1,128)S(1)} %get-tuple-element.206), channel_id=1, source_target_pairs={{0,4},{1,5},{2,6},{3,7},{8,12},{9,13},{10,14},{11,15},{16,20},{17,... | collective-permute-start | bytes 116744 | tf_op jit(solution)/shard_map/ppermute | solution.py:54
  129.8 1.6 collective-permute-done.21
  133.9 4.7 %collective-permute-start.23 = (f32[19,4,10,1]{0,1,3,2:T(4,128)S(1)}, f32[19,4,10,1]{0,1,3,2:T(4,128)S(1)}, u32[]{:S(2)}, u32[]{:S(2)}) collective-permute-start(f32[19,4,10,1]{0,1,3,2:T(4,128)S(1)} %copy.108), channel_id=1, source_target_pairs={{0,1},{1,2},{2,3},{4,5},{5,6},{6,7},{8,9},{9,10},{10,11},{12,13},{... | collective-permute-start | bytes 9128 | tf_op jit(solution)/shard_map/ppermute | solution.py:54
  143.8 1.3 collective-permute-start.36
  145.1 6.1 %collective-permute-start.37 = (f32[19,1,8,128]{3,2,1,0:T(8,128)S(1)}, f32[19,1,8,128]{3,2,1,0:T(8,128)S(1)}, u32[]{:S(2)}, u32[]{:S(2)}) collective-permute-start(f32[19,1,8,128]{3,2,1,0:T(8,128)S(1)} %get-tuple-element.346), channel_id=1, source_target_pairs={{0,8},{8,16},{16,24},{1,9},{9,17},{17,25},{2,10},{10,18},{18,26},{... | collective-permute-start | bytes 233480 | tf_op jit(solution)/shard_map/ppermute | solution.py:54
  152.2 1.3 collective-permute-start.38
  153.5 4.5 %collective-permute-start.39 = (f32[19,4,1,128]{3,2,1,0:T(1,128)S(1)}, f32[19,4,1,128]{3,2,1,0:T(1,128)S(1)}, u32[]{:S(2)}, u32[]{:S(2)}) collective-permute-start(f32[19,4,1,128]{3,2,1,0:T(1,128)S(1)} %get-tuple-element.202), channel_id=1, source_target_pairs={{0,4},{1,5},{2,6},{3,7},{8,12},{9,13},{10,14},{11,15},{16,20},{17,... | collective-permute-start | bytes 116744 | tf_op jit(solution)/shard_map/ppermute | solution.py:54
  158.1 1.6 collective-permute-done.39
  162.3 4.5 %collective-permute-start.41 = (f32[19,4,10,1]{0,1,3,2:T(4,128)S(1)}, f32[19,4,10,1]{0,1,3,2:T(4,128)S(1)}, u32[]{:S(2)}, u32[]{:S(2)}) collective-permute-start(f32[19,4,10,1]{0,1,3,2:T(4,128)S(1)} %copy.120), channel_id=1, source_target_pairs={{0,1},{1,2},{2,3},{4,5},{5,6},{6,7},{8,9},{9,10},{10,11},{12,13},{... | collective-permute-start | bytes 9128 | tf_op jit(solution)/shard_map/ppermute | solution.py:54
  170.1 1.4 fusion.483
  171.7 1.3 collective-permute-start.42
  173.0 5.6 %collective-permute-start.43 = (f32[19,1,8,128]{3,2,1,0:T(8,128)S(1)}, f32[19,1,8,128]{3,2,1,0:T(8,128)S(1)}, u32[]{:S(2)}, u32[]{:S(2)}) collective-permute-start(f32[19,1,8,128]{3,2,1,0:T(8,128)S(1)} %get-tuple-element.326), channel_id=1, source_target_pairs={{0,8},{8,16},{16,24},{1,9},{9,17},{17,25},{2,10},{10,18},{18,26},{... | collective-permute-start | bytes 233480 | tf_op jit(solution)/shard_map/ppermute | solution.py:54
  178.7 6.3 %collective-permute-start.24 = (f32[19,1,8,128]{3,2,1,0:T(8,128)S(1)}, f32[19,1,8,128]{3,2,1,0:T(8,128)S(1)}, u32[]{:S(2)}, u32[]{:S(2)}) collective-permute-start(f32[19,1,8,128]{3,2,1,0:T(8,128)S(1)} %get-tuple-element.367), channel_id=1, source_target_pairs={{0,8},{8,16},{16,24},{1,9},{9,17},{17,25},{2,10},{10,18},{18,26},{... | collective-permute-start | bytes 233480 | tf_op jit(solution)/shard_map/ppermute | solution.py:54
  184.9 1.3 collective-permute-start.25
  186.3 1.3 collective-permute-start.44
  187.6 4.5 %collective-permute-start.45 = (f32[19,4,1,128]{3,2,1,0:T(1,128)S(1)}, f32[19,4,1,128]{3,2,1,0:T(1,128)S(1)}, u32[]{:S(2)}, u32[]{:S(2)}) collective-permute-start(f32[19,4,1,128]{3,2,1,0:T(1,128)S(1)} %get-tuple-element.200), channel_id=1, source_target_pairs={{0,4},{1,5},{2,6},{3,7},{8,12},{9,13},{10,14},{11,15},{16,20},{17,... | collective-permute-start | bytes 116744 | tf_op jit(solution)/shard_map/ppermute | solution.py:54
  197.5 4.8 %collective-permute-start.47 = (f32[19,4,10,1]{0,1,3,2:T(4,128)S(1)}, f32[19,4,10,1]{0,1,3,2:T(4,128)S(1)}, u32[]{:S(2)}, u32[]{:S(2)}) collective-permute-start(f32[19,4,10,1]{0,1,3,2:T(4,128)S(1)} %copy.124), channel_id=1, source_target_pairs={{0,1},{1,2},{2,3},{4,5},{5,6},{6,7},{8,9},{9,10},{10,11},{12,13},{... | collective-permute-start | bytes 9128 | tf_op jit(solution)/shard_map/ppermute | solution.py:54
  203.2 3.9 %collective-permute-start.28 = (f32[19,4,10,1]{0,1,3,2:T(4,128)S(1)}, f32[19,4,10,1]{0,1,3,2:T(4,128)S(1)}, u32[]{:S(2)}, u32[]{:S(2)}) collective-permute-start(f32[19,4,10,1]{0,1,3,2:T(4,128)S(1)} %copy.110), channel_id=1, source_target_pairs={{0,1},{1,2},{2,3},{4,5},{5,6},{6,7},{8,9},{9,10},{10,11},{12,13},{... | collective-permute-start | bytes 9128 | tf_op jit(solution)/shard_map/ppermute | solution.py:54
  211.4 1.4 fusion.462
  213.0 1.3 collective-permute-start.48
  214.3 3.6 %collective-permute-start.49 = (f32[19,1,8,128]{3,2,1,0:T(8,128)S(1)}, f32[19,1,8,128]{3,2,1,0:T(8,128)S(1)}, u32[]{:S(2)}, u32[]{:S(2)}) collective-permute-start(f32[19,1,8,128]{3,2,1,0:T(8,128)S(1)} %get-tuple-element.306), channel_id=1, source_target_pairs={{0,8},{8,16},{16,24},{1,9},{9,17},{17,25},{2,10},{10,18},{18,26},{... | collective-permute-start | bytes 233480 | tf_op jit(solution)/shard_map/ppermute | solution.py:54
  222.0 4.5 %collective-permute-start.51 = (f32[19,4,1,128]{3,2,1,0:T(1,128)S(1)}, f32[19,4,1,128]{3,2,1,0:T(1,128)S(1)}, u32[]{:S(2)}, u32[]{:S(2)}) collective-permute-start(f32[19,4,1,128]{3,2,1,0:T(1,128)S(1)} %get-tuple-element.198), channel_id=1, source_target_pairs={{0,4},{1,5},{2,6},{3,7},{8,12},{9,13},{10,14},{11,15},{16,20},{17,... | collective-permute-start | bytes 116744 | tf_op jit(solution)/shard_map/ppermute | solution.py:54
  226.6 1.6 collective-permute-done.51
  231.4 5.5 %collective-permute-start.53 = (f32[19,4,10,1]{0,1,3,2:T(4,128)S(1)}, f32[19,4,10,1]{0,1,3,2:T(4,128)}, u32[]{:S(2)}, u32[]{:S(2)}) collective-permute-start(f32[19,4,10,1]{0,1,3,2:T(4,128)S(1)} %copy.128), channel_id=1, source_target_pairs={{0,1},{1,2},{2,3},{4,5},{5,6},{6,7},{8,9},{9,10},{10,11},{12,13},{... | collective-permute-start | bytes 9128 | tf_op jit(solution)/shard_map/ppermute | solution.py:54
  237.7 1.5 copy.129
  241.7 2.8 %collective-permute-start.54 = (f32[1,8,128]{2,1,0:T(8,128)S(1)}, f32[1,8,128]{2,1,0:T(8,128)S(1)}, u32[]{:S(2)}, u32[]{:S(2)}) collective-permute-start(f32[1,8,128]{2,1,0:T(8,128)S(1)} %get-tuple-element.402), channel_id=1, source_target_pairs={{0,8},{8,16},{16,24},{1,9},{9,17},{17,25},{2,10},{10,18},{18,26},{... | collective-permute-start | bytes 12296 | tf_op jit(solution)/shard_map/ppermute | solution.py:54
  246.4 2.9 %collective-permute-done.55 = f32[1,8,128]{2,1,0:T(8,128)S(1)} collective-permute-done((f32[1,8,128]{2,1,0:T(8,128)S(1)}, f32[1,8,128]{2,1,0:T(8,128)S(1)}, u32[]{:S(2)}, u32[]{:S(2)}) %collective-permute-start.55) | collective-permute-done | bytes 4128 | tf_op jit(solution)/shard_map/ppermute | solution.py:55
  249.3 4.2 %collective-permute-start.56 = (f32[4,1,128]{2,1,0:T(1,128)S(1)}, f32[4,1,128]{2,1,0:T(1,128)S(1)}, u32[]{:S(2)}, u32[]{:S(2)}) collective-permute-start(f32[4,1,128]{2,1,0:T(1,128)S(1)} %get-tuple-element.380), channel_id=1, source_target_pairs={{0,4},{1,5},{2,6},{3,7},{8,12},{9,13},{10,14},{11,15},{16,20},{17,... | collective-permute-start | bytes 6152 | tf_op jit(solution)/shard_map/ppermute | solution.py:54
  255.5 3.5 %collective-permute-done.57 = f32[4,1,128]{2,1,0:T(1,128)S(1)} collective-permute-done((f32[4,1,128]{2,1,0:T(1,128)S(1)}, f32[4,1,128]{2,1,0:T(1,128)S(1)}, u32[]{:S(2)}, u32[]{:S(2)}) %collective-permute-start.57) | collective-permute-done | bytes 2080 | tf_op jit(solution)/shard_map/ppermute | solution.py:55
  259.1 4.3 %collective-permute-start.58 = (f32[4,10,1]{2,1,0:T(8,128)S(1)}, f32[4,10,1]{2,1,0:T(8,128)S(1)}, u32[]{:S(2)}, u32[]{:S(2)}) collective-permute-start(f32[4,10,1]{2,1,0:T(8,128)S(1)} %get-tuple-element.376), channel_id=1, source_target_pairs={{0,1},{1,2},{2,3},{4,5},{5,6},{6,7},{8,9},{9,10},{10,11},{12,13},{... | collective-permute-start | bytes 488 | tf_op jit(solution)/shard_map/ppermute | solution.py:54
  265.4 4.1 %collective-permute-done.59 = f32[4,10,1]{2,1,0:T(8,128)S(1)} collective-permute-done((f32[4,10,1]{2,1,0:T(8,128)S(1)}, f32[4,10,1]{2,1,0:T(8,128)S(1)}, u32[]{:S(2)}, u32[]{:S(2)}) %collective-permute-start.59) | collective-permute-done | bytes 192 | tf_op jit(solution)/shard_map/ppermute | solution.py:55
  (479 shorter events, 68.0 us)
Async XLA Ops:
  1.3 12.2 %collective-permute-start = (f32[1,8,128]{2,1,0:T(8,128)S(1)}, f32[1,8,128]{2,1,0:T(8,128)S(1)}, u32[]{:S(2)}, u32[]{:S(2)}) collective-permute-start(f32[1,8,128]{2,1,0:T(8,128)S(1)} %get-tuple-element.471), channel_id=1, source_target_pairs={{0,8},{8,16},{16,24},{1,9},{9,17},{17,25},{2,10},{10,18},{18,26},{... | collective-permute-start | bytes 12296 | tf_op jit(solution)/shard_map/ppermute | solution.py:54
  3.7 8.9 %copy-start = (f32[19,2,8,128]{3,2,1,0:T(8,128)S(1)}, f32[19,2,8,128]{3,2,1,0:T(8,128)}, u32[]{:S(2)}) copy-start(f32[19,2,8,128]{3,2,1,0:T(8,128)} %param.8) | copy-start | bytes 466948
  3.7 8.9 %copy-start.2 = (f32[19,2,8,128]{3,2,1,0:T(8,128)S(1)}, f32[19,2,8,128]{3,2,1,0:T(8,128)}, u32[]{:S(2)}) copy-start(f32[19,2,8,128]{3,2,1,0:T(8,128)} %param.7) | copy-start | bytes 466948
  3.7 10.5 %collective-permute-start.1 = (f32[1,8,128]{2,1,0:T(8,128)S(1)}, f32[1,8,128]{2,1,0:T(8,128)S(1)}, u32[]{:S(2)}, u32[]{:S(2)}) collective-permute-start(f32[1,8,128]{2,1,0:T(8,128)S(1)} %get-tuple-element.470), channel_id=1, source_target_pairs={{8,0},{16,8},{24,16},{9,1},{17,9},{25,17},{10,2},{18,10},{26,18},{... | collective-permute-start | bytes 12296 | tf_op jit(solution)/shard_map/ppermute | solution.py:55
  6.1 33.7 %collective-permute-start.31 = (f32[19,1,8,128]{3,2,1,0:T(8,128)S(1)}, f32[19,1,8,128]{3,2,1,0:T(8,128)S(1)}, u32[]{:S(2)}, u32[]{:S(2)}) collective-permute-start(f32[19,1,8,128]{3,2,1,0:T(8,128)S(1)} %get-tuple-element.370), channel_id=1, source_target_pairs={{0,8},{8,16},{16,24},{1,9},{9,17},{17,25},{2,10},{10,18},{18,26},{... | collective-permute-start | bytes 233480 | tf_op jit(solution)/shard_map/ppermute | solution.py:54
  11.3 28.6 %collective-permute-start.30 = (f32[19,1,8,128]{3,2,1,0:T(8,128)S(1)}, f32[19,1,8,128]{3,2,1,0:T(8,128)S(1)}, u32[]{:S(2)}, u32[]{:S(2)}) collective-permute-start(f32[19,1,8,128]{3,2,1,0:T(8,128)S(1)} %get-tuple-element.371), channel_id=1, source_target_pairs={{8,0},{16,8},{24,16},{9,1},{17,9},{25,17},{10,2},{18,10},{26,18},{... | collective-permute-start | bytes 233480 | tf_op jit(solution)/shard_map/ppermute | solution.py:55
  14.2 5.4 %collective-permute-start.2 = (f32[4,1,128]{2,1,0:T(1,128)S(1)}, f32[4,1,128]{2,1,0:T(1,128)S(1)}, u32[]{:S(2)}, u32[]{:S(2)}) collective-permute-start(f32[4,1,128]{2,1,0:T(1,128)S(1)} %get-tuple-element.400), channel_id=1, source_target_pairs={{0,4},{1,5},{2,6},{3,7},{8,12},{9,13},{10,14},{11,15},{16,20},{17,... | collective-permute-start | bytes 6152 | tf_op jit(solution)/shard_map/ppermute | solution.py:54
  17.6 5.5 %collective-permute-start.3 = (f32[4,1,128]{2,1,0:T(1,128)S(1)}, f32[4,1,128]{2,1,0:T(1,128)S(1)}, u32[]{:S(2)}, u32[]{:S(2)}) collective-permute-start(f32[4,1,128]{2,1,0:T(1,128)S(1)} %get-tuple-element.401), channel_id=1, source_target_pairs={{4,0},{5,1},{6,2},{7,3},{12,8},{13,9},{14,10},{15,11},{20,16},{21,... | collective-permute-start | bytes 6152 | tf_op jit(solution)/shard_map/ppermute | solution.py:55
  23.2 5.2 %collective-permute-start.4 = (f32[4,10,1]{2,1,0:T(8,128)S(1)}, f32[4,10,1]{2,1,0:T(8,128)S(1)}, u32[]{:S(2)}, u32[]{:S(2)}) collective-permute-start(f32[4,10,1]{2,1,0:T(8,128)S(1)} %get-tuple-element.378), channel_id=1, source_target_pairs={{0,1},{1,2},{2,3},{4,5},{5,6},{6,7},{8,9},{9,10},{10,11},{12,13},{... | collective-permute-start | bytes 488 | tf_op jit(solution)/shard_map/ppermute | solution.py:54
  26.7 5.8 %collective-permute-start.5 = (f32[4,10,1]{2,1,0:T(8,128)S(1)}, f32[4,10,1]{2,1,0:T(8,128)S(1)}, u32[]{:S(2)}, u32[]{:S(2)}) collective-permute-start(f32[4,10,1]{2,1,0:T(8,128)S(1)} %get-tuple-element.379), channel_id=1, source_target_pairs={{1,0},{2,1},{3,2},{5,4},{6,5},{7,6},{9,8},{10,9},{11,10},{13,12},{... | collective-permute-start | bytes 488 | tf_op jit(solution)/shard_map/ppermute | solution.py:55
  33.5 23.9 %all-to-all-start = ((f32[32,2,8,128]{3,2,1,0:T(8,128)}), f32[32,2,8,128]{3,2,1,0:T(8,128)S(1)}, u32[]{:S(2)}, u32[]{:S(2)}) async-start(f32[32,2,8,128]{3,2,1,0:T(8,128)} %broadcast_in_dim.119), calls=%async_computation | async-start | bytes 524288 | tf_op jit(solution)/shard_map/all_to_all | solution.py:183
  39.9 6.1 %collective-permute-start.32 = (f32[19,4,1,128]{3,2,1,0:T(1,128)S(1)}, f32[19,4,1,128]{3,2,1,0:T(1,128)S(1)}, u32[]{:S(2)}, u32[]{:S(2)}) collective-permute-start(f32[19,4,1,128]{3,2,1,0:T(1,128)S(1)} %get-tuple-element.209), channel_id=1, source_target_pairs={{4,0},{5,1},{6,2},{7,3},{12,8},{13,9},{14,10},{15,11},{20,16},{21,... | collective-permute-start | bytes 116744 | tf_op jit(solution)/shard_map/ppermute | solution.py:55
  41.2 6.2 %collective-permute-start.33 = (f32[19,4,1,128]{3,2,1,0:T(1,128)S(1)}, f32[19,4,1,128]{3,2,1,0:T(1,128)S(1)}, u32[]{:S(2)}, u32[]{:S(2)}) collective-permute-start(f32[19,4,1,128]{3,2,1,0:T(1,128)S(1)} %get-tuple-element.208), channel_id=1, source_target_pairs={{0,4},{1,5},{2,6},{3,7},{8,12},{9,13},{10,14},{11,15},{16,20},{17,... | collective-permute-start | bytes 116744 | tf_op jit(solution)/shard_map/ppermute | solution.py:54
  48.2 6.3 %collective-permute-start.34 = (f32[19,4,10,1]{0,1,3,2:T(4,128)S(1)}, f32[19,4,10,1]{0,1,3,2:T(4,128)S(1)}, u32[]{:S(2)}, u32[]{:S(2)}) collective-permute-start(f32[19,4,10,1]{0,1,3,2:T(4,128)S(1)} %copy.114), channel_id=1, source_target_pairs={{1,0},{2,1},{3,2},{5,4},{6,5},{7,6},{9,8},{10,9},{11,10},{13,12},{... | collective-permute-start | bytes 9128 | tf_op jit(solution)/shard_map/ppermute | solution.py:55
  50.0 6.0 %collective-permute-start.35 = (f32[19,4,10,1]{0,1,3,2:T(4,128)S(1)}, f32[19,4,10,1]{0,1,3,2:T(4,128)S(1)}, u32[]{:S(2)}, u32[]{:S(2)}) collective-permute-start(f32[19,4,10,1]{0,1,3,2:T(4,128)S(1)} %copy.116), channel_id=1, source_target_pairs={{0,1},{1,2},{2,3},{4,5},{5,6},{6,7},{8,9},{9,10},{10,11},{12,13},{... | collective-permute-start | bytes 9128 | tf_op jit(solution)/shard_map/ppermute | solution.py:54
  66.2 0.9 copy-start.1
  67.2 4.4 %collective-permute-start.6 = (f32[19,1,8,128]{3,2,1,0:T(8,128)S(1)}, f32[19,1,8,128]{3,2,1,0:T(8,128)S(1)}, u32[]{:S(2)}, u32[]{:S(2)}) collective-permute-start(f32[19,1,8,128]{3,2,1,0:T(8,128)S(1)} %get-tuple-element.375), channel_id=1, source_target_pairs={{8,0},{16,8},{24,16},{9,1},{17,9},{25,17},{10,2},{18,10},{26,18},{... | collective-permute-start | bytes 233480 | tf_op jit(solution)/shard_map/ppermute | solution.py:55
  68.5 3.9 %collective-permute-start.7 = (f32[19,1,8,128]{3,2,1,0:T(8,128)S(1)}, f32[19,1,8,128]{3,2,1,0:T(8,128)S(1)}, u32[]{:S(2)}, u32[]{:S(2)}) collective-permute-start(f32[19,1,8,128]{3,2,1,0:T(8,128)S(1)} %get-tuple-element.374), channel_id=1, source_target_pairs={{0,8},{8,16},{16,24},{1,9},{9,17},{17,25},{2,10},{10,18},{18,26},{... | collective-permute-start | bytes 233480 | tf_op jit(solution)/shard_map/ppermute | solution.py:54
  72.5 5.9 %collective-permute-start.8 = (f32[19,4,1,128]{3,2,1,0:T(1,128)S(1)}, f32[19,4,1,128]{3,2,1,0:T(1,128)S(1)}, u32[]{:S(2)}, u32[]{:S(2)}) collective-permute-start(f32[19,4,1,128]{3,2,1,0:T(1,128)S(1)} %get-tuple-element.213), channel_id=1, source_target_pairs={{4,0},{5,1},{6,2},{7,3},{12,8},{13,9},{14,10},{15,11},{20,16},{21,... | collective-permute-start | bytes 116744 | tf_op jit(solution)/shard_map/ppermute | solution.py:55
  73.8 6.2 %collective-permute-start.9 = (f32[19,4,1,128]{3,2,1,0:T(1,128)S(1)}, f32[19,4,1,128]{3,2,1,0:T(1,128)S(1)}, u32[]{:S(2)}, u32[]{:S(2)}) collective-permute-start(f32[19,4,1,128]{3,2,1,0:T(1,128)S(1)} %get-tuple-element.212), channel_id=1, source_target_pairs={{0,4},{1,5},{2,6},{3,7},{8,12},{9,13},{10,14},{11,15},{16,20},{17,... | collective-permute-start | bytes 116744 | tf_op jit(solution)/shard_map/ppermute | solution.py:54
  80.8 6.0 %collective-permute-start.11 = (f32[19,4,10,1]{0,1,3,2:T(4,128)S(1)}, f32[19,4,10,1]{0,1,3,2:T(4,128)S(1)}, u32[]{:S(2)}, u32[]{:S(2)}) collective-permute-start(f32[19,4,10,1]{0,1,3,2:T(4,128)S(1)} %copy.100), channel_id=1, source_target_pairs={{0,1},{1,2},{2,3},{4,5},{5,6},{6,7},{8,9},{9,10},{10,11},{12,13},{... | collective-permute-start | bytes 9128 | tf_op jit(solution)/shard_map/ppermute | solution.py:54
  85.4 5.7 %collective-permute-start.10 = (f32[19,4,10,1]{0,1,3,2:T(4,128)S(1)}, f32[19,4,10,1]{0,1,3,2:T(4,128)S(1)}, u32[]{:S(2)}, u32[]{:S(2)}) collective-permute-start(f32[19,4,10,1]{0,1,3,2:T(4,128)S(1)} %copy.98), channel_id=1, source_target_pairs={{1,0},{2,1},{3,2},{5,4},{6,5},{7,6},{9,8},{10,9},{11,10},{13,12},{... | collective-permute-start | bytes 9128 | tf_op jit(solution)/shard_map/ppermute | solution.py:55
  93.4 4.3 %collective-permute-start.12 = (f32[19,1,8,128]{3,2,1,0:T(8,128)S(1)}, f32[19,1,8,128]{3,2,1,0:T(8,128)S(1)}, u32[]{:S(2)}, u32[]{:S(2)}) collective-permute-start(f32[19,1,8,128]{3,2,1,0:T(8,128)S(1)} %get-tuple-element.373), channel_id=1, source_target_pairs={{8,0},{16,8},{24,16},{9,1},{17,9},{25,17},{10,2},{18,10},{26,18},{... | collective-permute-start | bytes 233480 | tf_op jit(solution)/shard_map/ppermute | solution.py:55
  94.7 3.9 %collective-permute-start.13 = (f32[19,1,8,128]{3,2,1,0:T(8,128)S(1)}, f32[19,1,8,128]{3,2,1,0:T(8,128)S(1)}, u32[]{:S(2)}, u32[]{:S(2)}) collective-permute-start(f32[19,1,8,128]{3,2,1,0:T(8,128)S(1)} %get-tuple-element.372), channel_id=1, source_target_pairs={{0,8},{8,16},{16,24},{1,9},{9,17},{17,25},{2,10},{10,18},{18,26},{... | collective-permute-start | bytes 233480 | tf_op jit(solution)/shard_map/ppermute | solution.py:54
  98.7 5.9 %collective-permute-start.14 = (f32[19,4,1,128]{3,2,1,0:T(1,128)S(1)}, f32[19,4,1,128]{3,2,1,0:T(1,128)S(1)}, u32[]{:S(2)}, u32[]{:S(2)}) collective-permute-start(f32[19,4,1,128]{3,2,1,0:T(1,128)S(1)} %get-tuple-element.211), channel_id=1, source_target_pairs={{4,0},{5,1},{6,2},{7,3},{12,8},{13,9},{14,10},{15,11},{20,16},{21,... | collective-permute-start | bytes 116744 | tf_op jit(solution)/shard_map/ppermute | solution.py:55
  100.0 6.2 %collective-permute-start.15 = (f32[19,4,1,128]{3,2,1,0:T(1,128)S(1)}, f32[19,4,1,128]{3,2,1,0:T(1,128)S(1)}, u32[]{:S(2)}, u32[]{:S(2)}) collective-permute-start(f32[19,4,1,128]{3,2,1,0:T(1,128)S(1)} %get-tuple-element.210), channel_id=1, source_target_pairs={{0,4},{1,5},{2,6},{3,7},{8,12},{9,13},{10,14},{11,15},{16,20},{17,... | collective-permute-start | bytes 116744 | tf_op jit(solution)/shard_map/ppermute | solution.py:54
  107.0 6.3 %collective-permute-start.16 = (f32[19,4,10,1]{0,1,3,2:T(4,128)S(1)}, f32[19,4,10,1]{0,1,3,2:T(4,128)S(1)}, u32[]{:S(2)}, u32[]{:S(2)}) collective-permute-start(f32[19,4,10,1]{0,1,3,2:T(4,128)S(1)} %copy.102), channel_id=1, source_target_pairs={{1,0},{2,1},{3,2},{5,4},{6,5},{7,6},{9,8},{10,9},{11,10},{13,12},{... | collective-permute-start | bytes 9128 | tf_op jit(solution)/shard_map/ppermute | solution.py:55
  108.7 6.0 %collective-permute-start.17 = (f32[19,4,10,1]{0,1,3,2:T(4,128)S(1)}, f32[19,4,10,1]{0,1,3,2:T(4,128)S(1)}, u32[]{:S(2)}, u32[]{:S(2)}) collective-permute-start(f32[19,4,10,1]{0,1,3,2:T(4,128)S(1)} %copy.104), channel_id=1, source_target_pairs={{0,1},{1,2},{2,3},{4,5},{5,6},{6,7},{8,9},{9,10},{10,11},{12,13},{... | collective-permute-start | bytes 9128 | tf_op jit(solution)/shard_map/ppermute | solution.py:54
  117.0 5.9 %collective-permute-start.18 = (f32[19,1,8,128]{3,2,1,0:T(8,128)S(1)}, f32[19,1,8,128]{3,2,1,0:T(8,128)S(1)}, u32[]{:S(2)}, u32[]{:S(2)}) collective-permute-start(f32[19,1,8,128]{3,2,1,0:T(8,128)S(1)} %get-tuple-element.369), channel_id=1, source_target_pairs={{8,0},{16,8},{24,16},{9,1},{17,9},{25,17},{10,2},{18,10},{26,18},{... | collective-permute-start | bytes 233480 | tf_op jit(solution)/shard_map/ppermute | solution.py:55
  118.3 5.5 %collective-permute-start.19 = (f32[19,1,8,128]{3,2,1,0:T(8,128)S(1)}, f32[19,1,8,128]{3,2,1,0:T(8,128)S(1)}, u32[]{:S(2)}, u32[]{:S(2)}) collective-permute-start(f32[19,1,8,128]{3,2,1,0:T(8,128)S(1)} %get-tuple-element.368), channel_id=1, source_target_pairs={{0,8},{8,16},{16,24},{1,9},{9,17},{17,25},{2,10},{10,18},{18,26},{... | collective-permute-start | bytes 233480 | tf_op jit(solution)/shard_map/ppermute | solution.py:54
  123.9 5.9 %collective-permute-start.20 = (f32[19,4,1,128]{3,2,1,0:T(1,128)S(1)}, f32[19,4,1,128]{3,2,1,0:T(1,128)S(1)}, u32[]{:S(2)}, u32[]{:S(2)}) collective-permute-start(f32[19,4,1,128]{3,2,1,0:T(1,128)S(1)} %get-tuple-element.207), channel_id=1, source_target_pairs={{4,0},{5,1},{6,2},{7,3},{12,8},{13,9},{14,10},{15,11},{20,16},{21,... | collective-permute-start | bytes 116744 | tf_op jit(solution)/shard_map/ppermute | solution.py:55
  125.2 6.2 %collective-permute-start.21 = (f32[19,4,1,128]{3,2,1,0:T(1,128)S(1)}, f32[19,4,1,128]{3,2,1,0:T(1,128)S(1)}, u32[]{:S(2)}, u32[]{:S(2)}) collective-permute-start(f32[19,4,1,128]{3,2,1,0:T(1,128)S(1)} %get-tuple-element.206), channel_id=1, source_target_pairs={{0,4},{1,5},{2,6},{3,7},{8,12},{9,13},{10,14},{11,15},{16,20},{17,... | collective-permute-start | bytes 116744 | tf_op jit(solution)/shard_map/ppermute | solution.py:54
  132.2 6.5 %collective-permute-start.22 = (f32[19,4,10,1]{0,1,3,2:T(4,128)S(1)}, f32[19,4,10,1]{0,1,3,2:T(4,128)S(1)}, u32[]{:S(2)}, u32[]{:S(2)}) collective-permute-start(f32[19,4,10,1]{0,1,3,2:T(4,128)S(1)} %copy.106), channel_id=1, source_target_pairs={{1,0},{2,1},{3,2},{5,4},{6,5},{7,6},{9,8},{10,9},{11,10},{13,12},{... | collective-permute-start | bytes 9128 | tf_op jit(solution)/shard_map/ppermute | solution.py:55
  133.9 6.0 %collective-permute-start.23 = (f32[19,4,10,1]{0,1,3,2:T(4,128)S(1)}, f32[19,4,10,1]{0,1,3,2:T(4,128)S(1)}, u32[]{:S(2)}, u32[]{:S(2)}) collective-permute-start(f32[19,4,10,1]{0,1,3,2:T(4,128)S(1)} %copy.108), channel_id=1, source_target_pairs={{0,1},{1,2},{2,3},{4,5},{5,6},{6,7},{8,9},{9,10},{10,11},{12,13},{... | collective-permute-start | bytes 9128 | tf_op jit(solution)/shard_map/ppermute | solution.py:54
  143.8 7.5 %collective-permute-start.36 = (f32[19,1,8,128]{3,2,1,0:T(8,128)S(1)}, f32[19,1,8,128]{3,2,1,0:T(8,128)S(1)}, u32[]{:S(2)}, u32[]{:S(2)}) collective-permute-start(f32[19,1,8,128]{3,2,1,0:T(8,128)S(1)} %get-tuple-element.347), channel_id=1, source_target_pairs={{8,0},{16,8},{24,16},{9,1},{17,9},{25,17},{10,2},{18,10},{26,18},{... | collective-permute-start | bytes 233480 | tf_op jit(solution)/shard_map/ppermute | solution.py:55
  145.1 7.0 %collective-permute-start.37 = (f32[19,1,8,128]{3,2,1,0:T(8,128)S(1)}, f32[19,1,8,128]{3,2,1,0:T(8,128)S(1)}, u32[]{:S(2)}, u32[]{:S(2)}) collective-permute-start(f32[19,1,8,128]{3,2,1,0:T(8,128)S(1)} %get-tuple-element.346), channel_id=1, source_target_pairs={{0,8},{8,16},{16,24},{1,9},{9,17},{17,25},{2,10},{10,18},{18,26},{... | collective-permute-start | bytes 233480 | tf_op jit(solution)/shard_map/ppermute | solution.py:54
  152.2 5.9 %collective-permute-start.38 = (f32[19,4,1,128]{3,2,1,0:T(1,128)S(1)}, f32[19,4,1,128]{3,2,1,0:T(1,128)S(1)}, u32[]{:S(2)}, u32[]{:S(2)}) collective-permute-start(f32[19,4,1,128]{3,2,1,0:T(1,128)S(1)} %get-tuple-element.203), channel_id=1, source_target_pairs={{4,0},{5,1},{6,2},{7,3},{12,8},{13,9},{14,10},{15,11},{20,16},{21,... | collective-permute-start | bytes 116744 | tf_op jit(solution)/shard_map/ppermute | solution.py:55
  153.5 6.2 %collective-permute-start.39 = (f32[19,4,1,128]{3,2,1,0:T(1,128)S(1)}, f32[19,4,1,128]{3,2,1,0:T(1,128)S(1)}, u32[]{:S(2)}, u32[]{:S(2)}) collective-permute-start(f32[19,4,1,128]{3,2,1,0:T(1,128)S(1)} %get-tuple-element.202), channel_id=1, source_target_pairs={{0,4},{1,5},{2,6},{3,7},{8,12},{9,13},{10,14},{11,15},{16,20},{17,... | collective-permute-start | bytes 116744 | tf_op jit(solution)/shard_map/ppermute | solution.py:54
  160.5 6.3 %collective-permute-start.40 = (f32[19,4,10,1]{0,1,3,2:T(4,128)S(1)}, f32[19,4,10,1]{0,1,3,2:T(4,128)S(1)}, u32[]{:S(2)}, u32[]{:S(2)}) collective-permute-start(f32[19,4,10,1]{0,1,3,2:T(4,128)S(1)} %copy.118), channel_id=1, source_target_pairs={{1,0},{2,1},{3,2},{5,4},{6,5},{7,6},{9,8},{10,9},{11,10},{13,12},{... | collective-permute-start | bytes 9128 | tf_op jit(solution)/shard_map/ppermute | solution.py:55
  162.3 6.0 %collective-permute-start.41 = (f32[19,4,10,1]{0,1,3,2:T(4,128)S(1)}, f32[19,4,10,1]{0,1,3,2:T(4,128)S(1)}, u32[]{:S(2)}, u32[]{:S(2)}) collective-permute-start(f32[19,4,10,1]{0,1,3,2:T(4,128)S(1)} %copy.120), channel_id=1, source_target_pairs={{0,1},{1,2},{2,3},{4,5},{5,6},{6,7},{8,9},{9,10},{10,11},{12,13},{... | collective-permute-start | bytes 9128 | tf_op jit(solution)/shard_map/ppermute | solution.py:54
  171.7 14.5 %collective-permute-start.42 = (f32[19,1,8,128]{3,2,1,0:T(8,128)S(1)}, f32[19,1,8,128]{3,2,1,0:T(8,128)S(1)}, u32[]{:S(2)}, u32[]{:S(2)}) collective-permute-start(f32[19,1,8,128]{3,2,1,0:T(8,128)S(1)} %get-tuple-element.327), channel_id=1, source_target_pairs={{8,0},{16,8},{24,16},{9,1},{17,9},{25,17},{10,2},{18,10},{26,18},{... | collective-permute-start | bytes 233480 | tf_op jit(solution)/shard_map/ppermute | solution.py:55
  173.0 13.2 %collective-permute-start.43 = (f32[19,1,8,128]{3,2,1,0:T(8,128)S(1)}, f32[19,1,8,128]{3,2,1,0:T(8,128)S(1)}, u32[]{:S(2)}, u32[]{:S(2)}) collective-permute-start(f32[19,1,8,128]{3,2,1,0:T(8,128)S(1)} %get-tuple-element.326), channel_id=1, source_target_pairs={{0,8},{8,16},{16,24},{1,9},{9,17},{17,25},{2,10},{10,18},{18,26},{... | collective-permute-start | bytes 233480 | tf_op jit(solution)/shard_map/ppermute | solution.py:54
  178.7 13.5 %collective-permute-start.24 = (f32[19,1,8,128]{3,2,1,0:T(8,128)S(1)}, f32[19,1,8,128]{3,2,1,0:T(8,128)S(1)}, u32[]{:S(2)}, u32[]{:S(2)}) collective-permute-start(f32[19,1,8,128]{3,2,1,0:T(8,128)S(1)} %get-tuple-element.367), channel_id=1, source_target_pairs={{0,8},{8,16},{16,24},{1,9},{9,17},{17,25},{2,10},{10,18},{18,26},{... | collective-permute-start | bytes 233480 | tf_op jit(solution)/shard_map/ppermute | solution.py:54
  184.9 7.2 %collective-permute-start.25 = (f32[19,1,8,128]{3,2,1,0:T(8,128)S(1)}, f32[19,1,8,128]{3,2,1,0:T(8,128)S(1)}, u32[]{:S(2)}, u32[]{:S(2)}) collective-permute-start(f32[19,1,8,128]{3,2,1,0:T(8,128)S(1)} %get-tuple-element.366), channel_id=1, source_target_pairs={{8,0},{16,8},{24,16},{9,1},{17,9},{25,17},{10,2},{18,10},{26,18},{... | collective-permute-start | bytes 233480 | tf_op jit(solution)/shard_map/ppermute | solution.py:55
  186.3 8.6 %collective-permute-start.44 = (f32[19,4,1,128]{3,2,1,0:T(1,128)S(1)}, f32[19,4,1,128]{3,2,1,0:T(1,128)S(1)}, u32[]{:S(2)}, u32[]{:S(2)}) collective-permute-start(f32[19,4,1,128]{3,2,1,0:T(1,128)S(1)} %get-tuple-element.201), channel_id=1, source_target_pairs={{4,0},{5,1},{6,2},{7,3},{12,8},{13,9},{14,10},{15,11},{20,16},{21,... | collective-permute-start | bytes 116744 | tf_op jit(solution)/shard_map/ppermute | solution.py:55
  187.6 7.3 %collective-permute-start.45 = (f32[19,4,1,128]{3,2,1,0:T(1,128)S(1)}, f32[19,4,1,128]{3,2,1,0:T(1,128)S(1)}, u32[]{:S(2)}, u32[]{:S(2)}) collective-permute-start(f32[19,4,1,128]{3,2,1,0:T(1,128)S(1)} %get-tuple-element.200), channel_id=1, source_target_pairs={{0,4},{1,5},{2,6},{3,7},{8,12},{9,13},{10,14},{11,15},{16,20},{17,... | collective-permute-start | bytes 116744 | tf_op jit(solution)/shard_map/ppermute | solution.py:54
  192.2 10.1 %collective-permute-start.26 = (f32[19,4,1,128]{3,2,1,0:T(1,128)S(1)}, f32[19,4,1,128]{3,2,1,0:T(1,128)S(1)}, u32[]{:S(2)}, u32[]{:S(2)}) collective-permute-start(f32[19,4,1,128]{3,2,1,0:T(1,128)S(1)} %get-tuple-element.205), channel_id=1, source_target_pairs={{0,4},{1,5},{2,6},{3,7},{8,12},{9,13},{10,14},{11,15},{16,20},{17,... | collective-permute-start | bytes 116744 | tf_op jit(solution)/shard_map/ppermute | solution.py:54
  193.5 8.8 %collective-permute-start.27 = (f32[19,4,1,128]{3,2,1,0:T(1,128)S(1)}, f32[19,4,1,128]{3,2,1,0:T(1,128)S(1)}, u32[]{:S(2)}, u32[]{:S(2)}) collective-permute-start(f32[19,4,1,128]{3,2,1,0:T(1,128)S(1)} %get-tuple-element.204), channel_id=1, source_target_pairs={{4,0},{5,1},{6,2},{7,3},{12,8},{13,9},{14,10},{15,11},{20,16},{21,... | collective-permute-start | bytes 116744 | tf_op jit(solution)/shard_map/ppermute | solution.py:55
  195.7 13.2 %collective-permute-start.46 = (f32[19,4,10,1]{0,1,3,2:T(4,128)S(1)}, f32[19,4,10,1]{0,1,3,2:T(4,128)S(1)}, u32[]{:S(2)}, u32[]{:S(2)}) collective-permute-start(f32[19,4,10,1]{0,1,3,2:T(4,128)S(1)} %copy.122), channel_id=1, source_target_pairs={{1,0},{2,1},{3,2},{5,4},{6,5},{7,6},{9,8},{10,9},{11,10},{13,12},{... | collective-permute-start | bytes 9128 | tf_op jit(solution)/shard_map/ppermute | solution.py:55
  197.5 12.2 %collective-permute-start.47 = (f32[19,4,10,1]{0,1,3,2:T(4,128)S(1)}, f32[19,4,10,1]{0,1,3,2:T(4,128)S(1)}, u32[]{:S(2)}, u32[]{:S(2)}) collective-permute-start(f32[19,4,10,1]{0,1,3,2:T(4,128)S(1)} %copy.124), channel_id=1, source_target_pairs={{0,1},{1,2},{2,3},{4,5},{5,6},{6,7},{8,9},{9,10},{10,11},{12,13},{... | collective-permute-start | bytes 9128 | tf_op jit(solution)/shard_map/ppermute | solution.py:54
  203.2 14.8 %collective-permute-start.28 = (f32[19,4,10,1]{0,1,3,2:T(4,128)S(1)}, f32[19,4,10,1]{0,1,3,2:T(4,128)S(1)}, u32[]{:S(2)}, u32[]{:S(2)}) collective-permute-start(f32[19,4,10,1]{0,1,3,2:T(4,128)S(1)} %copy.110), channel_id=1, source_target_pairs={{0,1},{1,2},{2,3},{4,5},{5,6},{6,7},{8,9},{9,10},{10,11},{12,13},{... | collective-permute-start | bytes 9128 | tf_op jit(solution)/shard_map/ppermute | solution.py:54
  207.5 11.2 %collective-permute-start.29 = (f32[19,4,10,1]{0,1,3,2:T(4,128)S(1)}, f32[19,4,10,1]{0,1,3,2:T(4,128)S(1)}, u32[]{:S(2)}, u32[]{:S(2)}) collective-permute-start(f32[19,4,10,1]{0,1,3,2:T(4,128)S(1)} %copy.112), channel_id=1, source_target_pairs={{1,0},{2,1},{3,2},{5,4},{6,5},{7,6},{9,8},{10,9},{11,10},{13,12},{... | collective-permute-start | bytes 9128 | tf_op jit(solution)/shard_map/ppermute | solution.py:55
  213.0 7.0 %collective-permute-start.48 = (f32[19,1,8,128]{3,2,1,0:T(8,128)S(1)}, f32[19,1,8,128]{3,2,1,0:T(8,128)S(1)}, u32[]{:S(2)}, u32[]{:S(2)}) collective-permute-start(f32[19,1,8,128]{3,2,1,0:T(8,128)S(1)} %get-tuple-element.307), channel_id=1, source_target_pairs={{8,0},{16,8},{24,16},{9,1},{17,9},{25,17},{10,2},{18,10},{26,18},{... | collective-permute-start | bytes 233480 | tf_op jit(solution)/shard_map/ppermute | solution.py:55
  214.3 5.7 %collective-permute-start.49 = (f32[19,1,8,128]{3,2,1,0:T(8,128)S(1)}, f32[19,1,8,128]{3,2,1,0:T(8,128)S(1)}, u32[]{:S(2)}, u32[]{:S(2)}) collective-permute-start(f32[19,1,8,128]{3,2,1,0:T(8,128)S(1)} %get-tuple-element.306), channel_id=1, source_target_pairs={{0,8},{8,16},{16,24},{1,9},{9,17},{17,25},{2,10},{10,18},{18,26},{... | collective-permute-start | bytes 233480 | tf_op jit(solution)/shard_map/ppermute | solution.py:54
  220.7 5.9 %collective-permute-start.50 = (f32[19,4,1,128]{3,2,1,0:T(1,128)S(1)}, f32[19,4,1,128]{3,2,1,0:T(1,128)S(1)}, u32[]{:S(2)}, u32[]{:S(2)}) collective-permute-start(f32[19,4,1,128]{3,2,1,0:T(1,128)S(1)} %get-tuple-element.199), channel_id=1, source_target_pairs={{4,0},{5,1},{6,2},{7,3},{12,8},{13,9},{14,10},{15,11},{20,16},{21,... | collective-permute-start | bytes 116744 | tf_op jit(solution)/shard_map/ppermute | solution.py:55
  222.0 6.2 %collective-permute-start.51 = (f32[19,4,1,128]{3,2,1,0:T(1,128)S(1)}, f32[19,4,1,128]{3,2,1,0:T(1,128)S(1)}, u32[]{:S(2)}, u32[]{:S(2)}) collective-permute-start(f32[19,4,1,128]{3,2,1,0:T(1,128)S(1)} %get-tuple-element.198), channel_id=1, source_target_pairs={{0,4},{1,5},{2,6},{3,7},{8,12},{9,13},{10,14},{11,15},{16,20},{17,... | collective-permute-start | bytes 116744 | tf_op jit(solution)/shard_map/ppermute | solution.py:54
  229.6 7.3 %collective-permute-start.52 = (f32[19,4,10,1]{0,1,3,2:T(4,128)}, f32[19,4,10,1]{0,1,3,2:T(4,128)S(1)}, u32[]{:S(2)}, u32[]{:S(2)}) collective-permute-start(f32[19,4,10,1]{0,1,3,2:T(4,128)} %copy.126), channel_id=1, source_target_pairs={{1,0},{2,1},{3,2},{5,4},{6,5},{7,6},{9,8},{10,9},{11,10},{13,12},{... | collective-permute-start | bytes 9128 | tf_op jit(solution)/shard_map/ppermute | solution.py:55
  231.4 6.4 %collective-permute-start.53 = (f32[19,4,10,1]{0,1,3,2:T(4,128)S(1)}, f32[19,4,10,1]{0,1,3,2:T(4,128)}, u32[]{:S(2)}, u32[]{:S(2)}) collective-permute-start(f32[19,4,10,1]{0,1,3,2:T(4,128)S(1)} %copy.128), channel_id=1, source_target_pairs={{0,1},{1,2},{2,3},{4,5},{5,6},{6,7},{8,9},{9,10},{10,11},{12,13},{... | collective-permute-start | bytes 9128 | tf_op jit(solution)/shard_map/ppermute | solution.py:54
  241.7 4.8 %collective-permute-start.54 = (f32[1,8,128]{2,1,0:T(8,128)S(1)}, f32[1,8,128]{2,1,0:T(8,128)S(1)}, u32[]{:S(2)}, u32[]{:S(2)}) collective-permute-start(f32[1,8,128]{2,1,0:T(8,128)S(1)} %get-tuple-element.402), channel_id=1, source_target_pairs={{0,8},{8,16},{16,24},{1,9},{9,17},{17,25},{2,10},{10,18},{18,26},{... | collective-permute-start | bytes 12296 | tf_op jit(solution)/shard_map/ppermute | solution.py:54
  244.5 4.8 %collective-permute-start.55 = (f32[1,8,128]{2,1,0:T(8,128)S(1)}, f32[1,8,128]{2,1,0:T(8,128)S(1)}, u32[]{:S(2)}, u32[]{:S(2)}) collective-permute-start(f32[1,8,128]{2,1,0:T(8,128)S(1)} %get-tuple-element.403), channel_id=1, source_target_pairs={{8,0},{16,8},{24,16},{9,1},{17,9},{25,17},{10,2},{18,10},{26,18},{... | collective-permute-start | bytes 12296 | tf_op jit(solution)/shard_map/ppermute | solution.py:55
  249.3 6.2 %collective-permute-start.56 = (f32[4,1,128]{2,1,0:T(1,128)S(1)}, f32[4,1,128]{2,1,0:T(1,128)S(1)}, u32[]{:S(2)}, u32[]{:S(2)}) collective-permute-start(f32[4,1,128]{2,1,0:T(1,128)S(1)} %get-tuple-element.380), channel_id=1, source_target_pairs={{0,4},{1,5},{2,6},{3,7},{8,12},{9,13},{10,14},{11,15},{16,20},{17,... | collective-permute-start | bytes 6152 | tf_op jit(solution)/shard_map/ppermute | solution.py:54
  253.5 5.5 %collective-permute-start.57 = (f32[4,1,128]{2,1,0:T(1,128)S(1)}, f32[4,1,128]{2,1,0:T(1,128)S(1)}, u32[]{:S(2)}, u32[]{:S(2)}) collective-permute-start(f32[4,1,128]{2,1,0:T(1,128)S(1)} %get-tuple-element.381), channel_id=1, source_target_pairs={{4,0},{5,1},{6,2},{7,3},{12,8},{13,9},{14,10},{15,11},{20,16},{21,... | collective-permute-start | bytes 6152 | tf_op jit(solution)/shard_map/ppermute | solution.py:55
  259.1 6.3 %collective-permute-start.58 = (f32[4,10,1]{2,1,0:T(8,128)S(1)}, f32[4,10,1]{2,1,0:T(8,128)S(1)}, u32[]{:S(2)}, u32[]{:S(2)}) collective-permute-start(f32[4,10,1]{2,1,0:T(8,128)S(1)} %get-tuple-element.376), channel_id=1, source_target_pairs={{0,1},{1,2},{2,3},{4,5},{5,6},{6,7},{8,9},{9,10},{10,11},{12,13},{... | collective-permute-start | bytes 488 | tf_op jit(solution)/shard_map/ppermute | solution.py:54
  263.4 6.1 %collective-permute-start.59 = (f32[4,10,1]{2,1,0:T(8,128)S(1)}, f32[4,10,1]{2,1,0:T(8,128)S(1)}, u32[]{:S(2)}, u32[]{:S(2)}) collective-permute-start(f32[4,10,1]{2,1,0:T(8,128)S(1)} %get-tuple-element.377), channel_id=1, source_target_pairs={{1,0},{2,1},{3,2},{5,4},{6,5},{7,6},{9,8},{10,9},{11,10},{13,12},{... | collective-permute-start | bytes 488 | tf_op jit(solution)/shard_map/ppermute | solution.py:55
  (11 other events, 7.8 us)

commit v3 on v2

--- a/solution.py
+++ b/solution.py
@@ -174,7 +174,7 @@
     return eta[0, 0]
 
 
-def body(design, populations, cotangent, wall_mask, inlet_mask, beta_step):
+def body_by_blocks(design, populations, cotangent, wall_mask, inlet_mask, beta_step):
     beta = jnp.exp2(beta_step.astype(jnp.float32) / 16.0)
     filtered = smooth_field(design)
     cells = design.size * lax.axis_size("grp") * lax.axis_size("gy") * lax.axis_size("gx")
@@ -207,6 +207,461 @@
     return (popul, design_grad)
 
 
+HALO = 8
+LANES = 128
+AROUND = ((1, 0), (-1, 0), (0, 1), (0, -1), (1, 1), (-1, -1), (1, -1), (-1, 1))
+FIELDS = 40
+PACKED = 20
+
+
+def rolled(value, amount):
+    amount = amount % LANES
+    return value if amount == 0 else pltpu.roll(value, amount, 1)
+
+
+def lane_index():
+    return lax.broadcasted_iota(jnp.int32, (8, LANES), 1)
+
+
+def merge(parts, width):
+    lanes = lane_index()
+    total = parts[0]
+    for index in range(1, len(parts)):
+        total = jnp.where(lanes >= index * width, parts[index], total)
+    return total
+
+
+def field(refs, index, layer):
+    populations_ref, cotangent_ref, wall_ref, inlet_ref = refs
+    if index < 19:
+        return populations_ref[index, layer]
+    if index < 38:
+        return cotangent_ref[index - 19, layer]
+    return (wall_ref if index == 38 else inlet_ref)[layer].astype(jnp.float32)
+
+
+def edge_kernel(design_ref, populations_ref, cotangent_ref, wall_ref, inlet_ref, copies_ref, edges_ref):
+    refs = (populations_ref, cotangent_ref, wall_ref, inlet_ref)
+    me = lax.axis_index("gx")
+    zero = jnp.zeros((8, LANES), jnp.float32)
+    for layer in range(design_ref.shape[0]):
+        for device in range(copies_ref.shape[0]):
+            copies_ref[device, layer] = design_ref[layer]
+        for group in range(edges_ref.shape[1]):
+            first, last = [], []
+            for slot in range(16):
+                index = group * 16 + slot
+                if index < FIELDS:
+                    value = field(refs, index, layer)
+                    first.append(rolled(value, 8 * slot))
+                    last.append(rolled(value, 8 * slot + HALO))
+                else:
+                    first.append(zero)
+                    last.append(zero)
+            first, last = merge(first, 8), merge(last, 8)
+            for device in range(edges_ref.shape[0]):
+                edges_ref[device, group, layer] = jnp.where(me > device, first, last)
+
+
+def window_kernel(populations_ref, cotangent_ref, wall_ref, inlet_ref, edges_ref, windows_ref):
+    refs = (populations_ref, cotangent_ref, wall_ref, inlet_ref)
+    me, size = lax.axis_index("gx"), edges_ref.shape[0]
+    before, after = jnp.maximum(me - 1, 0), jnp.minimum(me + 1, size - 1)
+    lanes = lane_index()
+    column = lanes % 32
+    devices = windows_ref.shape[0]
+    for layer in range(wall_ref.shape[0]):
+        for group in range(FIELDS // 4):
+            values = [field(refs, group * 4 + slot, layer) for slot in range(4)]
+            for device in range(devices):
+                start = 16 * device - HALO
+                window = merge([rolled(values[slot], 32 * slot - start) for slot in range(4)], 32)
+                if device in (0, devices - 1):
+                    source, offset = (before, 0) if device == 0 else (after, 24)
+                    known = (me > 0) if device == 0 else (me < size - 1)
+                    edge = edges_ref[source, group // 4, layer]
+                    place = (group % 4) * 4
+                    outer = merge(
+                        [rolled(edge, 32 * slot + offset - 8 * (place + slot)) for slot in range(4)], 32
+                    )
+                    outer = jnp.where(known, outer, 0.0)
+                    inside = (column >= HALO) if device == 0 else (column < 24)
+                    window = jnp.where(inside, window, outer)
+                windows_ref[device, group, layer] = window
+
+
+def exponent(step_ref):
+    steps = jnp.full((8, LANES), step_ref[0], jnp.int32).astype(jnp.float32)
+    return jnp.exp2(steps / 16.0)
+
+
+def plane_masks(rows):
+    lanes = lane_index()
+    depth, place_z, place_y = LANES // rows, lanes // rows, lanes % rows
+    masks = {}
+    for cz, cy in AROUND:
+        inside = None
+        for shift, place, count in ((cz, place_z, depth), (cy, place_y, rows)):
+            if shift:
+                here = (place >= 1) if shift > 0 else (place < count - 1)
+                inside = here if inside is None else inside & here
+        masks[cz, cy] = inside
+    return masks
+
+
+def plane_shift(value, cz, cy, rows, masks):
+    if cz == 0 and cy == 0:
+        return value
+    return jnp.where(masks[cz, cy], rolled(value, cz * rows + cy), 0.0)
+
+
+def plane_smooth(value, rows, masks):
+    for cz, cy in ((1, 0), (0, 1)):
+        value = 0.5 * value + 0.25 * (
+            plane_shift(value, cz, cy, rows, masks) + plane_shift(value, -cz, -cy, rows, masks)
+        )
+    return value
+
+
+def gather_plane(read, planes, splits):
+    blocks = []
+    for z in range(planes):
+        for part in range(splits):
+            blocks.append(read(z, part))
+    return jnp.concatenate(blocks, axis=0)
+
+
+def level_kernel(rows, splits, size, step_ref, copies_ref, eta_ref, window_ref, design_ref, filtered_ref, raised_ref):
+    layers = copies_ref.shape[1]
+    planes = LANES // rows
+    columns = size * LANES
+    masks = plane_masks(rows)
+    zero = jnp.zeros((8, LANES), jnp.float32)
+    for ref in (design_ref, filtered_ref):
+        ref[0:8, :] = zero
+        ref[columns + 8 : columns + 16, :] = zero
+    for block in range(size):
+        plane = gather_plane(
+            lambda z, part: copies_ref[((z // layers) * splits + part) * size + block, z % layers],
+            planes,
+            splits,
+        )
+        design_ref[8 + block * LANES : 8 + (block + 1) * LANES, :] = plane.T
+    for row in range(8, columns + 8, 8):
+        design_ref[row : row + 8, :] = plane_smooth(design_ref[row : row + 8, :], rows, masks)
+    beta = exponent(step_ref)
+    for row in range(8, columns + 8, 8):
+        value = 0.5 * design_ref[row : row + 8, :] + 0.25 * (
+            design_ref[row - 1 : row + 7, :] + design_ref[row + 1 : row + 9, :]
+        )
+        filtered_ref[row : row + 8, :] = value
+        raised_ref[row - 8 : row, :] = jnp.exp(2.0 * beta * value)
+    top = jnp.exp(2.0 * beta)
+
+    def halve(step, ends):
+        low, high = ends
+        middle = 0.5 * (low + high)
+        level = jnp.exp(2.0 * beta * middle)
+        totals = [zero] * 4
+        for index, row in enumerate(range(0, columns, 8)):
+            raised = raised_ref[row : row + 8, :]
+            totals[index % 4] = totals[index % 4] + (raised - 1.0) / (raised + level)
+        total = (totals[0] + totals[1]) + (totals[2] + totals[3])
+        volume = jnp.sum(jnp.sum(total, axis=0, keepdims=True), axis=1, keepdims=True)
+        above = volume * ((top + level) / (top - 1.0)) > fluid_share * (columns * LANES)
+        return jnp.where(above, middle, low), jnp.where(above, high, middle)
+
+    low, high = lax.fori_loop(0, BISECT, halve, (zero, jnp.ones((8, LANES), jnp.float32)))
+    eta_ref[...] = 0.5 * (low + high)
+    place = (lax.axis_index("gx") * lax.axis_size("grp") + lax.axis_index("grp")) * splits + lax.axis_index("gy")
+    window_ref[...] = filtered_ref[pl.ds(pl.multiple_of(place * 16, 8), 32), :]
+
+
+def flow(rho, speed):
+    square = 1.0 - 1.5 * (speed[0] * speed[0] + speed[1] * speed[1] + speed[2] * speed[2])
+    comps = [lattice_weights[0] * rho * square]
+    weighted = {1.0 / 18.0: rho * (1.0 / 18.0), 1.0 / 36.0: rho * (1.0 / 36.0)}
+    for i in range(1, 19, 2):
+        along = along_of(speed, i)
+        weight = weighted[lattice_weights[i]]
+        even = weight * (square + 4.5 * along * along)
+        odd = weight * (3.0 * along)
+        comps += [even + odd, even - odd]
+    return comps
+
+
+def along_of(speed, i):
+    total = None
+    for axis in range(3):
+        sign = int(velocities[i][axis])
+        if sign:
+            if total is None:
+                total = speed[axis] if sign > 0 else -speed[axis]
+            else:
+                total = total + speed[axis] if sign > 0 else total - speed[axis]
+    return total
+
+
+def add_along(totals, value, i):
+    for axis in range(3):
+        sign = int(velocities[i][axis])
+        if sign:
+            if totals[axis] is None:
+                totals[axis] = value if sign > 0 else -value
+            else:
+                totals[axis] = totals[axis] + value if sign > 0 else totals[axis] - value
+
+
+def inlet_value(i):
+    along = float(velocities[i][0]) * inlet_speed
+    return lattice_weights[i] * (1.0 + 3.0 * along + 4.5 * along * along - 1.5 * inlet_speed * inlet_speed)
+
+
+def flow_kernel(
+    rows, splits, size, step_ref, eta_ref, filtered_ref, windows_ref, packed_ref,
+    input_ref, even_ref, odd_ref, kept_ref, share_ref, grad_ref, smooth_ref, output_ref,
+):
+    layers = windows_ref.shape[2]
+    planes = LANES // rows
+    masks = plane_masks(rows)
+    zero = jnp.zeros((8, LANES), jnp.float32)
+    place = (lax.axis_index("gx") * lax.axis_size("grp") + lax.axis_index("grp")) * splits + lax.axis_index("gy")
+    last = size * (planes // layers) * splits - 1
+
+    def inside(value, block):
+        if block == 0:
+            return jnp.where(place > 0, value, 0.0)
+        if block == 3:
+            return jnp.where(place < last, value, 0.0)
+        return value
+
+    input_ref[0:8, :] = zero
+    input_ref[FIELDS * 32 + 8 : FIELDS * 32 + 16, :] = zero
+    for group in range(FIELDS // 4):
+        plane = gather_plane(
+            lambda z, part: windows_ref[(z // layers) * splits + part, group, z % layers],
+            planes,
+            splits,
+        )
+        input_ref[8 + group * LANES : 8 + (group + 1) * LANES, :] = plane.T
+
+    def initial(i, row):
+        return input_ref[8 + 32 * i + row : 16 + 32 * i + row, :]
+
+    beta = exponent(step_ref)
+    level = jnp.exp(2.0 * beta * eta_ref[...])
+    top = jnp.exp(2.0 * beta)
+    whole = (top + level) / (top - 1.0)
+    for block in range(4):
+        at = slice(8 * block, 8 * block + 8)
+        raised = jnp.exp(2.0 * beta * filtered_ref[at, :])
+        part = 1.0 / (raised + level)
+        density_hat = ((raised - 1.0) * part) * whole
+        strength = alpha_most * penalty_shape
+        share_ref[0, at, :] = (penalty_shape + density_hat) / (
+            penalty_shape + strength + (1.0 - strength) * density_hat
+        )
+        slope = 2.0 * beta * (raised * part) * ((level + 1.0) * part) * whole
+        factor = -strength * (1.0 + penalty_shape) / (
+            (penalty_shape + density_hat) * (penalty_shape + density_hat)
+        )
+        share_ref[1, at, :] = slope * factor
+
+    for ref in (even_ref, odd_ref):
+        for i in range(19):
+            ref[i, 0:8, :] = zero
+            ref[i, 40:48, :] = zero
+
+    def arrived(ref, i, row):
+        cz, cy, cx = (int(c) for c in velocities[i])
+        return plane_shift(ref[i, row + 8 - cx : row + 16 - cx, :], cz, cy, rows, masks)
+
+    buffers = (even_ref, odd_ref)
+    for step in range(STEPS):
+        source, target = buffers[(step + 1) % 2], buffers[step % 2]
+        for block in range(4):
+            row = 8 * block
+            at = slice(row, row + 8)
+            if step == 0:
+                popul = [initial(i, row) for i in range(19)]
+            else:
+                popul = [arrived(source, i, row) for i in range(19)]
+            wall = initial(38, row) > 0.0
+            inlet = initial(39, row) > 0.0
+            rho = popul[0]
+            momentum = [None, None, None]
+            for i in range(1, 19, 2):
+                rho = rho + (popul[i] + popul[i + 1])
+                add_along(momentum, popul[i] - popul[i + 1], i)
+            scale = share_ref[0, at, :] / rho
+            speed = [value * scale for value in momentum]
+            kept_ref[step, 0, at, :] = rho
+            for axis in range(3):
+                kept_ref[step, 1 + axis, at, :] = speed[axis]
+            settled = flow(relax_rate * rho, speed)
+            for i in range(19):
+                post = (1.0 - relax_rate) * popul[i] + settled[i]
+                post = jnp.where(wall, popul[opposite[i]], jnp.where(inlet, inlet_value(i), post))
+                target[i, row + 8 : row + 16, :] = inside(post, block)
+    output_ref[16 * PACKED :, :] = jnp.zeros((3 * LANES - 16 * PACKED, LANES), jnp.float32)
+    source = buffers[(STEPS - 1) % 2]
+    for i in range(19):
+        for row in (8, 16):
+            output_ref[16 * i + row - 8 : 16 * i + row, :] = arrived(source, i, row)
+
+    for step in reversed(range(STEPS)):
+        source, target = buffers[step % 2], buffers[(step + 1) % 2]
+        for block in range(4):
+            row = 8 * block
+            at = slice(row, row + 8)
+            back = []
+            for i in range(19):
+                cz, cy, cx = (int(c) for c in velocities[i])
+                value = initial(19 + i, row + cx) if step == STEPS - 1 else source[i, row + 8 + cx : row + 16 + cx, :]
+                back.append(plane_shift(value, -cz, -cy, rows, masks))
+            wall = initial(38, row) > 0.0
+            inlet = initial(39, row) > 0.0
+            rho = kept_ref[step, 0, at, :]
+            speed = [kept_ref[step, 1 + axis, at, :] for axis in range(3)]
+            square = speed[0] * speed[0] + speed[1] * speed[1] + speed[2] * speed[2]
+            share = share_ref[0, at, :]
+            faces, edges = None, None
+            first, second = [None, None, None], [None, None, None]
+            for i in range(1, 19, 2):
+                both, apart = back[i] + back[i + 1], back[i] - back[i + 1]
+                if i < 7:
+                    faces = both if faces is None else faces + both
+                    both, apart = 2.0 * both, 2.0 * apart
+                else:
+                    edges = both if edges is None else edges + both
+                add_along(first, apart, i)
+                add_along(second, along_of(speed, i) * both, i)
+            mean = lattice_weights[0] * back[0] + (1.0 / 18.0) * faces + (1.0 / 36.0) * edges
+            first = [value * (3.0 / 36.0) for value in first]
+            second = [value * (9.0 / 36.0) for value in second]
+            twice = speed[0] * second[0] + speed[1] * second[1] + speed[2] * second[2]
+            once = speed[0] * first[0] + speed[1] * first[1] + speed[2] * first[2]
+            drag = once + twice - 3.0 * square * mean
+            term = jnp.where(wall | inlet, 0.0, -relax_rate * (rho * share * drag))
+            grad_ref[at, :] = term if step == STEPS - 1 else grad_ref[at, :] + term
+            if step == 0:
+                continue
+            rest = relax_rate * (mean * (1.0 + 1.5 * square) - 0.5 * twice)
+            push = [
+                (relax_rate * share) * (first[axis] + second[axis] - 3.0 * mean * speed[axis]) for axis in range(3)
+            ]
+            for i in range(19):
+                if i == 0:
+                    post = (1.0 - relax_rate) * back[0] + rest
+                else:
+                    way = along_of(push, i if i % 2 else i - 1)
+                    post = (1.0 - relax_rate) * back[i] + (rest + way if i % 2 else rest - way)
+                post = jnp.where(wall, back[opposite[i]], jnp.where(inlet, 0.0, post))
+                target[i, row + 8 : row + 16, :] = inside(post, block)
+
+    smooth_ref[0:8, :] = zero
+    smooth_ref[40:48, :] = zero
+    for block in range(4):
+        at = slice(8 * block, 8 * block + 8)
+        value = inside(grad_ref[at, :] * share_ref[1, at, :], block)
+        smooth_ref[8 * block + 8 : 8 * block + 16, :] = plane_smooth(value, rows, masks)
+    for row in (8, 16):
+        output_ref[16 * 19 + row - 8 : 16 * 19 + row, :] = 0.5 * smooth_ref[row + 8 : row + 16, :] + 0.25 * (
+            smooth_ref[row + 7 : row + 15, :] + smooth_ref[row + 9 : row + 17, :]
+        )
+    for group in range(packed_ref.shape[1]):
+        plane = output_ref[group * LANES : (group + 1) * LANES, :].T
+        for z in range(planes):
+            for part in range(splits):
+                at = (z * splits + part) * 8
+                packed_ref[(z // layers) * splits + part, group, z % layers] = plane[at : at + 8, :]
+
+
+def result_kernel(packed_ref, populations_ref, grad_ref):
+    for layer in range(grad_ref.shape[0]):
+        for index in range(PACKED):
+            group, slot = divmod(index, 8)
+            value = merge(
+                [rolled(packed_ref[device, group, layer], 16 * (device - slot)) for device in range(packed_ref.shape[0])],
+                16,
+            )
+            if index < 19:
+                populations_ref[index, layer] = value
+            else:
+                grad_ref[layer] = value
+
+
+def in_vmem(kernel, outs, name, scalars=0, scratch=()):
+    vmem = pl.BlockSpec(memory_space=pltpu.VMEM)
+    many = len(outs) > 1
+    shapes = tuple(jax.ShapeDtypeStruct(shape, jnp.float32) for shape in outs)
+
+    def call(*operands):
+        return pl.pallas_call(
+            kernel,
+            out_shape=shapes if many else shapes[0],
+            in_specs=[pl.BlockSpec(memory_space=pltpu.SMEM)] * scalars + [vmem] * (len(operands) - scalars),
+            out_specs=(vmem,) * len(outs) if many else vmem,
+            scratch_shapes=[pltpu.VMEM(shape, jnp.float32) for shape in scratch],
+            compiler_params=pltpu.CompilerParams(vmem_limit_bytes=40 * 2**20),
+            name=name,
+        )(*operands)
+
+    return call
+
+
+def body_by_columns(design, populations, cotangent, wall_mask, inlet_mask, beta_step):
+    grp, splits, size = (lax.axis_size(axis) for axis in ("grp", "gy", "gx"))
+    layers, height, width = design.shape
+    rows, plane = height * splits, (grp * splits)
+    step = beta_step.reshape(1)
+    tile = (layers, 8, LANES)
+    copies, edges = in_vmem(edge_kernel, ((plane * size, *tile), (size, 3, *tile)), "edges")(
+        design, populations, cotangent, wall_mask, inlet_mask
+    )
+    copies = lax.all_to_all(copies, ("grp", "gy", "gx"), 0, 0)
+    edges = lax.all_to_all(edges, "gx", 0, 0)
+    windows = in_vmem(window_kernel, ((plane, FIELDS // 4, *tile),), "windows")(
+        populations, cotangent, wall_mask, inlet_mask, edges
+    )
+    windows = lax.all_to_all(windows, ("grp", "gy"), 0, 0)
+    columns = size * LANES
+    padded = (columns + 16, LANES)
+    eta, filtered = in_vmem(
+        functools.partial(level_kernel, rows, splits, size),
+        ((8, LANES), (32, LANES)),
+        "level",
+        1,
+        (padded, padded, (columns, LANES)),
+    )(step, copies)
+    packed = in_vmem(
+        functools.partial(flow_kernel, rows, splits, size),
+        ((plane, 3, *tile),),
+        "flow",
+        1,
+        (
+            (FIELDS * 32 + 16, LANES),
+            (19, 48, LANES),
+            (19, 48, LANES),
+            (STEPS, 4, 32, LANES),
+            (2, 32, LANES),
+            (32, LANES),
+            (48, LANES),
+            (3 * LANES, LANES),
+        ),
+    )(step, eta, filtered, windows)
+    packed = lax.all_to_all(packed, ("grp", "gy"), 0, 0)
+    return in_vmem(result_kernel, (populations.shape, design.shape), "result")(packed)
+
+
+def body(design, populations, cotangent, wall_mask, inlet_mask, beta_step):
+    grp, splits = lax.axis_size("grp"), lax.axis_size("gy")
+    layers, height, width = design.shape
+    fits = height == 8 and width == LANES and layers * grp * height * splits == LANES
+    whole = body_by_columns if fits and grp * splits * 16 == LANES else body_by_blocks
+    return whole(design, populations, cotangent, wall_mask, inlet_mask, beta_step)
+
+
 def solution(mesh):
     placed = (
         P("grp", "gy", "gx"),

time: 272 us -> 57.1 us (0.21)
  starting transfers between devices: 173 us -> 6.88 us
  local copies, waits for them, and re-layouts: 30.4 us -> 3.92 us
  waiting for transfers between devices: 37.7 us -> 12.8 us
  blocking collectives: 0 us -> 20.1 us
  other arithmetic: 18.6 us -> 0 us
  Pallas kernels: 5.11 us -> 11.5 us
  between operations: 5.51 us -> 1.35 us
    ppermute x60 -> x0, starting transfers between devices: 167 us -> none  [the longest x30 128 us: extended(): before = lax.ppermute(last, axis, up)]
    ppermute x60 -> x0, waiting for transfers between devices: 37.7 us -> none  [the longest x30 21.9 us: extended(): after = lax.ppermute(leading, axis, down)]
    all_to_all x0 -> x2, blocking collectives: none -> 20.1 us  [the longest x1 11.9 us: body_by_columns(): edges = lax.all_to_all(edges, 'gx', 0, 0)]
    ppermute x16 -> x0, local copies, waits for them, and re-layouts: 12.9 us -> none  [the longest x8 6.82 us: extended(): before = lax.ppermute(last, axis, up)]
    all_to_all x1 -> x2, waiting for transfers between devices: 0.01 us -> 12.8 us  [the longest x1 8.98 us: body_by_columns(): copies = lax.all_to_all(copies, ('grp', 'gy', 'gx'), 0, 0)]
    slice x39 -> x0, local copies, waits for them, and re-layouts: 12.1 us -> none  [the longest x27 6.4 us: extended(): last = lax.slice_in_dim(value, length - width, length, axis=dim)]
    unnamed x157 -> x0, other arithmetic: 8.86 us -> none
    pallas_call x1 -> x5, Pallas kernels: 5.11 us -> 11.5 us  [call(): pl.pallas_call(kernel, out_shape=shapes if many else shapes[0], in_specs=...]
  transfers between devices with their start and end apart: 61 -> 2, of which waited for: 23 -> 2; matrix products, arithmetic and copies ran while one was open for 8% -> 0% of each run, Pallas kernels for 0% -> 14%
where the time goes in v3:
time: 57.1 us; the launch traced here: 56.6 us
  blocking collectives  20.1 us (35%)
  waiting for transfers between devices  12.8 us (22%)
  Pallas kernels  11.5 us (20%)
  starting transfers between devices  6.88 us (12%)
  local copies, waits for them, and re-layouts  3.92 us (7%)
  between operations  1.35 us (2%)
    all_to_all x1, blocking collectives, body_by_columns(): edges = lax.all_to_all(edges, 'gx', 0, 0)  11.9 us
    pallas_call x5, Pallas kernels, call(): pl.pallas_call(kernel, out_shape=shapes if many else shapes[0], in_specs=...  11.5 us
    all_to_all x1, waiting for transfers between devices, body_by_columns(): copies = lax.all_to_all(copies, ('grp', 'gy', 'gx'), 0, 0)  8.98 us
    all_to_all x1, blocking collectives, body_by_columns(): packed = lax.all_to_all(packed, ('grp', 'gy'), 0, 0)  8.15 us
    unnamed x18, local copies, waits for them, and re-layouts  3.92 us
    all_to_all x1, waiting for transfers between devices, body_by_columns(): windows = lax.all_to_all(windows, ('grp', 'gy'), 0, 0)  3.84 us
    all_to_all x1, starting transfers between devices, body_by_columns(): windows = lax.all_to_all(windows, ('grp', 'gy'), 0, 0)  3.54 us
    all_to_all x1, starting transfers between devices, body_by_columns(): copies = lax.all_to_all(copies, ('grp', 'gy', 'gx'), 0, 0)  3.34 us
  transfers between devices with their start and end apart: 2, of which 2 were waited for; matrix products, arithmetic and copies ran while one was open for 0% of the time, Pallas kernels for 14%

profile of v3, /device:TPU:0, one launch (start us, length us, event | category | flops | bytes accessed | tf_op | source)
XLA Modules:
  0.0 56.6 jit_solution(2589725818519535481)
XLA Ops:
  0.6 0.0 copy-start
  0.6 0.9 %copy-done = f32[19,2,8,128]{3,2,1,0:T(8,128)S(1)} copy-done((f32[19,2,8,128]{3,2,1,0:T(8,128)S(1)}, f32[19,2,8,128]{3,2,1,0:T(8,128)}, u32[]{:S(2)}) %copy-start) | copy-done | bytes 155672
  1.5 0.0 copy-start.2
  1.5 0.9 %copy-done.2 = f32[19,2,8,128]{3,2,1,0:T(8,128)S(1)} copy-done((f32[19,2,8,128]{3,2,1,0:T(8,128)S(1)}, f32[19,2,8,128]{3,2,1,0:T(8,128)}, u32[]{:S(2)}) %copy-start.2) | copy-done | bytes 155672
  2.5 0.0 copy-start.4
  2.5 0.7 %copy-done.4 = s32[2,8,128]{2,1,0:T(8,128)S(1)} copy-done((s32[2,8,128]{2,1,0:T(8,128)S(1)}, s32[2,8,128]{2,1,0:T(8,128)}, u32[]{:S(2)}) %copy-start.4) | copy-done | bytes 8216
  3.2 0.0 copy-start.6
  3.2 0.7 %copy-done.6 = s32[2,8,128]{2,1,0:T(8,128)S(1)} copy-done((s32[2,8,128]{2,1,0:T(8,128)S(1)}, s32[2,8,128]{2,1,0:T(8,128)}, u32[]{:S(2)}) %copy-start.6) | copy-done | bytes 8216
  3.9 0.0 copy-start.8
  3.9 0.7 %copy-done.8 = f32[2,8,128]{2,1,0:T(8,128)S(1)} copy-done((f32[2,8,128]{2,1,0:T(8,128)S(1)}, f32[2,8,128]{2,1,0:T(8,128)}, u32[]{:S(2)}) %copy-start.8) | copy-done | bytes 8216
  4.5 0.8 %edges.1 = (f32[32,2,8,128]{3,2,1,0:T(8,128)}, f32[4,3,2,8,128]{4,3,2,1,0:T(8,128)S(1)}) custom-call(f32[2,8,128]{2,1,0:T(8,128)S(1)} %copy-done.8, f32[19,2,8,128]{3,2,1,0:T(8,128)S(1)} %copy-done, f32[19,2,8,128]{3,2,1,0:T(8,128)S(1)} %copy-done.2, s32[2,8,128]{2,1,0:T(8,128)S(1)} %copy-done.4, s32[2,8,128]{2,1,0:T(8,128)S(1)} %copy-done.6), custom_call_target="tpu_custom_call" | custom-call | tf_op jit(solution)/shard_map/edges/pallas_call | solution.py:600
  5.4 11.9 %all_to_all.20.edges_ref = f32[4,3,2,8,128]{4,3,2,1,0:T(8,128)S(1)} all-to-all(f32[4,3,2,8,128]{4,3,2,1,0:T(8,128)S(1)} %get-tuple-element.9), channel_id=1, replica_groups=mesh['grp'=4,'gy'=2,'gx'=4] {'gx'}, dimensions={0} | all-to-all | bytes 196608 | tf_op jit(solution)/shard_map/all_to_all | solution.py:623
  17.3 0.0 copy-start.1
  17.3 0.0 copy-start.3
  17.3 0.0 copy-start.5
  17.3 0.0 copy-start.7
  17.4 3.3 %all-to-all-start = ((f32[32,2,8,128]{3,2,1,0:T(8,128)}), f32[32,2,8,128]{3,2,1,0:T(8,128)S(1)}, u32[]{:S(2)}, u32[]{:S(2)}) async-start(f32[32,2,8,128]{3,2,1,0:T(8,128)} %get-tuple-element.6), calls=%async_computation | async-start | bytes 524288 | tf_op jit(solution)/shard_map/all_to_all | solution.py:622
  20.7 0.0 copy-done.1
  20.7 0.0 copy-done.3
  20.7 0.0 copy-done.5
  20.7 0.0 copy-done.7
  20.7 1.8 %windows.1 = f32[8,10,2,8,128]{4,3,2,1,0:T(8,128)} custom-call(f32[19,2,8,128]{3,2,1,0:T(8,128)S(1)} %copy-done.1, f32[19,2,8,128]{3,2,1,0:T(8,128)S(1)} %copy-done.3, s32[2,8,128]{2,1,0:T(8,128)S(1)} %copy-done.5, s32[2,8,128]{2,1,0:T(8,128)S(1)} %copy-done.7, f32[4,3,2,8,128]{4,3,2,1,0:T(8,128)S(1)} %all_to_all.20.edges_ref), custom_call_target="tpu_custom_call" | custom-call | tf_op jit(solution)/shard_map/windows/pallas_call | solution.py:600
  22.5 9.0 %all-to-all-done.copies_ref = f32[32,2,8,128]{3,2,1,0:T(8,128)S(1)} async-done(((f32[32,2,8,128]{3,2,1,0:T(8,128)}), f32[32,2,8,128]{3,2,1,0:T(8,128)S(1)}, u32[]{:S(2)}, u32[]{:S(2)}) %all-to-all-start) | async-done | bytes 262176 | tf_op jit(solution)/shard_map/all_to_all | solution.py:622
  31.5 3.5 %all-to-all-start.2 = ((f32[8,10,2,8,128]{4,3,2,1,0:T(8,128)}), f32[8,10,2,8,128]{4,3,2,1,0:T(8,128)S(1)}, u32[]{:S(2)}, u32[]{:S(2)}) async-start(f32[8,10,2,8,128]{4,3,2,1,0:T(8,128)} %windows.1), calls=%async_computation.2 | async-start | bytes 1310720 | tf_op jit(solution)/shard_map/all_to_all | solution.py:627
  35.7 6.1 %level.1 = (f32[8,128]{1,0:T(8,128)S(1)}, f32[32,128]{1,0:T(8,128)S(1)}) custom-call(s32[1]{0:T(128)} %bitcast.1.step_ref, f32[32,2,8,128]{3,2,1,0:T(8,128)S(1)} %all-to-all-done.copies_ref), custom_call_target="tpu_custom_call" | custom-call | tf_op jit(solution)/shard_map/level/pallas_call | solution.py:600
  41.8 3.8 %all-to-all-done.2.windows_ref = f32[8,10,2,8,128]{4,3,2,1,0:T(8,128)S(1)} async-done(((f32[8,10,2,8,128]{4,3,2,1,0:T(8,128)}), f32[8,10,2,8,128]{4,3,2,1,0:T(8,128)S(1)}, u32[]{:S(2)}, u32[]{:S(2)}) %all-to-all-start.2) | async-done | bytes 655392 | tf_op jit(solution)/shard_map/all_to_all | solution.py:627
  45.6 1.8 %flow.1 = f32[8,3,2,8,128]{4,3,2,1,0:T(8,128)S(1)} custom-call(s32[1]{0:T(128)} %bitcast.2.step_ref, f32[8,128]{1,0:T(8,128)S(1)} %get-tuple-element.7.eta_ref, f32[32,128]{1,0:T(8,128)S(1)} %get-tuple-element.8.filtered_ref, f32[8,10,2,8,128]{4,3,2,1,0:T(8,128)S(1)} %all-to-all-done.2.windows_ref), custom_call_target="tpu_custom_call" | custom-call | tf_op jit(solution)/shard_map/flow/pallas_call | solution.py:600
  47.4 8.2 %all_to_all.21.packed_ref = f32[8,3,2,8,128]{4,3,2,1,0:T(8,128)S(1)} all-to-all(f32[8,3,2,8,128]{4,3,2,1,0:T(8,128)S(1)} %flow.1), channel_id=1, replica_groups=mesh['grp'=4,'gy'=2,'gx'=4] {'grp','gy'}, dimensions={0} | all-to-all | bytes 393216 | tf_op jit(solution)/shard_map/all_to_all | solution.py:653
  55.5 1.0 %result.1 = (f32[19,2,8,128]{3,2,1,0:T(8,128)}, f32[2,8,128]{2,1,0:T(8,128)}) custom-call(f32[8,3,2,8,128]{4,3,2,1,0:T(8,128)S(1)} %all_to_all.21.packed_ref), custom_call_target="tpu_custom_call" | custom-call | tf_op jit(solution)/shard_map/result/pallas_call | solution.py:600
Async XLA Ops:
  0.6 0.9 %copy-start = (f32[19,2,8,128]{3,2,1,0:T(8,128)S(1)}, f32[19,2,8,128]{3,2,1,0:T(8,128)}, u32[]{:S(2)}) copy-start(f32[19,2,8,128]{3,2,1,0:T(8,128)} %populations_ref.3) | copy-start | bytes 466948
  1.5 0.9 %copy-start.2 = (f32[19,2,8,128]{3,2,1,0:T(8,128)S(1)}, f32[19,2,8,128]{3,2,1,0:T(8,128)}, u32[]{:S(2)}) copy-start(f32[19,2,8,128]{3,2,1,0:T(8,128)} %cotangent_ref.3) | copy-start | bytes 466948
  2.5 0.7 %copy-start.4 = (s32[2,8,128]{2,1,0:T(8,128)S(1)}, s32[2,8,128]{2,1,0:T(8,128)}, u32[]{:S(2)}) copy-start(s32[2,8,128]{2,1,0:T(8,128)} %wall_ref.3) | copy-start | bytes 24580
  3.2 0.7 %copy-start.6 = (s32[2,8,128]{2,1,0:T(8,128)S(1)}, s32[2,8,128]{2,1,0:T(8,128)}, u32[]{:S(2)}) copy-start(s32[2,8,128]{2,1,0:T(8,128)} %inlet_ref.3) | copy-start | bytes 24580
  3.9 0.7 %copy-start.8 = (f32[2,8,128]{2,1,0:T(8,128)S(1)}, f32[2,8,128]{2,1,0:T(8,128)}, u32[]{:S(2)}) copy-start(f32[2,8,128]{2,1,0:T(8,128)} %design_ref.1) | copy-start | bytes 24580
  17.3 3.4 %copy-start.1 = (f32[19,2,8,128]{3,2,1,0:T(8,128)S(1)}, f32[19,2,8,128]{3,2,1,0:T(8,128)}, u32[]{:S(2)}) copy-start(f32[19,2,8,128]{3,2,1,0:T(8,128)} %populations_ref.3) | copy-start | bytes 466948
  17.3 3.4 %copy-start.3 = (f32[19,2,8,128]{3,2,1,0:T(8,128)S(1)}, f32[19,2,8,128]{3,2,1,0:T(8,128)}, u32[]{:S(2)}) copy-start(f32[19,2,8,128]{3,2,1,0:T(8,128)} %cotangent_ref.3) | copy-start | bytes 466948
  17.3 3.4 %copy-start.5 = (s32[2,8,128]{2,1,0:T(8,128)S(1)}, s32[2,8,128]{2,1,0:T(8,128)}, u32[]{:S(2)}) copy-start(s32[2,8,128]{2,1,0:T(8,128)} %wall_ref.3) | copy-start | bytes 24580
  17.3 3.4 %copy-start.7 = (s32[2,8,128]{2,1,0:T(8,128)S(1)}, s32[2,8,128]{2,1,0:T(8,128)}, u32[]{:S(2)}) copy-start(s32[2,8,128]{2,1,0:T(8,128)} %inlet_ref.3) | copy-start | bytes 24580
  17.4 14.1 %all-to-all-start = ((f32[32,2,8,128]{3,2,1,0:T(8,128)}), f32[32,2,8,128]{3,2,1,0:T(8,128)S(1)}, u32[]{:S(2)}, u32[]{:S(2)}) async-start(f32[32,2,8,128]{3,2,1,0:T(8,128)} %get-tuple-element.6), calls=%async_computation | async-start | bytes 524288 | tf_op jit(solution)/shard_map/all_to_all | solution.py:622
  31.5 14.1 %all-to-all-start.2 = ((f32[8,10,2,8,128]{4,3,2,1,0:T(8,128)}), f32[8,10,2,8,128]{4,3,2,1,0:T(8,128)S(1)}, u32[]{:S(2)}, u32[]{:S(2)}) async-start(f32[8,10,2,8,128]{4,3,2,1,0:T(8,128)} %windows.1), calls=%async_computation.2 | async-start | bytes 1310720 | tf_op jit(solution)/shard_map/all_to_all | solution.py:627

commit v4 on v3

--- a/solution.py
+++ b/solution.py
@@ -207,11 +207,11 @@
     return (popul, design_grad)
 
 
-HALO = 8
 LANES = 128
 AROUND = ((1, 0), (-1, 0), (0, 1), (0, -1), (1, 1), (-1, -1), (1, -1), (-1, 1))
 FIELDS = 40
 PACKED = 20
+CLOSE = 2.0**-20
 
 
 def rolled(value, amount):
@@ -223,71 +223,64 @@
     return lax.broadcasted_iota(jnp.int32, (8, LANES), 1)
 
 
-def merge(parts, width):
-    lanes = lane_index()
-    total = parts[0]
-    for index in range(1, len(parts)):
-        total = jnp.where(lanes >= index * width, parts[index], total)
-    return total
-
-
-def field(refs, index, layer):
-    populations_ref, cotangent_ref, wall_ref, inlet_ref = refs
-    if index < 19:
-        return populations_ref[index, layer]
-    if index < 38:
-        return cotangent_ref[index - 19, layer]
-    return (wall_ref if index == 38 else inlet_ref)[layer].astype(jnp.float32)
-
-
-def edge_kernel(design_ref, populations_ref, cotangent_ref, wall_ref, inlet_ref, copies_ref, edges_ref):
-    refs = (populations_ref, cotangent_ref, wall_ref, inlet_ref)
-    me = lax.axis_index("gx")
-    zero = jnp.zeros((8, LANES), jnp.float32)
-    for layer in range(design_ref.shape[0]):
+def mixed(values):
+    place = lane_index() // 16
+    for half in (4, 2, 1):
+        upper = (place & half) != 0
+        values = [jnp.where(upper, values[(index + half) % 8], values[index]) for index in range(8)]
+    return values
+
+
+def pack_kernel(
+    design_ref, populations_ref, cotangent_ref, wall_ref, inlet_ref, design_out_ref, packed_ref,
+    fields_ref, masks_ref, sems,
+):
+    moves = [
+        pltpu.make_async_copy(populations_ref, fields_ref.at[0:19], sems.at[0]),
+        pltpu.make_async_copy(cotangent_ref, fields_ref.at[19:38], sems.at[1]),
+        pltpu.make_async_copy(wall_ref, masks_ref.at[0], sems.at[2]),
+        pltpu.make_async_copy(inlet_ref, masks_ref.at[1], sems.at[3]),
+        pltpu.make_async_copy(design_ref, design_out_ref, sems.at[4]),
+    ]
+    for move in moves:
+        move.start()
+    for move in moves:
+        move.wait()
+    for layer in range(masks_ref.shape[1]):
+        for group in range(FIELDS // 8):
+            values = []
+            for slot in range(8):
+                index = group * 8 + slot
+                if index < 38:
+                    value = fields_ref[index, layer]
+                else:
+                    value = masks_ref[index - 38, layer].astype(jnp.float32)
+                values.append(rolled(value, 16 * slot))
+            values = mixed(values)
+            for device in range(8):
+                packed_ref[device, group, layer] = values[-device % 8]
+
+
+def arrange_kernel(size, splits, packed_ref, *refs):
+    design_refs, (body_ref, first_ref, last_ref, copies_ref) = refs[:size], refs[size:]
+    layers = packed_ref.shape[2]
+    planes = packed_ref.shape[0] // splits * layers
+    me = lax.axis_index("grp") * splits + lax.axis_index("gy")
+    for group in range(FIELDS // 8):
+        plane = gather_plane(
+            lambda z, part: packed_ref[(z // layers) * splits + part, group, z % layers], planes, splits
+        ).T
+        for slot in range(8):
+            index = group * 8 + lax.rem(slot + 8 - me, 8)
+            body_ref[index] = plane[16 * slot : 16 * slot + 16, :]
+            first_ref[index] = plane[16 * slot : 16 * slot + 8, :]
+            last_ref[index] = plane[16 * slot + 8 : 16 * slot + 16, :]
+    here = lax.axis_index("gx")
+    for turn in range(size):
+        index = lax.rem(here + size - turn, size)
+        value = design_refs[turn][...]
         for device in range(copies_ref.shape[0]):
-            copies_ref[device, layer] = design_ref[layer]
-        for group in range(edges_ref.shape[1]):
-            first, last = [], []
-            for slot in range(16):
-                index = group * 16 + slot
-                if index < FIELDS:
-                    value = field(refs, index, layer)
-                    first.append(rolled(value, 8 * slot))
-                    last.append(rolled(value, 8 * slot + HALO))
-                else:
-                    first.append(zero)
-                    last.append(zero)
-            first, last = merge(first, 8), merge(last, 8)
-            for device in range(edges_ref.shape[0]):
-                edges_ref[device, group, layer] = jnp.where(me > device, first, last)
-
-
-def window_kernel(populations_ref, cotangent_ref, wall_ref, inlet_ref, edges_ref, windows_ref):
-    refs = (populations_ref, cotangent_ref, wall_ref, inlet_ref)
-    me, size = lax.axis_index("gx"), edges_ref.shape[0]
-    before, after = jnp.maximum(me - 1, 0), jnp.minimum(me + 1, size - 1)
-    lanes = lane_index()
-    column = lanes % 32
-    devices = windows_ref.shape[0]
-    for layer in range(wall_ref.shape[0]):
-        for group in range(FIELDS // 4):
-            values = [field(refs, group * 4 + slot, layer) for slot in range(4)]
-            for device in range(devices):
-                start = 16 * device - HALO
-                window = merge([rolled(values[slot], 32 * slot - start) for slot in range(4)], 32)
-                if device in (0, devices - 1):
-                    source, offset = (before, 0) if device == 0 else (after, 24)
-                    known = (me > 0) if device == 0 else (me < size - 1)
-                    edge = edges_ref[source, group // 4, layer]
-                    place = (group % 4) * 4
-                    outer = merge(
-                        [rolled(edge, 32 * slot + offset - 8 * (place + slot)) for slot in range(4)], 32
-                    )
-                    outer = jnp.where(known, outer, 0.0)
-                    inside = (column >= HALO) if device == 0 else (column < 24)
-                    window = jnp.where(inside, window, outer)
-                windows_ref[device, group, layer] = window
+            copies_ref[device, index] = value
 
 
 def exponent(step_ref):
@@ -331,50 +324,68 @@
     return jnp.concatenate(blocks, axis=0)
 
 
-def level_kernel(rows, splits, size, step_ref, copies_ref, eta_ref, window_ref, design_ref, filtered_ref, raised_ref):
-    layers = copies_ref.shape[1]
+def volume_root(raised_ref, columns, beta):
+    zero = jnp.zeros((8, LANES), jnp.float32)
+    wanted = fluid_share * (columns * LANES)
+    top = jnp.exp(2.0 * beta)
+    scale = 1.0 / (top - 1.0)
+
+    def total(parts):
+        value = (parts[0] + parts[1]) + (parts[2] + parts[3])
+        return jnp.sum(jnp.sum(value, axis=0, keepdims=True), axis=1, keepdims=True)
+
+    def advance(state):
+        low, high, middle, _ = state
+        level = jnp.exp(2.0 * beta * middle)
+        sums, slopes = [zero] * 4, [zero] * 4
+        for index, row in enumerate(range(0, columns, 8)):
+            raised = raised_ref[row : row + 8, :]
+            part = 1.0 / (raised + level)
+            share = (raised - 1.0) * part
+            sums[index % 4] = sums[index % 4] + share
+            slopes[index % 4] = slopes[index % 4] + share * part
+        volume, slope = total(sums), total(slopes)
+        excess = volume * ((top + level) * scale) - wanted
+        slope = (2.0 * beta * level) * (volume - (top + level) * slope) * scale
+        low = jnp.where(excess > 0.0, middle, low)
+        high = jnp.where(excess > 0.0, high, middle)
+        guess = middle - excess / slope
+        taken = (guess >= low) & (guess <= high)
+        change = jnp.where(taken, jnp.abs(guess - middle), 1024.0 * (high - low))
+        return low, high, jnp.where(taken, guess, 0.5 * (low + high)), change
+
+    def going(carry):
+        step, state = carry
+        return (step < 64) & (jnp.max(state[3]) > CLOSE)
+
+    state = (zero, jnp.ones((8, LANES), jnp.float32), jnp.full((8, LANES), 0.5, jnp.float32), zero)
+    state = lax.fori_loop(0, 4, lambda step, state: advance(state), state)
+    step, state = lax.while_loop(going, lambda carry: (carry[0] + 1, advance(carry[1])), (4, state))
+    return state[2]
+
+
+def filtered_level(rows, splits, size, beta, copies_ref, design_ref, filtered_ref, raised_ref, masks):
+    layers = copies_ref.shape[2]
     planes = LANES // rows
     columns = size * LANES
-    masks = plane_masks(rows)
     zero = jnp.zeros((8, LANES), jnp.float32)
     for ref in (design_ref, filtered_ref):
         ref[0:8, :] = zero
         ref[columns + 8 : columns + 16, :] = zero
     for block in range(size):
         plane = gather_plane(
-            lambda z, part: copies_ref[((z // layers) * splits + part) * size + block, z % layers],
-            planes,
-            splits,
+            lambda z, part: copies_ref[(z // layers) * splits + part, block, z % layers], planes, splits
         )
         design_ref[8 + block * LANES : 8 + (block + 1) * LANES, :] = plane.T
     for row in range(8, columns + 8, 8):
         design_ref[row : row + 8, :] = plane_smooth(design_ref[row : row + 8, :], rows, masks)
-    beta = exponent(step_ref)
     for row in range(8, columns + 8, 8):
         value = 0.5 * design_ref[row : row + 8, :] + 0.25 * (
             design_ref[row - 1 : row + 7, :] + design_ref[row + 1 : row + 9, :]
         )
         filtered_ref[row : row + 8, :] = value
         raised_ref[row - 8 : row, :] = jnp.exp(2.0 * beta * value)
-    top = jnp.exp(2.0 * beta)
-
-    def halve(step, ends):
-        low, high = ends
-        middle = 0.5 * (low + high)
-        level = jnp.exp(2.0 * beta * middle)
-        totals = [zero] * 4
-        for index, row in enumerate(range(0, columns, 8)):
-            raised = raised_ref[row : row + 8, :]
-            totals[index % 4] = totals[index % 4] + (raised - 1.0) / (raised + level)
-        total = (totals[0] + totals[1]) + (totals[2] + totals[3])
-        volume = jnp.sum(jnp.sum(total, axis=0, keepdims=True), axis=1, keepdims=True)
-        above = volume * ((top + level) / (top - 1.0)) > fluid_share * (columns * LANES)
-        return jnp.where(above, middle, low), jnp.where(above, high, middle)
-
-    low, high = lax.fori_loop(0, BISECT, halve, (zero, jnp.ones((8, LANES), jnp.float32)))
-    eta_ref[...] = 0.5 * (low + high)
-    place = (lax.axis_index("gx") * lax.axis_size("grp") + lax.axis_index("grp")) * splits + lax.axis_index("gy")
-    window_ref[...] = filtered_ref[pl.ds(pl.multiple_of(place * 16, 8), 32), :]
+    return volume_root(raised_ref, columns, beta)
 
 
 def flow(rho, speed):
@@ -418,15 +429,19 @@
 
 
 def flow_kernel(
-    rows, splits, size, step_ref, eta_ref, filtered_ref, windows_ref, packed_ref,
-    input_ref, even_ref, odd_ref, kept_ref, share_ref, grad_ref, smooth_ref, output_ref,
+    rows, splits, size, step_ref, copies_ref, body_ref, before_ref, after_ref, packed_ref,
+    design_ref, filtered_ref, raised_ref,
+    cotangent_ref, even_ref, odd_ref, kept_ref, share_ref, grad_ref, smooth_ref, output_ref,
 ):
-    layers = windows_ref.shape[2]
+    layers = copies_ref.shape[2]
     planes = LANES // rows
     masks = plane_masks(rows)
     zero = jnp.zeros((8, LANES), jnp.float32)
-    place = (lax.axis_index("gx") * lax.axis_size("grp") + lax.axis_index("grp")) * splits + lax.axis_index("gy")
-    last = size * (planes // layers) * splits - 1
+    me = lax.axis_index("grp") * splits + lax.axis_index("gy")
+    place = lax.axis_index("gx") * copies_ref.shape[0] + me
+    last = size * copies_ref.shape[0] - 1
+    beta = exponent(step_ref)
+    eta = filtered_level(rows, splits, size, beta, copies_ref, design_ref, filtered_ref, raised_ref, masks)
 
     def inside(value, block):
         if block == 0:
@@ -435,26 +450,20 @@
             return jnp.where(place < last, value, 0.0)
         return value
 
-    input_ref[0:8, :] = zero
-    input_ref[FIELDS * 32 + 8 : FIELDS * 32 + 16, :] = zero
-    for group in range(FIELDS // 4):
-        plane = gather_plane(
-            lambda z, part: windows_ref[(z // layers) * splits + part, group, z % layers],
-            planes,
-            splits,
-        )
-        input_ref[8 + group * LANES : 8 + (group + 1) * LANES, :] = plane.T
-
     def initial(i, row):
-        return input_ref[8 + 32 * i + row : 16 + 32 * i + row, :]
-
-    beta = exponent(step_ref)
-    level = jnp.exp(2.0 * beta * eta_ref[...])
+        if row == 0:
+            return before_ref[i]
+        if row == 24:
+            return after_ref[i]
+        return body_ref[i, row - 8 : row, :]
+
+    level = jnp.exp(2.0 * beta * eta)
     top = jnp.exp(2.0 * beta)
     whole = (top + level) / (top - 1.0)
     for block in range(4):
         at = slice(8 * block, 8 * block + 8)
-        raised = jnp.exp(2.0 * beta * filtered_ref[at, :])
+        start = pl.multiple_of(place * 16 + 8 * block, 8)
+        raised = jnp.exp(2.0 * beta * filtered_ref[pl.ds(start, 8), :])
         part = 1.0 / (raised + level)
         density_hat = ((raised - 1.0) * part) * whole
         strength = alpha_most * penalty_shape
@@ -467,10 +476,13 @@
         )
         share_ref[1, at, :] = slope * factor
 
-    for ref in (even_ref, odd_ref):
+    for ref in (even_ref, odd_ref, cotangent_ref):
         for i in range(19):
             ref[i, 0:8, :] = zero
             ref[i, 40:48, :] = zero
+    for i in range(19):
+        for row in range(0, 32, 8):
+            cotangent_ref[i, row + 8 : row + 16, :] = initial(19 + i, row)
 
     def arrived(ref, i, row):
         cz, cy, cx = (int(c) for c in velocities[i])
@@ -503,21 +515,25 @@
                 post = (1.0 - relax_rate) * popul[i] + settled[i]
                 post = jnp.where(wall, popul[opposite[i]], jnp.where(inlet, inlet_value(i), post))
                 target[i, row + 8 : row + 16, :] = inside(post, block)
-    output_ref[16 * PACKED :, :] = jnp.zeros((3 * LANES - 16 * PACKED, LANES), jnp.float32)
+    def turned(index):
+        return (index // 8) * LANES + 16 * lax.rem(index + me, 8)
+
+    output_ref[16 * PACKED // LANES * LANES :, :] = jnp.zeros((LANES, LANES), jnp.float32)
     source = buffers[(STEPS - 1) % 2]
     for i in range(19):
         for row in (8, 16):
-            output_ref[16 * i + row - 8 : 16 * i + row, :] = arrived(source, i, row)
+            output_ref[pl.ds(pl.multiple_of(turned(i) + row - 8, 8), 8), :] = arrived(source, i, row)
 
     for step in reversed(range(STEPS)):
-        source, target = buffers[step % 2], buffers[(step + 1) % 2]
+        source = cotangent_ref if step == STEPS - 1 else buffers[step % 2]
+        target = buffers[(step + 1) % 2]
         for block in range(4):
             row = 8 * block
             at = slice(row, row + 8)
             back = []
             for i in range(19):
                 cz, cy, cx = (int(c) for c in velocities[i])
-                value = initial(19 + i, row + cx) if step == STEPS - 1 else source[i, row + 8 + cx : row + 16 + cx, :]
+                value = source[i, row + 8 + cx : row + 16 + cx, :]
                 back.append(plane_shift(value, -cz, -cy, rows, masks))
             wall = initial(38, row) > 0.0
             inlet = initial(39, row) > 0.0
@@ -566,7 +582,7 @@
         value = inside(grad_ref[at, :] * share_ref[1, at, :], block)
         smooth_ref[8 * block + 8 : 8 * block + 16, :] = plane_smooth(value, rows, masks)
     for row in (8, 16):
-        output_ref[16 * 19 + row - 8 : 16 * 19 + row, :] = 0.5 * smooth_ref[row + 8 : row + 16, :] + 0.25 * (
+        output_ref[pl.ds(pl.multiple_of(turned(19) + row - 8, 8), 8), :] = 0.5 * smooth_ref[row + 8 : row + 16, :] + 0.25 * (
             smooth_ref[row + 7 : row + 15, :] + smooth_ref[row + 9 : row + 17, :]
         )
     for group in range(packed_ref.shape[1]):
@@ -579,79 +595,87 @@
 
 def result_kernel(packed_ref, populations_ref, grad_ref):
     for layer in range(grad_ref.shape[0]):
-        for index in range(PACKED):
-            group, slot = divmod(index, 8)
-            value = merge(
-                [rolled(packed_ref[device, group, layer], 16 * (device - slot)) for device in range(packed_ref.shape[0])],
-                16,
-            )
-            if index < 19:
-                populations_ref[index, layer] = value
-            else:
-                grad_ref[layer] = value
-
-
-def in_vmem(kernel, outs, name, scalars=0, scratch=()):
+        for group in range(packed_ref.shape[1]):
+            values = mixed([packed_ref[device, group, layer] for device in range(8)])
+            for slot in range(min(8, PACKED - 8 * group)):
+                index, value = 8 * group + slot, rolled(values[-slot % 8], -16 * slot)
+                if index < 19:
+                    populations_ref[index, layer] = value
+                else:
+                    grad_ref[layer] = value
+
+
+def call(kernel, outs, name, operands, spaces, scratch=(), room=32):
     vmem = pl.BlockSpec(memory_space=pltpu.VMEM)
+    shapes = tuple(jax.ShapeDtypeStruct(shape, jnp.float32) for shape in outs)
     many = len(outs) > 1
-    shapes = tuple(jax.ShapeDtypeStruct(shape, jnp.float32) for shape in outs)
-
-    def call(*operands):
-        return pl.pallas_call(
-            kernel,
-            out_shape=shapes if many else shapes[0],
-            in_specs=[pl.BlockSpec(memory_space=pltpu.SMEM)] * scalars + [vmem] * (len(operands) - scalars),
-            out_specs=(vmem,) * len(outs) if many else vmem,
-            scratch_shapes=[pltpu.VMEM(shape, jnp.float32) for shape in scratch],
-            compiler_params=pltpu.CompilerParams(vmem_limit_bytes=40 * 2**20),
-            name=name,
-        )(*operands)
-
-    return call
+    return pl.pallas_call(
+        kernel,
+        out_shape=shapes if many else shapes[0],
+        in_specs=[pl.BlockSpec(memory_space=space) for space in spaces],
+        out_specs=(vmem,) * len(outs) if many else vmem,
+        scratch_shapes=list(scratch),
+        compiler_params=pltpu.CompilerParams(vmem_limit_bytes=room * 2**20),
+        name=name,
+    )(*operands)
 
 
 def body_by_columns(design, populations, cotangent, wall_mask, inlet_mask, beta_step):
     grp, splits, size = (lax.axis_size(axis) for axis in ("grp", "gy", "gx"))
     layers, height, width = design.shape
-    rows, plane = height * splits, (grp * splits)
-    step = beta_step.reshape(1)
+    rows, plane = height * splits, grp * splits
     tile = (layers, 8, LANES)
-    copies, edges = in_vmem(edge_kernel, ((plane * size, *tile), (size, 3, *tile)), "edges")(
-        design, populations, cotangent, wall_mask, inlet_mask
+    vmem, real = pltpu.VMEM, jnp.float32
+    design, packed = call(
+        pack_kernel,
+        (tile, (plane, FIELDS // 8, *tile)),
+        "pack",
+        (design, populations, cotangent, wall_mask, inlet_mask),
+        [pl.ANY] * 5,
+        [vmem((38, *tile), real), vmem((2, *tile), jnp.int32), pltpu.SemaphoreType.DMA((5,))],
+        60,
     )
-    copies = lax.all_to_all(copies, ("grp", "gy", "gx"), 0, 0)
-    edges = lax.all_to_all(edges, "gx", 0, 0)
-    windows = in_vmem(window_kernel, ((plane, FIELDS // 4, *tile),), "windows")(
-        populations, cotangent, wall_mask, inlet_mask, edges
+    packed = lax.all_to_all(packed, ("grp", "gy"), 0, 0)
+    designs = [design]
+    for turn in range(1, size):
+        designs.append(lax.ppermute(design, "gx", [(i, (i + turn) % size) for i in range(size)]))
+    body, first, last, copies = call(
+        functools.partial(arrange_kernel, size, splits),
+        ((FIELDS, 16, LANES), (FIELDS, 8, LANES), (FIELDS, 8, LANES), (plane, size, *tile)),
+        "arrange",
+        (packed, *designs),
+        [vmem] * (1 + size),
     )
-    windows = lax.all_to_all(windows, ("grp", "gy"), 0, 0)
+    copies = lax.all_to_all(copies, ("grp", "gy"), 0, 0)
+    order = [(i % plane) * size + i // plane for i in range(size * plane)]
+    up = list(zip(order[:-1], order[1:]))
+    line = ("grp", "gy", "gx")
+    before = lax.ppermute(last, line, up)
+    after = lax.ppermute(first, line, [(j, i) for i, j in up])
     columns = size * LANES
-    padded = (columns + 16, LANES)
-    eta, filtered = in_vmem(
-        functools.partial(level_kernel, rows, splits, size),
-        ((8, LANES), (32, LANES)),
-        "level",
-        1,
-        (padded, padded, (columns, LANES)),
-    )(step, copies)
-    packed = in_vmem(
+    shapes = [
+        (columns + 16, LANES),
+        (columns + 16, LANES),
+        (columns, LANES),
+        (19, 48, LANES),
+        (19, 48, LANES),
+        (19, 48, LANES),
+        (STEPS, 4, 32, LANES),
+        (2, 32, LANES),
+        (32, LANES),
+        (48, LANES),
+        (3 * LANES, LANES),
+    ]
+    packed = call(
         functools.partial(flow_kernel, rows, splits, size),
         ((plane, 3, *tile),),
         "flow",
-        1,
-        (
-            (FIELDS * 32 + 16, LANES),
-            (19, 48, LANES),
-            (19, 48, LANES),
-            (STEPS, 4, 32, LANES),
-            (2, 32, LANES),
-            (32, LANES),
-            (48, LANES),
-            (3 * LANES, LANES),
-        ),
-    )(step, eta, filtered, windows)
+        (beta_step.reshape(1), copies, body, before, after),
+        [pltpu.SMEM] + [vmem] * 4,
+        [vmem(shape, real) for shape in shapes],
+    )
     packed = lax.all_to_all(packed, ("grp", "gy"), 0, 0)
-    return in_vmem(result_kernel, (populations.shape, design.shape), "result")(packed)
+    return call(result_kernel, (populations.shape, design.shape), "result", (packed,), [vmem])
 
 
 def body(design, populations, cotangent, wall_mask, inlet_mask, beta_step):

time: 57.1 us -> 47.2 us (0.83)
  starting transfers between devices: 6.88 us -> 20.1 us
  blocking collectives: 20.1 us -> 8.15 us
  local copies, waits for them, and re-layouts: 3.92 us -> 0.01 us
  Pallas kernels: 11.5 us -> 7.8 us
  waiting for transfers between devices: 12.8 us -> 9.39 us
    all_to_all x2, waiting for transfers between devices: 12.8 us -> 0.01 us  [the longest x1 0.01 us: body_by_columns(): packed = lax.all_to_all(packed, ('grp', 'gy'), 0, 0)]
    all_to_all x1 -> x0, blocking collectives: 11.9 us -> none  [body_by_columns(): edges = lax.all_to_all(edges, 'gx', 0, 0)]
    ppermute x0 -> x5, starting transfers between devices: none -> 10.8 us  [the longest x3 5.57 us: body_by_columns(): lax.ppermute(design, 'gx', [(i, (i + turn) % size) for i in range(size)])]
    ppermute x0 -> x5, waiting for transfers between devices: none -> 9.39 us  [the longest x1 4.5 us: body_by_columns(): after = lax.ppermute(first, line, [(j, i) for i, j in up])]
    unnamed x18 -> x2, local copies, waits for them, and re-layouts: 3.92 us -> 0.01 us
    pallas_call x5 -> x4, Pallas kernels: 11.5 us -> 7.8 us  [call(): pl.pallas_call(kernel, out_shape=shapes if many else shapes[0], in_specs=...]
    all_to_all x2, starting transfers between devices: 6.88 us -> 9.33 us  [the longest x1 5.18 us: body_by_columns(): packed = lax.all_to_all(packed, ('grp', 'gy'), 0, 0)]
  transfers between devices with their start and end apart: 2 -> 7, of which waited for: 2 -> 4; matrix products, arithmetic and copies ran while one was open for 0% -> 0% of each run, Pallas kernels for 14% -> 0%
where the time goes in v4:
time: 47.2 us; the launch traced here: 46.8 us
  starting transfers between devices  20.1 us (43%)
  waiting for transfers between devices  9.39 us (20%)
  blocking collectives  8.15 us (17%)
  Pallas kernels  7.8 us (17%)
  between operations  1.32 us (3%)
    all_to_all x1, blocking collectives, body_by_columns(): packed = lax.all_to_all(packed, ('grp', 'gy'), 0, 0)  8.15 us
    pallas_call x4, Pallas kernels, call(): pl.pallas_call(kernel, out_shape=shapes if many else shapes[0], in_specs=...  7.8 us
    ppermute x3, starting transfers between devices, body_by_columns(): lax.ppermute(design, 'gx', [(i, (i + turn) % size) for i in range(size)])  5.57 us
    all_to_all x1, starting transfers between devices, body_by_columns(): packed = lax.all_to_all(packed, ('grp', 'gy'), 0, 0)  5.18 us
    ppermute x1, waiting for transfers between devices, body_by_columns(): after = lax.ppermute(first, line, [(j, i) for i, j in up])  4.5 us
    all_to_all x1, starting transfers between devices, body_by_columns(): copies = lax.all_to_all(copies, ('grp', 'gy'), 0, 0)  4.14 us
    ppermute x1, starting transfers between devices, body_by_columns(): before = lax.ppermute(last, line, up)  3.92 us
    ppermute x1, waiting for transfers between devices, body_by_columns(): before = lax.ppermute(last, line, up)  2.59 us
  transfers between devices with their start and end apart: 7, of which 4 were waited for; matrix products, arithmetic and copies ran while one was open for 0% of the time, Pallas kernels for 0%

profile of v4, /device:TPU:0, one launch (start us, length us, event | category | flops | bytes accessed | tf_op | source)
XLA Modules:
  0.0 46.8 jit_solution(3144262262622616487)
XLA Ops:
  0.6 1.9 %pack.1 = (f32[2,8,128]{2,1,0:T(8,128)}, f32[8,5,2,8,128]{4,3,2,1,0:T(8,128)}) custom-call(f32[2,8,128]{2,1,0:T(8,128)} %design_ref.1, f32[19,2,8,128]{3,2,1,0:T(8,128)} %populations_ref.1, f32[19,2,8,128]{3,2,1,0:T(8,128)} %cotangent_ref.1, s32[2,8,128]{2,1,0:T(8,128)} %wall_ref.1, s32[2,8,128]{2,1,0:T(8,128)} %inlet_ref.1), custom_call_target="tpu_custom_call" | custom-call | tf_op jit(solution)/shard_map/pack/pallas_call | solution.py:612
  2.5 0.0 copy-start
  2.6 5.2 %all-to-all-start = ((f32[8,5,2,8,128]{4,3,2,1,0:T(8,128)}), f32[8,5,2,8,128]{4,3,2,1,0:T(8,128)S(1)}, u32[]{:S(2)}, u32[]{:S(2)}) async-start(f32[8,5,2,8,128]{4,3,2,1,0:T(8,128)} %get-tuple-element.8), calls=%async_computation | async-start | bytes 655360 | tf_op jit(solution)/shard_map/all_to_all | solution.py:638
  7.7 0.0 copy-done
  7.7 1.6 %collective-permute-start = (f32[2,8,128]{2,1,0:T(8,128)S(1)}, f32[2,8,128]{2,1,0:T(8,128)S(1)}, u32[]{:S(2)}, u32[]{:S(2)}) collective-permute-start(f32[2,8,128]{2,1,0:T(8,128)S(1)} %copy-done), channel_id=1, source_target_pairs={{0,1},{1,2},{2,3},{3,0},{4,5},{5,6},{6,7},{7,4},{8,9},{9,10},{10,1... | collective-permute-start | bytes 24584 | tf_op jit(solution)/shard_map/ppermute | solution.py:641
  9.4 2.6 %collective-permute-start.1 = (f32[2,8,128]{2,1,0:T(8,128)S(1)}, f32[2,8,128]{2,1,0:T(8,128)S(1)}, u32[]{:S(2)}, u32[]{:S(2)}) collective-permute-start(f32[2,8,128]{2,1,0:T(8,128)S(1)} %copy-done), channel_id=1, source_target_pairs={{0,2},{1,3},{2,0},{3,1},{4,6},{5,7},{6,4},{7,5},{8,10},{9,11},{10,... | collective-permute-start | bytes 24584 | tf_op jit(solution)/shard_map/ppermute | solution.py:641
  12.0 1.3 %collective-permute-start.2 = (f32[2,8,128]{2,1,0:T(8,128)S(1)}, f32[2,8,128]{2,1,0:T(8,128)S(1)}, u32[]{:S(2)}, u32[]{:S(2)}) collective-permute-start(f32[2,8,128]{2,1,0:T(8,128)S(1)} %copy-done), channel_id=1, source_target_pairs={{0,3},{1,0},{2,1},{3,2},{4,7},{5,4},{6,5},{7,6},{8,11},{9,8},{10,9... | collective-permute-start | bytes 24584 | tf_op jit(solution)/shard_map/ppermute | solution.py:641
  13.3 0.0 collective-permute-done.refs_1_
  13.3 0.6 %collective-permute-done.1.refs_2_ = f32[2,8,128]{2,1,0:T(8,128)S(1)} collective-permute-done((f32[2,8,128]{2,1,0:T(8,128)S(1)}, f32[2,8,128]{2,1,0:T(8,128)S(1)}, u32[]{:S(2)}, u32[]{:S(2)}) %collective-permute-start.1) | collective-permute-done | bytes 8224 | tf_op jit(solution)/shard_map/ppermute | solution.py:641
  13.9 1.7 %collective-permute-done.2.refs_3_ = f32[2,8,128]{2,1,0:T(8,128)S(1)} collective-permute-done((f32[2,8,128]{2,1,0:T(8,128)S(1)}, f32[2,8,128]{2,1,0:T(8,128)S(1)}, u32[]{:S(2)}, u32[]{:S(2)}) %collective-permute-start.2) | collective-permute-done | bytes 8224 | tf_op jit(solution)/shard_map/ppermute | solution.py:641
  15.6 0.0 all-to-all-done.packed_ref
  15.6 0.8 %arrange.1 = (f32[40,16,128]{2,1,0:T(8,128)S(1)}, f32[40,8,128]{2,1,0:T(8,128)S(1)}, f32[40,8,128]{2,1,0:T(8,128)S(1)}, f32[8,4,2,8,128]{4,3,2,1,0:T(8,128)}) custom-call(f32[8,5,2,8,128]{4,3,2,1,0:T(8,128)S(1)} %all-to-all-done.packed_ref, f32[2,8,128]{2,1,0:T(8,128)S(1)} %copy-done, f32[2,8,128]{2,1,0:T(8,128)S(1)} %collective-permute-done.refs_1_, ...), custom_call_target="tpu_custom_call" | custom-call | tf_op jit(solution)/shard_map/arrange/pallas_call | solution.py:612
  16.4 4.1 %all-to-all-start.1 = ((f32[8,4,2,8,128]{4,3,2,1,0:T(8,128)}), f32[8,4,2,8,128]{4,3,2,1,0:T(8,128)S(1)}, u32[]{:S(2)}, u32[]{:S(2)}) async-start(f32[8,4,2,8,128]{4,3,2,1,0:T(8,128)} %get-tuple-element.10), calls=%async_computation.1 | async-start | bytes 524288 | tf_op jit(solution)/shard_map/all_to_all | solution.py:649
  20.6 3.9 %collective-permute-start.3 = (f32[40,8,128]{2,1,0:T(8,128)S(1)}, f32[40,8,128]{2,1,0:T(8,128)S(1)}, u32[]{:S(2)}, u32[]{:S(2)}) collective-permute-start(f32[40,8,128]{2,1,0:T(8,128)S(1)} %get-tuple-element.12), channel_id=1, source_target_pairs={{0,4},{4,8},{8,12},{12,16},{16,20},{20,24},{24,28},{28,1},{1,5},{5... | collective-permute-start | bytes 491528 | tf_op jit(solution)/shard_map/ppermute | solution.py:653
  24.5 1.3 %collective-permute-start.4 = (f32[40,8,128]{2,1,0:T(8,128)S(1)}, f32[40,8,128]{2,1,0:T(8,128)S(1)}, u32[]{:S(2)}, u32[]{:S(2)}) collective-permute-start(f32[40,8,128]{2,1,0:T(8,128)S(1)} %get-tuple-element.13), channel_id=1, source_target_pairs={{4,0},{8,4},{12,8},{16,12},{20,16},{24,20},{28,24},{1,28},{5,1},{9... | collective-permute-start | bytes 491528 | tf_op jit(solution)/shard_map/ppermute | solution.py:654
  26.5 2.6 %collective-permute-done.3.before_ref = f32[40,8,128]{2,1,0:T(8,128)S(1)} collective-permute-done((f32[40,8,128]{2,1,0:T(8,128)S(1)}, f32[40,8,128]{2,1,0:T(8,128)S(1)}, u32[]{:S(2)}, u32[]{:S(2)}) %collective-permute-start.3) | collective-permute-done | bytes 163872 | tf_op jit(solution)/shard_map/ppermute | solution.py:653
  29.0 4.5 %collective-permute-done.4.after_ref = f32[40,8,128]{2,1,0:T(8,128)S(1)} collective-permute-done((f32[40,8,128]{2,1,0:T(8,128)S(1)}, f32[40,8,128]{2,1,0:T(8,128)S(1)}, u32[]{:S(2)}, u32[]{:S(2)}) %collective-permute-start.4) | collective-permute-done | bytes 163872 | tf_op jit(solution)/shard_map/ppermute | solution.py:654
  33.5 0.0 all-to-all-done.1.copies_ref
  33.5 4.3 %flow.1 = f32[8,3,2,8,128]{4,3,2,1,0:T(8,128)S(1)} custom-call(s32[1]{0:T(128)} %bitcast.1.step_ref, f32[8,4,2,8,128]{4,3,2,1,0:T(8,128)S(1)} %all-to-all-done.1.copies_ref, f32[40,16,128]{2,1,0:T(8,128)S(1)} %get-tuple-element.11.body_ref, f32[40,8,128]{2,1,0:T(8,128)S(1)} %collective-permute-done.3.before_ref, ...), custom_call_target="tpu_custom_call" | custom-call | tf_op jit(solution)/shard_map/flow/pallas_call | solution.py:612
  37.8 8.2 %all_to_all.15.packed_ref = f32[8,3,2,8,128]{4,3,2,1,0:T(8,128)S(1)} all-to-all(f32[8,3,2,8,128]{4,3,2,1,0:T(8,128)S(1)} %flow.1), channel_id=1, replica_groups=mesh['grp'=4,'gy'=2,'gx'=4] {'grp','gy'}, dimensions={0} | all-to-all | bytes 393216 | tf_op jit(solution)/shard_map/all_to_all | solution.py:677
  46.0 0.8 %result.1 = (f32[19,2,8,128]{3,2,1,0:T(8,128)}, f32[2,8,128]{2,1,0:T(8,128)}) custom-call(f32[8,3,2,8,128]{4,3,2,1,0:T(8,128)S(1)} %all_to_all.15.packed_ref), custom_call_target="tpu_custom_call" | custom-call | tf_op jit(solution)/shard_map/result/pallas_call | solution.py:612
Async XLA Ops:
  2.5 5.2 %copy-start = (f32[2,8,128]{2,1,0:T(8,128)S(1)}, f32[2,8,128]{2,1,0:T(8,128)}, u32[]{:S(2)}) copy-start(f32[2,8,128]{2,1,0:T(8,128)} %get-tuple-element.9.refs_0_) | copy-start | bytes 24580
  2.6 13.1 %all-to-all-start = ((f32[8,5,2,8,128]{4,3,2,1,0:T(8,128)}), f32[8,5,2,8,128]{4,3,2,1,0:T(8,128)S(1)}, u32[]{:S(2)}, u32[]{:S(2)}) async-start(f32[8,5,2,8,128]{4,3,2,1,0:T(8,128)} %get-tuple-element.8), calls=%async_computation | async-start | bytes 655360 | tf_op jit(solution)/shard_map/all_to_all | solution.py:638
  7.7 5.6 %collective-permute-start = (f32[2,8,128]{2,1,0:T(8,128)S(1)}, f32[2,8,128]{2,1,0:T(8,128)S(1)}, u32[]{:S(2)}, u32[]{:S(2)}) collective-permute-start(f32[2,8,128]{2,1,0:T(8,128)S(1)} %copy-done), channel_id=1, source_target_pairs={{0,1},{1,2},{2,3},{3,0},{4,5},{5,6},{6,7},{7,4},{8,9},{9,10},{10,1... | collective-permute-start | bytes 24584 | tf_op jit(solution)/shard_map/ppermute | solution.py:641
  9.4 4.5 %collective-permute-start.1 = (f32[2,8,128]{2,1,0:T(8,128)S(1)}, f32[2,8,128]{2,1,0:T(8,128)S(1)}, u32[]{:S(2)}, u32[]{:S(2)}) collective-permute-start(f32[2,8,128]{2,1,0:T(8,128)S(1)} %copy-done), channel_id=1, source_target_pairs={{0,2},{1,3},{2,0},{3,1},{4,6},{5,7},{6,4},{7,5},{8,10},{9,11},{10,... | collective-permute-start | bytes 24584 | tf_op jit(solution)/shard_map/ppermute | solution.py:641
  12.0 3.7 %collective-permute-start.2 = (f32[2,8,128]{2,1,0:T(8,128)S(1)}, f32[2,8,128]{2,1,0:T(8,128)S(1)}, u32[]{:S(2)}, u32[]{:S(2)}) collective-permute-start(f32[2,8,128]{2,1,0:T(8,128)S(1)} %copy-done), channel_id=1, source_target_pairs={{0,3},{1,0},{2,1},{3,2},{4,7},{5,4},{6,5},{7,6},{8,11},{9,8},{10,9... | collective-permute-start | bytes 24584 | tf_op jit(solution)/shard_map/ppermute | solution.py:641
  16.4 17.1 %all-to-all-start.1 = ((f32[8,4,2,8,128]{4,3,2,1,0:T(8,128)}), f32[8,4,2,8,128]{4,3,2,1,0:T(8,128)S(1)}, u32[]{:S(2)}, u32[]{:S(2)}) async-start(f32[8,4,2,8,128]{4,3,2,1,0:T(8,128)} %get-tuple-element.10), calls=%async_computation.1 | async-start | bytes 524288 | tf_op jit(solution)/shard_map/all_to_all | solution.py:649
  20.6 8.5 %collective-permute-start.3 = (f32[40,8,128]{2,1,0:T(8,128)S(1)}, f32[40,8,128]{2,1,0:T(8,128)S(1)}, u32[]{:S(2)}, u32[]{:S(2)}) collective-permute-start(f32[40,8,128]{2,1,0:T(8,128)S(1)} %get-tuple-element.12), channel_id=1, source_target_pairs={{0,4},{4,8},{8,12},{12,16},{16,20},{20,24},{24,28},{28,1},{1,5},{5... | collective-permute-start | bytes 491528 | tf_op jit(solution)/shard_map/ppermute | solution.py:653
  24.5 9.0 %collective-permute-start.4 = (f32[40,8,128]{2,1,0:T(8,128)S(1)}, f32[40,8,128]{2,1,0:T(8,128)S(1)}, u32[]{:S(2)}, u32[]{:S(2)}) collective-permute-start(f32[40,8,128]{2,1,0:T(8,128)S(1)} %get-tuple-element.13), channel_id=1, source_target_pairs={{4,0},{8,4},{12,8},{16,12},{20,16},{24,20},{28,24},{1,28},{5,1},{9... | collective-permute-start | bytes 491528 | tf_op jit(solution)/shard_map/ppermute | solution.py:654

commit v5 on v4

--- a/solution.py
+++ b/solution.py
@@ -223,6 +223,22 @@
     return lax.broadcasted_iota(jnp.int32, (8, LANES), 1)
 
 
+def on_path(index, grp, splits):
+    part, step = index // grp, index % grp
+    return (step if part % 2 == 0 else grp - 1 - step) * splits + part
+
+
+def device_at(index, grp, splits):
+    odd = lax.rem(lax.axis_index("gx"), 2)
+    return jnp.where(odd == 0, on_path(index, grp, splits), on_path(grp * splits - 1 - index, grp, splits))
+
+
+def block_here(grp, splits):
+    step, part = lax.axis_index("grp"), lax.axis_index("gy")
+    index = part * grp + jnp.where(lax.rem(part, 2) == 0, step, grp - 1 - step)
+    return jnp.where(lax.rem(lax.axis_index("gx"), 2) == 0, index, grp * splits - 1 - index)
+
+
 def mixed(values):
     place = lane_index() // 16
     for half in (4, 2, 1):
@@ -232,7 +248,7 @@
 
 
 def pack_kernel(
-    design_ref, populations_ref, cotangent_ref, wall_ref, inlet_ref, design_out_ref, packed_ref,
+    splits, design_ref, populations_ref, cotangent_ref, wall_ref, inlet_ref, design_out_ref, packed_ref,
     fields_ref, masks_ref, sems,
 ):
     moves = [
@@ -246,6 +262,7 @@
         move.start()
     for move in moves:
         move.wait()
+    devices = [device_at(index, 8 // splits, splits) for index in range(8)]
     for layer in range(masks_ref.shape[1]):
         for group in range(FIELDS // 8):
             values = []
@@ -257,15 +274,15 @@
                     value = masks_ref[index - 38, layer].astype(jnp.float32)
                 values.append(rolled(value, 16 * slot))
             values = mixed(values)
-            for device in range(8):
-                packed_ref[device, group, layer] = values[-device % 8]
+            for index in range(8):
+                packed_ref[devices[index], group, layer] = values[-index % 8]
 
 
 def arrange_kernel(size, splits, packed_ref, *refs):
     design_refs, (body_ref, first_ref, last_ref, copies_ref) = refs[:size], refs[size:]
     layers = packed_ref.shape[2]
     planes = packed_ref.shape[0] // splits * layers
-    me = lax.axis_index("grp") * splits + lax.axis_index("gy")
+    me = block_here(packed_ref.shape[0] // splits, splits)
     for group in range(FIELDS // 8):
         plane = gather_plane(
             lambda z, part: packed_ref[(z // layers) * splits + part, group, z % layers], planes, splits
@@ -437,7 +454,7 @@
     planes = LANES // rows
     masks = plane_masks(rows)
     zero = jnp.zeros((8, LANES), jnp.float32)
-    me = lax.axis_index("grp") * splits + lax.axis_index("gy")
+    me = block_here(copies_ref.shape[0] // splits, splits)
     place = lax.axis_index("gx") * copies_ref.shape[0] + me
     last = size * copies_ref.shape[0] - 1
     beta = exponent(step_ref)
@@ -593,10 +610,11 @@
                 packed_ref[(z // layers) * splits + part, group, z % layers] = plane[at : at + 8, :]
 
 
-def result_kernel(packed_ref, populations_ref, grad_ref):
+def result_kernel(splits, packed_ref, populations_ref, grad_ref):
+    devices = [device_at(index, 8 // splits, splits) for index in range(8)]
     for layer in range(grad_ref.shape[0]):
         for group in range(packed_ref.shape[1]):
-            values = mixed([packed_ref[device, group, layer] for device in range(8)])
+            values = mixed([packed_ref[device, group, layer] for device in devices])
             for slot in range(min(8, PACKED - 8 * group)):
                 index, value = 8 * group + slot, rolled(values[-slot % 8], -16 * slot)
                 if index < 19:
@@ -627,7 +645,7 @@
     tile = (layers, 8, LANES)
     vmem, real = pltpu.VMEM, jnp.float32
     design, packed = call(
-        pack_kernel,
+        functools.partial(pack_kernel, splits),
         (tile, (plane, FIELDS // 8, *tile)),
         "pack",
         (design, populations, cotangent, wall_mask, inlet_mask),
@@ -647,7 +665,8 @@
         [vmem] * (1 + size),
     )
     copies = lax.all_to_all(copies, ("grp", "gy"), 0, 0)
-    order = [(i % plane) * size + i // plane for i in range(size * plane)]
+    path = [on_path(index, grp, splits) for index in range(plane)]
+    order = [(path if gx % 2 == 0 else path[::-1])[index] * size + gx for gx in range(size) for index in range(plane)]
     up = list(zip(order[:-1], order[1:]))
     line = ("grp", "gy", "gx")
     before = lax.ppermute(last, line, up)
@@ -675,7 +694,7 @@
         [vmem(shape, real) for shape in shapes],
     )
     packed = lax.all_to_all(packed, ("grp", "gy"), 0, 0)
-    return call(result_kernel, (populations.shape, design.shape), "result", (packed,), [vmem])
+    return call(functools.partial(result_kernel, splits), (populations.shape, design.shape), "result", (packed,), [vmem])
 
 
 def body(design, populations, cotangent, wall_mask, inlet_mask, beta_step):

time: 47.2 us -> 44.7 us (0.947)
  waiting for transfers between devices: 9.39 us -> 4.77 us
  blocking collectives: 8.15 us -> 11.8 us
  starting transfers between devices: 20.1 us -> 18.6 us
    all_to_all x1, blocking collectives: 8.15 us -> 11.8 us  [body_by_columns(): packed = lax.all_to_all(packed, ('grp', 'gy'), 0, 0)]
    ppermute x1, waiting for transfers between devices: 2.59 us -> 0.01 us  [body_by_columns(): before = lax.ppermute(last, line, up)]
    ppermute x1, waiting for transfers between devices: 4.5 us -> 2.46 us  [body_by_columns(): after = lax.ppermute(first, line, [(j, i) for i, j in up])]
    ppermute x1, starting transfers between devices: 3.92 us -> 2.41 us  [body_by_columns(): before = lax.ppermute(last, line, up)]
  transfers between devices with their start and end apart: 7 -> 7, of which waited for: 4 -> 3; matrix products, arithmetic and copies ran while one was open for 0% -> 0% of each run, Pallas kernels for 0% -> 0%
where the time goes in v5:
time: 44.7 us; the launch traced here: 44.3 us
  starting transfers between devices  18.6 us (42%)
  blocking collectives  11.8 us (26%)
  Pallas kernels  7.8 us (17%)
  waiting for transfers between devices  4.77 us (11%)
  between operations  1.33 us (3%)
    all_to_all x1, blocking collectives, body_by_columns(): packed = lax.all_to_all(packed, ('grp', 'gy'), 0, 0)  11.8 us
    pallas_call x4, Pallas kernels, call(): pl.pallas_call(kernel, out_shape=shapes if many else shapes[0], in_specs=...  7.8 us
    ppermute x3, starting transfers between devices, body_by_columns(): lax.ppermute(design, 'gx', [(i, (i + turn) % size) for i in range(size)])  5.57 us
    all_to_all x1, starting transfers between devices, body_by_columns(): packed = lax.all_to_all(packed, ('grp', 'gy'), 0, 0)  5.18 us
    all_to_all x1, starting transfers between devices, body_by_columns(): copies = lax.all_to_all(copies, ('grp', 'gy'), 0, 0)  4.14 us
    ppermute x1, waiting for transfers between devices, body_by_columns(): after = lax.ppermute(first, line, [(j, i) for i, j in up])  2.46 us
    ppermute x1, starting transfers between devices, body_by_columns(): before = lax.ppermute(last, line, up)  2.41 us
    ppermute x3, waiting for transfers between devices, body_by_columns(): lax.ppermute(design, 'gx', [(i, (i + turn) % size) for i in range(size)])  2.3 us
  transfers between devices with their start and end apart: 7, of which 3 were waited for; matrix products, arithmetic and copies ran while one was open for 0% of the time, Pallas kernels for 0%

profile of v5, /device:TPU:0, one launch (start us, length us, event | category | flops | bytes accessed | tf_op | source)
XLA Modules:
  0.0 44.3 jit_solution(16305694152940990194)
XLA Ops:
  0.6 1.9 %pack.1 = (f32[2,8,128]{2,1,0:T(8,128)}, f32[8,5,2,8,128]{4,3,2,1,0:T(8,128)}) custom-call(f32[2,8,128]{2,1,0:T(8,128)} %design_ref.1, f32[19,2,8,128]{3,2,1,0:T(8,128)} %populations_ref.1, f32[19,2,8,128]{3,2,1,0:T(8,128)} %cotangent_ref.1, s32[2,8,128]{2,1,0:T(8,128)} %wall_ref.1, s32[2,8,128]{2,1,0:T(8,128)} %inlet_ref.1), custom_call_target="tpu_custom_call" | custom-call | tf_op jit(solution)/shard_map/pack/pallas_call | solution.py:630
  2.5 0.0 copy-start
  2.6 5.2 %all-to-all-start = ((f32[8,5,2,8,128]{4,3,2,1,0:T(8,128)}), f32[8,5,2,8,128]{4,3,2,1,0:T(8,128)S(1)}, u32[]{:S(2)}, u32[]{:S(2)}) async-start(f32[8,5,2,8,128]{4,3,2,1,0:T(8,128)} %get-tuple-element.8), calls=%async_computation | async-start | bytes 655360 | tf_op jit(solution)/shard_map/all_to_all | solution.py:656
  7.7 0.0 copy-done
  7.7 1.6 %collective-permute-start = (f32[2,8,128]{2,1,0:T(8,128)S(1)}, f32[2,8,128]{2,1,0:T(8,128)S(1)}, u32[]{:S(2)}, u32[]{:S(2)}) collective-permute-start(f32[2,8,128]{2,1,0:T(8,128)S(1)} %copy-done), channel_id=1, source_target_pairs={{0,1},{1,2},{2,3},{3,0},{4,5},{5,6},{6,7},{7,4},{8,9},{9,10},{10,1... | collective-permute-start | bytes 24584 | tf_op jit(solution)/shard_map/ppermute | solution.py:659
  9.4 2.6 %collective-permute-start.1 = (f32[2,8,128]{2,1,0:T(8,128)S(1)}, f32[2,8,128]{2,1,0:T(8,128)S(1)}, u32[]{:S(2)}, u32[]{:S(2)}) collective-permute-start(f32[2,8,128]{2,1,0:T(8,128)S(1)} %copy-done), channel_id=1, source_target_pairs={{0,2},{1,3},{2,0},{3,1},{4,6},{5,7},{6,4},{7,5},{8,10},{9,11},{10,... | collective-permute-start | bytes 24584 | tf_op jit(solution)/shard_map/ppermute | solution.py:659
  12.0 1.3 %collective-permute-start.2 = (f32[2,8,128]{2,1,0:T(8,128)S(1)}, f32[2,8,128]{2,1,0:T(8,128)S(1)}, u32[]{:S(2)}, u32[]{:S(2)}) collective-permute-start(f32[2,8,128]{2,1,0:T(8,128)S(1)} %copy-done), channel_id=1, source_target_pairs={{0,3},{1,0},{2,1},{3,2},{4,7},{5,4},{6,5},{7,6},{8,11},{9,8},{10,9... | collective-permute-start | bytes 24584 | tf_op jit(solution)/shard_map/ppermute | solution.py:659
  13.3 0.0 collective-permute-done.refs_1_
  13.3 0.6 %collective-permute-done.1.refs_2_ = f32[2,8,128]{2,1,0:T(8,128)S(1)} collective-permute-done((f32[2,8,128]{2,1,0:T(8,128)S(1)}, f32[2,8,128]{2,1,0:T(8,128)S(1)}, u32[]{:S(2)}, u32[]{:S(2)}) %collective-permute-start.1) | collective-permute-done | bytes 8224 | tf_op jit(solution)/shard_map/ppermute | solution.py:659
  13.9 1.7 %collective-permute-done.2.refs_3_ = f32[2,8,128]{2,1,0:T(8,128)S(1)} collective-permute-done((f32[2,8,128]{2,1,0:T(8,128)S(1)}, f32[2,8,128]{2,1,0:T(8,128)S(1)}, u32[]{:S(2)}, u32[]{:S(2)}) %collective-permute-start.2) | collective-permute-done | bytes 8224 | tf_op jit(solution)/shard_map/ppermute | solution.py:659
  15.6 0.0 all-to-all-done.packed_ref
  15.6 0.8 %arrange.1 = (f32[40,16,128]{2,1,0:T(8,128)S(1)}, f32[40,8,128]{2,1,0:T(8,128)S(1)}, f32[40,8,128]{2,1,0:T(8,128)S(1)}, f32[8,4,2,8,128]{4,3,2,1,0:T(8,128)}) custom-call(f32[8,5,2,8,128]{4,3,2,1,0:T(8,128)S(1)} %all-to-all-done.packed_ref, f32[2,8,128]{2,1,0:T(8,128)S(1)} %copy-done, f32[2,8,128]{2,1,0:T(8,128)S(1)} %collective-permute-done.refs_1_, ...), custom_call_target="tpu_custom_call" | custom-call | tf_op jit(solution)/shard_map/arrange/pallas_call | solution.py:630
  16.4 4.1 %all-to-all-start.1 = ((f32[8,4,2,8,128]{4,3,2,1,0:T(8,128)}), f32[8,4,2,8,128]{4,3,2,1,0:T(8,128)S(1)}, u32[]{:S(2)}, u32[]{:S(2)}) async-start(f32[8,4,2,8,128]{4,3,2,1,0:T(8,128)} %get-tuple-element.10), calls=%async_computation.1 | async-start | bytes 524288 | tf_op jit(solution)/shard_map/all_to_all | solution.py:667
  20.6 2.4 %collective-permute-start.3 = (f32[40,8,128]{2,1,0:T(8,128)S(1)}, f32[40,8,128]{2,1,0:T(8,128)S(1)}, u32[]{:S(2)}, u32[]{:S(2)}) collective-permute-start(f32[40,8,128]{2,1,0:T(8,128)S(1)} %get-tuple-element.12), channel_id=1, source_target_pairs={{0,8},{8,16},{16,24},{24,28},{28,20},{20,12},{12,4},{4,5},{5,13},{... | collective-permute-start | bytes 491528 | tf_op jit(solution)/shard_map/ppermute | solution.py:672
  23.0 1.3 %collective-permute-start.4 = (f32[40,8,128]{2,1,0:T(8,128)S(1)}, f32[40,8,128]{2,1,0:T(8,128)S(1)}, u32[]{:S(2)}, u32[]{:S(2)}) collective-permute-start(f32[40,8,128]{2,1,0:T(8,128)S(1)} %get-tuple-element.13), channel_id=1, source_target_pairs={{8,0},{16,8},{24,16},{28,24},{20,28},{12,20},{4,12},{5,4},{13,5},{... | collective-permute-start | bytes 491528 | tf_op jit(solution)/shard_map/ppermute | solution.py:673
  24.9 0.0 collective-permute-done.3.before_ref
  25.0 2.5 %collective-permute-done.4.after_ref = f32[40,8,128]{2,1,0:T(8,128)S(1)} collective-permute-done((f32[40,8,128]{2,1,0:T(8,128)S(1)}, f32[40,8,128]{2,1,0:T(8,128)S(1)}, u32[]{:S(2)}, u32[]{:S(2)}) %collective-permute-start.4) | collective-permute-done | bytes 163872 | tf_op jit(solution)/shard_map/ppermute | solution.py:673
  27.4 0.0 all-to-all-done.1.copies_ref
  27.4 4.3 %flow.1 = f32[8,3,2,8,128]{4,3,2,1,0:T(8,128)S(1)} custom-call(s32[1]{0:T(128)} %bitcast.1.step_ref, f32[8,4,2,8,128]{4,3,2,1,0:T(8,128)S(1)} %all-to-all-done.1.copies_ref, f32[40,16,128]{2,1,0:T(8,128)S(1)} %get-tuple-element.11.body_ref, f32[40,8,128]{2,1,0:T(8,128)S(1)} %collective-permute-done.3.before_ref, ...), custom_call_target="tpu_custom_call" | custom-call | tf_op jit(solution)/shard_map/flow/pallas_call | solution.py:630
  31.7 11.8 %all_to_all.15.packed_ref = f32[8,3,2,8,128]{4,3,2,1,0:T(8,128)S(1)} all-to-all(f32[8,3,2,8,128]{4,3,2,1,0:T(8,128)S(1)} %flow.1), channel_id=1, replica_groups=mesh['grp'=4,'gy'=2,'gx'=4] {'grp','gy'}, dimensions={0} | all-to-all | bytes 393216 | tf_op jit(solution)/shard_map/all_to_all | solution.py:696
  43.5 0.8 %result.1 = (f32[19,2,8,128]{3,2,1,0:T(8,128)}, f32[2,8,128]{2,1,0:T(8,128)}) custom-call(f32[8,3,2,8,128]{4,3,2,1,0:T(8,128)S(1)} %all_to_all.15.packed_ref), custom_call_target="tpu_custom_call" | custom-call | tf_op jit(solution)/shard_map/result/pallas_call | solution.py:630
Async XLA Ops:
  2.5 5.2 %copy-start = (f32[2,8,128]{2,1,0:T(8,128)S(1)}, f32[2,8,128]{2,1,0:T(8,128)}, u32[]{:S(2)}) copy-start(f32[2,8,128]{2,1,0:T(8,128)} %get-tuple-element.9.refs_0_) | copy-start | bytes 24580
  2.6 13.1 %all-to-all-start = ((f32[8,5,2,8,128]{4,3,2,1,0:T(8,128)}), f32[8,5,2,8,128]{4,3,2,1,0:T(8,128)S(1)}, u32[]{:S(2)}, u32[]{:S(2)}) async-start(f32[8,5,2,8,128]{4,3,2,1,0:T(8,128)} %get-tuple-element.8), calls=%async_computation | async-start | bytes 655360 | tf_op jit(solution)/shard_map/all_to_all | solution.py:656
  7.7 5.6 %collective-permute-start = (f32[2,8,128]{2,1,0:T(8,128)S(1)}, f32[2,8,128]{2,1,0:T(8,128)S(1)}, u32[]{:S(2)}, u32[]{:S(2)}) collective-permute-start(f32[2,8,128]{2,1,0:T(8,128)S(1)} %copy-done), channel_id=1, source_target_pairs={{0,1},{1,2},{2,3},{3,0},{4,5},{5,6},{6,7},{7,4},{8,9},{9,10},{10,1... | collective-permute-start | bytes 24584 | tf_op jit(solution)/shard_map/ppermute | solution.py:659
  9.4 4.5 %collective-permute-start.1 = (f32[2,8,128]{2,1,0:T(8,128)S(1)}, f32[2,8,128]{2,1,0:T(8,128)S(1)}, u32[]{:S(2)}, u32[]{:S(2)}) collective-permute-start(f32[2,8,128]{2,1,0:T(8,128)S(1)} %copy-done), channel_id=1, source_target_pairs={{0,2},{1,3},{2,0},{3,1},{4,6},{5,7},{6,4},{7,5},{8,10},{9,11},{10,... | collective-permute-start | bytes 24584 | tf_op jit(solution)/shard_map/ppermute | solution.py:659
  12.0 3.7 %collective-permute-start.2 = (f32[2,8,128]{2,1,0:T(8,128)S(1)}, f32[2,8,128]{2,1,0:T(8,128)S(1)}, u32[]{:S(2)}, u32[]{:S(2)}) collective-permute-start(f32[2,8,128]{2,1,0:T(8,128)S(1)} %copy-done), channel_id=1, source_target_pairs={{0,3},{1,0},{2,1},{3,2},{4,7},{5,4},{6,5},{7,6},{8,11},{9,8},{10,9... | collective-permute-start | bytes 24584 | tf_op jit(solution)/shard_map/ppermute | solution.py:659
  16.4 11.0 %all-to-all-start.1 = ((f32[8,4,2,8,128]{4,3,2,1,0:T(8,128)}), f32[8,4,2,8,128]{4,3,2,1,0:T(8,128)S(1)}, u32[]{:S(2)}, u32[]{:S(2)}) async-start(f32[8,4,2,8,128]{4,3,2,1,0:T(8,128)} %get-tuple-element.10), calls=%async_computation.1 | async-start | bytes 524288 | tf_op jit(solution)/shard_map/all_to_all | solution.py:667
  20.6 4.4 %collective-permute-start.3 = (f32[40,8,128]{2,1,0:T(8,128)S(1)}, f32[40,8,128]{2,1,0:T(8,128)S(1)}, u32[]{:S(2)}, u32[]{:S(2)}) collective-permute-start(f32[40,8,128]{2,1,0:T(8,128)S(1)} %get-tuple-element.12), channel_id=1, source_target_pairs={{0,8},{8,16},{16,24},{24,28},{28,20},{20,12},{12,4},{4,5},{5,13},{... | collective-permute-start | bytes 491528 | tf_op jit(solution)/shard_map/ppermute | solution.py:672
  23.0 4.4 %collective-permute-start.4 = (f32[40,8,128]{2,1,0:T(8,128)S(1)}, f32[40,8,128]{2,1,0:T(8,128)S(1)}, u32[]{:S(2)}, u32[]{:S(2)}) collective-permute-start(f32[40,8,128]{2,1,0:T(8,128)S(1)} %get-tuple-element.13), channel_id=1, source_target_pairs={{8,0},{16,8},{24,16},{28,24},{20,28},{12,20},{4,12},{5,4},{13,5},{... | collective-permute-start | bytes 491528 | tf_op jit(solution)/shard_map/ppermute | solution.py:673

commit v6 on v5

--- a/solution.py
+++ b/solution.py
@@ -210,8 +210,7 @@
 LANES = 128
 AROUND = ((1, 0), (-1, 0), (0, 1), (0, -1), (1, 1), (-1, -1), (1, -1), (-1, 1))
 FIELDS = 40
-PACKED = 20
-CLOSE = 2.0**-20
+CLOSE = 2.0**-14
 
 
 def rolled(value, amount):
@@ -279,7 +278,7 @@
 
 
 def arrange_kernel(size, splits, packed_ref, *refs):
-    design_refs, (body_ref, first_ref, last_ref, copies_ref) = refs[:size], refs[size:]
+    design_refs, (body_ref, first_ref, last_ref, copies_ref, design_ref) = refs[:size], refs[size:]
     layers = packed_ref.shape[2]
     planes = packed_ref.shape[0] // splits * layers
     me = block_here(packed_ref.shape[0] // splits, splits)
@@ -294,10 +293,20 @@
             last_ref[index] = plane[16 * slot + 8 : 16 * slot + 16, :]
     here = lax.axis_index("gx")
     for turn in range(size):
-        index = lax.rem(here + size - turn, size)
-        value = design_refs[turn][...]
-        for device in range(copies_ref.shape[0]):
-            copies_ref[device, index] = value
+        design_ref[lax.rem(here + size - turn, size)] = design_refs[turn][...]
+    lanes = lane_index()
+    zero = jnp.zeros((8, LANES), jnp.float32)
+    for layer in range(layers):
+        tiles = [zero] + [design_ref[index, layer] for index in range(size)] + [zero]
+        ahead = [rolled(tile, 1) for tile in tiles]
+        behind = [rolled(tile, -1) for tile in tiles]
+        for index in range(1, size + 1):
+            value = 0.5 * tiles[index] + 0.25 * (
+                jnp.where(lanes == 0, ahead[index - 1], ahead[index])
+                + jnp.where(lanes == LANES - 1, behind[index + 1], behind[index])
+            )
+            for device in range(copies_ref.shape[0]):
+                copies_ref[device, index - 1, layer] = value
 
 
 def exponent(step_ref):
@@ -343,7 +352,8 @@
 
 def volume_root(raised_ref, columns, beta):
     zero = jnp.zeros((8, LANES), jnp.float32)
-    wanted = fluid_share * (columns * LANES)
+    one = jnp.ones((8, LANES), jnp.float32)
+    cells = columns * LANES
     top = jnp.exp(2.0 * beta)
     scale = 1.0 / (top - 1.0)
 
@@ -352,57 +362,81 @@
         return jnp.sum(jnp.sum(value, axis=0, keepdims=True), axis=1, keepdims=True)
 
     def advance(state):
-        low, high, middle, _ = state
+        low, high, low_known, high_known, middle, _ = state
         level = jnp.exp(2.0 * beta * middle)
-        sums, slopes = [zero] * 4, [zero] * 4
+        sums, squares = [zero] * 4, [zero] * 4
         for index, row in enumerate(range(0, columns, 8)):
-            raised = raised_ref[row : row + 8, :]
-            part = 1.0 / (raised + level)
-            share = (raised - 1.0) * part
-            sums[index % 4] = sums[index % 4] + share
-            slopes[index % 4] = slopes[index % 4] + share * part
-        volume, slope = total(sums), total(slopes)
-        excess = volume * ((top + level) * scale) - wanted
-        slope = (2.0 * beta * level) * (volume - (top + level) * slope) * scale
-        low = jnp.where(excess > 0.0, middle, low)
-        high = jnp.where(excess > 0.0, high, middle)
+            raised = raised_ref[row : row + 8, :] + level
+            part = pl.reciprocal(raised, approx=True)
+            part = part * (2.0 - raised * part)
+            sums[index % 4] = sums[index % 4] + part
+            squares[index % 4] = squares[index % 4] + part * part
+        first, second = total(sums), total(squares)
+        volume = cells - (1.0 + level) * first
+        slope = first - (1.0 + level) * second
+        whole = (top + level) * scale
+        excess = volume * whole - fluid_share * cells
+        slope = (2.0 * beta * level) * (volume * scale - whole * slope)
+        above = excess > 0.0
+        low, low_known = jnp.where(above, middle, low), jnp.where(above, 1.0, low_known)
+        high, high_known = jnp.where(above, high, middle), jnp.where(above, high_known, 1.0)
         guess = middle - excess / slope
         taken = (guess >= low) & (guess <= high)
-        change = jnp.where(taken, jnp.abs(guess - middle), 1024.0 * (high - low))
-        return low, high, jnp.where(taken, guess, 0.5 * (low + high)), change
+        other = jnp.where(
+            (guess > high) & (high_known == 0.0),
+            high,
+            jnp.where((guess < low) & (low_known == 0.0), low, 0.5 * (low + high)),
+        )
+        change = jnp.where(taken, jnp.abs(guess - middle), 2.0**16 * (high - low))
+        return low, high, low_known, high_known, jnp.where(taken, guess, other), change
 
     def going(carry):
         step, state = carry
-        return (step < 64) & (jnp.max(state[3]) > CLOSE)
-
-    state = (zero, jnp.ones((8, LANES), jnp.float32), jnp.full((8, LANES), 0.5, jnp.float32), zero)
-    state = lax.fori_loop(0, 4, lambda step, state: advance(state), state)
-    step, state = lax.while_loop(going, lambda carry: (carry[0] + 1, advance(carry[1])), (4, state))
-    return state[2]
-
-
-def filtered_level(rows, splits, size, beta, copies_ref, design_ref, filtered_ref, raised_ref, masks):
+        return (step < 64) & (jnp.max(state[5]) > CLOSE)
+
+    state = advance(advance((zero, one, zero, zero, 0.5 * one, zero)))
+    _, state = lax.while_loop(going, lambda carry: (carry[0] + 1, advance(carry[1])), (2, state))
+    return jnp.clip(state[4], 0.5**31, 1.0)
+
+
+def level_kernel(rows, splits, size, step_ref, copies_ref, share_ref, filtered_ref, raised_ref):
     layers = copies_ref.shape[2]
     planes = LANES // rows
     columns = size * LANES
+    masks = plane_masks(rows)
     zero = jnp.zeros((8, LANES), jnp.float32)
-    for ref in (design_ref, filtered_ref):
-        ref[0:8, :] = zero
-        ref[columns + 8 : columns + 16, :] = zero
+    beta = exponent(step_ref)
+    filtered_ref[0:8, :] = zero
+    filtered_ref[columns + 8 : columns + 16, :] = zero
     for block in range(size):
         plane = gather_plane(
             lambda z, part: copies_ref[(z // layers) * splits + part, block, z % layers], planes, splits
         )
-        design_ref[8 + block * LANES : 8 + (block + 1) * LANES, :] = plane.T
+        filtered_ref[8 + block * LANES : 8 + (block + 1) * LANES, :] = plane.T
     for row in range(8, columns + 8, 8):
-        design_ref[row : row + 8, :] = plane_smooth(design_ref[row : row + 8, :], rows, masks)
-    for row in range(8, columns + 8, 8):
-        value = 0.5 * design_ref[row : row + 8, :] + 0.25 * (
-            design_ref[row - 1 : row + 7, :] + design_ref[row + 1 : row + 9, :]
-        )
+        value = plane_smooth(filtered_ref[row : row + 8, :], rows, masks)
         filtered_ref[row : row + 8, :] = value
         raised_ref[row - 8 : row, :] = jnp.exp(2.0 * beta * value)
-    return volume_root(raised_ref, columns, beta)
+    eta = volume_root(raised_ref, columns, beta)
+    place = lax.axis_index("gx") * copies_ref.shape[0] + block_here(copies_ref.shape[0] // splits, splits)
+    level = jnp.exp(2.0 * beta * eta)
+    top = jnp.exp(2.0 * beta)
+    whole = (top + level) / (top - 1.0)
+    strength = alpha_most * penalty_shape
+    for block in range(4):
+        at = slice(8 * block, 8 * block + 8)
+        start = pl.multiple_of(place * 16 + 8 * block, 8)
+        raised = jnp.exp(2.0 * beta * filtered_ref[pl.ds(start, 8), :])
+        part = 1.0 / (raised + level)
+        density_hat = ((raised - 1.0) * part) * whole
+        share_ref[0, at, :] = (penalty_shape + density_hat) / (
+            penalty_shape + strength + (1.0 - strength) * density_hat
+        )
+        slope = 2.0 * beta * (raised * part) * ((level + 1.0) * part) * whole
+        factor = -strength * (1.0 + penalty_shape) / (
+            (penalty_shape + density_hat) * (penalty_shape + density_hat)
+        )
+        share_ref[1, at, :] = slope * factor
 
 
 def flow(rho, speed):
@@ -446,19 +480,17 @@
 
 
 def flow_kernel(
-    rows, splits, size, step_ref, copies_ref, body_ref, before_ref, after_ref, packed_ref,
-    design_ref, filtered_ref, raised_ref,
-    cotangent_ref, even_ref, odd_ref, kept_ref, share_ref, grad_ref, smooth_ref, output_ref,
+    rows, splits, size, share_ref, body_ref, before_ref, after_ref, packed_ref,
+    cotangent_ref, even_ref, odd_ref, kept_ref, grad_ref, smooth_ref, output_ref,
 ):
-    layers = copies_ref.shape[2]
+    devices = packed_ref.shape[0]
     planes = LANES // rows
+    layers = planes * splits // devices
     masks = plane_masks(rows)
     zero = jnp.zeros((8, LANES), jnp.float32)
-    me = block_here(copies_ref.shape[0] // splits, splits)
-    place = lax.axis_index("gx") * copies_ref.shape[0] + me
-    last = size * copies_ref.shape[0] - 1
-    beta = exponent(step_ref)
-    eta = filtered_level(rows, splits, size, beta, copies_ref, design_ref, filtered_ref, raised_ref, masks)
+    me = block_here(devices // splits, splits)
+    place = lax.axis_index("gx") * devices + me
+    last = size * devices - 1
 
     def inside(value, block):
         if block == 0:
@@ -473,25 +505,6 @@
         if row == 24:
             return after_ref[i]
         return body_ref[i, row - 8 : row, :]
-
-    level = jnp.exp(2.0 * beta * eta)
-    top = jnp.exp(2.0 * beta)
-    whole = (top + level) / (top - 1.0)
-    for block in range(4):
-        at = slice(8 * block, 8 * block + 8)
-        start = pl.multiple_of(place * 16 + 8 * block, 8)
-        raised = jnp.exp(2.0 * beta * filtered_ref[pl.ds(start, 8), :])
-        part = 1.0 / (raised + level)
-        density_hat = ((raised - 1.0) * part) * whole
-        strength = alpha_most * penalty_shape
-        share_ref[0, at, :] = (penalty_shape + density_hat) / (
-            penalty_shape + strength + (1.0 - strength) * density_hat
-        )
-        slope = 2.0 * beta * (raised * part) * ((level + 1.0) * part) * whole
-        factor = -strength * (1.0 + penalty_shape) / (
-            (penalty_shape + density_hat) * (penalty_shape + density_hat)
-        )
-        share_ref[1, at, :] = slope * factor
 
     for ref in (even_ref, odd_ref, cotangent_ref):
         for i in range(19):
@@ -532,14 +545,16 @@
                 post = (1.0 - relax_rate) * popul[i] + settled[i]
                 post = jnp.where(wall, popul[opposite[i]], jnp.where(inlet, inlet_value(i), post))
                 target[i, row + 8 : row + 16, :] = inside(post, block)
-    def turned(index):
-        return (index // 8) * LANES + 16 * lax.rem(index + me, 8)
-
-    output_ref[16 * PACKED // LANES * LANES :, :] = jnp.zeros((LANES, LANES), jnp.float32)
+    def put(index, row, value):
+        group, slot = divmod(index, 8)
+        for slot in (slot,) if group < 2 else (slot, slot + 4):
+            start = group * LANES + 16 * lax.rem(slot + me, 8) + row
+            output_ref[pl.ds(pl.multiple_of(start, 8), 8), :] = value
+
     source = buffers[(STEPS - 1) % 2]
     for i in range(19):
         for row in (8, 16):
-            output_ref[pl.ds(pl.multiple_of(turned(i) + row - 8, 8), 8), :] = arrived(source, i, row)
+            put(i, row - 8, arrived(source, i, row))
 
     for step in reversed(range(STEPS)):
         source = cotangent_ref if step == STEPS - 1 else buffers[step % 2]
@@ -599,28 +614,37 @@
         value = inside(grad_ref[at, :] * share_ref[1, at, :], block)
         smooth_ref[8 * block + 8 : 8 * block + 16, :] = plane_smooth(value, rows, masks)
     for row in (8, 16):
-        output_ref[pl.ds(pl.multiple_of(turned(19) + row - 8, 8), 8), :] = 0.5 * smooth_ref[row + 8 : row + 16, :] + 0.25 * (
+        value = 0.5 * smooth_ref[row + 8 : row + 16, :] + 0.25 * (
             smooth_ref[row + 7 : row + 15, :] + smooth_ref[row + 9 : row + 17, :]
         )
-    for group in range(packed_ref.shape[1]):
+        put(19, row - 8, value)
+    second = lax.rem(lane_index() // 16 + 8 - me, 8) >= 4
+    for group in range(3):
         plane = output_ref[group * LANES : (group + 1) * LANES, :].T
-        for z in range(planes):
-            for part in range(splits):
-                at = (z * splits + part) * 8
-                packed_ref[(z // layers) * splits + part, group, z % layers] = plane[at : at + 8, :]
+        for device in range(devices):
+            tiles = []
+            for layer in range(layers):
+                at = (((device // splits) * layers + layer) * splits + device % splits) * 8
+                tiles.append(plane[at : at + 8, :])
+            if group < 2:
+                for layer in range(layers):
+                    packed_ref[device, group * layers + layer] = tiles[layer]
+            else:
+                packed_ref[device, group * layers] = jnp.where(second, tiles[1], tiles[0])
 
 
 def result_kernel(splits, packed_ref, populations_ref, grad_ref):
     devices = [device_at(index, 8 // splits, splits) for index in range(8)]
-    for layer in range(grad_ref.shape[0]):
-        for group in range(packed_ref.shape[1]):
-            values = mixed([packed_ref[device, group, layer] for device in devices])
-            for slot in range(min(8, PACKED - 8 * group)):
-                index, value = 8 * group + slot, rolled(values[-slot % 8], -16 * slot)
-                if index < 19:
-                    populations_ref[index, layer] = value
-                else:
-                    grad_ref[layer] = value
+    for tile in range(packed_ref.shape[1]):
+        values = mixed([packed_ref[device, tile] for device in devices])
+        for slot in range(8):
+            value = rolled(values[-slot % 8], -16 * slot)
+            if tile < 4:
+                populations_ref[tile // 2 * 8 + slot, tile % 2] = value
+            elif slot % 4 < 3:
+                populations_ref[16 + slot % 4, slot // 4] = value
+            else:
+                grad_ref[slot // 4] = value
 
 
 def call(kernel, outs, name, operands, spaces, scratch=(), room=32):
@@ -663,6 +687,7 @@
         "arrange",
         (packed, *designs),
         [vmem] * (1 + size),
+        [vmem((size, *tile), real)],
     )
     copies = lax.all_to_all(copies, ("grp", "gy"), 0, 0)
     path = [on_path(index, grp, splits) for index in range(plane)]
@@ -672,25 +697,29 @@
     before = lax.ppermute(last, line, up)
     after = lax.ppermute(first, line, [(j, i) for i, j in up])
     columns = size * LANES
+    share = call(
+        functools.partial(level_kernel, rows, splits, size),
+        ((2, 32, LANES),),
+        "level",
+        (beta_step.reshape(1), copies),
+        [pltpu.SMEM, vmem],
+        [vmem((columns + 16, LANES), real), vmem((columns, LANES), real)],
+    )
     shapes = [
-        (columns + 16, LANES),
-        (columns + 16, LANES),
-        (columns, LANES),
         (19, 48, LANES),
         (19, 48, LANES),
         (19, 48, LANES),
         (STEPS, 4, 32, LANES),
-        (2, 32, LANES),
         (32, LANES),
         (48, LANES),
         (3 * LANES, LANES),
     ]
     packed = call(
         functools.partial(flow_kernel, rows, splits, size),
-        ((plane, 3, *tile),),
+        ((plane, 5, 8, LANES),),
         "flow",
-        (beta_step.reshape(1), copies, body, before, after),
-        [pltpu.SMEM] + [vmem] * 4,
+        (share, body, before, after),
+        [vmem] * 4,
         [vmem(shape, real) for shape in shapes],
     )
     packed = lax.all_to_all(packed, ("grp", "gy"), 0, 0)

time: 44.7 us -> 41.8 us (0.935)
  Pallas kernels: 7.8 us -> 6.25 us
  blocking collectives: 11.8 us -> 10.8 us
    ppermute x1, waiting for transfers between devices: 2.46 us -> 0.01 us  [body_by_columns(): after = lax.ppermute(first, line, [(j, i) for i, j in up])]
    all_to_all x1, waiting for transfers between devices: 0.01 us -> 2.09 us  [body_by_columns(): copies = lax.all_to_all(copies, ('grp', 'gy'), 0, 0)]
    pallas_call x4 -> x5, Pallas kernels: 7.8 us -> 6.25 us  [call(): pl.pallas_call(kernel, out_shape=shapes if many else shapes[0], in_specs=...]
    all_to_all x1, blocking collectives: 11.8 us -> 10.8 us  [body_by_columns(): packed = lax.all_to_all(packed, ('grp', 'gy'), 0, 0)]
  transfers between devices with their start and end apart: 7 -> 7, of which waited for: 3 -> 3; matrix products, arithmetic and copies ran while one was open for 0% -> 0% of each run, Pallas kernels for 0% -> 3%
where the time goes in v6:
time: 41.8 us; the launch traced here: 41.4 us
  starting transfers between devices  18.6 us (44%)
  blocking collectives  10.8 us (26%)
  Pallas kernels  6.25 us (15%)
  waiting for transfers between devices  4.4 us (11%)
  between operations  1.34 us (3%)
    all_to_all x1, blocking collectives, body_by_columns(): packed = lax.all_to_all(packed, ('grp', 'gy'), 0, 0)  10.8 us
    pallas_call x5, Pallas kernels, call(): pl.pallas_call(kernel, out_shape=shapes if many else shapes[0], in_specs=...  6.25 us
    ppermute x3, starting transfers between devices, body_by_columns(): lax.ppermute(design, 'gx', [(i, (i + turn) % size) for i in range(size)])  5.57 us
    all_to_all x1, starting transfers between devices, body_by_columns(): packed = lax.all_to_all(packed, ('grp', 'gy'), 0, 0)  5.18 us
    all_to_all x1, starting transfers between devices, body_by_columns(): copies = lax.all_to_all(copies, ('grp', 'gy'), 0, 0)  4.14 us
    ppermute x1, starting transfers between devices, body_by_columns(): before = lax.ppermute(last, line, up)  2.41 us
    ppermute x3, waiting for transfers between devices, body_by_columns(): lax.ppermute(design, 'gx', [(i, (i + turn) % size) for i in range(size)])  2.3 us
    all_to_all x1, waiting for transfers between devices, body_by_columns(): copies = lax.all_to_all(copies, ('grp', 'gy'), 0, 0)  2.09 us
  transfers between devices with their start and end apart: 7, of which 3 were waited for; matrix products, arithmetic and copies ran while one was open for 0% of the time, Pallas kernels for 3%

profile of v6, /device:TPU:0, one launch (start us, length us, event | category | flops | bytes accessed | tf_op | source)
XLA Modules:
  0.0 41.4 jit_solution(13852526737787455168)
XLA Ops:
  0.6 1.9 %pack.1 = (f32[2,8,128]{2,1,0:T(8,128)}, f32[8,5,2,8,128]{4,3,2,1,0:T(8,128)}) custom-call(f32[2,8,128]{2,1,0:T(8,128)} %design_ref.1, f32[19,2,8,128]{3,2,1,0:T(8,128)} %populations_ref.1, f32[19,2,8,128]{3,2,1,0:T(8,128)} %cotangent_ref.1, s32[2,8,128]{2,1,0:T(8,128)} %wall_ref.1, s32[2,8,128]{2,1,0:T(8,128)} %inlet_ref.1), custom_call_target="tpu_custom_call" | custom-call | tf_op jit(solution)/shard_map/pack/pallas_call | solution.py:654
  2.5 0.0 copy-start
  2.6 5.2 %all-to-all-start = ((f32[8,5,2,8,128]{4,3,2,1,0:T(8,128)}), f32[8,5,2,8,128]{4,3,2,1,0:T(8,128)S(1)}, u32[]{:S(2)}, u32[]{:S(2)}) async-start(f32[8,5,2,8,128]{4,3,2,1,0:T(8,128)} %get-tuple-element.8), calls=%async_computation | async-start | bytes 655360 | tf_op jit(solution)/shard_map/all_to_all | solution.py:680
  7.7 0.0 copy-done
  7.7 1.6 %collective-permute-start = (f32[2,8,128]{2,1,0:T(8,128)S(1)}, f32[2,8,128]{2,1,0:T(8,128)S(1)}, u32[]{:S(2)}, u32[]{:S(2)}) collective-permute-start(f32[2,8,128]{2,1,0:T(8,128)S(1)} %copy-done), channel_id=1, source_target_pairs={{0,1},{1,2},{2,3},{3,0},{4,5},{5,6},{6,7},{7,4},{8,9},{9,10},{10,1... | collective-permute-start | bytes 24584 | tf_op jit(solution)/shard_map/ppermute | solution.py:683
  9.4 2.6 %collective-permute-start.1 = (f32[2,8,128]{2,1,0:T(8,128)S(1)}, f32[2,8,128]{2,1,0:T(8,128)S(1)}, u32[]{:S(2)}, u32[]{:S(2)}) collective-permute-start(f32[2,8,128]{2,1,0:T(8,128)S(1)} %copy-done), channel_id=1, source_target_pairs={{0,2},{1,3},{2,0},{3,1},{4,6},{5,7},{6,4},{7,5},{8,10},{9,11},{10,... | collective-permute-start | bytes 24584 | tf_op jit(solution)/shard_map/ppermute | solution.py:683
  12.0 1.3 %collective-permute-start.2 = (f32[2,8,128]{2,1,0:T(8,128)S(1)}, f32[2,8,128]{2,1,0:T(8,128)S(1)}, u32[]{:S(2)}, u32[]{:S(2)}) collective-permute-start(f32[2,8,128]{2,1,0:T(8,128)S(1)} %copy-done), channel_id=1, source_target_pairs={{0,3},{1,0},{2,1},{3,2},{4,7},{5,4},{6,5},{7,6},{8,11},{9,8},{10,9... | collective-permute-start | bytes 24584 | tf_op jit(solution)/shard_map/ppermute | solution.py:683
  13.3 0.0 collective-permute-done.refs_1_
  13.3 0.6 %collective-permute-done.1.refs_2_ = f32[2,8,128]{2,1,0:T(8,128)S(1)} collective-permute-done((f32[2,8,128]{2,1,0:T(8,128)S(1)}, f32[2,8,128]{2,1,0:T(8,128)S(1)}, u32[]{:S(2)}, u32[]{:S(2)}) %collective-permute-start.1) | collective-permute-done | bytes 8224 | tf_op jit(solution)/shard_map/ppermute | solution.py:683
  13.9 1.7 %collective-permute-done.2.refs_3_ = f32[2,8,128]{2,1,0:T(8,128)S(1)} collective-permute-done((f32[2,8,128]{2,1,0:T(8,128)S(1)}, f32[2,8,128]{2,1,0:T(8,128)S(1)}, u32[]{:S(2)}, u32[]{:S(2)}) %collective-permute-start.2) | collective-permute-done | bytes 8224 | tf_op jit(solution)/shard_map/ppermute | solution.py:683
  15.6 0.0 all-to-all-done.packed_ref
  15.6 0.9 %arrange.1 = (f32[40,16,128]{2,1,0:T(8,128)S(1)}, f32[40,8,128]{2,1,0:T(8,128)S(1)}, f32[40,8,128]{2,1,0:T(8,128)S(1)}, f32[8,4,2,8,128]{4,3,2,1,0:T(8,128)}) custom-call(f32[8,5,2,8,128]{4,3,2,1,0:T(8,128)S(1)} %all-to-all-done.packed_ref, f32[2,8,128]{2,1,0:T(8,128)S(1)} %copy-done, f32[2,8,128]{2,1,0:T(8,128)S(1)} %collective-permute-done.refs_1_, ...), custom_call_target="tpu_custom_call" | custom-call | tf_op jit(solution)/shard_map/arrange/pallas_call | solution.py:654
  16.5 4.1 %all-to-all-start.1 = ((f32[8,4,2,8,128]{4,3,2,1,0:T(8,128)}), f32[8,4,2,8,128]{4,3,2,1,0:T(8,128)S(1)}, u32[]{:S(2)}, u32[]{:S(2)}) async-start(f32[8,4,2,8,128]{4,3,2,1,0:T(8,128)} %get-tuple-element.10), calls=%async_computation.1 | async-start | bytes 524288 | tf_op jit(solution)/shard_map/all_to_all | solution.py:692
  20.7 2.4 %collective-permute-start.3 = (f32[40,8,128]{2,1,0:T(8,128)S(1)}, f32[40,8,128]{2,1,0:T(8,128)S(1)}, u32[]{:S(2)}, u32[]{:S(2)}) collective-permute-start(f32[40,8,128]{2,1,0:T(8,128)S(1)} %get-tuple-element.12), channel_id=1, source_target_pairs={{0,8},{8,16},{16,24},{24,28},{28,20},{20,12},{12,4},{4,5},{5,13},{... | collective-permute-start | bytes 491528 | tf_op jit(solution)/shard_map/ppermute | solution.py:697
  23.1 1.3 %collective-permute-start.4 = (f32[40,8,128]{2,1,0:T(8,128)S(1)}, f32[40,8,128]{2,1,0:T(8,128)S(1)}, u32[]{:S(2)}, u32[]{:S(2)}) collective-permute-start(f32[40,8,128]{2,1,0:T(8,128)S(1)} %get-tuple-element.13), channel_id=1, source_target_pairs={{8,0},{16,8},{24,16},{28,24},{20,28},{12,20},{4,12},{5,4},{13,5},{... | collective-permute-start | bytes 491528 | tf_op jit(solution)/shard_map/ppermute | solution.py:698
  25.0 2.1 %all-to-all-done.1.copies_ref = f32[8,4,2,8,128]{4,3,2,1,0:T(8,128)S(1)} async-done(((f32[8,4,2,8,128]{4,3,2,1,0:T(8,128)}), f32[8,4,2,8,128]{4,3,2,1,0:T(8,128)S(1)}, u32[]{:S(2)}, u32[]{:S(2)}) %all-to-all-start.1) | async-done | bytes 262176 | tf_op jit(solution)/shard_map/all_to_all | solution.py:692
  27.1 1.0 %level.1.share_ref = f32[2,32,128]{2,1,0:T(8,128)S(1)} custom-call(s32[1]{0:T(128)} %bitcast.1.step_ref, f32[8,4,2,8,128]{4,3,2,1,0:T(8,128)S(1)} %all-to-all-done.1.copies_ref), custom_call_target="tpu_custom_call" | custom-call | tf_op jit(solution)/shard_map/level/pallas_call | solution.py:654
  28.2 0.0 collective-permute-done.3.before_ref
  28.2 0.0 collective-permute-done.4.after_ref
  28.2 1.6 %flow.1 = f32[8,5,8,128]{3,2,1,0:T(8,128)S(1)} custom-call(f32[2,32,128]{2,1,0:T(8,128)S(1)} %level.1.share_ref, f32[40,16,128]{2,1,0:T(8,128)S(1)} %get-tuple-element.11.body_ref, f32[40,8,128]{2,1,0:T(8,128)S(1)} %collective-permute-done.3.before_ref, f32[40,8,128]{2,1,0:T(8,128)S(1)} %collective-permute-done.4.after_ref), custom_call_target="tpu_custom_call" | custom-call | tf_op jit(solution)/shard_map/flow/pallas_call | solution.py:654
  29.8 10.8 %all_to_all.15.packed_ref = f32[8,5,8,128]{3,2,1,0:T(8,128)S(1)} all-to-all(f32[8,5,8,128]{3,2,1,0:T(8,128)S(1)} %flow.1), channel_id=1, replica_groups=mesh['grp'=4,'gy'=2,'gx'=4] {'grp','gy'}, dimensions={0} | all-to-all | bytes 327680 | tf_op jit(solution)/shard_map/all_to_all | solution.py:725
  40.6 0.8 %result.1 = (f32[19,2,8,128]{3,2,1,0:T(8,128)}, f32[2,8,128]{2,1,0:T(8,128)}) custom-call(f32[8,5,8,128]{3,2,1,0:T(8,128)S(1)} %all_to_all.15.packed_ref), custom_call_target="tpu_custom_call" | custom-call | tf_op jit(solution)/shard_map/result/pallas_call | solution.py:654
Async XLA Ops:
  2.5 5.2 %copy-start = (f32[2,8,128]{2,1,0:T(8,128)S(1)}, f32[2,8,128]{2,1,0:T(8,128)}, u32[]{:S(2)}) copy-start(f32[2,8,128]{2,1,0:T(8,128)} %get-tuple-element.9.refs_0_) | copy-start | bytes 24580
  2.6 13.1 %all-to-all-start = ((f32[8,5,2,8,128]{4,3,2,1,0:T(8,128)}), f32[8,5,2,8,128]{4,3,2,1,0:T(8,128)S(1)}, u32[]{:S(2)}, u32[]{:S(2)}) async-start(f32[8,5,2,8,128]{4,3,2,1,0:T(8,128)} %get-tuple-element.8), calls=%async_computation | async-start | bytes 655360 | tf_op jit(solution)/shard_map/all_to_all | solution.py:680
  7.7 5.6 %collective-permute-start = (f32[2,8,128]{2,1,0:T(8,128)S(1)}, f32[2,8,128]{2,1,0:T(8,128)S(1)}, u32[]{:S(2)}, u32[]{:S(2)}) collective-permute-start(f32[2,8,128]{2,1,0:T(8,128)S(1)} %copy-done), channel_id=1, source_target_pairs={{0,1},{1,2},{2,3},{3,0},{4,5},{5,6},{6,7},{7,4},{8,9},{9,10},{10,1... | collective-permute-start | bytes 24584 | tf_op jit(solution)/shard_map/ppermute | solution.py:683
  9.4 4.5 %collective-permute-start.1 = (f32[2,8,128]{2,1,0:T(8,128)S(1)}, f32[2,8,128]{2,1,0:T(8,128)S(1)}, u32[]{:S(2)}, u32[]{:S(2)}) collective-permute-start(f32[2,8,128]{2,1,0:T(8,128)S(1)} %copy-done), channel_id=1, source_target_pairs={{0,2},{1,3},{2,0},{3,1},{4,6},{5,7},{6,4},{7,5},{8,10},{9,11},{10,... | collective-permute-start | bytes 24584 | tf_op jit(solution)/shard_map/ppermute | solution.py:683
  12.0 3.7 %collective-permute-start.2 = (f32[2,8,128]{2,1,0:T(8,128)S(1)}, f32[2,8,128]{2,1,0:T(8,128)S(1)}, u32[]{:S(2)}, u32[]{:S(2)}) collective-permute-start(f32[2,8,128]{2,1,0:T(8,128)S(1)} %copy-done), channel_id=1, source_target_pairs={{0,3},{1,0},{2,1},{3,2},{4,7},{5,4},{6,5},{7,6},{8,11},{9,8},{10,9... | collective-permute-start | bytes 24584 | tf_op jit(solution)/shard_map/ppermute | solution.py:683
  16.5 10.6 %all-to-all-start.1 = ((f32[8,4,2,8,128]{4,3,2,1,0:T(8,128)}), f32[8,4,2,8,128]{4,3,2,1,0:T(8,128)S(1)}, u32[]{:S(2)}, u32[]{:S(2)}) async-start(f32[8,4,2,8,128]{4,3,2,1,0:T(8,128)} %get-tuple-element.10), calls=%async_computation.1 | async-start | bytes 524288 | tf_op jit(solution)/shard_map/all_to_all | solution.py:692
  20.7 7.5 %collective-permute-start.3 = (f32[40,8,128]{2,1,0:T(8,128)S(1)}, f32[40,8,128]{2,1,0:T(8,128)S(1)}, u32[]{:S(2)}, u32[]{:S(2)}) collective-permute-start(f32[40,8,128]{2,1,0:T(8,128)S(1)} %get-tuple-element.12), channel_id=1, source_target_pairs={{0,8},{8,16},{16,24},{24,28},{28,20},{20,12},{12,4},{4,5},{5,13},{... | collective-permute-start | bytes 491528 | tf_op jit(solution)/shard_map/ppermute | solution.py:697
  23.1 5.1 %collective-permute-start.4 = (f32[40,8,128]{2,1,0:T(8,128)S(1)}, f32[40,8,128]{2,1,0:T(8,128)S(1)}, u32[]{:S(2)}, u32[]{:S(2)}) collective-permute-start(f32[40,8,128]{2,1,0:T(8,128)S(1)} %get-tuple-element.13), channel_id=1, source_target_pairs={{8,0},{16,8},{24,16},{28,24},{20,28},{12,20},{4,12},{5,4},{13,5},{... | collective-permute-start | bytes 491528 | tf_op jit(solution)/shard_map/ppermute | solution.py:698

commit v7 on v6

--- a/solution.py
+++ b/solution.py
@@ -210,6 +210,8 @@
 LANES = 128
 AROUND = ((1, 0), (-1, 0), (0, 1), (0, -1), (1, 1), (-1, -1), (1, -1), (-1, 1))
 FIELDS = 40
+NEAR = STEPS + 1
+OUTER = 8 * 21 + NEAR * 19
 CLOSE = 2.0**-14
 
 
@@ -267,18 +269,17 @@
             values = []
             for slot in range(8):
                 index = group * 8 + slot
-                if index < 38:
-                    value = fields_ref[index, layer]
+                if index in (19, 20):
+                    value = masks_ref[index - 19, layer].astype(jnp.float32)
                 else:
-                    value = masks_ref[index - 38, layer].astype(jnp.float32)
+                    value = fields_ref[index if index < 19 else index - 2, layer]
                 values.append(rolled(value, 16 * slot))
             values = mixed(values)
             for index in range(8):
                 packed_ref[devices[index], group, layer] = values[-index % 8]
 
 
-def arrange_kernel(size, splits, packed_ref, *refs):
-    design_refs, (body_ref, first_ref, last_ref, copies_ref, design_ref) = refs[:size], refs[size:]
+def arrange_kernel(splits, packed_ref, body_ref, first_ref, last_ref):
     layers = packed_ref.shape[2]
     planes = packed_ref.shape[0] // splits * layers
     me = block_here(packed_ref.shape[0] // splits, splits)
@@ -289,14 +290,27 @@
         for slot in range(8):
             index = group * 8 + lax.rem(slot + 8 - me, 8)
             body_ref[index] = plane[16 * slot : 16 * slot + 16, :]
-            first_ref[index] = plane[16 * slot : 16 * slot + 8, :]
-            last_ref[index] = plane[16 * slot + 8 : 16 * slot + 16, :]
+    for index in range(FIELDS):
+        if index < 21:
+            first_ref[8 * index : 8 * index + 8, :] = body_ref[index, 0:8, :]
+            last_ref[8 * index : 8 * index + 8, :] = body_ref[index, 8:16, :]
+        else:
+            start = 8 * 21 + NEAR * (index - 21)
+            first_ref[start : start + NEAR, :] = body_ref[index, 0:NEAR, :]
+            last_ref[start : start + NEAR, :] = body_ref[index, 16 - NEAR : 16, :]
+    for ref in (first_ref, last_ref):
+        rest = ref.shape[0] - OUTER
+        ref[OUTER:, :] = jnp.zeros((rest, LANES), jnp.float32)
+
+
+def spread_kernel(size, *refs):
+    design_refs, (copies_ref, design_ref) = refs[:size], refs[size:]
     here = lax.axis_index("gx")
     for turn in range(size):
         design_ref[lax.rem(here + size - turn, size)] = design_refs[turn][...]
     lanes = lane_index()
     zero = jnp.zeros((8, LANES), jnp.float32)
-    for layer in range(layers):
+    for layer in range(copies_ref.shape[2]):
         tiles = [zero] + [design_ref[index, layer] for index in range(size)] + [zero]
         ahead = [rolled(tile, 1) for tile in tiles]
         behind = [rolled(tile, -1) for tile in tiles]
@@ -501,9 +515,9 @@
 
     def initial(i, row):
         if row == 0:
-            return before_ref[i]
+            return before_ref[8 * i : 8 * i + 8, :]
         if row == 24:
-            return after_ref[i]
+            return after_ref[8 * i : 8 * i + 8, :]
         return body_ref[i, row - 8 : row, :]
 
     for ref in (even_ref, odd_ref, cotangent_ref):
@@ -511,8 +525,12 @@
             ref[i, 0:8, :] = zero
             ref[i, 40:48, :] = zero
     for i in range(19):
-        for row in range(0, 32, 8):
-            cotangent_ref[i, row + 8 : row + 16, :] = initial(19 + i, row)
+        start = 8 * 21 + NEAR * i
+        cotangent_ref[i, 8:16, :] = zero
+        cotangent_ref[i, 16 - NEAR : 16, :] = before_ref[start : start + NEAR, :]
+        cotangent_ref[i, 16:32, :] = body_ref[21 + i]
+        cotangent_ref[i, 32:40, :] = zero
+        cotangent_ref[i, 32 : 32 + NEAR, :] = after_ref[start : start + NEAR, :]
 
     def arrived(ref, i, row):
         cz, cy, cx = (int(c) for c in velocities[i])
@@ -528,8 +546,8 @@
                 popul = [initial(i, row) for i in range(19)]
             else:
                 popul = [arrived(source, i, row) for i in range(19)]
-            wall = initial(38, row) > 0.0
-            inlet = initial(39, row) > 0.0
+            wall = initial(19, row) > 0.0
+            inlet = initial(20, row) > 0.0
             rho = popul[0]
             momentum = [None, None, None]
             for i in range(1, 19, 2):
@@ -567,8 +585,8 @@
                 cz, cy, cx = (int(c) for c in velocities[i])
                 value = source[i, row + 8 + cx : row + 16 + cx, :]
                 back.append(plane_shift(value, -cz, -cy, rows, masks))
-            wall = initial(38, row) > 0.0
-            inlet = initial(39, row) > 0.0
+            wall = initial(19, row) > 0.0
+            inlet = initial(20, row) > 0.0
             rho = kept_ref[step, 0, at, :]
             speed = [kept_ref[step, 1 + axis, at, :] for axis in range(3)]
             square = speed[0] * speed[0] + speed[1] * speed[1] + speed[2] * speed[2]
@@ -681,13 +699,21 @@
     designs = [design]
     for turn in range(1, size):
         designs.append(lax.ppermute(design, "gx", [(i, (i + turn) % size) for i in range(size)]))
-    body, first, last, copies = call(
-        functools.partial(arrange_kernel, size, splits),
-        ((FIELDS, 16, LANES), (FIELDS, 8, LANES), (FIELDS, 8, LANES), (plane, size, *tile)),
+    copies = call(
+        functools.partial(spread_kernel, size),
+        ((plane, size, *tile),),
+        "spread",
+        designs,
+        [vmem] * size,
+        [vmem((size, *tile), real)],
+    )
+    outer = (-(-OUTER // 8) * 8, LANES)
+    body, first, last = call(
+        functools.partial(arrange_kernel, splits),
+        ((FIELDS, 16, LANES), outer, outer),
         "arrange",
-        (packed, *designs),
-        [vmem] * (1 + size),
-        [vmem((size, *tile), real)],
+        (packed,),
+        [vmem],
     )
     copies = lax.all_to_all(copies, ("grp", "gy"), 0, 0)
     path = [on_path(index, grp, splits) for index in range(plane)]

time: 41.8 us -> 42.9 us (1.026)
  waiting for transfers between devices: 4.4 us -> 6.33 us
  starting transfers between devices: 18.6 us -> 17.7 us
    ppermute x3, waiting for transfers between devices: 2.3 us -> 4.44 us  [body_by_columns(): lax.ppermute(design, 'gx', [(i, (i + turn) % size) for i in range(size)])]
    ppermute x3, starting transfers between devices: 5.57 us -> 4.67 us  [body_by_columns(): lax.ppermute(design, 'gx', [(i, (i + turn) % size) for i in range(size)])]
    pallas_call x5 -> x6, Pallas kernels: 6.25 us -> 6.58 us  [call(): pl.pallas_call(kernel, out_shape=shapes if many else shapes[0], in_specs=...]
  transfers between devices with their start and end apart: 7 -> 7, of which waited for: 3 -> 4; matrix products, arithmetic and copies ran while one was open for 0% -> 0% of each run, Pallas kernels for 3% -> 5%
where the time goes in v7:
time: 42.9 us; the launch traced here: 42.4 us
  starting transfers between devices  17.7 us (41%)
  blocking collectives  10.4 us (24%)
  Pallas kernels  6.58 us (15%)
  waiting for transfers between devices  6.33 us (15%)
  between operations  1.35 us (3%)
    all_to_all x1, blocking collectives, body_by_columns(): packed = lax.all_to_all(packed, ('grp', 'gy'), 0, 0)  10.4 us
    pallas_call x6, Pallas kernels, call(): pl.pallas_call(kernel, out_shape=shapes if many else shapes[0], in_specs=...  6.58 us
    all_to_all x1, starting transfers between devices, body_by_columns(): packed = lax.all_to_all(packed, ('grp', 'gy'), 0, 0)  5.18 us
    ppermute x3, starting transfers between devices, body_by_columns(): lax.ppermute(design, 'gx', [(i, (i + turn) % size) for i in range(size)])  4.67 us
    ppermute x3, waiting for transfers between devices, body_by_columns(): lax.ppermute(design, 'gx', [(i, (i + turn) % size) for i in range(size)])  4.44 us
    all_to_all x1, starting transfers between devices, body_by_columns(): copies = lax.all_to_all(copies, ('grp', 'gy'), 0, 0)  4.14 us
    ppermute x1, starting transfers between devices, body_by_columns(): before = lax.ppermute(last, line, up)  2.42 us
    all_to_all x1, waiting for transfers between devices, body_by_columns(): copies = lax.all_to_all(copies, ('grp', 'gy'), 0, 0)  1.89 us
  transfers between devices with their start and end apart: 7, of which 4 were waited for; matrix products, arithmetic and copies ran while one was open for 0% of the time, Pallas kernels for 5%

profile of v7, /device:TPU:0, one launch (start us, length us, event | category | flops | bytes accessed | tf_op | source)
XLA Modules:
  0.0 42.4 jit_solution(16013944690828785690)
XLA Ops:
  0.6 1.9 %pack.1 = (f32[2,8,128]{2,1,0:T(8,128)}, f32[8,5,2,8,128]{4,3,2,1,0:T(8,128)}) custom-call(f32[2,8,128]{2,1,0:T(8,128)} %design_ref.1, f32[19,2,8,128]{3,2,1,0:T(8,128)} %populations_ref.1, f32[19,2,8,128]{3,2,1,0:T(8,128)} %cotangent_ref.1, s32[2,8,128]{2,1,0:T(8,128)} %wall_ref.1, s32[2,8,128]{2,1,0:T(8,128)} %inlet_ref.1), custom_call_target="tpu_custom_call" | custom-call | tf_op jit(solution)/shard_map/pack/pallas_call | solution.py:672
  2.5 0.0 copy-start
  2.6 5.2 %all-to-all-start.1 = ((f32[8,5,2,8,128]{4,3,2,1,0:T(8,128)}), f32[8,5,2,8,128]{4,3,2,1,0:T(8,128)S(1)}, u32[]{:S(2)}, u32[]{:S(2)}) async-start(f32[8,5,2,8,128]{4,3,2,1,0:T(8,128)} %get-tuple-element.8), calls=%async_computation.1 | async-start | bytes 655360 | tf_op jit(solution)/shard_map/all_to_all | solution.py:698
  7.7 0.0 copy-done
  7.7 3.7 %collective-permute-start.2 = (f32[2,8,128]{2,1,0:T(8,128)S(1)}, f32[2,8,128]{2,1,0:T(8,128)S(1)}, u32[]{:S(2)}, u32[]{:S(2)}) collective-permute-start(f32[2,8,128]{2,1,0:T(8,128)S(1)} %copy-done), channel_id=1, source_target_pairs={{0,3},{1,0},{2,1},{3,2},{4,7},{5,4},{6,5},{7,6},{8,11},{9,8},{10,9... | collective-permute-start | bytes 24584 | tf_op jit(solution)/shard_map/ppermute | solution.py:701
  11.4 0.0 collective-permute-start.1
  11.4 1.0 %collective-permute-start = (f32[2,8,128]{2,1,0:T(8,128)S(1)}, f32[2,8,128]{2,1,0:T(8,128)S(1)}, u32[]{:S(2)}, u32[]{:S(2)}) collective-permute-start(f32[2,8,128]{2,1,0:T(8,128)S(1)} %copy-done), channel_id=1, source_target_pairs={{0,1},{1,2},{2,3},{3,0},{4,5},{5,6},{6,7},{7,4},{8,9},{9,10},{10,1... | collective-permute-start | bytes 24584 | tf_op jit(solution)/shard_map/ppermute | solution.py:701
  12.4 0.4 collective-permute-done.2.refs_3_
  12.8 3.2 %collective-permute-done.1.refs_2_ = f32[2,8,128]{2,1,0:T(8,128)S(1)} collective-permute-done((f32[2,8,128]{2,1,0:T(8,128)S(1)}, f32[2,8,128]{2,1,0:T(8,128)S(1)}, u32[]{:S(2)}, u32[]{:S(2)}) %collective-permute-start.1) | collective-permute-done | bytes 8224 | tf_op jit(solution)/shard_map/ppermute | solution.py:701
  16.0 0.9 %collective-permute-done.refs_1_ = f32[2,8,128]{2,1,0:T(8,128)S(1)} collective-permute-done((f32[2,8,128]{2,1,0:T(8,128)S(1)}, f32[2,8,128]{2,1,0:T(8,128)S(1)}, u32[]{:S(2)}, u32[]{:S(2)}) %collective-permute-start) | collective-permute-done | bytes 8224 | tf_op jit(solution)/shard_map/ppermute | solution.py:701
  16.9 0.8 %spread.1 = f32[8,4,2,8,128]{4,3,2,1,0:T(8,128)} custom-call(f32[2,8,128]{2,1,0:T(8,128)S(1)} %copy-done, f32[2,8,128]{2,1,0:T(8,128)S(1)} %collective-permute-done.refs_1_, f32[2,8,128]{2,1,0:T(8,128)S(1)} %collective-permute-done.1.refs_2_, f32[2,8,128]{2,1,0:T(8,128)S(1)} %collective-permute-done.2.refs_3_), custom_call_target="tpu_custom_call" | custom-call | tf_op jit(solution)/shard_map/spread/pallas_call | solution.py:672
  17.7 0.0 all-to-all-done.1.packed_ref
  17.7 4.1 %all-to-all-start = ((f32[8,4,2,8,128]{4,3,2,1,0:T(8,128)}), f32[8,4,2,8,128]{4,3,2,1,0:T(8,128)S(1)}, u32[]{:S(2)}, u32[]{:S(2)}) async-start(f32[8,4,2,8,128]{4,3,2,1,0:T(8,128)} %spread.1), calls=%async_computation | async-start | bytes 524288 | tf_op jit(solution)/shard_map/all_to_all | solution.py:718
  21.8 0.2 arrange.1
  22.0 2.4 %collective-permute-start.3 = (f32[264,128]{1,0:T(8,128)S(1)}, f32[264,128]{1,0:T(8,128)S(1)}, u32[]{:S(2)}, u32[]{:S(2)}) collective-permute-start(f32[264,128]{1,0:T(8,128)S(1)} %get-tuple-element.10), channel_id=1, source_target_pairs={{0,8},{8,16},{16,24},{24,28},{28,20},{20,12},{12,4},{4,5},{5,13},{... | collective-permute-start | bytes 405512 | tf_op jit(solution)/shard_map/ppermute | solution.py:723
  24.4 1.3 %collective-permute-start.4 = (f32[264,128]{1,0:T(8,128)S(1)}, f32[264,128]{1,0:T(8,128)S(1)}, u32[]{:S(2)}, u32[]{:S(2)}) collective-permute-start(f32[264,128]{1,0:T(8,128)S(1)} %get-tuple-element.11), channel_id=1, source_target_pairs={{8,0},{16,8},{24,16},{28,24},{20,28},{12,20},{4,12},{5,4},{13,5},{... | collective-permute-start | bytes 405512 | tf_op jit(solution)/shard_map/ppermute | solution.py:724
  26.4 1.9 %all-to-all-done.copies_ref = f32[8,4,2,8,128]{4,3,2,1,0:T(8,128)S(1)} async-done(((f32[8,4,2,8,128]{4,3,2,1,0:T(8,128)}), f32[8,4,2,8,128]{4,3,2,1,0:T(8,128)S(1)}, u32[]{:S(2)}, u32[]{:S(2)}) %all-to-all-start) | async-done | bytes 262176 | tf_op jit(solution)/shard_map/all_to_all | solution.py:718
  28.3 1.3 %level.1.share_ref = f32[2,32,128]{2,1,0:T(8,128)S(1)} custom-call(s32[1]{0:T(128)} %bitcast.1.step_ref, f32[8,4,2,8,128]{4,3,2,1,0:T(8,128)S(1)} %all-to-all-done.copies_ref), custom_call_target="tpu_custom_call" | custom-call | tf_op jit(solution)/shard_map/level/pallas_call | solution.py:672
  29.5 0.0 collective-permute-done.3.before_ref
  29.5 0.0 collective-permute-done.4.after_ref
  29.6 1.6 %flow.1 = f32[8,5,8,128]{3,2,1,0:T(8,128)S(1)} custom-call(f32[2,32,128]{2,1,0:T(8,128)S(1)} %level.1.share_ref, f32[40,16,128]{2,1,0:T(8,128)S(1)} %get-tuple-element.9.body_ref, f32[264,128]{1,0:T(8,128)S(1)} %collective-permute-done.3.before_ref, f32[264,128]{1,0:T(8,128)S(1)} %collective-permute-done.4.after_ref), custom_call_target="tpu_custom_call" | custom-call | tf_op jit(solution)/shard_map/flow/pallas_call | solution.py:672
  31.2 10.4 %all_to_all.15.packed_ref = f32[8,5,8,128]{3,2,1,0:T(8,128)S(1)} all-to-all(f32[8,5,8,128]{3,2,1,0:T(8,128)S(1)} %flow.1), channel_id=1, replica_groups=mesh['grp'=4,'gy'=2,'gx'=4] {'grp','gy'}, dimensions={0} | all-to-all | bytes 327680 | tf_op jit(solution)/shard_map/all_to_all | solution.py:751
  41.6 0.8 %result.1 = (f32[19,2,8,128]{3,2,1,0:T(8,128)}, f32[2,8,128]{2,1,0:T(8,128)}) custom-call(f32[8,5,8,128]{3,2,1,0:T(8,128)S(1)} %all_to_all.15.packed_ref), custom_call_target="tpu_custom_call" | custom-call | tf_op jit(solution)/shard_map/result/pallas_call | solution.py:672
Async XLA Ops:
  2.5 5.2 %copy-start = (f32[2,8,128]{2,1,0:T(8,128)S(1)}, f32[2,8,128]{2,1,0:T(8,128)}, u32[]{:S(2)}) copy-start(f32[2,8,128]{2,1,0:T(8,128)} %get-tuple-element.7.refs_0_) | copy-start | bytes 24580
  2.6 15.1 %all-to-all-start.1 = ((f32[8,5,2,8,128]{4,3,2,1,0:T(8,128)}), f32[8,5,2,8,128]{4,3,2,1,0:T(8,128)S(1)}, u32[]{:S(2)}, u32[]{:S(2)}) async-start(f32[8,5,2,8,128]{4,3,2,1,0:T(8,128)} %get-tuple-element.8), calls=%async_computation.1 | async-start | bytes 655360 | tf_op jit(solution)/shard_map/all_to_all | solution.py:698
  7.7 5.0 %collective-permute-start.2 = (f32[2,8,128]{2,1,0:T(8,128)S(1)}, f32[2,8,128]{2,1,0:T(8,128)S(1)}, u32[]{:S(2)}, u32[]{:S(2)}) collective-permute-start(f32[2,8,128]{2,1,0:T(8,128)S(1)} %copy-done), channel_id=1, source_target_pairs={{0,3},{1,0},{2,1},{3,2},{4,7},{5,4},{6,5},{7,6},{8,11},{9,8},{10,9... | collective-permute-start | bytes 24584 | tf_op jit(solution)/shard_map/ppermute | solution.py:701
  11.4 4.5 %collective-permute-start.1 = (f32[2,8,128]{2,1,0:T(8,128)S(1)}, f32[2,8,128]{2,1,0:T(8,128)S(1)}, u32[]{:S(2)}, u32[]{:S(2)}) collective-permute-start(f32[2,8,128]{2,1,0:T(8,128)S(1)} %copy-done), channel_id=1, source_target_pairs={{0,2},{1,3},{2,0},{3,1},{4,6},{5,7},{6,4},{7,5},{8,10},{9,11},{10,... | collective-permute-start | bytes 24584 | tf_op jit(solution)/shard_map/ppermute | solution.py:701
  11.4 5.4 %collective-permute-start = (f32[2,8,128]{2,1,0:T(8,128)S(1)}, f32[2,8,128]{2,1,0:T(8,128)S(1)}, u32[]{:S(2)}, u32[]{:S(2)}) collective-permute-start(f32[2,8,128]{2,1,0:T(8,128)S(1)} %copy-done), channel_id=1, source_target_pairs={{0,1},{1,2},{2,3},{3,0},{4,5},{5,6},{6,7},{7,4},{8,9},{9,10},{10,1... | collective-permute-start | bytes 24584 | tf_op jit(solution)/shard_map/ppermute | solution.py:701
  17.7 10.6 %all-to-all-start = ((f32[8,4,2,8,128]{4,3,2,1,0:T(8,128)}), f32[8,4,2,8,128]{4,3,2,1,0:T(8,128)S(1)}, u32[]{:S(2)}, u32[]{:S(2)}) async-start(f32[8,4,2,8,128]{4,3,2,1,0:T(8,128)} %spread.1), calls=%async_computation | async-start | bytes 524288 | tf_op jit(solution)/shard_map/all_to_all | solution.py:718
  22.0 7.5 %collective-permute-start.3 = (f32[264,128]{1,0:T(8,128)S(1)}, f32[264,128]{1,0:T(8,128)S(1)}, u32[]{:S(2)}, u32[]{:S(2)}) collective-permute-start(f32[264,128]{1,0:T(8,128)S(1)} %get-tuple-element.10), channel_id=1, source_target_pairs={{0,8},{8,16},{16,24},{24,28},{28,20},{20,12},{12,4},{4,5},{5,13},{... | collective-permute-start | bytes 405512 | tf_op jit(solution)/shard_map/ppermute | solution.py:723
  24.4 5.1 %collective-permute-start.4 = (f32[264,128]{1,0:T(8,128)S(1)}, f32[264,128]{1,0:T(8,128)S(1)}, u32[]{:S(2)}, u32[]{:S(2)}) collective-permute-start(f32[264,128]{1,0:T(8,128)S(1)} %get-tuple-element.11), channel_id=1, source_target_pairs={{8,0},{16,8},{24,16},{28,24},{20,28},{12,20},{4,12},{5,4},{13,5},{... | collective-permute-start | bytes 405512 | tf_op jit(solution)/shard_map/ppermute | solution.py:724

commit v8 on v7

--- a/solution.py
+++ b/solution.py
@@ -696,9 +696,9 @@
         60,
     )
     packed = lax.all_to_all(packed, ("grp", "gy"), 0, 0)
-    designs = [design]
-    for turn in range(1, size):
-        designs.append(lax.ppermute(design, "gx", [(i, (i + turn) % size) for i in range(size)]))
+    designs = [design] * size
+    for turn in reversed(range(1, size)):
+        designs[turn] = lax.ppermute(design, "gx", [(i, (i + turn) % size) for i in range(size)])
     copies = call(
         functools.partial(spread_kernel, size),
         ((plane, size, *tile),),

time: 42.9 us -> 42.9 us (level)
  no operation moved by 1% of the time
where the time goes in v8:
time: 42.9 us; the launch traced here: 42.4 us
  starting transfers between devices  17.7 us (41%)
  blocking collectives  10.7 us (25%)
  Pallas kernels  6.36 us (15%)
  waiting for transfers between devices  6.33 us (15%)
  between operations  1.35 us (3%)
    all_to_all x1, blocking collectives, body_by_columns(): packed = lax.all_to_all(packed, ('grp', 'gy'), 0, 0)  10.7 us
    pallas_call x6, Pallas kernels, call(): pl.pallas_call(kernel, out_shape=shapes if many else shapes[0], in_specs=...  6.36 us
    all_to_all x1, starting transfers between devices, body_by_columns(): packed = lax.all_to_all(packed, ('grp', 'gy'), 0, 0)  5.18 us
    ppermute x3, starting transfers between devices, body_by_columns(): lax.ppermute(design, 'gx', [(i, (i + turn) % size) for i in range(size)])  4.67 us
    ppermute x3, waiting for transfers between devices, body_by_columns(): lax.ppermute(design, 'gx', [(i, (i + turn) % size) for i in range(size)])  4.44 us
    all_to_all x1, starting transfers between devices, body_by_columns(): copies = lax.all_to_all(copies, ('grp', 'gy'), 0, 0)  4.14 us
    ppermute x1, starting transfers between devices, body_by_columns(): before = lax.ppermute(last, line, up)  2.42 us
    all_to_all x1, waiting for transfers between devices, body_by_columns(): copies = lax.all_to_all(copies, ('grp', 'gy'), 0, 0)  1.89 us
  transfers between devices with their start and end apart: 7, of which 4 were waited for; matrix products, arithmetic and copies ran while one was open for 0% of the time, Pallas kernels for 5%

profile of v8, /device:TPU:0, one launch (start us, length us, event | category | flops | bytes accessed | tf_op | source)
XLA Modules:
  0.0 42.4 jit_solution(16013944690828785690)
XLA Ops:
  0.6 1.9 %pack.1 = (f32[2,8,128]{2,1,0:T(8,128)}, f32[8,5,2,8,128]{4,3,2,1,0:T(8,128)}) custom-call(f32[2,8,128]{2,1,0:T(8,128)} %design_ref.1, f32[19,2,8,128]{3,2,1,0:T(8,128)} %populations_ref.1, f32[19,2,8,128]{3,2,1,0:T(8,128)} %cotangent_ref.1, s32[2,8,128]{2,1,0:T(8,128)} %wall_ref.1, s32[2,8,128]{2,1,0:T(8,128)} %inlet_ref.1), custom_call_target="tpu_custom_call" | custom-call | tf_op jit(solution)/shard_map/pack/pallas_call | solution.py:672
  2.5 0.0 copy-start
  2.6 5.2 %all-to-all-start.1 = ((f32[8,5,2,8,128]{4,3,2,1,0:T(8,128)}), f32[8,5,2,8,128]{4,3,2,1,0:T(8,128)S(1)}, u32[]{:S(2)}, u32[]{:S(2)}) async-start(f32[8,5,2,8,128]{4,3,2,1,0:T(8,128)} %get-tuple-element.8), calls=%async_computation.1 | async-start | bytes 655360 | tf_op jit(solution)/shard_map/all_to_all | solution.py:698
  7.7 0.0 copy-done
  7.7 3.7 %collective-permute-start.2 = (f32[2,8,128]{2,1,0:T(8,128)S(1)}, f32[2,8,128]{2,1,0:T(8,128)S(1)}, u32[]{:S(2)}, u32[]{:S(2)}) collective-permute-start(f32[2,8,128]{2,1,0:T(8,128)S(1)} %copy-done), channel_id=1, source_target_pairs={{0,3},{1,0},{2,1},{3,2},{4,7},{5,4},{6,5},{7,6},{8,11},{9,8},{10,9... | collective-permute-start | bytes 24584 | tf_op jit(solution)/shard_map/ppermute | solution.py:701
  11.4 0.0 collective-permute-start.1
  11.4 1.0 %collective-permute-start = (f32[2,8,128]{2,1,0:T(8,128)S(1)}, f32[2,8,128]{2,1,0:T(8,128)S(1)}, u32[]{:S(2)}, u32[]{:S(2)}) collective-permute-start(f32[2,8,128]{2,1,0:T(8,128)S(1)} %copy-done), channel_id=1, source_target_pairs={{0,1},{1,2},{2,3},{3,0},{4,5},{5,6},{6,7},{7,4},{8,9},{9,10},{10,1... | collective-permute-start | bytes 24584 | tf_op jit(solution)/shard_map/ppermute | solution.py:701
  12.4 0.4 collective-permute-done.2.refs_3_
  12.8 3.2 %collective-permute-done.1.refs_2_ = f32[2,8,128]{2,1,0:T(8,128)S(1)} collective-permute-done((f32[2,8,128]{2,1,0:T(8,128)S(1)}, f32[2,8,128]{2,1,0:T(8,128)S(1)}, u32[]{:S(2)}, u32[]{:S(2)}) %collective-permute-start.1) | collective-permute-done | bytes 8224 | tf_op jit(solution)/shard_map/ppermute | solution.py:701
  16.0 0.9 %collective-permute-done.refs_1_ = f32[2,8,128]{2,1,0:T(8,128)S(1)} collective-permute-done((f32[2,8,128]{2,1,0:T(8,128)S(1)}, f32[2,8,128]{2,1,0:T(8,128)S(1)}, u32[]{:S(2)}, u32[]{:S(2)}) %collective-permute-start) | collective-permute-done | bytes 8224 | tf_op jit(solution)/shard_map/ppermute | solution.py:701
  16.9 0.8 %spread.1 = f32[8,4,2,8,128]{4,3,2,1,0:T(8,128)} custom-call(f32[2,8,128]{2,1,0:T(8,128)S(1)} %copy-done, f32[2,8,128]{2,1,0:T(8,128)S(1)} %collective-permute-done.refs_1_, f32[2,8,128]{2,1,0:T(8,128)S(1)} %collective-permute-done.1.refs_2_, f32[2,8,128]{2,1,0:T(8,128)S(1)} %collective-permute-done.2.refs_3_), custom_call_target="tpu_custom_call" | custom-call | tf_op jit(solution)/shard_map/spread/pallas_call | solution.py:672
  17.7 0.0 all-to-all-done.1.packed_ref
  17.7 4.1 %all-to-all-start = ((f32[8,4,2,8,128]{4,3,2,1,0:T(8,128)}), f32[8,4,2,8,128]{4,3,2,1,0:T(8,128)S(1)}, u32[]{:S(2)}, u32[]{:S(2)}) async-start(f32[8,4,2,8,128]{4,3,2,1,0:T(8,128)} %spread.1), calls=%async_computation | async-start | bytes 524288 | tf_op jit(solution)/shard_map/all_to_all | solution.py:718
  21.8 0.2 arrange.1
  22.0 2.4 %collective-permute-start.3 = (f32[264,128]{1,0:T(8,128)S(1)}, f32[264,128]{1,0:T(8,128)S(1)}, u32[]{:S(2)}, u32[]{:S(2)}) collective-permute-start(f32[264,128]{1,0:T(8,128)S(1)} %get-tuple-element.10), channel_id=1, source_target_pairs={{0,8},{8,16},{16,24},{24,28},{28,20},{20,12},{12,4},{4,5},{5,13},{... | collective-permute-start | bytes 405512 | tf_op jit(solution)/shard_map/ppermute | solution.py:723
  24.4 1.3 %collective-permute-start.4 = (f32[264,128]{1,0:T(8,128)S(1)}, f32[264,128]{1,0:T(8,128)S(1)}, u32[]{:S(2)}, u32[]{:S(2)}) collective-permute-start(f32[264,128]{1,0:T(8,128)S(1)} %get-tuple-element.11), channel_id=1, source_target_pairs={{8,0},{16,8},{24,16},{28,24},{20,28},{12,20},{4,12},{5,4},{13,5},{... | collective-permute-start | bytes 405512 | tf_op jit(solution)/shard_map/ppermute | solution.py:724
  26.4 1.9 %all-to-all-done.copies_ref = f32[8,4,2,8,128]{4,3,2,1,0:T(8,128)S(1)} async-done(((f32[8,4,2,8,128]{4,3,2,1,0:T(8,128)}), f32[8,4,2,8,128]{4,3,2,1,0:T(8,128)S(1)}, u32[]{:S(2)}, u32[]{:S(2)}) %all-to-all-start) | async-done | bytes 262176 | tf_op jit(solution)/shard_map/all_to_all | solution.py:718
  28.3 1.0 %level.1.share_ref = f32[2,32,128]{2,1,0:T(8,128)S(1)} custom-call(s32[1]{0:T(128)} %bitcast.1.step_ref, f32[8,4,2,8,128]{4,3,2,1,0:T(8,128)S(1)} %all-to-all-done.copies_ref), custom_call_target="tpu_custom_call" | custom-call | tf_op jit(solution)/shard_map/level/pallas_call | solution.py:672
  29.3 0.0 collective-permute-done.3.before_ref
  29.3 0.0 collective-permute-done.4.after_ref
  29.3 1.6 %flow.1 = f32[8,5,8,128]{3,2,1,0:T(8,128)S(1)} custom-call(f32[2,32,128]{2,1,0:T(8,128)S(1)} %level.1.share_ref, f32[40,16,128]{2,1,0:T(8,128)S(1)} %get-tuple-element.9.body_ref, f32[264,128]{1,0:T(8,128)S(1)} %collective-permute-done.3.before_ref, f32[264,128]{1,0:T(8,128)S(1)} %collective-permute-done.4.after_ref), custom_call_target="tpu_custom_call" | custom-call | tf_op jit(solution)/shard_map/flow/pallas_call | solution.py:672
  31.0 10.7 %all_to_all.15.packed_ref = f32[8,5,8,128]{3,2,1,0:T(8,128)S(1)} all-to-all(f32[8,5,8,128]{3,2,1,0:T(8,128)S(1)} %flow.1), channel_id=1, replica_groups=mesh['grp'=4,'gy'=2,'gx'=4] {'grp','gy'}, dimensions={0} | all-to-all | bytes 327680 | tf_op jit(solution)/shard_map/all_to_all | solution.py:751
  41.6 0.8 %result.1 = (f32[19,2,8,128]{3,2,1,0:T(8,128)}, f32[2,8,128]{2,1,0:T(8,128)}) custom-call(f32[8,5,8,128]{3,2,1,0:T(8,128)S(1)} %all_to_all.15.packed_ref), custom_call_target="tpu_custom_call" | custom-call | tf_op jit(solution)/shard_map/result/pallas_call | solution.py:672
Async XLA Ops:
  2.5 5.2 %copy-start = (f32[2,8,128]{2,1,0:T(8,128)S(1)}, f32[2,8,128]{2,1,0:T(8,128)}, u32[]{:S(2)}) copy-start(f32[2,8,128]{2,1,0:T(8,128)} %get-tuple-element.7.refs_0_) | copy-start | bytes 24580
  2.6 15.1 %all-to-all-start.1 = ((f32[8,5,2,8,128]{4,3,2,1,0:T(8,128)}), f32[8,5,2,8,128]{4,3,2,1,0:T(8,128)S(1)}, u32[]{:S(2)}, u32[]{:S(2)}) async-start(f32[8,5,2,8,128]{4,3,2,1,0:T(8,128)} %get-tuple-element.8), calls=%async_computation.1 | async-start | bytes 655360 | tf_op jit(solution)/shard_map/all_to_all | solution.py:698
  7.7 5.0 %collective-permute-start.2 = (f32[2,8,128]{2,1,0:T(8,128)S(1)}, f32[2,8,128]{2,1,0:T(8,128)S(1)}, u32[]{:S(2)}, u32[]{:S(2)}) collective-permute-start(f32[2,8,128]{2,1,0:T(8,128)S(1)} %copy-done), channel_id=1, source_target_pairs={{0,3},{1,0},{2,1},{3,2},{4,7},{5,4},{6,5},{7,6},{8,11},{9,8},{10,9... | collective-permute-start | bytes 24584 | tf_op jit(solution)/shard_map/ppermute | solution.py:701
  11.4 4.5 %collective-permute-start.1 = (f32[2,8,128]{2,1,0:T(8,128)S(1)}, f32[2,8,128]{2,1,0:T(8,128)S(1)}, u32[]{:S(2)}, u32[]{:S(2)}) collective-permute-start(f32[2,8,128]{2,1,0:T(8,128)S(1)} %copy-done), channel_id=1, source_target_pairs={{0,2},{1,3},{2,0},{3,1},{4,6},{5,7},{6,4},{7,5},{8,10},{9,11},{10,... | collective-permute-start | bytes 24584 | tf_op jit(solution)/shard_map/ppermute | solution.py:701
  11.4 5.4 %collective-permute-start = (f32[2,8,128]{2,1,0:T(8,128)S(1)}, f32[2,8,128]{2,1,0:T(8,128)S(1)}, u32[]{:S(2)}, u32[]{:S(2)}) collective-permute-start(f32[2,8,128]{2,1,0:T(8,128)S(1)} %copy-done), channel_id=1, source_target_pairs={{0,1},{1,2},{2,3},{3,0},{4,5},{5,6},{6,7},{7,4},{8,9},{9,10},{10,1... | collective-permute-start | bytes 24584 | tf_op jit(solution)/shard_map/ppermute | solution.py:701
  17.7 10.6 %all-to-all-start = ((f32[8,4,2,8,128]{4,3,2,1,0:T(8,128)}), f32[8,4,2,8,128]{4,3,2,1,0:T(8,128)S(1)}, u32[]{:S(2)}, u32[]{:S(2)}) async-start(f32[8,4,2,8,128]{4,3,2,1,0:T(8,128)} %spread.1), calls=%async_computation | async-start | bytes 524288 | tf_op jit(solution)/shard_map/all_to_all | solution.py:718
  22.0 7.3 %collective-permute-start.3 = (f32[264,128]{1,0:T(8,128)S(1)}, f32[264,128]{1,0:T(8,128)S(1)}, u32[]{:S(2)}, u32[]{:S(2)}) collective-permute-start(f32[264,128]{1,0:T(8,128)S(1)} %get-tuple-element.10), channel_id=1, source_target_pairs={{0,8},{8,16},{16,24},{24,28},{28,20},{20,12},{12,4},{4,5},{5,13},{... | collective-permute-start | bytes 405512 | tf_op jit(solution)/shard_map/ppermute | solution.py:723
  24.4 4.9 %collective-permute-start.4 = (f32[264,128]{1,0:T(8,128)S(1)}, f32[264,128]{1,0:T(8,128)S(1)}, u32[]{:S(2)}, u32[]{:S(2)}) collective-permute-start(f32[264,128]{1,0:T(8,128)S(1)} %get-tuple-element.11), channel_id=1, source_target_pairs={{8,0},{16,8},{24,16},{28,24},{20,28},{12,20},{4,12},{5,4},{13,5},{... | collective-permute-start | bytes 405512 | tf_op jit(solution)/shard_map/ppermute | solution.py:724

commit v9 on v8

--- a/solution.py
+++ b/solution.py
@@ -307,7 +307,7 @@
     design_refs, (copies_ref, design_ref) = refs[:size], refs[size:]
     here = lax.axis_index("gx")
     for turn in range(size):
-        design_ref[lax.rem(here + size - turn, size)] = design_refs[turn][...]
+        design_ref[lax.rem(here + turn, size)] = design_refs[turn][...]
     lanes = lane_index()
     zero = jnp.zeros((8, LANES), jnp.float32)
     for layer in range(copies_ref.shape[2]):
@@ -698,7 +698,7 @@
     packed = lax.all_to_all(packed, ("grp", "gy"), 0, 0)
     designs = [design] * size
     for turn in reversed(range(1, size)):
-        designs[turn] = lax.ppermute(design, "gx", [(i, (i + turn) % size) for i in range(size)])
+        designs[turn] = lax.ppermute(design, "gx", [((i + turn) % size, i) for i in range(size)])
     copies = call(
         functools.partial(spread_kernel, size),
         ((plane, size, *tile),),

time: 42.9 us -> 41.6 us (0.970)
  waiting for transfers between devices: 6.33 us -> 4.2 us
  starting transfers between devices: 17.7 us -> 18.6 us
    ppermute x3, waiting for transfers between devices: 4.44 us -> 2.3 us  [body_by_columns(): lax.ppermute(design, 'gx', [((i + turn) % size, i) for i in range(size)])]
    ppermute x3, starting transfers between devices: 4.67 us -> 5.57 us  [body_by_columns(): lax.ppermute(design, 'gx', [((i + turn) % size, i) for i in range(size)])]
  transfers between devices with their start and end apart: 7 -> 7, of which waited for: 4 -> 3; matrix products, arithmetic and copies ran while one was open for 0% -> 0% of each run, Pallas kernels for 5% -> 4%
where the time goes in v9:
time: 41.6 us; the launch traced here: 41.2 us
  starting transfers between devices  18.6 us (45%)
  blocking collectives  10.9 us (26%)
  Pallas kernels  6.15 us (15%)
  waiting for transfers between devices  4.2 us (10%)
  between operations  1.35 us (3%)
    all_to_all x1, blocking collectives, body_by_columns(): packed = lax.all_to_all(packed, ('grp', 'gy'), 0, 0)  10.9 us
    pallas_call x6, Pallas kernels, call(): pl.pallas_call(kernel, out_shape=shapes if many else shapes[0], in_specs=...  6.15 us
    ppermute x3, starting transfers between devices, body_by_columns(): lax.ppermute(design, 'gx', [((i + turn) % size, i) for i in range(size)])  5.57 us
    all_to_all x1, starting transfers between devices, body_by_columns(): packed = lax.all_to_all(packed, ('grp', 'gy'), 0, 0)  5.18 us
    all_to_all x1, starting transfers between devices, body_by_columns(): copies = lax.all_to_all(copies, ('grp', 'gy'), 0, 0)  4.14 us
    ppermute x1, starting transfers between devices, body_by_columns(): before = lax.ppermute(last, line, up)  2.42 us
    ppermute x3, waiting for transfers between devices, body_by_columns(): lax.ppermute(design, 'gx', [((i + turn) % size, i) for i in range(size)])  2.3 us
    all_to_all x1, waiting for transfers between devices, body_by_columns(): copies = lax.all_to_all(copies, ('grp', 'gy'), 0, 0)  1.89 us
  transfers between devices with their start and end apart: 7, of which 3 were waited for; matrix products, arithmetic and copies ran while one was open for 0% of the time, Pallas kernels for 4%

profile of v9, /device:TPU:0, one launch (start us, length us, event | category | flops | bytes accessed | tf_op | source)
XLA Modules:
  0.0 41.2 jit_solution(18348039056298446715)
XLA Ops:
  0.6 1.9 %pack.1 = (f32[2,8,128]{2,1,0:T(8,128)}, f32[8,5,2,8,128]{4,3,2,1,0:T(8,128)}) custom-call(f32[2,8,128]{2,1,0:T(8,128)} %design_ref.1, f32[19,2,8,128]{3,2,1,0:T(8,128)} %populations_ref.1, f32[19,2,8,128]{3,2,1,0:T(8,128)} %cotangent_ref.1, s32[2,8,128]{2,1,0:T(8,128)} %wall_ref.1, s32[2,8,128]{2,1,0:T(8,128)} %inlet_ref.1), custom_call_target="tpu_custom_call" | custom-call | tf_op jit(solution)/shard_map/pack/pallas_call | solution.py:672
  2.5 0.0 copy-start
  2.6 5.2 %all-to-all-start.1 = ((f32[8,5,2,8,128]{4,3,2,1,0:T(8,128)}), f32[8,5,2,8,128]{4,3,2,1,0:T(8,128)S(1)}, u32[]{:S(2)}, u32[]{:S(2)}) async-start(f32[8,5,2,8,128]{4,3,2,1,0:T(8,128)} %get-tuple-element.8), calls=%async_computation.1 | async-start | bytes 655360 | tf_op jit(solution)/shard_map/all_to_all | solution.py:698
  7.7 0.0 copy-done
  7.7 1.6 %collective-permute-start.2 = (f32[2,8,128]{2,1,0:T(8,128)S(1)}, f32[2,8,128]{2,1,0:T(8,128)S(1)}, u32[]{:S(2)}, u32[]{:S(2)}) collective-permute-start(f32[2,8,128]{2,1,0:T(8,128)S(1)} %copy-done), channel_id=1, source_target_pairs={{3,0},{0,1},{1,2},{2,3},{7,4},{4,5},{5,6},{6,7},{11,8},{8,9},{9,10... | collective-permute-start | bytes 24584 | tf_op jit(solution)/shard_map/ppermute | solution.py:701
  9.4 2.6 %collective-permute-start.1 = (f32[2,8,128]{2,1,0:T(8,128)S(1)}, f32[2,8,128]{2,1,0:T(8,128)S(1)}, u32[]{:S(2)}, u32[]{:S(2)}) collective-permute-start(f32[2,8,128]{2,1,0:T(8,128)S(1)} %copy-done), channel_id=1, source_target_pairs={{2,0},{3,1},{0,2},{1,3},{6,4},{7,5},{4,6},{5,7},{10,8},{11,9},{8,1... | collective-permute-start | bytes 24584 | tf_op jit(solution)/shard_map/ppermute | solution.py:701
  12.0 1.3 %collective-permute-start = (f32[2,8,128]{2,1,0:T(8,128)S(1)}, f32[2,8,128]{2,1,0:T(8,128)S(1)}, u32[]{:S(2)}, u32[]{:S(2)}) collective-permute-start(f32[2,8,128]{2,1,0:T(8,128)S(1)} %copy-done), channel_id=1, source_target_pairs={{1,0},{2,1},{3,2},{0,3},{5,4},{6,5},{7,6},{4,7},{9,8},{10,9},{11,1... | collective-permute-start | bytes 24584 | tf_op jit(solution)/shard_map/ppermute | solution.py:701
  13.3 0.0 collective-permute-done.2.refs_3_
  13.3 0.6 %collective-permute-done.1.refs_2_ = f32[2,8,128]{2,1,0:T(8,128)S(1)} collective-permute-done((f32[2,8,128]{2,1,0:T(8,128)S(1)}, f32[2,8,128]{2,1,0:T(8,128)S(1)}, u32[]{:S(2)}, u32[]{:S(2)}) %collective-permute-start.1) | collective-permute-done | bytes 8224 | tf_op jit(solution)/shard_map/ppermute | solution.py:701
  13.9 1.7 %collective-permute-done.refs_1_ = f32[2,8,128]{2,1,0:T(8,128)S(1)} collective-permute-done((f32[2,8,128]{2,1,0:T(8,128)S(1)}, f32[2,8,128]{2,1,0:T(8,128)S(1)}, u32[]{:S(2)}, u32[]{:S(2)}) %collective-permute-start) | collective-permute-done | bytes 8224 | tf_op jit(solution)/shard_map/ppermute | solution.py:701
  15.6 0.8 %spread.1 = f32[8,4,2,8,128]{4,3,2,1,0:T(8,128)} custom-call(f32[2,8,128]{2,1,0:T(8,128)S(1)} %copy-done, f32[2,8,128]{2,1,0:T(8,128)S(1)} %collective-permute-done.refs_1_, f32[2,8,128]{2,1,0:T(8,128)S(1)} %collective-permute-done.1.refs_2_, f32[2,8,128]{2,1,0:T(8,128)S(1)} %collective-permute-done.2.refs_3_), custom_call_target="tpu_custom_call" | custom-call | tf_op jit(solution)/shard_map/spread/pallas_call | solution.py:672
  16.4 0.0 all-to-all-done.1.packed_ref
  16.4 4.1 %all-to-all-start = ((f32[8,4,2,8,128]{4,3,2,1,0:T(8,128)}), f32[8,4,2,8,128]{4,3,2,1,0:T(8,128)S(1)}, u32[]{:S(2)}, u32[]{:S(2)}) async-start(f32[8,4,2,8,128]{4,3,2,1,0:T(8,128)} %spread.1), calls=%async_computation | async-start | bytes 524288 | tf_op jit(solution)/shard_map/all_to_all | solution.py:718
  20.6 0.2 arrange.1
  20.8 2.4 %collective-permute-start.3 = (f32[264,128]{1,0:T(8,128)S(1)}, f32[264,128]{1,0:T(8,128)S(1)}, u32[]{:S(2)}, u32[]{:S(2)}) collective-permute-start(f32[264,128]{1,0:T(8,128)S(1)} %get-tuple-element.10), channel_id=1, source_target_pairs={{0,8},{8,16},{16,24},{24,28},{28,20},{20,12},{12,4},{4,5},{5,13},{... | collective-permute-start | bytes 405512 | tf_op jit(solution)/shard_map/ppermute | solution.py:723
  23.2 1.3 %collective-permute-start.4 = (f32[264,128]{1,0:T(8,128)S(1)}, f32[264,128]{1,0:T(8,128)S(1)}, u32[]{:S(2)}, u32[]{:S(2)}) collective-permute-start(f32[264,128]{1,0:T(8,128)S(1)} %get-tuple-element.11), channel_id=1, source_target_pairs={{8,0},{16,8},{24,16},{28,24},{20,28},{12,20},{4,12},{5,4},{13,5},{... | collective-permute-start | bytes 405512 | tf_op jit(solution)/shard_map/ppermute | solution.py:724
  25.1 1.9 %all-to-all-done.copies_ref = f32[8,4,2,8,128]{4,3,2,1,0:T(8,128)S(1)} async-done(((f32[8,4,2,8,128]{4,3,2,1,0:T(8,128)}), f32[8,4,2,8,128]{4,3,2,1,0:T(8,128)S(1)}, u32[]{:S(2)}, u32[]{:S(2)}) %all-to-all-start) | async-done | bytes 262176 | tf_op jit(solution)/shard_map/all_to_all | solution.py:718
  27.0 0.8 %level.1.share_ref = f32[2,32,128]{2,1,0:T(8,128)S(1)} custom-call(s32[1]{0:T(128)} %bitcast.1.step_ref, f32[8,4,2,8,128]{4,3,2,1,0:T(8,128)S(1)} %all-to-all-done.copies_ref), custom_call_target="tpu_custom_call" | custom-call | tf_op jit(solution)/shard_map/level/pallas_call | solution.py:672
  27.9 0.0 collective-permute-done.3.before_ref
  27.9 0.0 collective-permute-done.4.after_ref
  27.9 1.6 %flow.1 = f32[8,5,8,128]{3,2,1,0:T(8,128)S(1)} custom-call(f32[2,32,128]{2,1,0:T(8,128)S(1)} %level.1.share_ref, f32[40,16,128]{2,1,0:T(8,128)S(1)} %get-tuple-element.9.body_ref, f32[264,128]{1,0:T(8,128)S(1)} %collective-permute-done.3.before_ref, f32[264,128]{1,0:T(8,128)S(1)} %collective-permute-done.4.after_ref), custom_call_target="tpu_custom_call" | custom-call | tf_op jit(solution)/shard_map/flow/pallas_call | solution.py:672
  29.5 10.9 %all_to_all.15.packed_ref = f32[8,5,8,128]{3,2,1,0:T(8,128)S(1)} all-to-all(f32[8,5,8,128]{3,2,1,0:T(8,128)S(1)} %flow.1), channel_id=1, replica_groups=mesh['grp'=4,'gy'=2,'gx'=4] {'grp','gy'}, dimensions={0} | all-to-all | bytes 327680 | tf_op jit(solution)/shard_map/all_to_all | solution.py:751
  40.4 0.8 %result.1 = (f32[19,2,8,128]{3,2,1,0:T(8,128)}, f32[2,8,128]{2,1,0:T(8,128)}) custom-call(f32[8,5,8,128]{3,2,1,0:T(8,128)S(1)} %all_to_all.15.packed_ref), custom_call_target="tpu_custom_call" | custom-call | tf_op jit(solution)/shard_map/result/pallas_call | solution.py:672
Async XLA Ops:
  2.5 5.2 %copy-start = (f32[2,8,128]{2,1,0:T(8,128)S(1)}, f32[2,8,128]{2,1,0:T(8,128)}, u32[]{:S(2)}) copy-start(f32[2,8,128]{2,1,0:T(8,128)} %get-tuple-element.7.refs_0_) | copy-start | bytes 24580
  2.6 13.9 %all-to-all-start.1 = ((f32[8,5,2,8,128]{4,3,2,1,0:T(8,128)}), f32[8,5,2,8,128]{4,3,2,1,0:T(8,128)S(1)}, u32[]{:S(2)}, u32[]{:S(2)}) async-start(f32[8,5,2,8,128]{4,3,2,1,0:T(8,128)} %get-tuple-element.8), calls=%async_computation.1 | async-start | bytes 655360 | tf_op jit(solution)/shard_map/all_to_all | solution.py:698
  7.7 5.6 %collective-permute-start.2 = (f32[2,8,128]{2,1,0:T(8,128)S(1)}, f32[2,8,128]{2,1,0:T(8,128)S(1)}, u32[]{:S(2)}, u32[]{:S(2)}) collective-permute-start(f32[2,8,128]{2,1,0:T(8,128)S(1)} %copy-done), channel_id=1, source_target_pairs={{3,0},{0,1},{1,2},{2,3},{7,4},{4,5},{5,6},{6,7},{11,8},{8,9},{9,10... | collective-permute-start | bytes 24584 | tf_op jit(solution)/shard_map/ppermute | solution.py:701
  9.4 4.5 %collective-permute-start.1 = (f32[2,8,128]{2,1,0:T(8,128)S(1)}, f32[2,8,128]{2,1,0:T(8,128)S(1)}, u32[]{:S(2)}, u32[]{:S(2)}) collective-permute-start(f32[2,8,128]{2,1,0:T(8,128)S(1)} %copy-done), channel_id=1, source_target_pairs={{2,0},{3,1},{0,2},{1,3},{6,4},{7,5},{4,6},{5,7},{10,8},{11,9},{8,1... | collective-permute-start | bytes 24584 | tf_op jit(solution)/shard_map/ppermute | solution.py:701
  12.0 3.7 %collective-permute-start = (f32[2,8,128]{2,1,0:T(8,128)S(1)}, f32[2,8,128]{2,1,0:T(8,128)S(1)}, u32[]{:S(2)}, u32[]{:S(2)}) collective-permute-start(f32[2,8,128]{2,1,0:T(8,128)S(1)} %copy-done), channel_id=1, source_target_pairs={{1,0},{2,1},{3,2},{0,3},{5,4},{6,5},{7,6},{4,7},{9,8},{10,9},{11,1... | collective-permute-start | bytes 24584 | tf_op jit(solution)/shard_map/ppermute | solution.py:701
  16.4 10.6 %all-to-all-start = ((f32[8,4,2,8,128]{4,3,2,1,0:T(8,128)}), f32[8,4,2,8,128]{4,3,2,1,0:T(8,128)S(1)}, u32[]{:S(2)}, u32[]{:S(2)}) async-start(f32[8,4,2,8,128]{4,3,2,1,0:T(8,128)} %spread.1), calls=%async_computation | async-start | bytes 524288 | tf_op jit(solution)/shard_map/all_to_all | solution.py:718
  20.8 7.1 %collective-permute-start.3 = (f32[264,128]{1,0:T(8,128)S(1)}, f32[264,128]{1,0:T(8,128)S(1)}, u32[]{:S(2)}, u32[]{:S(2)}) collective-permute-start(f32[264,128]{1,0:T(8,128)S(1)} %get-tuple-element.10), channel_id=1, source_target_pairs={{0,8},{8,16},{16,24},{24,28},{28,20},{20,12},{12,4},{4,5},{5,13},{... | collective-permute-start | bytes 405512 | tf_op jit(solution)/shard_map/ppermute | solution.py:723
  23.2 4.7 %collective-permute-start.4 = (f32[264,128]{1,0:T(8,128)S(1)}, f32[264,128]{1,0:T(8,128)S(1)}, u32[]{:S(2)}, u32[]{:S(2)}) collective-permute-start(f32[264,128]{1,0:T(8,128)S(1)} %get-tuple-element.11), channel_id=1, source_target_pairs={{8,0},{16,8},{24,16},{28,24},{20,28},{12,20},{4,12},{5,4},{13,5},{... | collective-permute-start | bytes 405512 | tf_op jit(solution)/shard_map/ppermute | solution.py:724

commit v10 on v7

--- a/solution.py
+++ b/solution.py
@@ -250,22 +250,24 @@
 
 def pack_kernel(
     splits, design_ref, populations_ref, cotangent_ref, wall_ref, inlet_ref, design_out_ref, packed_ref,
-    fields_ref, masks_ref, sems,
+    fields_ref, masks_ref, stage_ref, sems, out_sems,
 ):
     moves = [
         pltpu.make_async_copy(populations_ref, fields_ref.at[0:19], sems.at[0]),
-        pltpu.make_async_copy(cotangent_ref, fields_ref.at[19:38], sems.at[1]),
-        pltpu.make_async_copy(wall_ref, masks_ref.at[0], sems.at[2]),
-        pltpu.make_async_copy(inlet_ref, masks_ref.at[1], sems.at[3]),
+        pltpu.make_async_copy(wall_ref, masks_ref.at[0], sems.at[1]),
+        pltpu.make_async_copy(inlet_ref, masks_ref.at[1], sems.at[2]),
+        pltpu.make_async_copy(cotangent_ref, fields_ref.at[19:38], sems.at[3]),
         pltpu.make_async_copy(design_ref, design_out_ref, sems.at[4]),
     ]
     for move in moves:
         move.start()
-    for move in moves:
-        move.wait()
     devices = [device_at(index, 8 // splits, splits) for index in range(8)]
-    for layer in range(masks_ref.shape[1]):
-        for group in range(FIELDS // 8):
+    needs = {0: moves[:1], 2: moves[1:4]}
+    results = []
+    for group in range(FIELDS // 8):
+        for move in needs.get(group, ()):
+            move.wait()
+        for layer in range(masks_ref.shape[1]):
             values = []
             for slot in range(8):
                 index = group * 8 + slot
@@ -276,7 +278,11 @@
                 values.append(rolled(value, 16 * slot))
             values = mixed(values)
             for index in range(8):
-                packed_ref[devices[index], group, layer] = values[-index % 8]
+                stage_ref[group, devices[index], layer] = values[-index % 8]
+        results.append(pltpu.make_async_copy(stage_ref.at[group], packed_ref.at[:, group], out_sems.at[group]))
+        results[-1].start()
+    for move in results + moves[4:]:
+        move.wait()
 
 
 def arrange_kernel(splits, packed_ref, body_ref, first_ref, last_ref):
@@ -304,10 +310,10 @@
 
 
 def spread_kernel(size, *refs):
-    design_refs, (copies_ref, design_ref) = refs[:size], refs[size:]
+    design_refs, (copies_ref, design_ref, smooth_ref, sems) = refs[:size], refs[size:]
     here = lax.axis_index("gx")
     for turn in range(size):
-        design_ref[lax.rem(here + size - turn, size)] = design_refs[turn][...]
+        design_ref[here ^ turn] = design_refs[turn][...]
     lanes = lane_index()
     zero = jnp.zeros((8, LANES), jnp.float32)
     for layer in range(copies_ref.shape[2]):
@@ -315,12 +321,18 @@
         ahead = [rolled(tile, 1) for tile in tiles]
         behind = [rolled(tile, -1) for tile in tiles]
         for index in range(1, size + 1):
-            value = 0.5 * tiles[index] + 0.25 * (
+            smooth_ref[index - 1, layer] = 0.5 * tiles[index] + 0.25 * (
                 jnp.where(lanes == 0, ahead[index - 1], ahead[index])
                 + jnp.where(lanes == LANES - 1, behind[index + 1], behind[index])
             )
-            for device in range(copies_ref.shape[0]):
-                copies_ref[device, index - 1, layer] = value
+    moves = [
+        pltpu.make_async_copy(smooth_ref, copies_ref.at[device], sems.at[device])
+        for device in range(copies_ref.shape[0])
+    ]
+    for move in moves:
+        move.start()
+    for move in moves:
+        move.wait()
 
 
 def exponent(step_ref):
@@ -665,15 +677,15 @@
                 grad_ref[slot // 4] = value
 
 
-def call(kernel, outs, name, operands, spaces, scratch=(), room=32):
-    vmem = pl.BlockSpec(memory_space=pltpu.VMEM)
+def call(kernel, outs, name, operands, spaces, scratch=(), room=32, results=None):
     shapes = tuple(jax.ShapeDtypeStruct(shape, jnp.float32) for shape in outs)
+    places = tuple(pl.BlockSpec(memory_space=space) for space in results or [pltpu.VMEM] * len(outs))
     many = len(outs) > 1
     return pl.pallas_call(
         kernel,
         out_shape=shapes if many else shapes[0],
         in_specs=[pl.BlockSpec(memory_space=space) for space in spaces],
-        out_specs=(vmem,) * len(outs) if many else vmem,
+        out_specs=places if many else places[0],
         scratch_shapes=list(scratch),
         compiler_params=pltpu.CompilerParams(vmem_limit_bytes=room * 2**20),
         name=name,
@@ -692,20 +704,29 @@
         "pack",
         (design, populations, cotangent, wall_mask, inlet_mask),
         [pl.ANY] * 5,
-        [vmem((38, *tile), real), vmem((2, *tile), jnp.int32), pltpu.SemaphoreType.DMA((5,))],
+        [
+            vmem((38, *tile), real),
+            vmem((2, *tile), jnp.int32),
+            vmem((FIELDS // 8, plane, *tile), real),
+            pltpu.SemaphoreType.DMA((5,)),
+            pltpu.SemaphoreType.DMA((FIELDS // 8,)),
+        ],
         60,
+        [pl.ANY, pl.ANY],
     )
     packed = lax.all_to_all(packed, ("grp", "gy"), 0, 0)
     designs = [design]
-    for turn in range(1, size):
-        designs.append(lax.ppermute(design, "gx", [(i, (i + turn) % size) for i in range(size)]))
+    while len(designs) < size:
+        pairs = [(i, i ^ len(designs)) for i in range(size)]
+        designs += [lax.ppermute(value, "gx", pairs) for value in designs]
     copies = call(
         functools.partial(spread_kernel, size),
         ((plane, size, *tile),),
         "spread",
         designs,
         [vmem] * size,
-        [vmem((size, *tile), real)],
+        [vmem((size, *tile), real), vmem((size, *tile), real), pltpu.SemaphoreType.DMA((plane,))],
+        results=[pl.ANY],
     )
     outer = (-(-OUTER // 8) * 8, LANES)
     body, first, last = call(
@@ -756,7 +777,9 @@
     grp, splits = lax.axis_size("grp"), lax.axis_size("gy")
     layers, height, width = design.shape
     fits = height == 8 and width == LANES and layers * grp * height * splits == LANES
-    whole = body_by_columns if fits and grp * splits * 16 == LANES else body_by_blocks
+    size = lax.axis_size("gx")
+    fits = fits and grp * splits * 16 == LANES and size & (size - 1) == 0
+    whole = body_by_columns if fits else body_by_blocks
     return whole(design, populations, cotangent, wall_mask, inlet_mask, beta_step)
 
 

time: 42.9 us -> 43 us (level)
  waiting for transfers between devices: 6.33 us -> 4.38 us
  starting transfers between devices: 17.7 us -> 19.3 us
  blocking collectives: 10.4 us -> 11.1 us
    ppermute x3, waiting for transfers between devices: 4.44 us -> 2.48 us  [body_by_columns(): designs += [lax.ppermute(value, 'gx', pairs) for value in designs]]
    ppermute x3, starting transfers between devices: 4.67 us -> 6.3 us  [body_by_columns(): designs += [lax.ppermute(value, 'gx', pairs) for value in designs]]
    all_to_all x1, blocking collectives: 10.4 us -> 11.1 us  [body_by_columns(): packed = lax.all_to_all(packed, ('grp', 'gy'), 0, 0)]
  transfers between devices with their start and end apart: 7 -> 7, of which waited for: 4 -> 2; matrix products, arithmetic and copies ran while one was open for 0% -> 0% of each run, Pallas kernels for 5% -> 5%
where the time goes in v10:
time: 43 us; the launch traced here: 42.6 us
  starting transfers between devices  19.3 us (45%)
  blocking collectives  11.1 us (26%)
  Pallas kernels  6.42 us (15%)
  waiting for transfers between devices  4.38 us (10%)
  between operations  1.37 us (3%)
    all_to_all x1, blocking collectives, body_by_columns(): packed = lax.all_to_all(packed, ('grp', 'gy'), 0, 0)  11.1 us
    pallas_call x6, Pallas kernels, call(): pl.pallas_call(kernel, out_shape=shapes if many else shapes[0], in_specs=...  6.42 us
    ppermute x3, starting transfers between devices, body_by_columns(): designs += [lax.ppermute(value, 'gx', pairs) for value in designs]  6.3 us
    all_to_all x1, starting transfers between devices, body_by_columns(): packed = lax.all_to_all(packed, ('grp', 'gy'), 0, 0)  5.18 us
    all_to_all x1, starting transfers between devices, body_by_columns(): copies = lax.all_to_all(copies, ('grp', 'gy'), 0, 0)  4.14 us
    ppermute x3, waiting for transfers between devices, body_by_columns(): designs += [lax.ppermute(value, 'gx', pairs) for value in designs]  2.48 us
    ppermute x1, starting transfers between devices, body_by_columns(): before = lax.ppermute(last, line, up)  2.42 us
    all_to_all x1, waiting for transfers between devices, body_by_columns(): copies = lax.all_to_all(copies, ('grp', 'gy'), 0, 0)  1.89 us
  transfers between devices with their start and end apart: 7, of which 2 were waited for; matrix products, arithmetic and copies ran while one was open for 0% of the time, Pallas kernels for 5%

profile of v10, /device:TPU:0, one launch (start us, length us, event | category | flops | bytes accessed | tf_op | source)
XLA Modules:
  0.0 42.6 jit_solution(15020764555948200558)
XLA Ops:
  0.6 1.9 %pack.1 = (f32[2,8,128]{2,1,0:T(8,128)}, f32[8,5,2,8,128]{4,3,2,1,0:T(8,128)}) custom-call(f32[2,8,128]{2,1,0:T(8,128)} %design_ref.1, f32[19,2,8,128]{3,2,1,0:T(8,128)} %populations_ref.1, f32[19,2,8,128]{3,2,1,0:T(8,128)} %cotangent_ref.1, s32[2,8,128]{2,1,0:T(8,128)} %wall_ref.1, s32[2,8,128]{2,1,0:T(8,128)} %inlet_ref.1), custom_call_target="tpu_custom_call" | custom-call | tf_op jit(solution)/shard_map/pack/pallas_call | solution.py:684
  2.5 0.0 copy-start
  2.6 5.2 %all-to-all-start.1 = ((f32[8,5,2,8,128]{4,3,2,1,0:T(8,128)}), f32[8,5,2,8,128]{4,3,2,1,0:T(8,128)S(1)}, u32[]{:S(2)}, u32[]{:S(2)}) async-start(f32[8,5,2,8,128]{4,3,2,1,0:T(8,128)} %get-tuple-element.8), calls=%async_computation.1 | async-start | bytes 655360 | tf_op jit(solution)/shard_map/all_to_all | solution.py:717
  7.7 0.0 copy-done
  7.7 1.6 %collective-permute-start = (f32[2,8,128]{2,1,0:T(8,128)S(1)}, f32[2,8,128]{2,1,0:T(8,128)S(1)}, u32[]{:S(2)}, u32[]{:S(2)}) collective-permute-start(f32[2,8,128]{2,1,0:T(8,128)S(1)} %copy-done), channel_id=1, source_target_pairs={{0,1},{1,0},{2,3},{3,2},{4,5},{5,4},{6,7},{7,6},{8,9},{9,8},{10,11... | collective-permute-start | bytes 24584 | tf_op jit(solution)/shard_map/ppermute | solution.py:721
  9.4 2.6 %collective-permute-start.1 = (f32[2,8,128]{2,1,0:T(8,128)S(1)}, f32[2,8,128]{2,1,0:T(8,128)S(1)}, u32[]{:S(2)}, u32[]{:S(2)}) collective-permute-start(f32[2,8,128]{2,1,0:T(8,128)S(1)} %copy-done), channel_id=1, source_target_pairs={{0,2},{1,3},{2,0},{3,1},{4,6},{5,7},{6,4},{7,5},{8,10},{9,11},{10,... | collective-permute-start | bytes 24584 | tf_op jit(solution)/shard_map/ppermute | solution.py:721
  12.0 0.0 collective-permute-done.refs_1_
  12.0 2.1 %collective-permute-start.2 = (f32[2,8,128]{2,1,0:T(8,128)S(1)}, f32[2,8,128]{2,1,0:T(8,128)S(1)}, u32[]{:S(2)}, u32[]{:S(2)}) collective-permute-start(f32[2,8,128]{2,1,0:T(8,128)S(1)} %collective-permute-done.refs_1_), channel_id=1, source_target_pairs={{0,2},{1,3},{2,0},{3,1},{4,6},{5,7},{6,4},{7,5},{8,10},{9,11},{10,... | collective-permute-start | bytes 24584 | tf_op jit(solution)/shard_map/ppermute | solution.py:721
  14.0 0.0 collective-permute-done.1.refs_2_
  14.1 2.5 %collective-permute-done.2.refs_3_ = f32[2,8,128]{2,1,0:T(8,128)S(1)} collective-permute-done((f32[2,8,128]{2,1,0:T(8,128)S(1)}, f32[2,8,128]{2,1,0:T(8,128)S(1)}, u32[]{:S(2)}, u32[]{:S(2)}) %collective-permute-start.2) | collective-permute-done | bytes 8224 | tf_op jit(solution)/shard_map/ppermute | solution.py:721
  16.5 0.9 %spread.1 = f32[8,4,2,8,128]{4,3,2,1,0:T(8,128)} custom-call(f32[2,8,128]{2,1,0:T(8,128)S(1)} %copy-done, f32[2,8,128]{2,1,0:T(8,128)S(1)} %collective-permute-done.refs_1_, f32[2,8,128]{2,1,0:T(8,128)S(1)} %collective-permute-done.1.refs_2_, f32[2,8,128]{2,1,0:T(8,128)S(1)} %collective-permute-done.2.refs_3_), custom_call_target="tpu_custom_call" | custom-call | tf_op jit(solution)/shard_map/spread/pallas_call | solution.py:684
  17.4 0.0 all-to-all-done.1.packed_ref
  17.4 4.1 %all-to-all-start = ((f32[8,4,2,8,128]{4,3,2,1,0:T(8,128)}), f32[8,4,2,8,128]{4,3,2,1,0:T(8,128)S(1)}, u32[]{:S(2)}, u32[]{:S(2)}) async-start(f32[8,4,2,8,128]{4,3,2,1,0:T(8,128)} %spread.1), calls=%async_computation | async-start | bytes 524288 | tf_op jit(solution)/shard_map/all_to_all | solution.py:739
  21.6 0.2 arrange.1
  21.8 2.4 %collective-permute-start.3 = (f32[264,128]{1,0:T(8,128)S(1)}, f32[264,128]{1,0:T(8,128)S(1)}, u32[]{:S(2)}, u32[]{:S(2)}) collective-permute-start(f32[264,128]{1,0:T(8,128)S(1)} %get-tuple-element.10), channel_id=1, source_target_pairs={{0,8},{8,16},{16,24},{24,28},{28,20},{20,12},{12,4},{4,5},{5,13},{... | collective-permute-start | bytes 405512 | tf_op jit(solution)/shard_map/ppermute | solution.py:744
  24.2 1.3 %collective-permute-start.4 = (f32[264,128]{1,0:T(8,128)S(1)}, f32[264,128]{1,0:T(8,128)S(1)}, u32[]{:S(2)}, u32[]{:S(2)}) collective-permute-start(f32[264,128]{1,0:T(8,128)S(1)} %get-tuple-element.11), channel_id=1, source_target_pairs={{8,0},{16,8},{24,16},{28,24},{20,28},{12,20},{4,12},{5,4},{13,5},{... | collective-permute-start | bytes 405512 | tf_op jit(solution)/shard_map/ppermute | solution.py:745
  26.1 1.9 %all-to-all-done.copies_ref = f32[8,4,2,8,128]{4,3,2,1,0:T(8,128)S(1)} async-done(((f32[8,4,2,8,128]{4,3,2,1,0:T(8,128)}), f32[8,4,2,8,128]{4,3,2,1,0:T(8,128)S(1)}, u32[]{:S(2)}, u32[]{:S(2)}) %all-to-all-start) | async-done | bytes 262176 | tf_op jit(solution)/shard_map/all_to_all | solution.py:739
  28.0 1.0 %level.1.share_ref = f32[2,32,128]{2,1,0:T(8,128)S(1)} custom-call(s32[1]{0:T(128)} %bitcast.1.step_ref, f32[8,4,2,8,128]{4,3,2,1,0:T(8,128)S(1)} %all-to-all-done.copies_ref), custom_call_target="tpu_custom_call" | custom-call | tf_op jit(solution)/shard_map/level/pallas_call | solution.py:684
  29.1 0.0 collective-permute-done.3.before_ref
  29.1 0.0 collective-permute-done.4.after_ref
  29.1 1.6 %flow.1 = f32[8,5,8,128]{3,2,1,0:T(8,128)S(1)} custom-call(f32[2,32,128]{2,1,0:T(8,128)S(1)} %level.1.share_ref, f32[40,16,128]{2,1,0:T(8,128)S(1)} %get-tuple-element.9.body_ref, f32[264,128]{1,0:T(8,128)S(1)} %collective-permute-done.3.before_ref, f32[264,128]{1,0:T(8,128)S(1)} %collective-permute-done.4.after_ref), custom_call_target="tpu_custom_call" | custom-call | tf_op jit(solution)/shard_map/flow/pallas_call | solution.py:684
  30.7 11.1 %all_to_all.15.packed_ref = f32[8,5,8,128]{3,2,1,0:T(8,128)S(1)} all-to-all(f32[8,5,8,128]{3,2,1,0:T(8,128)S(1)} %flow.1), channel_id=1, replica_groups=mesh['grp'=4,'gy'=2,'gx'=4] {'grp','gy'}, dimensions={0} | all-to-all | bytes 327680 | tf_op jit(solution)/shard_map/all_to_all | solution.py:772
  41.8 0.8 %result.1 = (f32[19,2,8,128]{3,2,1,0:T(8,128)}, f32[2,8,128]{2,1,0:T(8,128)}) custom-call(f32[8,5,8,128]{3,2,1,0:T(8,128)S(1)} %all_to_all.15.packed_ref), custom_call_target="tpu_custom_call" | custom-call | tf_op jit(solution)/shard_map/result/pallas_call | solution.py:684
Async XLA Ops:
  2.5 5.2 %copy-start = (f32[2,8,128]{2,1,0:T(8,128)S(1)}, f32[2,8,128]{2,1,0:T(8,128)}, u32[]{:S(2)}) copy-start(f32[2,8,128]{2,1,0:T(8,128)} %get-tuple-element.7.refs_0_) | copy-start | bytes 24580
  2.6 14.9 %all-to-all-start.1 = ((f32[8,5,2,8,128]{4,3,2,1,0:T(8,128)}), f32[8,5,2,8,128]{4,3,2,1,0:T(8,128)S(1)}, u32[]{:S(2)}, u32[]{:S(2)}) async-start(f32[8,5,2,8,128]{4,3,2,1,0:T(8,128)} %get-tuple-element.8), calls=%async_computation.1 | async-start | bytes 655360 | tf_op jit(solution)/shard_map/all_to_all | solution.py:717
  7.7 4.2 %collective-permute-start = (f32[2,8,128]{2,1,0:T(8,128)S(1)}, f32[2,8,128]{2,1,0:T(8,128)S(1)}, u32[]{:S(2)}, u32[]{:S(2)}) collective-permute-start(f32[2,8,128]{2,1,0:T(8,128)S(1)} %copy-done), channel_id=1, source_target_pairs={{0,1},{1,0},{2,3},{3,2},{4,5},{5,4},{6,7},{7,6},{8,9},{9,8},{10,11... | collective-permute-start | bytes 24584 | tf_op jit(solution)/shard_map/ppermute | solution.py:721
  9.4 4.7 %collective-permute-start.1 = (f32[2,8,128]{2,1,0:T(8,128)S(1)}, f32[2,8,128]{2,1,0:T(8,128)S(1)}, u32[]{:S(2)}, u32[]{:S(2)}) collective-permute-start(f32[2,8,128]{2,1,0:T(8,128)S(1)} %copy-done), channel_id=1, source_target_pairs={{0,2},{1,3},{2,0},{3,1},{4,6},{5,7},{6,4},{7,5},{8,10},{9,11},{10,... | collective-permute-start | bytes 24584 | tf_op jit(solution)/shard_map/ppermute | solution.py:721
  12.0 4.6 %collective-permute-start.2 = (f32[2,8,128]{2,1,0:T(8,128)S(1)}, f32[2,8,128]{2,1,0:T(8,128)S(1)}, u32[]{:S(2)}, u32[]{:S(2)}) collective-permute-start(f32[2,8,128]{2,1,0:T(8,128)S(1)} %collective-permute-done.refs_1_), channel_id=1, source_target_pairs={{0,2},{1,3},{2,0},{3,1},{4,6},{5,7},{6,4},{7,5},{8,10},{9,11},{10,... | collective-permute-start | bytes 24584 | tf_op jit(solution)/shard_map/ppermute | solution.py:721
  17.4 10.6 %all-to-all-start = ((f32[8,4,2,8,128]{4,3,2,1,0:T(8,128)}), f32[8,4,2,8,128]{4,3,2,1,0:T(8,128)S(1)}, u32[]{:S(2)}, u32[]{:S(2)}) async-start(f32[8,4,2,8,128]{4,3,2,1,0:T(8,128)} %spread.1), calls=%async_computation | async-start | bytes 524288 | tf_op jit(solution)/shard_map/all_to_all | solution.py:739
  21.8 7.3 %collective-permute-start.3 = (f32[264,128]{1,0:T(8,128)S(1)}, f32[264,128]{1,0:T(8,128)S(1)}, u32[]{:S(2)}, u32[]{:S(2)}) collective-permute-start(f32[264,128]{1,0:T(8,128)S(1)} %get-tuple-element.10), channel_id=1, source_target_pairs={{0,8},{8,16},{16,24},{24,28},{28,20},{20,12},{12,4},{4,5},{5,13},{... | collective-permute-start | bytes 405512 | tf_op jit(solution)/shard_map/ppermute | solution.py:744
  24.2 4.9 %collective-permute-start.4 = (f32[264,128]{1,0:T(8,128)S(1)}, f32[264,128]{1,0:T(8,128)S(1)}, u32[]{:S(2)}, u32[]{:S(2)}) collective-permute-start(f32[264,128]{1,0:T(8,128)S(1)} %get-tuple-element.11), channel_id=1, source_target_pairs={{8,0},{16,8},{24,16},{28,24},{20,28},{12,20},{4,12},{5,4},{13,5},{... | collective-permute-start | bytes 405512 | tf_op jit(solution)/shard_map/ppermute | solution.py:745

commit v11 on v9

--- a/solution.py
+++ b/solution.py
@@ -378,16 +378,16 @@
     def advance(state):
         low, high, low_known, high_known, middle, _ = state
         level = jnp.exp(2.0 * beta * middle)
-        sums, squares = [zero] * 4, [zero] * 4
+        sums, slopes = [zero] * 4, [zero] * 4
         for index, row in enumerate(range(0, columns, 8)):
-            raised = raised_ref[row : row + 8, :] + level
-            part = pl.reciprocal(raised, approx=True)
-            part = part * (2.0 - raised * part)
-            sums[index % 4] = sums[index % 4] + part
-            squares[index % 4] = squares[index % 4] + part * part
-        first, second = total(sums), total(squares)
-        volume = cells - (1.0 + level) * first
-        slope = first - (1.0 + level) * second
+            raised = raised_ref[row : row + 8, :]
+            below = raised + level
+            part = pl.reciprocal(below, approx=True)
+            part = part * (2.0 - below * part)
+            share = (raised - 1.0) * part
+            sums[index % 4] = sums[index % 4] + share
+            slopes[index % 4] = slopes[index % 4] + share * part
+        volume, slope = total(sums), total(slopes)
         whole = (top + level) * scale
         excess = volume * whole - fluid_share * cells
         slope = (2.0 * beta * level) * (volume * scale - whole * slope)

time: 41.6 us -> 41.6 us (level)
  transfers between devices with their start and end apart: 7 -> 7, of which waited for: 3 -> 3; matrix products, arithmetic and copies ran while one was open for 0% -> 0% of each run, Pallas kernels for 4% -> 5%
where the time goes in v11:
time: 41.6 us; the launch traced here: 41.2 us
  starting transfers between devices  18.6 us (45%)
  blocking collectives  10.6 us (25%)
  Pallas kernels  6.43 us (15%)
  waiting for transfers between devices  4.2 us (10%)
  between operations  1.35 us (3%)
    all_to_all x1, blocking collectives, body_by_columns(): packed = lax.all_to_all(packed, ('grp', 'gy'), 0, 0)  10.6 us
    pallas_call x6, Pallas kernels, call(): pl.pallas_call(kernel, out_shape=shapes if many else shapes[0], in_specs=...  6.43 us
    ppermute x3, starting transfers between devices, body_by_columns(): lax.ppermute(design, 'gx', [((i + turn) % size, i) for i in range(size)])  5.57 us
    all_to_all x1, starting transfers between devices, body_by_columns(): packed = lax.all_to_all(packed, ('grp', 'gy'), 0, 0)  5.18 us
    all_to_all x1, starting transfers between devices, body_by_columns(): copies = lax.all_to_all(copies, ('grp', 'gy'), 0, 0)  4.14 us
    ppermute x1, starting transfers between devices, body_by_columns(): before = lax.ppermute(last, line, up)  2.42 us
    ppermute x3, waiting for transfers between devices, body_by_columns(): lax.ppermute(design, 'gx', [((i + turn) % size, i) for i in range(size)])  2.3 us
    all_to_all x1, waiting for transfers between devices, body_by_columns(): copies = lax.all_to_all(copies, ('grp', 'gy'), 0, 0)  1.89 us
  transfers between devices with their start and end apart: 7, of which 3 were waited for; matrix products, arithmetic and copies ran while one was open for 0% of the time, Pallas kernels for 5%

profile of v11, /device:TPU:0, one launch (start us, length us, event | category | flops | bytes accessed | tf_op | source)
XLA Modules:
  0.0 41.2 jit_solution(6106223537110558901)
XLA Ops:
  0.6 1.9 %pack.1 = (f32[2,8,128]{2,1,0:T(8,128)}, f32[8,5,2,8,128]{4,3,2,1,0:T(8,128)}) custom-call(f32[2,8,128]{2,1,0:T(8,128)} %design_ref.1, f32[19,2,8,128]{3,2,1,0:T(8,128)} %populations_ref.1, f32[19,2,8,128]{3,2,1,0:T(8,128)} %cotangent_ref.1, s32[2,8,128]{2,1,0:T(8,128)} %wall_ref.1, s32[2,8,128]{2,1,0:T(8,128)} %inlet_ref.1), custom_call_target="tpu_custom_call" | custom-call | tf_op jit(solution)/shard_map/pack/pallas_call | solution.py:672
  2.5 0.0 copy-start
  2.6 5.2 %all-to-all-start.1 = ((f32[8,5,2,8,128]{4,3,2,1,0:T(8,128)}), f32[8,5,2,8,128]{4,3,2,1,0:T(8,128)S(1)}, u32[]{:S(2)}, u32[]{:S(2)}) async-start(f32[8,5,2,8,128]{4,3,2,1,0:T(8,128)} %get-tuple-element.8), calls=%async_computation.1 | async-start | bytes 655360 | tf_op jit(solution)/shard_map/all_to_all | solution.py:698
  7.7 0.0 copy-done
  7.7 1.6 %collective-permute-start.2 = (f32[2,8,128]{2,1,0:T(8,128)S(1)}, f32[2,8,128]{2,1,0:T(8,128)S(1)}, u32[]{:S(2)}, u32[]{:S(2)}) collective-permute-start(f32[2,8,128]{2,1,0:T(8,128)S(1)} %copy-done), channel_id=1, source_target_pairs={{3,0},{0,1},{1,2},{2,3},{7,4},{4,5},{5,6},{6,7},{11,8},{8,9},{9,10... | collective-permute-start | bytes 24584 | tf_op jit(solution)/shard_map/ppermute | solution.py:701
  9.4 2.6 %collective-permute-start.1 = (f32[2,8,128]{2,1,0:T(8,128)S(1)}, f32[2,8,128]{2,1,0:T(8,128)S(1)}, u32[]{:S(2)}, u32[]{:S(2)}) collective-permute-start(f32[2,8,128]{2,1,0:T(8,128)S(1)} %copy-done), channel_id=1, source_target_pairs={{2,0},{3,1},{0,2},{1,3},{6,4},{7,5},{4,6},{5,7},{10,8},{11,9},{8,1... | collective-permute-start | bytes 24584 | tf_op jit(solution)/shard_map/ppermute | solution.py:701
  12.0 1.3 %collective-permute-start = (f32[2,8,128]{2,1,0:T(8,128)S(1)}, f32[2,8,128]{2,1,0:T(8,128)S(1)}, u32[]{:S(2)}, u32[]{:S(2)}) collective-permute-start(f32[2,8,128]{2,1,0:T(8,128)S(1)} %copy-done), channel_id=1, source_target_pairs={{1,0},{2,1},{3,2},{0,3},{5,4},{6,5},{7,6},{4,7},{9,8},{10,9},{11,1... | collective-permute-start | bytes 24584 | tf_op jit(solution)/shard_map/ppermute | solution.py:701
  13.3 0.0 collective-permute-done.2.refs_3_
  13.3 0.6 %collective-permute-done.1.refs_2_ = f32[2,8,128]{2,1,0:T(8,128)S(1)} collective-permute-done((f32[2,8,128]{2,1,0:T(8,128)S(1)}, f32[2,8,128]{2,1,0:T(8,128)S(1)}, u32[]{:S(2)}, u32[]{:S(2)}) %collective-permute-start.1) | collective-permute-done | bytes 8224 | tf_op jit(solution)/shard_map/ppermute | solution.py:701
  13.9 1.7 %collective-permute-done.refs_1_ = f32[2,8,128]{2,1,0:T(8,128)S(1)} collective-permute-done((f32[2,8,128]{2,1,0:T(8,128)S(1)}, f32[2,8,128]{2,1,0:T(8,128)S(1)}, u32[]{:S(2)}, u32[]{:S(2)}) %collective-permute-start) | collective-permute-done | bytes 8224 | tf_op jit(solution)/shard_map/ppermute | solution.py:701
  15.6 0.8 %spread.1 = f32[8,4,2,8,128]{4,3,2,1,0:T(8,128)} custom-call(f32[2,8,128]{2,1,0:T(8,128)S(1)} %copy-done, f32[2,8,128]{2,1,0:T(8,128)S(1)} %collective-permute-done.refs_1_, f32[2,8,128]{2,1,0:T(8,128)S(1)} %collective-permute-done.1.refs_2_, f32[2,8,128]{2,1,0:T(8,128)S(1)} %collective-permute-done.2.refs_3_), custom_call_target="tpu_custom_call" | custom-call | tf_op jit(solution)/shard_map/spread/pallas_call | solution.py:672
  16.4 0.0 all-to-all-done.1.packed_ref
  16.4 4.1 %all-to-all-start = ((f32[8,4,2,8,128]{4,3,2,1,0:T(8,128)}), f32[8,4,2,8,128]{4,3,2,1,0:T(8,128)S(1)}, u32[]{:S(2)}, u32[]{:S(2)}) async-start(f32[8,4,2,8,128]{4,3,2,1,0:T(8,128)} %spread.1), calls=%async_computation | async-start | bytes 524288 | tf_op jit(solution)/shard_map/all_to_all | solution.py:718
  20.6 0.2 arrange.1
  20.8 2.4 %collective-permute-start.3 = (f32[264,128]{1,0:T(8,128)S(1)}, f32[264,128]{1,0:T(8,128)S(1)}, u32[]{:S(2)}, u32[]{:S(2)}) collective-permute-start(f32[264,128]{1,0:T(8,128)S(1)} %get-tuple-element.10), channel_id=1, source_target_pairs={{0,8},{8,16},{16,24},{24,28},{28,20},{20,12},{12,4},{4,5},{5,13},{... | collective-permute-start | bytes 405512 | tf_op jit(solution)/shard_map/ppermute | solution.py:723
  23.2 1.3 %collective-permute-start.4 = (f32[264,128]{1,0:T(8,128)S(1)}, f32[264,128]{1,0:T(8,128)S(1)}, u32[]{:S(2)}, u32[]{:S(2)}) collective-permute-start(f32[264,128]{1,0:T(8,128)S(1)} %get-tuple-element.11), channel_id=1, source_target_pairs={{8,0},{16,8},{24,16},{28,24},{20,28},{12,20},{4,12},{5,4},{13,5},{... | collective-permute-start | bytes 405512 | tf_op jit(solution)/shard_map/ppermute | solution.py:724
  25.1 1.9 %all-to-all-done.copies_ref = f32[8,4,2,8,128]{4,3,2,1,0:T(8,128)S(1)} async-done(((f32[8,4,2,8,128]{4,3,2,1,0:T(8,128)}), f32[8,4,2,8,128]{4,3,2,1,0:T(8,128)S(1)}, u32[]{:S(2)}, u32[]{:S(2)}) %all-to-all-start) | async-done | bytes 262176 | tf_op jit(solution)/shard_map/all_to_all | solution.py:718
  27.0 1.1 %level.1.share_ref = f32[2,32,128]{2,1,0:T(8,128)S(1)} custom-call(s32[1]{0:T(128)} %bitcast.1.step_ref, f32[8,4,2,8,128]{4,3,2,1,0:T(8,128)S(1)} %all-to-all-done.copies_ref), custom_call_target="tpu_custom_call" | custom-call | tf_op jit(solution)/shard_map/level/pallas_call | solution.py:672
  28.1 0.0 collective-permute-done.3.before_ref
  28.2 0.0 collective-permute-done.4.after_ref
  28.2 1.6 %flow.1 = f32[8,5,8,128]{3,2,1,0:T(8,128)S(1)} custom-call(f32[2,32,128]{2,1,0:T(8,128)S(1)} %level.1.share_ref, f32[40,16,128]{2,1,0:T(8,128)S(1)} %get-tuple-element.9.body_ref, f32[264,128]{1,0:T(8,128)S(1)} %collective-permute-done.3.before_ref, f32[264,128]{1,0:T(8,128)S(1)} %collective-permute-done.4.after_ref), custom_call_target="tpu_custom_call" | custom-call | tf_op jit(solution)/shard_map/flow/pallas_call | solution.py:672
  29.8 10.6 %all_to_all.15.packed_ref = f32[8,5,8,128]{3,2,1,0:T(8,128)S(1)} all-to-all(f32[8,5,8,128]{3,2,1,0:T(8,128)S(1)} %flow.1), channel_id=1, replica_groups=mesh['grp'=4,'gy'=2,'gx'=4] {'grp','gy'}, dimensions={0} | all-to-all | bytes 327680 | tf_op jit(solution)/shard_map/all_to_all | solution.py:751
  40.4 0.8 %result.1 = (f32[19,2,8,128]{3,2,1,0:T(8,128)}, f32[2,8,128]{2,1,0:T(8,128)}) custom-call(f32[8,5,8,128]{3,2,1,0:T(8,128)S(1)} %all_to_all.15.packed_ref), custom_call_target="tpu_custom_call" | custom-call | tf_op jit(solution)/shard_map/result/pallas_call | solution.py:672
Async XLA Ops:
  2.5 5.2 %copy-start = (f32[2,8,128]{2,1,0:T(8,128)S(1)}, f32[2,8,128]{2,1,0:T(8,128)}, u32[]{:S(2)}) copy-start(f32[2,8,128]{2,1,0:T(8,128)} %get-tuple-element.7.refs_0_) | copy-start | bytes 24580
  2.6 13.9 %all-to-all-start.1 = ((f32[8,5,2,8,128]{4,3,2,1,0:T(8,128)}), f32[8,5,2,8,128]{4,3,2,1,0:T(8,128)S(1)}, u32[]{:S(2)}, u32[]{:S(2)}) async-start(f32[8,5,2,8,128]{4,3,2,1,0:T(8,128)} %get-tuple-element.8), calls=%async_computation.1 | async-start | bytes 655360 | tf_op jit(solution)/shard_map/all_to_all | solution.py:698
  7.7 5.6 %collective-permute-start.2 = (f32[2,8,128]{2,1,0:T(8,128)S(1)}, f32[2,8,128]{2,1,0:T(8,128)S(1)}, u32[]{:S(2)}, u32[]{:S(2)}) collective-permute-start(f32[2,8,128]{2,1,0:T(8,128)S(1)} %copy-done), channel_id=1, source_target_pairs={{3,0},{0,1},{1,2},{2,3},{7,4},{4,5},{5,6},{6,7},{11,8},{8,9},{9,10... | collective-permute-start | bytes 24584 | tf_op jit(solution)/shard_map/ppermute | solution.py:701
  9.4 4.5 %collective-permute-start.1 = (f32[2,8,128]{2,1,0:T(8,128)S(1)}, f32[2,8,128]{2,1,0:T(8,128)S(1)}, u32[]{:S(2)}, u32[]{:S(2)}) collective-permute-start(f32[2,8,128]{2,1,0:T(8,128)S(1)} %copy-done), channel_id=1, source_target_pairs={{2,0},{3,1},{0,2},{1,3},{6,4},{7,5},{4,6},{5,7},{10,8},{11,9},{8,1... | collective-permute-start | bytes 24584 | tf_op jit(solution)/shard_map/ppermute | solution.py:701
  12.0 3.7 %collective-permute-start = (f32[2,8,128]{2,1,0:T(8,128)S(1)}, f32[2,8,128]{2,1,0:T(8,128)S(1)}, u32[]{:S(2)}, u32[]{:S(2)}) collective-permute-start(f32[2,8,128]{2,1,0:T(8,128)S(1)} %copy-done), channel_id=1, source_target_pairs={{1,0},{2,1},{3,2},{0,3},{5,4},{6,5},{7,6},{4,7},{9,8},{10,9},{11,1... | collective-permute-start | bytes 24584 | tf_op jit(solution)/shard_map/ppermute | solution.py:701
  16.4 10.6 %all-to-all-start = ((f32[8,4,2,8,128]{4,3,2,1,0:T(8,128)}), f32[8,4,2,8,128]{4,3,2,1,0:T(8,128)S(1)}, u32[]{:S(2)}, u32[]{:S(2)}) async-start(f32[8,4,2,8,128]{4,3,2,1,0:T(8,128)} %spread.1), calls=%async_computation | async-start | bytes 524288 | tf_op jit(solution)/shard_map/all_to_all | solution.py:718
  20.8 7.4 %collective-permute-start.3 = (f32[264,128]{1,0:T(8,128)S(1)}, f32[264,128]{1,0:T(8,128)S(1)}, u32[]{:S(2)}, u32[]{:S(2)}) collective-permute-start(f32[264,128]{1,0:T(8,128)S(1)} %get-tuple-element.10), channel_id=1, source_target_pairs={{0,8},{8,16},{16,24},{24,28},{28,20},{20,12},{12,4},{4,5},{5,13},{... | collective-permute-start | bytes 405512 | tf_op jit(solution)/shard_map/ppermute | solution.py:723
  23.2 5.0 %collective-permute-start.4 = (f32[264,128]{1,0:T(8,128)S(1)}, f32[264,128]{1,0:T(8,128)S(1)}, u32[]{:S(2)}, u32[]{:S(2)}) collective-permute-start(f32[264,128]{1,0:T(8,128)S(1)} %get-tuple-element.11), channel_id=1, source_target_pairs={{8,0},{16,8},{24,16},{28,24},{20,28},{12,20},{4,12},{5,4},{13,5},{... | collective-permute-start | bytes 405512 | tf_op jit(solution)/shard_map/ppermute | solution.py:724

commit v12 on v11

--- a/solution.py
+++ b/solution.py
@@ -303,11 +303,15 @@
         ref[OUTER:, :] = jnp.zeros((rest, LANES), jnp.float32)
 
 
+def turns_of(size):
+    return sorted(range(size), key=lambda turn: (turn != 0, turn != size // 2, turn))
+
+
 def spread_kernel(size, *refs):
     design_refs, (copies_ref, design_ref) = refs[:size], refs[size:]
     here = lax.axis_index("gx")
-    for turn in range(size):
-        design_ref[lax.rem(here + turn, size)] = design_refs[turn][...]
+    for turn, ref in zip(turns_of(size), design_refs):
+        design_ref[lax.rem(here + turn, size)] = ref[...]
     lanes = lane_index()
     zero = jnp.zeros((8, LANES), jnp.float32)
     for layer in range(copies_ref.shape[2]):
@@ -703,7 +707,7 @@
         functools.partial(spread_kernel, size),
         ((plane, size, *tile),),
         "spread",
-        designs,
+        [designs[turn] for turn in turns_of(size)],
         [vmem] * size,
         [vmem((size, *tile), real)],
     )

time: 41.6 us -> 42.2 us (1.014)
  waiting for transfers between devices: 4.2 us -> 5.65 us
  starting transfers between devices: 18.6 us -> 17.7 us
    ppermute x3, waiting for transfers between devices: 2.3 us -> 3.76 us  [body_by_columns(): lax.ppermute(design, 'gx', [((i + turn) % size, i) for i in range(size)])]
    ppermute x3, starting transfers between devices: 5.57 us -> 4.67 us  [body_by_columns(): lax.ppermute(design, 'gx', [((i + turn) % size, i) for i in range(size)])]
  transfers between devices with their start and end apart: 7 -> 7, of which waited for: 3 -> 3; matrix products, arithmetic and copies ran while one was open for 0% -> 0% of each run, Pallas kernels for 5% -> 6%
where the time goes in v12:
time: 42.2 us; the launch traced here: 41.7 us
  starting transfers between devices  17.7 us (42%)
  blocking collectives  10.4 us (25%)
  Pallas kernels  6.65 us (16%)
  waiting for transfers between devices  5.65 us (13%)
  between operations  1.35 us (3%)
    all_to_all x1, blocking collectives, body_by_columns(): packed = lax.all_to_all(packed, ('grp', 'gy'), 0, 0)  10.4 us
    pallas_call x6, Pallas kernels, call(): pl.pallas_call(kernel, out_shape=shapes if many else shapes[0], in_specs=...  6.65 us
    all_to_all x1, starting transfers between devices, body_by_columns(): packed = lax.all_to_all(packed, ('grp', 'gy'), 0, 0)  5.18 us
    ppermute x3, starting transfers between devices, body_by_columns(): lax.ppermute(design, 'gx', [((i + turn) % size, i) for i in range(size)])  4.67 us
    all_to_all x1, starting transfers between devices, body_by_columns(): copies = lax.all_to_all(copies, ('grp', 'gy'), 0, 0)  4.14 us
    ppermute x3, waiting for transfers between devices, body_by_columns(): lax.ppermute(design, 'gx', [((i + turn) % size, i) for i in range(size)])  3.76 us
    ppermute x1, starting transfers between devices, body_by_columns(): before = lax.ppermute(last, line, up)  2.42 us
    all_to_all x1, waiting for transfers between devices, body_by_columns(): copies = lax.all_to_all(copies, ('grp', 'gy'), 0, 0)  1.89 us
  transfers between devices with their start and end apart: 7, of which 3 were waited for; matrix products, arithmetic and copies ran while one was open for 0% of the time, Pallas kernels for 6%

profile of v12, /device:TPU:0, one launch (start us, length us, event | category | flops | bytes accessed | tf_op | source)
XLA Modules:
  0.0 41.7 jit_solution(12406928221943855091)
XLA Ops:
  0.6 1.9 %pack.1 = (f32[2,8,128]{2,1,0:T(8,128)}, f32[8,5,2,8,128]{4,3,2,1,0:T(8,128)}) custom-call(f32[2,8,128]{2,1,0:T(8,128)} %design_ref.1, f32[19,2,8,128]{3,2,1,0:T(8,128)} %populations_ref.1, f32[19,2,8,128]{3,2,1,0:T(8,128)} %cotangent_ref.1, s32[2,8,128]{2,1,0:T(8,128)} %wall_ref.1, s32[2,8,128]{2,1,0:T(8,128)} %inlet_ref.1), custom_call_target="tpu_custom_call" | custom-call | tf_op jit(solution)/shard_map/pack/pallas_call | solution.py:676
  2.5 0.0 copy-start
  2.6 5.2 %all-to-all-start.1 = ((f32[8,5,2,8,128]{4,3,2,1,0:T(8,128)}), f32[8,5,2,8,128]{4,3,2,1,0:T(8,128)S(1)}, u32[]{:S(2)}, u32[]{:S(2)}) async-start(f32[8,5,2,8,128]{4,3,2,1,0:T(8,128)} %get-tuple-element.8), calls=%async_computation.1 | async-start | bytes 655360 | tf_op jit(solution)/shard_map/all_to_all | solution.py:702
  7.7 0.0 copy-done
  7.7 1.6 %collective-permute-start.2 = (f32[2,8,128]{2,1,0:T(8,128)S(1)}, f32[2,8,128]{2,1,0:T(8,128)S(1)}, u32[]{:S(2)}, u32[]{:S(2)}) collective-permute-start(f32[2,8,128]{2,1,0:T(8,128)S(1)} %copy-done), channel_id=1, source_target_pairs={{3,0},{0,1},{1,2},{2,3},{7,4},{4,5},{5,6},{6,7},{11,8},{8,9},{9,10... | collective-permute-start | bytes 24584 | tf_op jit(solution)/shard_map/ppermute | solution.py:705
  9.4 2.2 %collective-permute-start.1 = (f32[2,8,128]{2,1,0:T(8,128)S(1)}, f32[2,8,128]{2,1,0:T(8,128)S(1)}, u32[]{:S(2)}, u32[]{:S(2)}) collective-permute-start(f32[2,8,128]{2,1,0:T(8,128)S(1)} %copy-done), channel_id=1, source_target_pairs={{1,0},{2,1},{3,2},{0,3},{5,4},{6,5},{7,6},{4,7},{9,8},{10,9},{11,1... | collective-permute-start | bytes 24584 | tf_op jit(solution)/shard_map/ppermute | solution.py:705
  11.6 0.8 %collective-permute-start = (f32[2,8,128]{2,1,0:T(8,128)S(1)}, f32[2,8,128]{2,1,0:T(8,128)S(1)}, u32[]{:S(2)}, u32[]{:S(2)}) collective-permute-start(f32[2,8,128]{2,1,0:T(8,128)S(1)} %copy-done), channel_id=1, source_target_pairs={{2,0},{3,1},{0,2},{1,3},{6,4},{7,5},{4,6},{5,7},{10,8},{11,9},{8,1... | collective-permute-start | bytes 24584 | tf_op jit(solution)/shard_map/ppermute | solution.py:705
  12.4 0.9 %collective-permute-done.2.refs_3_ = f32[2,8,128]{2,1,0:T(8,128)S(1)} collective-permute-done((f32[2,8,128]{2,1,0:T(8,128)S(1)}, f32[2,8,128]{2,1,0:T(8,128)S(1)}, u32[]{:S(2)}, u32[]{:S(2)}) %collective-permute-start.2) | collective-permute-done | bytes 8224 | tf_op jit(solution)/shard_map/ppermute | solution.py:705
  13.3 0.0 collective-permute-done.1.refs_2_
  13.3 2.8 %collective-permute-done.refs_1_ = f32[2,8,128]{2,1,0:T(8,128)S(1)} collective-permute-done((f32[2,8,128]{2,1,0:T(8,128)S(1)}, f32[2,8,128]{2,1,0:T(8,128)S(1)}, u32[]{:S(2)}, u32[]{:S(2)}) %collective-permute-start) | collective-permute-done | bytes 8224 | tf_op jit(solution)/shard_map/ppermute | solution.py:705
  16.2 0.8 %spread.1 = f32[8,4,2,8,128]{4,3,2,1,0:T(8,128)} custom-call(f32[2,8,128]{2,1,0:T(8,128)S(1)} %copy-done, f32[2,8,128]{2,1,0:T(8,128)S(1)} %collective-permute-done.refs_1_, f32[2,8,128]{2,1,0:T(8,128)S(1)} %collective-permute-done.1.refs_2_, f32[2,8,128]{2,1,0:T(8,128)S(1)} %collective-permute-done.2.refs_3_), custom_call_target="tpu_custom_call" | custom-call | tf_op jit(solution)/shard_map/spread/pallas_call | solution.py:676
  17.0 0.0 all-to-all-done.1.packed_ref
  17.0 4.1 %all-to-all-start = ((f32[8,4,2,8,128]{4,3,2,1,0:T(8,128)}), f32[8,4,2,8,128]{4,3,2,1,0:T(8,128)S(1)}, u32[]{:S(2)}, u32[]{:S(2)}) async-start(f32[8,4,2,8,128]{4,3,2,1,0:T(8,128)} %spread.1), calls=%async_computation | async-start | bytes 524288 | tf_op jit(solution)/shard_map/all_to_all | solution.py:722
  21.1 0.2 arrange.1
  21.3 2.4 %collective-permute-start.3 = (f32[264,128]{1,0:T(8,128)S(1)}, f32[264,128]{1,0:T(8,128)S(1)}, u32[]{:S(2)}, u32[]{:S(2)}) collective-permute-start(f32[264,128]{1,0:T(8,128)S(1)} %get-tuple-element.10), channel_id=1, source_target_pairs={{0,8},{8,16},{16,24},{24,28},{28,20},{20,12},{12,4},{4,5},{5,13},{... | collective-permute-start | bytes 405512 | tf_op jit(solution)/shard_map/ppermute | solution.py:727
  23.8 1.3 %collective-permute-start.4 = (f32[264,128]{1,0:T(8,128)S(1)}, f32[264,128]{1,0:T(8,128)S(1)}, u32[]{:S(2)}, u32[]{:S(2)}) collective-permute-start(f32[264,128]{1,0:T(8,128)S(1)} %get-tuple-element.11), channel_id=1, source_target_pairs={{8,0},{16,8},{24,16},{28,24},{20,28},{12,20},{4,12},{5,4},{13,5},{... | collective-permute-start | bytes 405512 | tf_op jit(solution)/shard_map/ppermute | solution.py:728
  25.7 1.9 %all-to-all-done.copies_ref = f32[8,4,2,8,128]{4,3,2,1,0:T(8,128)S(1)} async-done(((f32[8,4,2,8,128]{4,3,2,1,0:T(8,128)}), f32[8,4,2,8,128]{4,3,2,1,0:T(8,128)S(1)}, u32[]{:S(2)}, u32[]{:S(2)}) %all-to-all-start) | async-done | bytes 262176 | tf_op jit(solution)/shard_map/all_to_all | solution.py:722
  27.6 1.3 %level.1.share_ref = f32[2,32,128]{2,1,0:T(8,128)S(1)} custom-call(s32[1]{0:T(128)} %bitcast.1.step_ref, f32[8,4,2,8,128]{4,3,2,1,0:T(8,128)S(1)} %all-to-all-done.copies_ref), custom_call_target="tpu_custom_call" | custom-call | tf_op jit(solution)/shard_map/level/pallas_call | solution.py:676
  28.9 0.0 collective-permute-done.3.before_ref
  28.9 0.0 collective-permute-done.4.after_ref
  29.0 1.6 %flow.1 = f32[8,5,8,128]{3,2,1,0:T(8,128)S(1)} custom-call(f32[2,32,128]{2,1,0:T(8,128)S(1)} %level.1.share_ref, f32[40,16,128]{2,1,0:T(8,128)S(1)} %get-tuple-element.9.body_ref, f32[264,128]{1,0:T(8,128)S(1)} %collective-permute-done.3.before_ref, f32[264,128]{1,0:T(8,128)S(1)} %collective-permute-done.4.after_ref), custom_call_target="tpu_custom_call" | custom-call | tf_op jit(solution)/shard_map/flow/pallas_call | solution.py:676
  30.6 10.4 %all_to_all.15.packed_ref = f32[8,5,8,128]{3,2,1,0:T(8,128)S(1)} all-to-all(f32[8,5,8,128]{3,2,1,0:T(8,128)S(1)} %flow.1), channel_id=1, replica_groups=mesh['grp'=4,'gy'=2,'gx'=4] {'grp','gy'}, dimensions={0} | all-to-all | bytes 327680 | tf_op jit(solution)/shard_map/all_to_all | solution.py:755
  41.0 0.8 %result.1 = (f32[19,2,8,128]{3,2,1,0:T(8,128)}, f32[2,8,128]{2,1,0:T(8,128)}) custom-call(f32[8,5,8,128]{3,2,1,0:T(8,128)S(1)} %all_to_all.15.packed_ref), custom_call_target="tpu_custom_call" | custom-call | tf_op jit(solution)/shard_map/result/pallas_call | solution.py:676
Async XLA Ops:
  2.5 5.2 %copy-start = (f32[2,8,128]{2,1,0:T(8,128)S(1)}, f32[2,8,128]{2,1,0:T(8,128)}, u32[]{:S(2)}) copy-start(f32[2,8,128]{2,1,0:T(8,128)} %get-tuple-element.7.refs_0_) | copy-start | bytes 24580
  2.6 14.4 %all-to-all-start.1 = ((f32[8,5,2,8,128]{4,3,2,1,0:T(8,128)}), f32[8,5,2,8,128]{4,3,2,1,0:T(8,128)S(1)}, u32[]{:S(2)}, u32[]{:S(2)}) async-start(f32[8,5,2,8,128]{4,3,2,1,0:T(8,128)} %get-tuple-element.8), calls=%async_computation.1 | async-start | bytes 655360 | tf_op jit(solution)/shard_map/all_to_all | solution.py:702
  7.7 5.6 %collective-permute-start.2 = (f32[2,8,128]{2,1,0:T(8,128)S(1)}, f32[2,8,128]{2,1,0:T(8,128)S(1)}, u32[]{:S(2)}, u32[]{:S(2)}) collective-permute-start(f32[2,8,128]{2,1,0:T(8,128)S(1)} %copy-done), channel_id=1, source_target_pairs={{3,0},{0,1},{1,2},{2,3},{7,4},{4,5},{5,6},{6,7},{11,8},{8,9},{9,10... | collective-permute-start | bytes 24584 | tf_op jit(solution)/shard_map/ppermute | solution.py:705
  9.4 4.0 %collective-permute-start.1 = (f32[2,8,128]{2,1,0:T(8,128)S(1)}, f32[2,8,128]{2,1,0:T(8,128)S(1)}, u32[]{:S(2)}, u32[]{:S(2)}) collective-permute-start(f32[2,8,128]{2,1,0:T(8,128)S(1)} %copy-done), channel_id=1, source_target_pairs={{1,0},{2,1},{3,2},{0,3},{5,4},{6,5},{7,6},{4,7},{9,8},{10,9},{11,1... | collective-permute-start | bytes 24584 | tf_op jit(solution)/shard_map/ppermute | solution.py:705
  11.6 4.5 %collective-permute-start = (f32[2,8,128]{2,1,0:T(8,128)S(1)}, f32[2,8,128]{2,1,0:T(8,128)S(1)}, u32[]{:S(2)}, u32[]{:S(2)}) collective-permute-start(f32[2,8,128]{2,1,0:T(8,128)S(1)} %copy-done), channel_id=1, source_target_pairs={{2,0},{3,1},{0,2},{1,3},{6,4},{7,5},{4,6},{5,7},{10,8},{11,9},{8,1... | collective-permute-start | bytes 24584 | tf_op jit(solution)/shard_map/ppermute | solution.py:705
  17.0 10.6 %all-to-all-start = ((f32[8,4,2,8,128]{4,3,2,1,0:T(8,128)}), f32[8,4,2,8,128]{4,3,2,1,0:T(8,128)S(1)}, u32[]{:S(2)}, u32[]{:S(2)}) async-start(f32[8,4,2,8,128]{4,3,2,1,0:T(8,128)} %spread.1), calls=%async_computation | async-start | bytes 524288 | tf_op jit(solution)/shard_map/all_to_all | solution.py:722
  21.3 7.6 %collective-permute-start.3 = (f32[264,128]{1,0:T(8,128)S(1)}, f32[264,128]{1,0:T(8,128)S(1)}, u32[]{:S(2)}, u32[]{:S(2)}) collective-permute-start(f32[264,128]{1,0:T(8,128)S(1)} %get-tuple-element.10), channel_id=1, source_target_pairs={{0,8},{8,16},{16,24},{24,28},{28,20},{20,12},{12,4},{4,5},{5,13},{... | collective-permute-start | bytes 405512 | tf_op jit(solution)/shard_map/ppermute | solution.py:727
  23.8 5.2 %collective-permute-start.4 = (f32[264,128]{1,0:T(8,128)S(1)}, f32[264,128]{1,0:T(8,128)S(1)}, u32[]{:S(2)}, u32[]{:S(2)}) collective-permute-start(f32[264,128]{1,0:T(8,128)S(1)} %get-tuple-element.11), channel_id=1, source_target_pairs={{8,0},{16,8},{24,16},{28,24},{20,28},{12,20},{4,12},{5,4},{13,5},{... | collective-permute-start | bytes 405512 | tf_op jit(solution)/shard_map/ppermute | solution.py:728

commit v13 on v12

--- a/solution.py
+++ b/solution.py
@@ -719,7 +719,6 @@
         (packed,),
         [vmem],
     )
-    copies = lax.all_to_all(copies, ("grp", "gy"), 0, 0)
     path = [on_path(index, grp, splits) for index in range(plane)]
     order = [(path if gx % 2 == 0 else path[::-1])[index] * size + gx for gx in range(size) for index in range(plane)]
     up = list(zip(order[:-1], order[1:]))
@@ -727,14 +726,20 @@
     before = lax.ppermute(last, line, up)
     after = lax.ppermute(first, line, [(j, i) for i, j in up])
     columns = size * LANES
-    share = call(
-        functools.partial(level_kernel, rows, splits, size),
-        ((2, 32, LANES),),
-        "level",
-        (beta_step.reshape(1), copies),
-        [pltpu.SMEM, vmem],
-        [vmem((columns + 16, LANES), real), vmem((columns, LANES), real)],
-    )
+    def level(turn, carry):
+        here = lax.all_to_all(carry[0], ("grp", "gy"), 0, 0)
+        share = call(
+            functools.partial(level_kernel, rows, splits, size),
+            ((2, 32, LANES),),
+            "level",
+            (beta_step.reshape(1), here),
+            [pltpu.SMEM, vmem],
+            [vmem((columns + 16, LANES), real), vmem((columns, LANES), real)],
+        )
+        return here, share
+
+    once = jnp.minimum(beta_step + 1, 1)
+    _, share = lax.fori_loop(0, once, level, (copies, jnp.zeros((2, 32, LANES), real)))
     shapes = [
         (19, 48, LANES),
         (19, 48, LANES),

time: 42.2 us -> 54.2 us (1.28)
  blocking collectives: 10.4 us -> 20.5 us
  starting transfers between devices: 17.7 us -> 14 us
  waiting for transfers between devices: 5.65 us -> 7.88 us
  Pallas kernels: 6.65 us -> 8.69 us
  local copies, waits for them, and re-layouts: 0.01 us -> 1.33 us
    all_to_all x1 -> x2, blocking collectives: 10.4 us -> 20.5 us  [body_by_columns(): packed = lax.all_to_all(packed, ('grp', 'gy'), 0, 0)]
    all_to_all x2 -> x1, starting transfers between devices: 9.33 us -> 3.53 us  [level(): here = lax.all_to_all(carry[0], ('grp', 'gy'), 0, 0)]
    all_to_all x2 -> x1, waiting for transfers between devices: 1.89 us -> 6.46 us  [level(): here = lax.all_to_all(carry[0], ('grp', 'gy'), 0, 0)]
    ppermute x3, starting transfers between devices: 4.67 us -> 7.19 us  [body_by_columns(): lax.ppermute(design, 'gx', [((i + turn) % size, i) for i in range(size)])]
    ppermute x3, waiting for transfers between devices: 3.76 us -> 1.42 us  [body_by_columns(): lax.ppermute(design, 'gx', [((i + turn) % size, i) for i in range(size)])]
    pallas_call x6, Pallas kernels: 6.65 us -> 8.69 us  [call(): pl.pallas_call(kernel, out_shape=shapes if many else shapes[0], in_specs=...]
    while x0 -> x1, local copies, waits for them, and re-layouts: none -> 0.71 us
    broadcast_in_dim x0 -> x1, local copies, waits for them, and re-layouts: none -> 0.62 us  [body_by_columns(): jnp.zeros((2, 32, LANES), real)]
  transfers between devices with their start and end apart: 7 -> 6, of which waited for: 3 -> 2; matrix products, arithmetic and copies ran while one was open for 0% -> 2% of each run, Pallas kernels for 6% -> 6%
where the time goes in v13:
time: 54.2 us; the launch traced here: 53.8 us
  blocking collectives  20.5 us (38%)
  starting transfers between devices  14 us (26%)
  Pallas kernels  8.69 us (16%)
  waiting for transfers between devices  7.88 us (15%)
  between operations  1.35 us (2%)
  local copies, waits for them, and re-layouts  1.33 us (2%)
    all_to_all x2, blocking collectives, body_by_columns(): packed = lax.all_to_all(packed, ('grp', 'gy'), 0, 0)  20.5 us
    pallas_call x6, Pallas kernels, call(): pl.pallas_call(kernel, out_shape=shapes if many else shapes[0], in_specs=...  8.69 us
    ppermute x3, starting transfers between devices, body_by_columns(): lax.ppermute(design, 'gx', [((i + turn) % size, i) for i in range(size)])  7.19 us
    all_to_all x1, waiting for transfers between devices, level(): here = lax.all_to_all(carry[0], ('grp', 'gy'), 0, 0)  6.46 us
    all_to_all x1, starting transfers between devices, level(): here = lax.all_to_all(carry[0], ('grp', 'gy'), 0, 0)  3.53 us
    ppermute x1, starting transfers between devices, body_by_columns(): before = lax.ppermute(last, line, up)  2.03 us
    ppermute x3, waiting for transfers between devices, body_by_columns(): lax.ppermute(design, 'gx', [((i + turn) % size, i) for i in range(size)])  1.42 us
    ppermute x1, starting transfers between devices, body_by_columns(): after = lax.ppermute(first, line, [(j, i) for i, j in up])  1.29 us
  transfers between devices with their start and end apart: 6, of which 2 were waited for; matrix products, arithmetic and copies ran while one was open for 2% of the time, Pallas kernels for 6%

profile of v13, /device:TPU:0, one launch (start us, length us, event | category | flops | bytes accessed | tf_op | source)
XLA Modules:
  0.0 53.8 jit_solution(4849680374108238736)
XLA Ops:
  0.6 1.9 %pack.1 = (f32[2,8,128]{2,1,0:T(8,128)}, f32[8,5,2,8,128]{4,3,2,1,0:T(8,128)}) custom-call(f32[2,8,128]{2,1,0:T(8,128)} %design_ref.1, f32[19,2,8,128]{3,2,1,0:T(8,128)} %populations_ref.1, f32[19,2,8,128]{3,2,1,0:T(8,128)} %cotangent_ref.1, s32[2,8,128]{2,1,0:T(8,128)} %wall_ref.1, s32[2,8,128]{2,1,0:T(8,128)} %inlet_ref.1), custom_call_target="tpu_custom_call" | custom-call | tf_op jit(solution)/shard_map/pack/pallas_call | solution.py:676
  2.5 12.6 %all_to_all.16.packed_ref = f32[8,5,2,8,128]{4,3,2,1,0:T(8,128)S(1)} all-to-all(f32[8,5,2,8,128]{4,3,2,1,0:T(8,128)} %get-tuple-element.36), channel_id=1, replica_groups=mesh['grp'=4,'gy'=2,'gx'=4] {'grp','gy'}, dimensions={0} | all-to-all | bytes 655360 | tf_op jit(solution)/shard_map/all_to_all | solution.py:702
  15.2 0.0 copy-start
  15.2 0.2 arrange.1
  15.4 2.0 %collective-permute-start.3 = (f32[264,128]{1,0:T(8,128)S(1)}, f32[264,128]{1,0:T(8,128)S(1)}, u32[]{:S(2)}, u32[]{:S(2)}) collective-permute-start(f32[264,128]{1,0:T(8,128)S(1)} %get-tuple-element.38), channel_id=1, source_target_pairs={{0,8},{8,16},{16,24},{24,28},{28,20},{20,12},{12,4},{4,5},{5,13},{... | collective-permute-start | bytes 405512 | tf_op jit(solution)/shard_map/ppermute | solution.py:726
  17.4 1.3 %collective-permute-start.4 = (f32[264,128]{1,0:T(8,128)S(1)}, f32[264,128]{1,0:T(8,128)S(1)}, u32[]{:S(2)}, u32[]{:S(2)}) collective-permute-start(f32[264,128]{1,0:T(8,128)S(1)} %get-tuple-element.39), channel_id=1, source_target_pairs={{8,0},{16,8},{24,16},{28,24},{20,28},{12,20},{4,12},{5,4},{13,5},{... | collective-permute-start | bytes 405512 | tf_op jit(solution)/shard_map/ppermute | solution.py:727
  18.7 0.0 copy-done
  18.7 3.7 %collective-permute-start.2 = (f32[2,8,128]{2,1,0:T(8,128)S(1)}, f32[2,8,128]{2,1,0:T(8,128)S(1)}, u32[]{:S(2)}, u32[]{:S(2)}) collective-permute-start(f32[2,8,128]{2,1,0:T(8,128)S(1)} %copy-done), channel_id=1, source_target_pairs={{3,0},{0,1},{1,2},{2,3},{7,4},{4,5},{5,6},{6,7},{11,8},{8,9},{9,10... | collective-permute-start | bytes 24584 | tf_op jit(solution)/shard_map/ppermute | solution.py:705
  22.4 1.0 %collective-permute-start.1 = (f32[2,8,128]{2,1,0:T(8,128)S(1)}, f32[2,8,128]{2,1,0:T(8,128)S(1)}, u32[]{:S(2)}, u32[]{:S(2)}) collective-permute-start(f32[2,8,128]{2,1,0:T(8,128)S(1)} %copy-done), channel_id=1, source_target_pairs={{1,0},{2,1},{3,2},{0,3},{5,4},{6,5},{7,6},{4,7},{9,8},{10,9},{11,1... | collective-permute-start | bytes 24584 | tf_op jit(solution)/shard_map/ppermute | solution.py:705
  23.5 2.5 %collective-permute-start = (f32[2,8,128]{2,1,0:T(8,128)S(1)}, f32[2,8,128]{2,1,0:T(8,128)S(1)}, u32[]{:S(2)}, u32[]{:S(2)}) collective-permute-start(f32[2,8,128]{2,1,0:T(8,128)S(1)} %copy-done), channel_id=1, source_target_pairs={{2,0},{3,1},{0,2},{1,3},{6,4},{7,5},{4,6},{5,7},{10,8},{11,9},{8,1... | collective-permute-start | bytes 24584 | tf_op jit(solution)/shard_map/ppermute | solution.py:705
  26.6 0.0 collective-permute-done.2.refs_3_
  26.6 0.0 collective-permute-done.1.refs_2_
  26.6 1.4 %collective-permute-done.refs_1_ = f32[2,8,128]{2,1,0:T(8,128)S(1)} collective-permute-done((f32[2,8,128]{2,1,0:T(8,128)S(1)}, f32[2,8,128]{2,1,0:T(8,128)S(1)}, u32[]{:S(2)}, u32[]{:S(2)}) %collective-permute-start) | collective-permute-done | bytes 8224 | tf_op jit(solution)/shard_map/ppermute | solution.py:705
  28.0 0.8 %spread.1 = f32[8,4,2,8,128]{4,3,2,1,0:T(8,128)} custom-call(f32[2,8,128]{2,1,0:T(8,128)S(1)} %copy-done, f32[2,8,128]{2,1,0:T(8,128)S(1)} %collective-permute-done.refs_1_, f32[2,8,128]{2,1,0:T(8,128)S(1)} %collective-permute-done.1.refs_2_, f32[2,8,128]{2,1,0:T(8,128)S(1)} %collective-permute-done.2.refs_3_), custom_call_target="tpu_custom_call" | custom-call | tf_op jit(solution)/shard_map/spread/pallas_call | solution.py:676
  28.8 0.6 %broadcast_in_dim.3 = f32[2,32,128]{2,1,0:T(8,128)} broadcast(f32[]{:T(128)} %constant.2.clone.1), dimensions={} | broadcast | bytes 32772 | tf_op jit(solution)/shard_map/broadcast_in_dim | solution.py:742
  29.5 13.3 %while.12 = (s32[]{:T(128)}, f32[8,4,2,8,128]{4,3,2,1,0:T(8,128)}, f32[2,32,128]{2,1,0:T(8,128)}, s32[]{:T(128)}, s32[]{:T(128)}, /*index=5*/s32[]{:T(128)}) while((s32[]{:T(128)}, f32[8,4,2,8,128]{4,3,2,1,0:T(8,128)}, f32[2,32,128]{2,1,0:T(8,128)}, s32[]{:T(128)}, s32[]{:T(128)}, /*index=5*/s32[]{:T(128)}) %tuple.20), condition=%wide.region_1.0_spmd, body=%wide.region_0.0_spmd.sunk | while | flops 2 | bytes 1310821 | solution.py:742
  29.5 3.5 %all-to-all-start = ((f32[8,4,2,8,128]{4,3,2,1,0:T(8,128)}), f32[8,4,2,8,128]{4,3,2,1,0:T(8,128)S(1)}, u32[]{:S(2)}, u32[]{:S(2)}) async-start(f32[8,4,2,8,128]{4,3,2,1,0:T(8,128)} %get-tuple-element.87), calls=%async_computation | async-start | bytes 524288 | tf_op jit(solution)/shard_map/while/body/all_to_all | solution.py:730
  33.0 6.5 %all-to-all-done.copies_ref = f32[8,4,2,8,128]{4,3,2,1,0:T(8,128)S(1)} async-done(((f32[8,4,2,8,128]{4,3,2,1,0:T(8,128)}), f32[8,4,2,8,128]{4,3,2,1,0:T(8,128)S(1)}, u32[]{:S(2)}, u32[]{:S(2)}) %all-to-all-start) | async-done | bytes 262176 | tf_op jit(solution)/shard_map/while/body/all_to_all | solution.py:730
  39.4 0.7 %copy.15 = f32[8,4,2,8,128]{4,3,2,1,0:T(8,128)} copy(f32[8,4,2,8,128]{4,3,2,1,0:T(8,128)S(1)} %all-to-all-done.copies_ref) | data formatting | bytes 524288 | tf_op jit(solution)/shard_map/while
  40.2 2.6 %level.1 = f32[2,32,128]{2,1,0:T(8,128)} custom-call(s32[1]{0:T(128)} %bitcast.2.step_ref, f32[8,4,2,8,128]{4,3,2,1,0:T(8,128)S(1)} %all-to-all-done.copies_ref), custom_call_target="tpu_custom_call" | custom-call | tf_op jit(solution)/shard_map/while/body/level/pallas_call | solution.py:676
  42.8 0.0 collective-permute-done.3.before_ref
  42.8 0.0 collective-permute-done.4.after_ref
  42.8 2.4 %flow.1 = f32[8,5,8,128]{3,2,1,0:T(8,128)S(1)} custom-call(f32[2,32,128]{2,1,0:T(8,128)} %get-tuple-element.35.share_ref, f32[40,16,128]{2,1,0:T(8,128)S(1)} %get-tuple-element.37.body_ref, f32[264,128]{1,0:T(8,128)S(1)} %collective-permute-done.3.before_ref, f32[264,128]{1,0:T(8,128)S(1)} %collective-permute-done.4.after_ref), custom_call_target="tpu_custom_call" | custom-call | tf_op jit(solution)/shard_map/flow/pallas_call | solution.py:676
  45.2 7.8 %all_to_all.17.packed_ref = f32[8,5,8,128]{3,2,1,0:T(8,128)S(1)} all-to-all(f32[8,5,8,128]{3,2,1,0:T(8,128)S(1)} %flow.1), channel_id=1, replica_groups=mesh['grp'=4,'gy'=2,'gx'=4] {'grp','gy'}, dimensions={0} | all-to-all | bytes 327680 | tf_op jit(solution)/shard_map/all_to_all | solution.py:760
  53.0 0.8 %result.1 = (f32[19,2,8,128]{3,2,1,0:T(8,128)}, f32[2,8,128]{2,1,0:T(8,128)}) custom-call(f32[8,5,8,128]{3,2,1,0:T(8,128)S(1)} %all_to_all.17.packed_ref), custom_call_target="tpu_custom_call" | custom-call | tf_op jit(solution)/shard_map/result/pallas_call | solution.py:676
Async XLA Ops:
  15.2 3.5 %copy-start = (f32[2,8,128]{2,1,0:T(8,128)S(1)}, f32[2,8,128]{2,1,0:T(8,128)}, u32[]{:S(2)}) copy-start(f32[2,8,128]{2,1,0:T(8,128)} %get-tuple-element.34.refs_0_) | copy-start | bytes 24580
  15.4 27.4 %collective-permute-start.3 = (f32[264,128]{1,0:T(8,128)S(1)}, f32[264,128]{1,0:T(8,128)S(1)}, u32[]{:S(2)}, u32[]{:S(2)}) collective-permute-start(f32[264,128]{1,0:T(8,128)S(1)} %get-tuple-element.38), channel_id=1, source_target_pairs={{0,8},{8,16},{16,24},{24,28},{28,20},{20,12},{12,4},{4,5},{5,13},{... | collective-permute-start | bytes 405512 | tf_op jit(solution)/shard_map/ppermute | solution.py:726
  17.4 25.3 %collective-permute-start.4 = (f32[264,128]{1,0:T(8,128)S(1)}, f32[264,128]{1,0:T(8,128)S(1)}, u32[]{:S(2)}, u32[]{:S(2)}) collective-permute-start(f32[264,128]{1,0:T(8,128)S(1)} %get-tuple-element.39), channel_id=1, source_target_pairs={{8,0},{16,8},{24,16},{28,24},{20,28},{12,20},{4,12},{5,4},{13,5},{... | collective-permute-start | bytes 405512 | tf_op jit(solution)/shard_map/ppermute | solution.py:727
  18.7 7.8 %collective-permute-start.2 = (f32[2,8,128]{2,1,0:T(8,128)S(1)}, f32[2,8,128]{2,1,0:T(8,128)S(1)}, u32[]{:S(2)}, u32[]{:S(2)}) collective-permute-start(f32[2,8,128]{2,1,0:T(8,128)S(1)} %copy-done), channel_id=1, source_target_pairs={{3,0},{0,1},{1,2},{2,3},{7,4},{4,5},{5,6},{6,7},{11,8},{8,9},{9,10... | collective-permute-start | bytes 24584 | tf_op jit(solution)/shard_map/ppermute | solution.py:705
  22.4 4.1 %collective-permute-start.1 = (f32[2,8,128]{2,1,0:T(8,128)S(1)}, f32[2,8,128]{2,1,0:T(8,128)S(1)}, u32[]{:S(2)}, u32[]{:S(2)}) collective-permute-start(f32[2,8,128]{2,1,0:T(8,128)S(1)} %copy-done), channel_id=1, source_target_pairs={{1,0},{2,1},{3,2},{0,3},{5,4},{6,5},{7,6},{4,7},{9,8},{10,9},{11,1... | collective-permute-start | bytes 24584 | tf_op jit(solution)/shard_map/ppermute | solution.py:705
  23.5 4.5 %collective-permute-start = (f32[2,8,128]{2,1,0:T(8,128)S(1)}, f32[2,8,128]{2,1,0:T(8,128)S(1)}, u32[]{:S(2)}, u32[]{:S(2)}) collective-permute-start(f32[2,8,128]{2,1,0:T(8,128)S(1)} %copy-done), channel_id=1, source_target_pairs={{2,0},{3,1},{0,2},{1,3},{6,4},{7,5},{4,6},{5,7},{10,8},{11,9},{8,1... | collective-permute-start | bytes 24584 | tf_op jit(solution)/shard_map/ppermute | solution.py:705
  29.5 10.0 %all-to-all-start = ((f32[8,4,2,8,128]{4,3,2,1,0:T(8,128)}), f32[8,4,2,8,128]{4,3,2,1,0:T(8,128)S(1)}, u32[]{:S(2)}, u32[]{:S(2)}) async-start(f32[8,4,2,8,128]{4,3,2,1,0:T(8,128)} %get-tuple-element.87), calls=%async_computation | async-start | bytes 524288 | tf_op jit(solution)/shard_map/while/body/all_to_all | solution.py:730

commit v14 on v12

--- a/solution.py
+++ b/solution.py
@@ -279,7 +279,7 @@
                 packed_ref[devices[index], group, layer] = values[-index % 8]
 
 
-def arrange_kernel(splits, packed_ref, body_ref, first_ref, last_ref):
+def arrange_kernel(splits, packed_ref, body_ref, near_ref, far_ref):
     layers = packed_ref.shape[2]
     planes = packed_ref.shape[0] // splits * layers
     me = block_here(packed_ref.shape[0] // splits, splits)
@@ -290,17 +290,20 @@
         for slot in range(8):
             index = group * 8 + lax.rem(slot + 8 - me, 8)
             body_ref[index] = plane[16 * slot : 16 * slot + 16, :]
+    even = lax.rem(me, 2) == 0
+
+    def send(start, first, last):
+        near_ref[start : start + first.shape[0], :] = jnp.where(even, last, first)
+        far_ref[start : start + first.shape[0], :] = jnp.where(even, first, last)
+
     for index in range(FIELDS):
         if index < 21:
-            first_ref[8 * index : 8 * index + 8, :] = body_ref[index, 0:8, :]
-            last_ref[8 * index : 8 * index + 8, :] = body_ref[index, 8:16, :]
+            send(8 * index, body_ref[index, 0:8, :], body_ref[index, 8:16, :])
         else:
             start = 8 * 21 + NEAR * (index - 21)
-            first_ref[start : start + NEAR, :] = body_ref[index, 0:NEAR, :]
-            last_ref[start : start + NEAR, :] = body_ref[index, 16 - NEAR : 16, :]
-    for ref in (first_ref, last_ref):
-        rest = ref.shape[0] - OUTER
-        ref[OUTER:, :] = jnp.zeros((rest, LANES), jnp.float32)
+            send(start, body_ref[index, 0:NEAR, :], body_ref[index, 16 - NEAR : 16, :])
+    for ref in (near_ref, far_ref):
+        ref[OUTER:, :] = jnp.zeros((ref.shape[0] - OUTER, LANES), jnp.float32)
 
 
 def turns_of(size):
@@ -498,7 +501,7 @@
 
 
 def flow_kernel(
-    rows, splits, size, share_ref, body_ref, before_ref, after_ref, packed_ref,
+    rows, splits, size, share_ref, body_ref, near_ref, far_ref, packed_ref,
     cotangent_ref, even_ref, odd_ref, kept_ref, grad_ref, smooth_ref, output_ref,
 ):
     devices = packed_ref.shape[0]
@@ -517,11 +520,17 @@
             return jnp.where(place < last, value, 0.0)
         return value
 
+    even = lax.rem(me, 2) == 0
+
+    def outer(start, count):
+        near, far = near_ref[start : start + count, :], far_ref[start : start + count, :]
+        return jnp.where(even, far, near), jnp.where(even, near, far)
+
     def initial(i, row):
         if row == 0:
-            return before_ref[8 * i : 8 * i + 8, :]
+            return outer(8 * i, 8)[0]
         if row == 24:
-            return after_ref[8 * i : 8 * i + 8, :]
+            return outer(8 * i, 8)[1]
         return body_ref[i, row - 8 : row, :]
 
     for ref in (even_ref, odd_ref, cotangent_ref):
@@ -531,10 +540,10 @@
     for i in range(19):
         start = 8 * 21 + NEAR * i
         cotangent_ref[i, 8:16, :] = zero
-        cotangent_ref[i, 16 - NEAR : 16, :] = before_ref[start : start + NEAR, :]
+        cotangent_ref[i, 16 - NEAR : 16, :] = outer(start, NEAR)[0]
         cotangent_ref[i, 16:32, :] = body_ref[21 + i]
         cotangent_ref[i, 32:40, :] = zero
-        cotangent_ref[i, 32 : 32 + NEAR, :] = after_ref[start : start + NEAR, :]
+        cotangent_ref[i, 32 : 32 + NEAR, :] = outer(start, NEAR)[1]
 
     def arrived(ref, i, row):
         cz, cy, cx = (int(c) for c in velocities[i])
@@ -712,7 +721,7 @@
         [vmem((size, *tile), real)],
     )
     outer = (-(-OUTER // 8) * 8, LANES)
-    body, first, last = call(
+    body, near, far = call(
         functools.partial(arrange_kernel, splits),
         ((FIELDS, 16, LANES), outer, outer),
         "arrange",
@@ -722,10 +731,13 @@
     copies = lax.all_to_all(copies, ("grp", "gy"), 0, 0)
     path = [on_path(index, grp, splits) for index in range(plane)]
     order = [(path if gx % 2 == 0 else path[::-1])[index] * size + gx for gx in range(size) for index in range(plane)]
-    up = list(zip(order[:-1], order[1:]))
     line = ("grp", "gy", "gx")
-    before = lax.ppermute(last, line, up)
-    after = lax.ppermute(first, line, [(j, i) for i, j in up])
+
+    def exchange(value, start):
+        pairs = [order[b : b + 2] for b in range(start, size * plane - 1, 2)]
+        return lax.ppermute(value, line, [pair for i, j in pairs for pair in ((i, j), (j, i))])
+
+    far, near = exchange(far, 1), exchange(near, 0)
     columns = size * LANES
     share = call(
         functools.partial(level_kernel, rows, splits, size),
@@ -748,7 +760,7 @@
         functools.partial(flow_kernel, rows, splits, size),
         ((plane, 5, 8, LANES),),
         "flow",
-        (share, body, before, after),
+        (share, body, near, far),
         [vmem] * 4,
         [vmem(shape, real) for shape in shapes],
     )

time: 42.2 us -> 40.2 us (0.953)
  waiting for transfers between devices: 5.65 us -> 8.2 us
  starting transfers between devices: 17.7 us -> 15.2 us
  blocking collectives: 10.4 us -> 8.52 us
    all_to_all x1, waiting for transfers between devices: 1.89 us -> 4.43 us  [body_by_columns(): copies = lax.all_to_all(copies, ('grp', 'gy'), 0, 0)]
    ppermute x2, starting transfers between devices: 3.71 us -> 1.23 us  [exchange(): lax.ppermute(value, line, [pair for i, j in pairs for pair in ((i, j), (j...]
    all_to_all x1, blocking collectives: 10.4 us -> 8.52 us  [body_by_columns(): packed = lax.all_to_all(packed, ('grp', 'gy'), 0, 0)]
  transfers between devices with their start and end apart: 7 -> 7, of which waited for: 3 -> 3; matrix products, arithmetic and copies ran while one was open for 0% -> 0% of each run, Pallas kernels for 6% -> 5%
where the time goes in v14:
time: 40.2 us; the launch traced here: 39.7 us
  starting transfers between devices  15.2 us (38%)
  blocking collectives  8.52 us (21%)
  waiting for transfers between devices  8.2 us (20%)
  Pallas kernels  6.45 us (16%)
  between operations  1.34 us (3%)
    all_to_all x1, blocking collectives, body_by_columns(): packed = lax.all_to_all(packed, ('grp', 'gy'), 0, 0)  8.52 us
    pallas_call x6, Pallas kernels, call(): pl.pallas_call(kernel, out_shape=shapes if many else shapes[0], in_specs=...  6.45 us
    all_to_all x1, starting transfers between devices, body_by_columns(): packed = lax.all_to_all(packed, ('grp', 'gy'), 0, 0)  5.18 us
    ppermute x3, starting transfers between devices, body_by_columns(): lax.ppermute(design, 'gx', [((i + turn) % size, i) for i in range(size)])  4.67 us
    all_to_all x1, waiting for transfers between devices, body_by_columns(): copies = lax.all_to_all(copies, ('grp', 'gy'), 0, 0)  4.43 us
    all_to_all x1, starting transfers between devices, body_by_columns(): copies = lax.all_to_all(copies, ('grp', 'gy'), 0, 0)  4.14 us
    ppermute x3, waiting for transfers between devices, body_by_columns(): lax.ppermute(design, 'gx', [((i + turn) % size, i) for i in range(size)])  3.76 us
    ppermute x2, starting transfers between devices, exchange(): lax.ppermute(value, line, [pair for i, j in pairs for pair in ((i, j), (j...  1.23 us
  transfers between devices with their start and end apart: 7, of which 3 were waited for; matrix products, arithmetic and copies ran while one was open for 0% of the time, Pallas kernels for 5%

profile of v14, /device:TPU:0, one launch (start us, length us, event | category | flops | bytes accessed | tf_op | source)
XLA Modules:
  0.0 39.7 jit_solution(14923362360357836673)
XLA Ops:
  0.6 1.9 %pack.1 = (f32[2,8,128]{2,1,0:T(8,128)}, f32[8,5,2,8,128]{4,3,2,1,0:T(8,128)}) custom-call(f32[2,8,128]{2,1,0:T(8,128)} %design_ref.1, f32[19,2,8,128]{3,2,1,0:T(8,128)} %populations_ref.1, f32[19,2,8,128]{3,2,1,0:T(8,128)} %cotangent_ref.1, s32[2,8,128]{2,1,0:T(8,128)} %wall_ref.1, s32[2,8,128]{2,1,0:T(8,128)} %inlet_ref.1), custom_call_target="tpu_custom_call" | custom-call | tf_op jit(solution)/shard_map/pack/pallas_call | solution.py:685
  2.5 0.0 copy-start
  2.6 5.2 %all-to-all-start.1 = ((f32[8,5,2,8,128]{4,3,2,1,0:T(8,128)}), f32[8,5,2,8,128]{4,3,2,1,0:T(8,128)S(1)}, u32[]{:S(2)}, u32[]{:S(2)}) async-start(f32[8,5,2,8,128]{4,3,2,1,0:T(8,128)} %get-tuple-element.8), calls=%async_computation.1 | async-start | bytes 655360 | tf_op jit(solution)/shard_map/all_to_all | solution.py:711
  7.7 0.0 copy-done
  7.7 1.6 %collective-permute-start.2 = (f32[2,8,128]{2,1,0:T(8,128)S(1)}, f32[2,8,128]{2,1,0:T(8,128)S(1)}, u32[]{:S(2)}, u32[]{:S(2)}) collective-permute-start(f32[2,8,128]{2,1,0:T(8,128)S(1)} %copy-done), channel_id=1, source_target_pairs={{3,0},{0,1},{1,2},{2,3},{7,4},{4,5},{5,6},{6,7},{11,8},{8,9},{9,10... | collective-permute-start | bytes 24584 | tf_op jit(solution)/shard_map/ppermute | solution.py:714
  9.4 2.2 %collective-permute-start.1 = (f32[2,8,128]{2,1,0:T(8,128)S(1)}, f32[2,8,128]{2,1,0:T(8,128)S(1)}, u32[]{:S(2)}, u32[]{:S(2)}) collective-permute-start(f32[2,8,128]{2,1,0:T(8,128)S(1)} %copy-done), channel_id=1, source_target_pairs={{1,0},{2,1},{3,2},{0,3},{5,4},{6,5},{7,6},{4,7},{9,8},{10,9},{11,1... | collective-permute-start | bytes 24584 | tf_op jit(solution)/shard_map/ppermute | solution.py:714
  11.6 0.8 %collective-permute-start = (f32[2,8,128]{2,1,0:T(8,128)S(1)}, f32[2,8,128]{2,1,0:T(8,128)S(1)}, u32[]{:S(2)}, u32[]{:S(2)}) collective-permute-start(f32[2,8,128]{2,1,0:T(8,128)S(1)} %copy-done), channel_id=1, source_target_pairs={{2,0},{3,1},{0,2},{1,3},{6,4},{7,5},{4,6},{5,7},{10,8},{11,9},{8,1... | collective-permute-start | bytes 24584 | tf_op jit(solution)/shard_map/ppermute | solution.py:714
  12.4 0.9 %collective-permute-done.2.refs_3_ = f32[2,8,128]{2,1,0:T(8,128)S(1)} collective-permute-done((f32[2,8,128]{2,1,0:T(8,128)S(1)}, f32[2,8,128]{2,1,0:T(8,128)S(1)}, u32[]{:S(2)}, u32[]{:S(2)}) %collective-permute-start.2) | collective-permute-done | bytes 8224 | tf_op jit(solution)/shard_map/ppermute | solution.py:714
  13.3 0.0 collective-permute-done.1.refs_2_
  13.3 2.8 %collective-permute-done.refs_1_ = f32[2,8,128]{2,1,0:T(8,128)S(1)} collective-permute-done((f32[2,8,128]{2,1,0:T(8,128)S(1)}, f32[2,8,128]{2,1,0:T(8,128)S(1)}, u32[]{:S(2)}, u32[]{:S(2)}) %collective-permute-start) | collective-permute-done | bytes 8224 | tf_op jit(solution)/shard_map/ppermute | solution.py:714
  16.2 0.8 %spread.1 = f32[8,4,2,8,128]{4,3,2,1,0:T(8,128)} custom-call(f32[2,8,128]{2,1,0:T(8,128)S(1)} %copy-done, f32[2,8,128]{2,1,0:T(8,128)S(1)} %collective-permute-done.refs_1_, f32[2,8,128]{2,1,0:T(8,128)S(1)} %collective-permute-done.1.refs_2_, f32[2,8,128]{2,1,0:T(8,128)S(1)} %collective-permute-done.2.refs_3_), custom_call_target="tpu_custom_call" | custom-call | tf_op jit(solution)/shard_map/spread/pallas_call | solution.py:685
  17.0 0.0 all-to-all-done.1.packed_ref
  17.0 4.1 %all-to-all-start = ((f32[8,4,2,8,128]{4,3,2,1,0:T(8,128)}), f32[8,4,2,8,128]{4,3,2,1,0:T(8,128)S(1)}, u32[]{:S(2)}, u32[]{:S(2)}) async-start(f32[8,4,2,8,128]{4,3,2,1,0:T(8,128)} %spread.1), calls=%async_computation | async-start | bytes 524288 | tf_op jit(solution)/shard_map/all_to_all | solution.py:731
  21.1 0.2 arrange.1
  21.3 0.6 %collective-permute-start.3 = (f32[264,128]{1,0:T(8,128)S(1)}, f32[264,128]{1,0:T(8,128)S(1)}, u32[]{:S(2)}, u32[]{:S(2)}) collective-permute-start(f32[264,128]{1,0:T(8,128)S(1)} %get-tuple-element.10), channel_id=1, source_target_pairs={{0,8},{8,0},{16,24},{24,16},{28,20},{20,28},{12,4},{4,12},{5,13},{... | collective-permute-start | bytes 405512 | tf_op jit(solution)/shard_map/ppermute | solution.py:738
  21.9 0.7 %collective-permute-start.4 = (f32[264,128]{1,0:T(8,128)S(1)}, f32[264,128]{1,0:T(8,128)S(1)}, u32[]{:S(2)}, u32[]{:S(2)}) collective-permute-start(f32[264,128]{1,0:T(8,128)S(1)} %get-tuple-element.11), channel_id=1, source_target_pairs={{8,16},{16,8},{24,28},{28,24},{20,12},{12,20},{4,5},{5,4},{13,21},... | collective-permute-start | bytes 405512 | tf_op jit(solution)/shard_map/ppermute | solution.py:738
  23.2 4.4 %all-to-all-done.copies_ref = f32[8,4,2,8,128]{4,3,2,1,0:T(8,128)S(1)} async-done(((f32[8,4,2,8,128]{4,3,2,1,0:T(8,128)}), f32[8,4,2,8,128]{4,3,2,1,0:T(8,128)S(1)}, u32[]{:S(2)}, u32[]{:S(2)}) %all-to-all-start) | async-done | bytes 262176 | tf_op jit(solution)/shard_map/all_to_all | solution.py:731
  27.6 1.1 %level.1.share_ref = f32[2,32,128]{2,1,0:T(8,128)S(1)} custom-call(s32[1]{0:T(128)} %bitcast.1.step_ref, f32[8,4,2,8,128]{4,3,2,1,0:T(8,128)S(1)} %all-to-all-done.copies_ref), custom_call_target="tpu_custom_call" | custom-call | tf_op jit(solution)/shard_map/level/pallas_call | solution.py:685
  28.8 0.0 collective-permute-done.3.near_ref
  28.8 0.0 collective-permute-done.4.far_ref
  28.8 1.7 %flow.1 = f32[8,5,8,128]{3,2,1,0:T(8,128)S(1)} custom-call(f32[2,32,128]{2,1,0:T(8,128)S(1)} %level.1.share_ref, f32[40,16,128]{2,1,0:T(8,128)S(1)} %get-tuple-element.9.body_ref, f32[264,128]{1,0:T(8,128)S(1)} %collective-permute-done.3.near_ref, f32[264,128]{1,0:T(8,128)S(1)} %collective-permute-done.4.far_ref), custom_call_target="tpu_custom_call" | custom-call | tf_op jit(solution)/shard_map/flow/pallas_call | solution.py:685
  30.4 8.5 %all_to_all.15.packed_ref = f32[8,5,8,128]{3,2,1,0:T(8,128)S(1)} all-to-all(f32[8,5,8,128]{3,2,1,0:T(8,128)S(1)} %flow.1), channel_id=1, replica_groups=mesh['grp'=4,'gy'=2,'gx'=4] {'grp','gy'}, dimensions={0} | all-to-all | bytes 327680 | tf_op jit(solution)/shard_map/all_to_all | solution.py:767
  39.0 0.8 %result.1 = (f32[19,2,8,128]{3,2,1,0:T(8,128)}, f32[2,8,128]{2,1,0:T(8,128)}) custom-call(f32[8,5,8,128]{3,2,1,0:T(8,128)S(1)} %all_to_all.15.packed_ref), custom_call_target="tpu_custom_call" | custom-call | tf_op jit(solution)/shard_map/result/pallas_call | solution.py:685
Async XLA Ops:
  2.5 5.2 %copy-start = (f32[2,8,128]{2,1,0:T(8,128)S(1)}, f32[2,8,128]{2,1,0:T(8,128)}, u32[]{:S(2)}) copy-start(f32[2,8,128]{2,1,0:T(8,128)} %get-tuple-element.7.refs_0_) | copy-start | bytes 24580
  2.6 14.4 %all-to-all-start.1 = ((f32[8,5,2,8,128]{4,3,2,1,0:T(8,128)}), f32[8,5,2,8,128]{4,3,2,1,0:T(8,128)S(1)}, u32[]{:S(2)}, u32[]{:S(2)}) async-start(f32[8,5,2,8,128]{4,3,2,1,0:T(8,128)} %get-tuple-element.8), calls=%async_computation.1 | async-start | bytes 655360 | tf_op jit(solution)/shard_map/all_to_all | solution.py:711
  7.7 5.6 %collective-permute-start.2 = (f32[2,8,128]{2,1,0:T(8,128)S(1)}, f32[2,8,128]{2,1,0:T(8,128)S(1)}, u32[]{:S(2)}, u32[]{:S(2)}) collective-permute-start(f32[2,8,128]{2,1,0:T(8,128)S(1)} %copy-done), channel_id=1, source_target_pairs={{3,0},{0,1},{1,2},{2,3},{7,4},{4,5},{5,6},{6,7},{11,8},{8,9},{9,10... | collective-permute-start | bytes 24584 | tf_op jit(solution)/shard_map/ppermute | solution.py:714
  9.4 4.0 %collective-permute-start.1 = (f32[2,8,128]{2,1,0:T(8,128)S(1)}, f32[2,8,128]{2,1,0:T(8,128)S(1)}, u32[]{:S(2)}, u32[]{:S(2)}) collective-permute-start(f32[2,8,128]{2,1,0:T(8,128)S(1)} %copy-done), channel_id=1, source_target_pairs={{1,0},{2,1},{3,2},{0,3},{5,4},{6,5},{7,6},{4,7},{9,8},{10,9},{11,1... | collective-permute-start | bytes 24584 | tf_op jit(solution)/shard_map/ppermute | solution.py:714
  11.6 4.5 %collective-permute-start = (f32[2,8,128]{2,1,0:T(8,128)S(1)}, f32[2,8,128]{2,1,0:T(8,128)S(1)}, u32[]{:S(2)}, u32[]{:S(2)}) collective-permute-start(f32[2,8,128]{2,1,0:T(8,128)S(1)} %copy-done), channel_id=1, source_target_pairs={{2,0},{3,1},{0,2},{1,3},{6,4},{7,5},{4,6},{5,7},{10,8},{11,9},{8,1... | collective-permute-start | bytes 24584 | tf_op jit(solution)/shard_map/ppermute | solution.py:714
  17.0 10.7 %all-to-all-start = ((f32[8,4,2,8,128]{4,3,2,1,0:T(8,128)}), f32[8,4,2,8,128]{4,3,2,1,0:T(8,128)S(1)}, u32[]{:S(2)}, u32[]{:S(2)}) async-start(f32[8,4,2,8,128]{4,3,2,1,0:T(8,128)} %spread.1), calls=%async_computation | async-start | bytes 524288 | tf_op jit(solution)/shard_map/all_to_all | solution.py:731
  21.3 7.4 %collective-permute-start.3 = (f32[264,128]{1,0:T(8,128)S(1)}, f32[264,128]{1,0:T(8,128)S(1)}, u32[]{:S(2)}, u32[]{:S(2)}) collective-permute-start(f32[264,128]{1,0:T(8,128)S(1)} %get-tuple-element.10), channel_id=1, source_target_pairs={{0,8},{8,0},{16,24},{24,16},{28,20},{20,28},{12,4},{4,12},{5,13},{... | collective-permute-start | bytes 405512 | tf_op jit(solution)/shard_map/ppermute | solution.py:738
  21.9 6.9 %collective-permute-start.4 = (f32[264,128]{1,0:T(8,128)S(1)}, f32[264,128]{1,0:T(8,128)S(1)}, u32[]{:S(2)}, u32[]{:S(2)}) collective-permute-start(f32[264,128]{1,0:T(8,128)S(1)} %get-tuple-element.11), channel_id=1, source_target_pairs={{8,16},{16,8},{24,28},{28,24},{20,12},{12,20},{4,5},{5,4},{13,21},... | collective-permute-start | bytes 405512 | tf_op jit(solution)/shard_map/ppermute | solution.py:738

commit v15 on v14

--- a/solution.py
+++ b/solution.py
@@ -314,7 +314,7 @@
     design_refs, (copies_ref, design_ref) = refs[:size], refs[size:]
     here = lax.axis_index("gx")
     for turn, ref in zip(turns_of(size), design_refs):
-        design_ref[lax.rem(here + turn, size)] = ref[...]
+        design_ref[here ^ turn] = ref[...]
     lanes = lane_index()
     zero = jnp.zeros((8, LANES), jnp.float32)
     for layer in range(copies_ref.shape[2]):
@@ -711,7 +711,7 @@
     packed = lax.all_to_all(packed, ("grp", "gy"), 0, 0)
     designs = [design] * size
     for turn in reversed(range(1, size)):
-        designs[turn] = lax.ppermute(design, "gx", [((i + turn) % size, i) for i in range(size)])
+        designs[turn] = lax.ppermute(design, "gx", [(i, i ^ turn) for i in range(size)])
     copies = call(
         functools.partial(spread_kernel, size),
         ((plane, size, *tile),),
@@ -772,7 +772,9 @@
     grp, splits = lax.axis_size("grp"), lax.axis_size("gy")
     layers, height, width = design.shape
     fits = height == 8 and width == LANES and layers * grp * height * splits == LANES
-    whole = body_by_columns if fits and grp * splits * 16 == LANES else body_by_blocks
+    size = lax.axis_size("gx")
+    fits = fits and grp * splits * 16 == LANES and size & (size - 1) == 0
+    whole = body_by_columns if fits else body_by_blocks
     return whole(design, populations, cotangent, wall_mask, inlet_mask, beta_step)
 
 

time: 40.2 us -> 40 us (level)
  transfers between devices with their start and end apart: 7 -> 7, of which waited for: 3 -> 4; matrix products, arithmetic and copies ran while one was open for 0% -> 0% of each run, Pallas kernels for 5% -> 6%
where the time goes in v15:
time: 40 us; the launch traced here: 39.5 us
  starting transfers between devices  15 us (38%)
  blocking collectives  8.29 us (21%)
  waiting for transfers between devices  8.21 us (21%)
  Pallas kernels  6.68 us (17%)
  between operations  1.34 us (3%)
    all_to_all x1, blocking collectives, body_by_columns(): packed = lax.all_to_all(packed, ('grp', 'gy'), 0, 0)  8.29 us
    pallas_call x6, Pallas kernels, call(): pl.pallas_call(kernel, out_shape=shapes if many else shapes[0], in_specs=...  6.68 us
    all_to_all x1, starting transfers between devices, body_by_columns(): packed = lax.all_to_all(packed, ('grp', 'gy'), 0, 0)  5.18 us
    ppermute x3, starting transfers between devices, body_by_columns(): lax.ppermute(design, 'gx', [(i, i ^ turn) for i in range(size)])  4.45 us
    all_to_all x1, waiting for transfers between devices, body_by_columns(): copies = lax.all_to_all(copies, ('grp', 'gy'), 0, 0)  4.43 us
    all_to_all x1, starting transfers between devices, body_by_columns(): copies = lax.all_to_all(copies, ('grp', 'gy'), 0, 0)  4.14 us
    ppermute x3, waiting for transfers between devices, body_by_columns(): lax.ppermute(design, 'gx', [(i, i ^ turn) for i in range(size)])  3.77 us
    ppermute x2, starting transfers between devices, exchange(): lax.ppermute(value, line, [pair for i, j in pairs for pair in ((i, j), (j...  1.23 us
  transfers between devices with their start and end apart: 7, of which 4 were waited for; matrix products, arithmetic and copies ran while one was open for 0% of the time, Pallas kernels for 6%

profile of v15, /device:TPU:0, one launch (start us, length us, event | category | flops | bytes accessed | tf_op | source)
XLA Modules:
  0.0 39.5 jit_solution(9726777686469222541)
XLA Ops:
  0.6 1.9 %pack.1 = (f32[2,8,128]{2,1,0:T(8,128)}, f32[8,5,2,8,128]{4,3,2,1,0:T(8,128)}) custom-call(f32[2,8,128]{2,1,0:T(8,128)} %design_ref.1, f32[19,2,8,128]{3,2,1,0:T(8,128)} %populations_ref.1, f32[19,2,8,128]{3,2,1,0:T(8,128)} %cotangent_ref.1, s32[2,8,128]{2,1,0:T(8,128)} %wall_ref.1, s32[2,8,128]{2,1,0:T(8,128)} %inlet_ref.1), custom_call_target="tpu_custom_call" | custom-call | tf_op jit(solution)/shard_map/pack/pallas_call | solution.py:685
  2.5 0.0 copy-start
  2.6 5.2 %all-to-all-start.1 = ((f32[8,5,2,8,128]{4,3,2,1,0:T(8,128)}), f32[8,5,2,8,128]{4,3,2,1,0:T(8,128)S(1)}, u32[]{:S(2)}, u32[]{:S(2)}) async-start(f32[8,5,2,8,128]{4,3,2,1,0:T(8,128)} %get-tuple-element.8), calls=%async_computation.1 | async-start | bytes 655360 | tf_op jit(solution)/shard_map/all_to_all | solution.py:711
  7.7 0.0 copy-done
  7.7 3.7 %collective-permute-start.2 = (f32[2,8,128]{2,1,0:T(8,128)S(1)}, f32[2,8,128]{2,1,0:T(8,128)S(1)}, u32[]{:S(2)}, u32[]{:S(2)}) collective-permute-start(f32[2,8,128]{2,1,0:T(8,128)S(1)} %copy-done), channel_id=1, source_target_pairs={{0,3},{1,2},{2,1},{3,0},{4,7},{5,6},{6,5},{7,4},{8,11},{9,10},{10,... | collective-permute-start | bytes 24584 | tf_op jit(solution)/shard_map/ppermute | solution.py:714
  11.4 0.0 collective-permute-start.1
  11.4 0.8 %collective-permute-start = (f32[2,8,128]{2,1,0:T(8,128)S(1)}, f32[2,8,128]{2,1,0:T(8,128)S(1)}, u32[]{:S(2)}, u32[]{:S(2)}) collective-permute-start(f32[2,8,128]{2,1,0:T(8,128)S(1)} %copy-done), channel_id=1, source_target_pairs={{0,2},{1,3},{2,0},{3,1},{4,6},{5,7},{6,4},{7,5},{8,10},{9,11},{10,... | collective-permute-start | bytes 24584 | tf_op jit(solution)/shard_map/ppermute | solution.py:714
  12.2 1.1 %collective-permute-done.2.refs_3_ = f32[2,8,128]{2,1,0:T(8,128)S(1)} collective-permute-done((f32[2,8,128]{2,1,0:T(8,128)S(1)}, f32[2,8,128]{2,1,0:T(8,128)S(1)}, u32[]{:S(2)}, u32[]{:S(2)}) %collective-permute-start.2) | collective-permute-done | bytes 8224 | tf_op jit(solution)/shard_map/ppermute | solution.py:714
  13.3 1.8 %collective-permute-done.1.refs_2_ = f32[2,8,128]{2,1,0:T(8,128)S(1)} collective-permute-done((f32[2,8,128]{2,1,0:T(8,128)S(1)}, f32[2,8,128]{2,1,0:T(8,128)S(1)}, u32[]{:S(2)}, u32[]{:S(2)}) %collective-permute-start.1) | collective-permute-done | bytes 8224 | tf_op jit(solution)/shard_map/ppermute | solution.py:714
  15.1 0.9 %collective-permute-done.refs_1_ = f32[2,8,128]{2,1,0:T(8,128)S(1)} collective-permute-done((f32[2,8,128]{2,1,0:T(8,128)S(1)}, f32[2,8,128]{2,1,0:T(8,128)S(1)}, u32[]{:S(2)}, u32[]{:S(2)}) %collective-permute-start) | collective-permute-done | bytes 8224 | tf_op jit(solution)/shard_map/ppermute | solution.py:714
  16.0 0.8 %spread.1 = f32[8,4,2,8,128]{4,3,2,1,0:T(8,128)} custom-call(f32[2,8,128]{2,1,0:T(8,128)S(1)} %copy-done, f32[2,8,128]{2,1,0:T(8,128)S(1)} %collective-permute-done.refs_1_, f32[2,8,128]{2,1,0:T(8,128)S(1)} %collective-permute-done.1.refs_2_, f32[2,8,128]{2,1,0:T(8,128)S(1)} %collective-permute-done.2.refs_3_), custom_call_target="tpu_custom_call" | custom-call | tf_op jit(solution)/shard_map/spread/pallas_call | solution.py:685
  16.8 0.0 all-to-all-done.1.packed_ref
  16.8 4.1 %all-to-all-start = ((f32[8,4,2,8,128]{4,3,2,1,0:T(8,128)}), f32[8,4,2,8,128]{4,3,2,1,0:T(8,128)S(1)}, u32[]{:S(2)}, u32[]{:S(2)}) async-start(f32[8,4,2,8,128]{4,3,2,1,0:T(8,128)} %spread.1), calls=%async_computation | async-start | bytes 524288 | tf_op jit(solution)/shard_map/all_to_all | solution.py:731
  20.9 0.2 arrange.1
  21.1 0.6 %collective-permute-start.3 = (f32[264,128]{1,0:T(8,128)S(1)}, f32[264,128]{1,0:T(8,128)S(1)}, u32[]{:S(2)}, u32[]{:S(2)}) collective-permute-start(f32[264,128]{1,0:T(8,128)S(1)} %get-tuple-element.10), channel_id=1, source_target_pairs={{0,8},{8,0},{16,24},{24,16},{28,20},{20,28},{12,4},{4,12},{5,13},{... | collective-permute-start | bytes 405512 | tf_op jit(solution)/shard_map/ppermute | solution.py:738
  21.7 0.7 %collective-permute-start.4 = (f32[264,128]{1,0:T(8,128)S(1)}, f32[264,128]{1,0:T(8,128)S(1)}, u32[]{:S(2)}, u32[]{:S(2)}) collective-permute-start(f32[264,128]{1,0:T(8,128)S(1)} %get-tuple-element.11), channel_id=1, source_target_pairs={{8,16},{16,8},{24,28},{28,24},{20,12},{12,20},{4,5},{5,4},{13,21},... | collective-permute-start | bytes 405512 | tf_op jit(solution)/shard_map/ppermute | solution.py:738
  23.0 4.4 %all-to-all-done.copies_ref = f32[8,4,2,8,128]{4,3,2,1,0:T(8,128)S(1)} async-done(((f32[8,4,2,8,128]{4,3,2,1,0:T(8,128)}), f32[8,4,2,8,128]{4,3,2,1,0:T(8,128)S(1)}, u32[]{:S(2)}, u32[]{:S(2)}) %all-to-all-start) | async-done | bytes 262176 | tf_op jit(solution)/shard_map/all_to_all | solution.py:731
  27.4 1.3 %level.1.share_ref = f32[2,32,128]{2,1,0:T(8,128)S(1)} custom-call(s32[1]{0:T(128)} %bitcast.1.step_ref, f32[8,4,2,8,128]{4,3,2,1,0:T(8,128)S(1)} %all-to-all-done.copies_ref), custom_call_target="tpu_custom_call" | custom-call | tf_op jit(solution)/shard_map/level/pallas_call | solution.py:685
  28.8 0.0 collective-permute-done.3.near_ref
  28.8 0.0 collective-permute-done.4.far_ref
  28.8 1.7 %flow.1 = f32[8,5,8,128]{3,2,1,0:T(8,128)S(1)} custom-call(f32[2,32,128]{2,1,0:T(8,128)S(1)} %level.1.share_ref, f32[40,16,128]{2,1,0:T(8,128)S(1)} %get-tuple-element.9.body_ref, f32[264,128]{1,0:T(8,128)S(1)} %collective-permute-done.3.near_ref, f32[264,128]{1,0:T(8,128)S(1)} %collective-permute-done.4.far_ref), custom_call_target="tpu_custom_call" | custom-call | tf_op jit(solution)/shard_map/flow/pallas_call | solution.py:685
  30.5 8.3 %all_to_all.15.packed_ref = f32[8,5,8,128]{3,2,1,0:T(8,128)S(1)} all-to-all(f32[8,5,8,128]{3,2,1,0:T(8,128)S(1)} %flow.1), channel_id=1, replica_groups=mesh['grp'=4,'gy'=2,'gx'=4] {'grp','gy'}, dimensions={0} | all-to-all | bytes 327680 | tf_op jit(solution)/shard_map/all_to_all | solution.py:767
  38.8 0.8 %result.1 = (f32[19,2,8,128]{3,2,1,0:T(8,128)}, f32[2,8,128]{2,1,0:T(8,128)}) custom-call(f32[8,5,8,128]{3,2,1,0:T(8,128)S(1)} %all_to_all.15.packed_ref), custom_call_target="tpu_custom_call" | custom-call | tf_op jit(solution)/shard_map/result/pallas_call | solution.py:685
Async XLA Ops:
  2.5 5.2 %copy-start = (f32[2,8,128]{2,1,0:T(8,128)S(1)}, f32[2,8,128]{2,1,0:T(8,128)}, u32[]{:S(2)}) copy-start(f32[2,8,128]{2,1,0:T(8,128)} %get-tuple-element.7.refs_0_) | copy-start | bytes 24580
  2.6 14.2 %all-to-all-start.1 = ((f32[8,5,2,8,128]{4,3,2,1,0:T(8,128)}), f32[8,5,2,8,128]{4,3,2,1,0:T(8,128)S(1)}, u32[]{:S(2)}, u32[]{:S(2)}) async-start(f32[8,5,2,8,128]{4,3,2,1,0:T(8,128)} %get-tuple-element.8), calls=%async_computation.1 | async-start | bytes 655360 | tf_op jit(solution)/shard_map/all_to_all | solution.py:711
  7.7 5.5 %collective-permute-start.2 = (f32[2,8,128]{2,1,0:T(8,128)S(1)}, f32[2,8,128]{2,1,0:T(8,128)S(1)}, u32[]{:S(2)}, u32[]{:S(2)}) collective-permute-start(f32[2,8,128]{2,1,0:T(8,128)S(1)} %copy-done), channel_id=1, source_target_pairs={{0,3},{1,2},{2,1},{3,0},{4,7},{5,6},{6,5},{7,4},{8,11},{9,10},{10,... | collective-permute-start | bytes 24584 | tf_op jit(solution)/shard_map/ppermute | solution.py:714
  11.4 3.7 %collective-permute-start.1 = (f32[2,8,128]{2,1,0:T(8,128)S(1)}, f32[2,8,128]{2,1,0:T(8,128)S(1)}, u32[]{:S(2)}, u32[]{:S(2)}) collective-permute-start(f32[2,8,128]{2,1,0:T(8,128)S(1)} %copy-done), channel_id=1, source_target_pairs={{0,1},{1,0},{2,3},{3,2},{4,5},{5,4},{6,7},{7,6},{8,9},{9,8},{10,11... | collective-permute-start | bytes 24584 | tf_op jit(solution)/shard_map/ppermute | solution.py:714
  11.4 4.5 %collective-permute-start = (f32[2,8,128]{2,1,0:T(8,128)S(1)}, f32[2,8,128]{2,1,0:T(8,128)S(1)}, u32[]{:S(2)}, u32[]{:S(2)}) collective-permute-start(f32[2,8,128]{2,1,0:T(8,128)S(1)} %copy-done), channel_id=1, source_target_pairs={{0,2},{1,3},{2,0},{3,1},{4,6},{5,7},{6,4},{7,5},{8,10},{9,11},{10,... | collective-permute-start | bytes 24584 | tf_op jit(solution)/shard_map/ppermute | solution.py:714
  16.8 10.7 %all-to-all-start = ((f32[8,4,2,8,128]{4,3,2,1,0:T(8,128)}), f32[8,4,2,8,128]{4,3,2,1,0:T(8,128)S(1)}, u32[]{:S(2)}, u32[]{:S(2)}) async-start(f32[8,4,2,8,128]{4,3,2,1,0:T(8,128)} %spread.1), calls=%async_computation | async-start | bytes 524288 | tf_op jit(solution)/shard_map/all_to_all | solution.py:731
  21.1 7.7 %collective-permute-start.3 = (f32[264,128]{1,0:T(8,128)S(1)}, f32[264,128]{1,0:T(8,128)S(1)}, u32[]{:S(2)}, u32[]{:S(2)}) collective-permute-start(f32[264,128]{1,0:T(8,128)S(1)} %get-tuple-element.10), channel_id=1, source_target_pairs={{0,8},{8,0},{16,24},{24,16},{28,20},{20,28},{12,4},{4,12},{5,13},{... | collective-permute-start | bytes 405512 | tf_op jit(solution)/shard_map/ppermute | solution.py:738
  21.7 7.1 %collective-permute-start.4 = (f32[264,128]{1,0:T(8,128)S(1)}, f32[264,128]{1,0:T(8,128)S(1)}, u32[]{:S(2)}, u32[]{:S(2)}) collective-permute-start(f32[264,128]{1,0:T(8,128)S(1)} %get-tuple-element.11), channel_id=1, source_target_pairs={{8,16},{16,8},{24,28},{28,24},{20,12},{12,20},{4,5},{5,4},{13,21},... | collective-permute-start | bytes 405512 | tf_op jit(solution)/shard_map/ppermute | solution.py:738

commit v16 on v15

--- a/solution.py
+++ b/solution.py
@@ -501,7 +501,7 @@
 
 
 def flow_kernel(
-    rows, splits, size, share_ref, body_ref, near_ref, far_ref, packed_ref,
+    rows, splits, size, share_ref, body_ref, far_ref, near_ref, packed_ref,
     cotangent_ref, even_ref, odd_ref, kept_ref, grad_ref, smooth_ref, output_ref,
 ):
     devices = packed_ref.shape[0]
@@ -737,7 +737,7 @@
         pairs = [order[b : b + 2] for b in range(start, size * plane - 1, 2)]
         return lax.ppermute(value, line, [pair for i, j in pairs for pair in ((i, j), (j, i))])
 
-    far, near = exchange(far, 1), exchange(near, 0)
+    near, far = exchange(near, 0), exchange(far, 1)
     columns = size * LANES
     share = call(
         functools.partial(level_kernel, rows, splits, size),
@@ -760,7 +760,7 @@
         functools.partial(flow_kernel, rows, splits, size),
         ((plane, 5, 8, LANES),),
         "flow",
-        (share, body, near, far),
+        (share, body, far, near),
         [vmem] * 4,
         [vmem(shape, real) for shape in shapes],
     )

time: 40 us -> 39.8 us (level)
  starting transfers between devices: 15 us -> 17.9 us
  waiting for transfers between devices: 8.21 us -> 5.32 us
    all_to_all x1, waiting for transfers between devices: 4.43 us -> 1.54 us  [body_by_columns(): copies = lax.all_to_all(copies, ('grp', 'gy'), 0, 0)]
    ppermute x2, starting transfers between devices: 1.23 us -> 4.11 us  [exchange(): lax.ppermute(value, line, [pair for i, j in pairs for pair in ((i, j), (j...]
  transfers between devices with their start and end apart: 7 -> 7, of which waited for: 4 -> 4; matrix products, arithmetic and copies ran while one was open for 0% -> 0% of each run, Pallas kernels for 6% -> 5%
where the time goes in v16:
time: 39.8 us; the launch traced here: 39.3 us
  starting transfers between devices  17.9 us (45%)
  blocking collectives  8.32 us (21%)
  Pallas kernels  6.45 us (16%)
  waiting for transfers between devices  5.32 us (13%)
  between operations  1.35 us (3%)
    all_to_all x1, blocking collectives, body_by_columns(): packed = lax.all_to_all(packed, ('grp', 'gy'), 0, 0)  8.32 us
    pallas_call x6, Pallas kernels, call(): pl.pallas_call(kernel, out_shape=shapes if many else shapes[0], in_specs=...  6.45 us
    all_to_all x1, starting transfers between devices, body_by_columns(): packed = lax.all_to_all(packed, ('grp', 'gy'), 0, 0)  5.18 us
    ppermute x3, starting transfers between devices, body_by_columns(): lax.ppermute(design, 'gx', [(i, i ^ turn) for i in range(size)])  4.45 us
    all_to_all x1, starting transfers between devices, body_by_columns(): copies = lax.all_to_all(copies, ('grp', 'gy'), 0, 0)  4.14 us
    ppermute x2, starting transfers between devices, exchange(): lax.ppermute(value, line, [pair for i, j in pairs for pair in ((i, j), (j...  4.11 us
    ppermute x3, waiting for transfers between devices, body_by_columns(): lax.ppermute(design, 'gx', [(i, i ^ turn) for i in range(size)])  3.77 us
    all_to_all x1, waiting for transfers between devices, body_by_columns(): copies = lax.all_to_all(copies, ('grp', 'gy'), 0, 0)  1.54 us
  transfers between devices with their start and end apart: 7, of which 4 were waited for; matrix products, arithmetic and copies ran while one was open for 0% of the time, Pallas kernels for 5%

profile of v16, /device:TPU:0, one launch (start us, length us, event | category | flops | bytes accessed | tf_op | source)
XLA Modules:
  0.0 39.3 jit_solution(1926800403586415454)
XLA Ops:
  0.6 1.9 %pack.1 = (f32[2,8,128]{2,1,0:T(8,128)}, f32[8,5,2,8,128]{4,3,2,1,0:T(8,128)}) custom-call(f32[2,8,128]{2,1,0:T(8,128)} %design_ref.1, f32[19,2,8,128]{3,2,1,0:T(8,128)} %populations_ref.1, f32[19,2,8,128]{3,2,1,0:T(8,128)} %cotangent_ref.1, s32[2,8,128]{2,1,0:T(8,128)} %wall_ref.1, s32[2,8,128]{2,1,0:T(8,128)} %inlet_ref.1), custom_call_target="tpu_custom_call" | custom-call | tf_op jit(solution)/shard_map/pack/pallas_call | solution.py:685
  2.5 0.0 copy-start
  2.6 5.2 %all-to-all-start.1 = ((f32[8,5,2,8,128]{4,3,2,1,0:T(8,128)}), f32[8,5,2,8,128]{4,3,2,1,0:T(8,128)S(1)}, u32[]{:S(2)}, u32[]{:S(2)}) async-start(f32[8,5,2,8,128]{4,3,2,1,0:T(8,128)} %get-tuple-element.8), calls=%async_computation.1 | async-start | bytes 655360 | tf_op jit(solution)/shard_map/all_to_all | solution.py:711
  7.7 0.0 copy-done
  7.7 3.7 %collective-permute-start.2 = (f32[2,8,128]{2,1,0:T(8,128)S(1)}, f32[2,8,128]{2,1,0:T(8,128)S(1)}, u32[]{:S(2)}, u32[]{:S(2)}) collective-permute-start(f32[2,8,128]{2,1,0:T(8,128)S(1)} %copy-done), channel_id=1, source_target_pairs={{0,3},{1,2},{2,1},{3,0},{4,7},{5,6},{6,5},{7,4},{8,11},{9,10},{10,... | collective-permute-start | bytes 24584 | tf_op jit(solution)/shard_map/ppermute | solution.py:714
  11.4 0.0 collective-permute-start.1
  11.4 0.8 %collective-permute-start = (f32[2,8,128]{2,1,0:T(8,128)S(1)}, f32[2,8,128]{2,1,0:T(8,128)S(1)}, u32[]{:S(2)}, u32[]{:S(2)}) collective-permute-start(f32[2,8,128]{2,1,0:T(8,128)S(1)} %copy-done), channel_id=1, source_target_pairs={{0,2},{1,3},{2,0},{3,1},{4,6},{5,7},{6,4},{7,5},{8,10},{9,11},{10,... | collective-permute-start | bytes 24584 | tf_op jit(solution)/shard_map/ppermute | solution.py:714
  12.2 1.1 %collective-permute-done.2.refs_3_ = f32[2,8,128]{2,1,0:T(8,128)S(1)} collective-permute-done((f32[2,8,128]{2,1,0:T(8,128)S(1)}, f32[2,8,128]{2,1,0:T(8,128)S(1)}, u32[]{:S(2)}, u32[]{:S(2)}) %collective-permute-start.2) | collective-permute-done | bytes 8224 | tf_op jit(solution)/shard_map/ppermute | solution.py:714
  13.3 1.8 %collective-permute-done.1.refs_2_ = f32[2,8,128]{2,1,0:T(8,128)S(1)} collective-permute-done((f32[2,8,128]{2,1,0:T(8,128)S(1)}, f32[2,8,128]{2,1,0:T(8,128)S(1)}, u32[]{:S(2)}, u32[]{:S(2)}) %collective-permute-start.1) | collective-permute-done | bytes 8224 | tf_op jit(solution)/shard_map/ppermute | solution.py:714
  15.1 0.9 %collective-permute-done.refs_1_ = f32[2,8,128]{2,1,0:T(8,128)S(1)} collective-permute-done((f32[2,8,128]{2,1,0:T(8,128)S(1)}, f32[2,8,128]{2,1,0:T(8,128)S(1)}, u32[]{:S(2)}, u32[]{:S(2)}) %collective-permute-start) | collective-permute-done | bytes 8224 | tf_op jit(solution)/shard_map/ppermute | solution.py:714
  16.0 0.8 %spread.1 = f32[8,4,2,8,128]{4,3,2,1,0:T(8,128)} custom-call(f32[2,8,128]{2,1,0:T(8,128)S(1)} %copy-done, f32[2,8,128]{2,1,0:T(8,128)S(1)} %collective-permute-done.refs_1_, f32[2,8,128]{2,1,0:T(8,128)S(1)} %collective-permute-done.1.refs_2_, f32[2,8,128]{2,1,0:T(8,128)S(1)} %collective-permute-done.2.refs_3_), custom_call_target="tpu_custom_call" | custom-call | tf_op jit(solution)/shard_map/spread/pallas_call | solution.py:685
  16.8 0.0 all-to-all-done.1.packed_ref
  16.8 4.1 %all-to-all-start = ((f32[8,4,2,8,128]{4,3,2,1,0:T(8,128)}), f32[8,4,2,8,128]{4,3,2,1,0:T(8,128)S(1)}, u32[]{:S(2)}, u32[]{:S(2)}) async-start(f32[8,4,2,8,128]{4,3,2,1,0:T(8,128)} %spread.1), calls=%async_computation | async-start | bytes 524288 | tf_op jit(solution)/shard_map/all_to_all | solution.py:731
  20.9 0.2 arrange.1
  21.1 0.7 %collective-permute-start.3 = (f32[264,128]{1,0:T(8,128)S(1)}, f32[264,128]{1,0:T(8,128)S(1)}, u32[]{:S(2)}, u32[]{:S(2)}) collective-permute-start(f32[264,128]{1,0:T(8,128)S(1)} %get-tuple-element.10), channel_id=1, source_target_pairs={{8,16},{16,8},{24,28},{28,24},{20,12},{12,20},{4,5},{5,4},{13,21},... | collective-permute-start | bytes 405512 | tf_op jit(solution)/shard_map/ppermute | solution.py:738
  21.8 3.4 %collective-permute-start.4 = (f32[264,128]{1,0:T(8,128)S(1)}, f32[264,128]{1,0:T(8,128)S(1)}, u32[]{:S(2)}, u32[]{:S(2)}) collective-permute-start(f32[264,128]{1,0:T(8,128)S(1)} %get-tuple-element.11), channel_id=1, source_target_pairs={{0,8},{8,0},{16,24},{24,16},{28,20},{20,28},{12,4},{4,12},{5,13},{... | collective-permute-start | bytes 405512 | tf_op jit(solution)/shard_map/ppermute | solution.py:738
  25.9 1.5 %all-to-all-done.copies_ref = f32[8,4,2,8,128]{4,3,2,1,0:T(8,128)S(1)} async-done(((f32[8,4,2,8,128]{4,3,2,1,0:T(8,128)}), f32[8,4,2,8,128]{4,3,2,1,0:T(8,128)S(1)}, u32[]{:S(2)}, u32[]{:S(2)}) %all-to-all-start) | async-done | bytes 262176 | tf_op jit(solution)/shard_map/all_to_all | solution.py:731
  27.4 1.1 %level.1.share_ref = f32[2,32,128]{2,1,0:T(8,128)S(1)} custom-call(s32[1]{0:T(128)} %bitcast.1.step_ref, f32[8,4,2,8,128]{4,3,2,1,0:T(8,128)S(1)} %all-to-all-done.copies_ref), custom_call_target="tpu_custom_call" | custom-call | tf_op jit(solution)/shard_map/level/pallas_call | solution.py:685
  28.6 0.0 collective-permute-done.3.far_ref
  28.6 0.0 collective-permute-done.4.near_ref
  28.6 1.7 %flow.1 = f32[8,5,8,128]{3,2,1,0:T(8,128)S(1)} custom-call(f32[2,32,128]{2,1,0:T(8,128)S(1)} %level.1.share_ref, f32[40,16,128]{2,1,0:T(8,128)S(1)} %get-tuple-element.9.body_ref, f32[264,128]{1,0:T(8,128)S(1)} %collective-permute-done.3.far_ref, f32[264,128]{1,0:T(8,128)S(1)} %collective-permute-done.4.near_ref), custom_call_target="tpu_custom_call" | custom-call | tf_op jit(solution)/shard_map/flow/pallas_call | solution.py:685
  30.2 8.3 %all_to_all.15.packed_ref = f32[8,5,8,128]{3,2,1,0:T(8,128)S(1)} all-to-all(f32[8,5,8,128]{3,2,1,0:T(8,128)S(1)} %flow.1), channel_id=1, replica_groups=mesh['grp'=4,'gy'=2,'gx'=4] {'grp','gy'}, dimensions={0} | all-to-all | bytes 327680 | tf_op jit(solution)/shard_map/all_to_all | solution.py:767
  38.6 0.8 %result.1 = (f32[19,2,8,128]{3,2,1,0:T(8,128)}, f32[2,8,128]{2,1,0:T(8,128)}) custom-call(f32[8,5,8,128]{3,2,1,0:T(8,128)S(1)} %all_to_all.15.packed_ref), custom_call_target="tpu_custom_call" | custom-call | tf_op jit(solution)/shard_map/result/pallas_call | solution.py:685
Async XLA Ops:
  2.5 5.2 %copy-start = (f32[2,8,128]{2,1,0:T(8,128)S(1)}, f32[2,8,128]{2,1,0:T(8,128)}, u32[]{:S(2)}) copy-start(f32[2,8,128]{2,1,0:T(8,128)} %get-tuple-element.7.refs_0_) | copy-start | bytes 24580
  2.6 14.2 %all-to-all-start.1 = ((f32[8,5,2,8,128]{4,3,2,1,0:T(8,128)}), f32[8,5,2,8,128]{4,3,2,1,0:T(8,128)S(1)}, u32[]{:S(2)}, u32[]{:S(2)}) async-start(f32[8,5,2,8,128]{4,3,2,1,0:T(8,128)} %get-tuple-element.8), calls=%async_computation.1 | async-start | bytes 655360 | tf_op jit(solution)/shard_map/all_to_all | solution.py:711
  7.7 5.5 %collective-permute-start.2 = (f32[2,8,128]{2,1,0:T(8,128)S(1)}, f32[2,8,128]{2,1,0:T(8,128)S(1)}, u32[]{:S(2)}, u32[]{:S(2)}) collective-permute-start(f32[2,8,128]{2,1,0:T(8,128)S(1)} %copy-done), channel_id=1, source_target_pairs={{0,3},{1,2},{2,1},{3,0},{4,7},{5,6},{6,5},{7,4},{8,11},{9,10},{10,... | collective-permute-start | bytes 24584 | tf_op jit(solution)/shard_map/ppermute | solution.py:714
  11.4 3.7 %collective-permute-start.1 = (f32[2,8,128]{2,1,0:T(8,128)S(1)}, f32[2,8,128]{2,1,0:T(8,128)S(1)}, u32[]{:S(2)}, u32[]{:S(2)}) collective-permute-start(f32[2,8,128]{2,1,0:T(8,128)S(1)} %copy-done), channel_id=1, source_target_pairs={{0,1},{1,0},{2,3},{3,2},{4,5},{5,4},{6,7},{7,6},{8,9},{9,8},{10,11... | collective-permute-start | bytes 24584 | tf_op jit(solution)/shard_map/ppermute | solution.py:714
  11.4 4.5 %collective-permute-start = (f32[2,8,128]{2,1,0:T(8,128)S(1)}, f32[2,8,128]{2,1,0:T(8,128)S(1)}, u32[]{:S(2)}, u32[]{:S(2)}) collective-permute-start(f32[2,8,128]{2,1,0:T(8,128)S(1)} %copy-done), channel_id=1, source_target_pairs={{0,2},{1,3},{2,0},{3,1},{4,6},{5,7},{6,4},{7,5},{8,10},{9,11},{10,... | collective-permute-start | bytes 24584 | tf_op jit(solution)/shard_map/ppermute | solution.py:714
  16.8 10.7 %all-to-all-start = ((f32[8,4,2,8,128]{4,3,2,1,0:T(8,128)}), f32[8,4,2,8,128]{4,3,2,1,0:T(8,128)S(1)}, u32[]{:S(2)}, u32[]{:S(2)}) async-start(f32[8,4,2,8,128]{4,3,2,1,0:T(8,128)} %spread.1), calls=%async_computation | async-start | bytes 524288 | tf_op jit(solution)/shard_map/all_to_all | solution.py:731
  21.1 7.4 %collective-permute-start.3 = (f32[264,128]{1,0:T(8,128)S(1)}, f32[264,128]{1,0:T(8,128)S(1)}, u32[]{:S(2)}, u32[]{:S(2)}) collective-permute-start(f32[264,128]{1,0:T(8,128)S(1)} %get-tuple-element.10), channel_id=1, source_target_pairs={{8,16},{16,8},{24,28},{28,24},{20,12},{12,20},{4,5},{5,4},{13,21},... | collective-permute-start | bytes 405512 | tf_op jit(solution)/shard_map/ppermute | solution.py:738
  21.8 6.8 %collective-permute-start.4 = (f32[264,128]{1,0:T(8,128)S(1)}, f32[264,128]{1,0:T(8,128)S(1)}, u32[]{:S(2)}, u32[]{:S(2)}) collective-permute-start(f32[264,128]{1,0:T(8,128)S(1)} %get-tuple-element.11), channel_id=1, source_target_pairs={{0,8},{8,0},{16,24},{24,16},{28,20},{20,28},{12,4},{4,12},{5,13},{... | collective-permute-start | bytes 405512 | tf_op jit(solution)/shard_map/ppermute | solution.py:738
